TPU v7x, 32 devices: a whole 2x2x4 slice. The times are simulated.
32 devices in a mesh: dp: 16 (over z, y, core), mp: 2 (over x).
Axes of the slice: x: 2, y: 2, z: 4, core: 2. Of those that a mesh axis runs over, the one named last changes fastest.
Arguments:
- cell_input: bfloat16 [8192, 512], P(('dp', 'mp')), may hold values from -6 to 6
- lengths: int32 [32], P(('dp', 'mp')), may hold values from 64 to 256, as said below
- out_grad: bfloat16 [8192, 512], P(('dp', 'mp')), may hold values from -6 to 6
- norm_params: bfloat16 [4, 2, 512], replicated, may hold values from -0.9 to 1.5, as said below
- gated_weight: bfloat16 [512, 1024], replicated, may hold values from -0.25 to 0.25
- gated_bias: bfloat16 [1024], replicated, may hold values from -3 to 3
- left_weight: bfloat16 [512, 2048], P(None, 'mp'), may hold values from -0.25 to 0.25
- left_bias: bfloat16 [2048], P('mp'), may hold values from -3.6 to 3.6
- conv_weight: bfloat16 [3, 512, 256], replicated, may hold values from -0.15625 to 0.15625
- conv_bias: bfloat16 [256], replicated, may hold values from -3 to 3
- inner_norm: bfloat16 [2, 2048], P(None, 'mp'), may hold values from -0.9 to 1.5, as said below
- depth_weight: bfloat16 [9, 2048], P(None, 'mp'), may hold values from -2 to 2
- point_weight: bfloat16 [2048, 256], P('mp'), may hold values from -0.125 to 0.125
- point_bias: bfloat16 [256], replicated, may hold values from -3 to 3
- project_weight: bfloat16 [512, 1536], replicated, may hold values from -0.25 to 0.25
- project_bias: bfloat16 [2, 512], replicated, may hold values from -3 to 3
- output_weight: bfloat16 [512, 512], replicated, may hold values from -2 to 2
- output_bias: bfloat16 [512], replicated, may hold values from -3 to 3
- expand_weight: bfloat16 [512, 2048], P(None, 'mp'), may hold values from -0.25 to 0.25
- expand_bias: bfloat16 [2048], P('mp'), may hold values from -3 to 3
- shrink_weight: bfloat16 [2048, 512], P('mp'), may hold values from -0.125 to 0.125
- shrink_bias: bfloat16 [512], replicated, may hold values from -3 to 3
Outputs:
- cell_output: bfloat16 [8192, 512], P(('dp', 'mp'))
- input_grad: float32 [8192, 512], P(('dp', 'mp'))
- grad_norm_params: float32 [4, 2, 512], replicated
- grad_gated_weight: float32 [512, 1024], replicated
- grad_gated_bias: float32 [1024], replicated
- grad_left_weight: float32 [512, 2048], P(None, 'mp')
- grad_left_bias: float32 [2048], P('mp')
- grad_conv_weight: float32 [3, 512, 256], replicated
- grad_conv_bias: float32 [256], replicated
- grad_inner_norm: float32 [2, 2048], P(None, 'mp')
- grad_depth_weight: float32 [9, 2048], P(None, 'mp')
- grad_point_weight: float32 [2048, 256], P('mp')
- grad_point_bias: float32 [256], replicated
- grad_project_weight: float32 [512, 1536], replicated
- grad_project_bias: float32 [2, 512], replicated
- grad_output_weight: float32 [512, 512], replicated
- grad_output_bias: float32 [512], replicated
- grad_expand_weight: float32 [512, 2048], P(None, 'mp')
- grad_expand_bias: float32 [2048], P('mp')
- grad_shrink_weight: float32 [2048, 512], P('mp')
- grad_shrink_bias: float32 [512], replicated
Inputs may be any that keep to these rules, and one draw needn't show every extreme that they name: Positions below lengths[r] of row r are real tokens, the others padding; some row is full in every draw. `norm_params`: index 0 of the second dimension holds gains, index 1 biases. `inner_norm`: index 0 holds gains, index 1 biases.
All inputs are finite; a program needn't handle non-finite values.
Results may differ from a plain program's by a relative error of at most 0.02.
Values may be sent and summed in bfloat16 or wider, within the bound.
No kernel may reach another device: no remote copies, remote signals or barrier semaphores. Data moves between devices by JAX's collectives and lax.ppermute only.
A program may use at most 192 MiB of HBM per device.

v0:
```python
import jax
import jax.numpy as jnp
from jax import lax
from jax.sharding import PartitionSpec as P

HEADS = 8
FF = 2048
SEQ = 256


EPS = 1e-06


def as_low(values):
    return values.astype(jnp.bfloat16)


def matmul(left, right):
    return jnp.dot(left, right, preferred_element_type=jnp.float32)


def left_turned(left, right):
    return lax.dot_general(
        left, right, (((0,), (0,)), ((), ())), preferred_element_type=jnp.float32
    )


def right_turned(left, right):
    return lax.dot_general(
        left, right, (((1,), (1,)), ((), ())), preferred_element_type=jnp.float32
    )


def shift_rows(values, offset):
    channels = values.shape[1]
    framed = values.reshape(-1, SEQ, channels)
    if offset > 0:
        framed = jnp.pad(framed[:, offset:], ((0, 0), (0, offset), (0, 0)))
    elif offset < 0:
        framed = jnp.pad(framed[:, :offset], ((0, 0), (-offset, 0), (0, 0)))
    return framed.reshape(-1, channels)


def silu_slope(values):
    sigma = jax.nn.sigmoid(values)
    return sigma * (1.0 + values * (1.0 - sigma))


def layer_norm(values, gain, bias):
    centre = jnp.mean(values, -1, keepdims=True)
    centered = values - centre
    variance = jnp.mean(centered * centered, -1, keepdims=True)
    rstd = lax.rsqrt(variance + EPS)
    normed = centered * rstd
    return (normed * gain + bias, normed, rstd)


def norm_back(grad_out, normed, rstd, gain):
    scaled = grad_out * gain
    first_mean = jnp.mean(scaled, -1, keepdims=True)
    second_mean = jnp.mean(scaled * normed, -1, keepdims=True)
    grad_in = rstd * (scaled - first_mean - normed * second_mean)
    return (grad_in, jnp.stack([jnp.sum(grad_out * normed, 0), jnp.sum(grad_out, 0)]))


def scores_of(query_heads, key_heads, keep_rows, head_size):
    row_count = query_heads.shape[0]
    scores = jnp.einsum(
        "rqhd,rkhd->rhqk", query_heads, key_heads, preferred_element_type=jnp.float32
    )
    scores = scores * head_size ** (-0.5)
    return jnp.where(keep_rows.reshape(row_count, 1, 1, SEQ) > 0, scores, -1000000000.0)


def attend_forward(queries, keys, values, keep_rows):
    row_count = queries.shape[0] // SEQ
    head_size = queries.shape[1] // HEADS
    shape = (row_count, SEQ, HEADS, head_size)
    scores = scores_of(queries.reshape(shape), keys.reshape(shape), keep_rows, head_size)
    highest = jnp.max(scores, -1, keepdims=True)
    weights = jnp.exp(scores - highest)
    total = jnp.sum(weights, -1, keepdims=True)
    probs_low = as_low(weights / total)
    mixed = jnp.einsum(
        "rhqk,rkhd->rqhd", probs_low, values.reshape(shape), preferred_element_type=jnp.float32
    )
    return (mixed.reshape(queries.shape), highest + jnp.log(total))


def attend_backward(queries, keys, values, log_total, grad_attended, keep_rows):
    row_count = queries.shape[0] // SEQ
    head_size = queries.shape[1] // HEADS
    shape = (row_count, SEQ, HEADS, head_size)
    query_heads = queries.reshape(shape)
    key_heads = keys.reshape(shape)
    grad_heads = grad_attended.reshape(shape)
    scores = scores_of(query_heads, key_heads, keep_rows, head_size)
    probs = jnp.exp(scores - log_total)
    probs_low = as_low(probs)
    grad_values = jnp.einsum(
        "rhqk,rqhd->rkhd", probs_low, grad_heads, preferred_element_type=jnp.float32
    )
    grad_probs = jnp.einsum(
        "rqhd,rkhd->rhqk", grad_heads, values.reshape(shape), preferred_element_type=jnp.float32
    )
    weighted = jnp.sum(grad_probs * probs, -1, keepdims=True)
    grad_scores = as_low(probs * (grad_probs - weighted))
    grad_queries = jnp.einsum(
        "rhqk,rkhd->rqhd", grad_scores, key_heads, preferred_element_type=jnp.float32
    ) * head_size ** (-0.5)
    grad_keys = jnp.einsum(
        "rhqk,rqhd->rkhd", grad_scores, query_heads, preferred_element_type=jnp.float32
    ) * head_size ** (-0.5)
    flat = queries.shape
    return (grad_queries.reshape(flat), grad_keys.reshape(flat), grad_values.reshape(flat))


def depthwise(values, taps):
    result = jnp.zeros_like(values)
    for tap in range(9):
        result = result + shift_rows(values, tap - 4) * taps[tap]
    return result


def inner_forward(
    rows_two, right_rows, keep_rows, left_w, left_b, norm_w, depth_w, offset, total_of
):
    channels = left_w.shape[1]
    left_pre = matmul(rows_two, left_w) + left_b.astype(jnp.float32)
    padded_right = jnp.pad(right_rows, ((0, 0), (0, channels)))
    right_part = lax.dynamic_slice_in_dim(padded_right, offset, channels, 1).astype(jnp.float32)
    mixed = jax.nn.silu(left_pre) + right_part
    sums = total_of((jnp.sum(mixed, 1), jnp.sum(mixed * mixed, 1)))
    centre = sums[0] / FF
    variance = sums[1] / FF - centre * centre
    rstd = lax.rsqrt(variance + EPS)[:, None]
    normed = (mixed - centre[:, None]) * rstd
    gains = norm_w.astype(jnp.float32)
    normal_out = (normed * gains[0] + gains[1]) * keep_rows[:, None]
    depth_low = as_low(depthwise(normal_out, depth_w.astype(jnp.float32)))
    return (left_pre, normed, rstd, normal_out, depth_low)


def inner_backward(
    grad_sep_rows, saved, rows_two, keep_rows, left_w, norm_w, depth_w, point_w, offset, total_of
):
    left_pre, normed, rstd, normal_out, depth_low = saved
    token_count = rows_two.shape[0]
    half_width = grad_sep_rows.shape[1]
    channels = left_w.shape[1]
    grad_point = left_turned(depth_low, grad_sep_rows)
    grad_depth = right_turned(grad_sep_rows, point_w)
    taps = depth_w.astype(jnp.float32)
    grad_taps = jnp.stack(
        [jnp.sum(shift_rows(normal_out, tap - 4) * grad_depth, 0) for tap in range(9)]
    )
    grad_normal = jnp.zeros_like(grad_depth)
    for tap in range(9):
        grad_normal = grad_normal + shift_rows(grad_depth * taps[tap], 4 - tap)
    grad_normal = grad_normal * keep_rows[:, None]
    gains = norm_w.astype(jnp.float32)
    scaled = grad_normal * gains[0]
    sums = total_of((jnp.sum(scaled, 1), jnp.sum(scaled * normed, 1)))
    grad_mixed = rstd * (scaled - sums[0][:, None] / FF - normed * sums[1][:, None] / FF)
    grad_norm = jnp.stack([jnp.sum(grad_normal * normed, 0), jnp.sum(grad_normal, 0)])
    grad_left_pre = as_low(grad_mixed * silu_slope(left_pre))
    grad_left_b = jnp.sum(grad_left_pre.astype(jnp.float32), 0)
    grad_left_w = left_turned(rows_two, grad_left_pre)
    grad_rows_two = right_turned(grad_left_pre, left_w)
    placed = lax.dynamic_update_slice_in_dim(
        jnp.zeros((token_count, half_width + channels), jnp.float32), grad_mixed, offset, 1
    )
    grad_right = placed[:, :half_width]
    return (grad_rows_two, grad_right, (grad_left_w, grad_left_b, grad_norm, grad_taps, grad_point))


def body(
    cell_input,
    lengths,
    out_grad,
    norm_params,
    gated_weight,
    gated_bias,
    left_weight,
    left_bias,
    conv_weight,
    conv_bias,
    inner_norm,
    depth_weight,
    point_weight,
    point_bias,
    project_weight,
    project_bias,
    output_weight,
    output_bias,
    expand_weight,
    expand_bias,
    shrink_weight,
    shrink_bias,
):
    width = cell_input.shape[1]
    half_width = conv_weight.shape[2]
    positions = jnp.arange(SEQ, dtype=jnp.int32)
    keep = (positions[None, :] < lengths[:, None]).astype(jnp.float32).reshape(-1)
    start_x = cell_input.astype(jnp.float32)
    norms = norm_params.astype(jnp.float32)
    norm_one, normed_one, rstd_one = layer_norm(start_x, norms[0, 0], norms[0, 1])
    low_one = as_low(norm_one)
    gated_pre = matmul(low_one, gated_weight) + gated_bias.astype(jnp.float32)
    values_one = gated_pre[:, :width]
    gates_one = jax.nn.sigmoid(gated_pre[:, width:])
    resid_one = start_x + values_one * gates_one
    norm_two, normed_two, rstd_two = layer_norm(resid_one, norms[1, 0], norms[1, 1])
    low_two = as_low(norm_two * keep[:, None])
    stacked = jnp.concatenate([shift_rows(low_two, -1), low_two, shift_rows(low_two, 1)], 1)
    conv_flat = conv_weight.reshape(3 * width, half_width)
    right_pre = matmul(stacked, conv_flat) + conv_bias.astype(jnp.float32)
    right_low = as_low(jax.nn.silu(right_pre))
    left_all, left_bias_all, inner_all, depth_all = (
        left_weight,
        left_bias,
        inner_norm,
        depth_weight,
    )
    point_all, expand_all, expand_bias_all, shrink_all = (
        point_weight,
        expand_weight,
        expand_bias,
        shrink_weight,
    )
    rows_two, right_rows, keep_low = (
        lax.all_gather(low_two, "mp", axis=0, tiled=True),
        lax.all_gather(right_low, "mp", axis=0, tiled=True),
        lax.all_gather(as_low(keep), "mp", axis=0, tiled=True),
    )
    keep_rows = keep_low.astype(jnp.float32)
    offset = lax.axis_index("mp") * left_weight.shape[1]

    def forward_total(pair):
        return lax.psum(pair, "mp")

    saved = inner_forward(
        rows_two,
        right_rows,
        keep_rows,
        left_all,
        left_bias_all,
        inner_all,
        depth_all,
        offset,
        forward_total,
    )
    depth_low = saved[4]
    sep_part = lax.psum_scatter(
        matmul(depth_low, point_all).astype(jnp.bfloat16), "mp", scatter_dimension=0, tiled=True
    ).astype(jnp.float32)
    sep = sep_part + point_bias.astype(jnp.float32)
    resid_two = resid_one + jnp.pad(sep, ((0, 0), (0, width - half_width)))
    norm_four, normed_four, rstd_four = layer_norm(resid_two, norms[2, 0], norms[2, 1])
    low_four = as_low(norm_four)
    projected = matmul(low_four, project_weight)
    biases = project_bias.astype(jnp.float32)
    queries = as_low(projected[:, :width] + biases[0])
    keys = as_low(projected[:, width : 2 * width])
    values = as_low(projected[:, 2 * width :] + biases[1])
    attended, log_total = attend_forward(queries, keys, values, keep)
    attended_low = as_low(attended)
    resid_three = resid_two + matmul(attended_low, output_weight) + output_bias.astype(jnp.float32)
    norm_five, normed_five, rstd_five = layer_norm(resid_three, norms[3, 0], norms[3, 1])
    low_five = as_low(norm_five)
    rows_five = lax.all_gather(low_five, "mp", axis=0, tiled=True)
    expand_pre = matmul(rows_five, expand_all) + expand_bias_all.astype(jnp.float32)
    hidden_low = as_low(jax.nn.silu(expand_pre))
    shrunk = lax.psum_scatter(
        matmul(hidden_low, shrink_all).astype(jnp.bfloat16), "mp", scatter_dimension=0, tiled=True
    ).astype(jnp.float32)
    cell_output = (resid_three + shrunk + shrink_bias.astype(jnp.float32)).astype(jnp.bfloat16)
    grad_top = out_grad.astype(jnp.float32)
    grad_shrink_bias = jnp.sum(grad_top, 0)
    grad_rows_top = lax.all_gather(out_grad, "mp", axis=0, tiled=True)
    grad_shrink = left_turned(hidden_low, grad_rows_top)
    grad_expand_pre = as_low(right_turned(grad_rows_top, shrink_all) * silu_slope(expand_pre))
    grad_expand_bias = jnp.sum(grad_expand_pre.astype(jnp.float32), 0)
    grad_expand = left_turned(rows_five, grad_expand_pre)
    grad_five = lax.psum_scatter(
        right_turned(grad_expand_pre, expand_all).astype(jnp.bfloat16),
        "mp",
        scatter_dimension=0,
        tiled=True,
    ).astype(jnp.float32)
    grad_in_five, grad_norm_five = norm_back(grad_five, normed_five, rstd_five, norms[3, 0])
    grad_three = grad_top + grad_in_five
    grad_attn_low = as_low(grad_three)
    grad_output_bias = jnp.sum(grad_attn_low.astype(jnp.float32), 0)
    grad_output_weight = left_turned(attended_low, grad_attn_low)
    grad_attended = as_low(right_turned(grad_attn_low, output_weight))
    grad_queries, grad_keys, grad_values = attend_backward(
        queries, keys, values, log_total, grad_attended, keep
    )
    grad_projected = as_low(jnp.concatenate([grad_queries, grad_keys, grad_values], 1))
    grad_project_weight = left_turned(low_four, grad_projected)
    grad_proj_float = grad_projected.astype(jnp.float32)
    grad_project_bias = jnp.stack(
        [jnp.sum(grad_proj_float[:, :width], 0), jnp.sum(grad_proj_float[:, 2 * width :], 0)]
    )
    grad_four = right_turned(grad_projected, project_weight)
    grad_in_four, grad_norm_four = norm_back(grad_four, normed_four, rstd_four, norms[2, 0])
    grad_two = grad_three + grad_in_four
    grad_sep = as_low(grad_two[:, :half_width])
    grad_point_bias = jnp.sum(grad_sep.astype(jnp.float32), 0)
    grad_sep_rows = lax.all_gather(grad_sep, "mp", axis=0, tiled=True)

    def backward_total(pair):
        return lax.psum(pair, "mp")

    grad_rows_part, grad_right_part, inner_parts = inner_backward(
        grad_sep_rows,
        saved,
        rows_two,
        keep_rows,
        left_all,
        inner_all,
        depth_all,
        point_all,
        offset,
        backward_total,
    )
    grad_low_left, grad_right = (
        lax.psum_scatter(
            grad_rows_part.astype(jnp.bfloat16), "mp", scatter_dimension=0, tiled=True
        ).astype(jnp.float32),
        lax.psum_scatter(
            grad_right_part.astype(jnp.bfloat16), "mp", scatter_dimension=0, tiled=True
        ).astype(jnp.float32),
    )
    grad_right_pre = as_low(grad_right * silu_slope(right_pre))
    grad_conv_bias = jnp.sum(grad_right_pre.astype(jnp.float32), 0)
    grad_conv_weight = left_turned(stacked, grad_right_pre).reshape(3, width, half_width)
    grad_stacked = right_turned(grad_right_pre, conv_flat)
    grad_low_two = (
        grad_low_left
        + shift_rows(grad_stacked[:, :width], 1)
        + grad_stacked[:, width : 2 * width]
        + shift_rows(grad_stacked[:, 2 * width :], -1)
    )
    grad_in_two, grad_norm_two = norm_back(
        grad_low_two * keep[:, None], normed_two, rstd_two, norms[1, 0]
    )
    grad_one = grad_two + grad_in_two
    grad_gated = as_low(
        jnp.concatenate(
            [grad_one * gates_one, grad_one * values_one * gates_one * (1.0 - gates_one)], 1
        )
    )
    grad_gated_bias = jnp.sum(grad_gated.astype(jnp.float32), 0)
    grad_gated_weight = left_turned(low_one, grad_gated)
    grad_in_one, grad_norm_one = norm_back(
        right_turned(grad_gated, gated_weight), normed_one, rstd_one, norms[0, 0]
    )
    input_grad = grad_one + grad_in_one
    grad_norms = jnp.stack([grad_norm_one, grad_norm_two, grad_norm_four, grad_norm_five])
    grad_left_w, grad_left_b, grad_inner, grad_taps, grad_point = inner_parts
    inner_set = (
        grad_left_w,
        grad_left_b,
        grad_inner,
        grad_taps,
        grad_point,
        grad_expand,
        grad_expand_bias,
        grad_shrink,
    )
    inner_set = (
        lax.psum(inner_set[0].astype(jnp.bfloat16), "dp").astype(jnp.float32),
        lax.psum(inner_set[1].astype(jnp.bfloat16), "dp").astype(jnp.float32),
        lax.psum(inner_set[2].astype(jnp.bfloat16), "dp").astype(jnp.float32),
        lax.psum(inner_set[3].astype(jnp.bfloat16), "dp").astype(jnp.float32),
        lax.psum(inner_set[4].astype(jnp.bfloat16), "dp").astype(jnp.float32),
        lax.psum(inner_set[5].astype(jnp.bfloat16), "dp").astype(jnp.float32),
        lax.psum(inner_set[6].astype(jnp.bfloat16), "dp").astype(jnp.float32),
        lax.psum(inner_set[7].astype(jnp.bfloat16), "dp").astype(jnp.float32),
    )
    shared = lax.psum(
        (
            grad_norms,
            grad_gated_weight,
            grad_gated_bias,
            grad_conv_weight,
            grad_conv_bias,
            grad_point_bias,
            grad_project_weight,
            grad_project_bias,
            grad_output_weight,
            grad_output_bias,
            grad_shrink_bias,
        ),
        ("dp", "mp"),
    )
    return (
        cell_output,
        input_grad,
        shared[0],
        shared[1],
        shared[2],
        inner_set[0],
        inner_set[1],
        shared[3],
        shared[4],
        inner_set[2],
        inner_set[3],
        inner_set[4],
        shared[5],
        shared[6],
        shared[7],
        shared[8],
        shared[9],
        inner_set[5],
        inner_set[6],
        inner_set[7],
        shared[10],
    )


def solution(mesh):
    return jax.shard_map(
        body,
        mesh=mesh,
        in_specs=(
            P(("dp", "mp"), None),
            P(("dp", "mp")),
            P(("dp", "mp"), None),
            P(),
            P(),
            P(),
            P(None, "mp"),
            P("mp"),
            P(),
            P(),
            P(None, "mp"),
            P(None, "mp"),
            P("mp", None),
            P(),
            P(),
            P(),
            P(),
            P(),
            P(None, "mp"),
            P("mp"),
            P("mp", None),
            P(),
        ),
        out_specs=(
            P(("dp", "mp"), None),
            P(("dp", "mp"), None),
            P(),
            P(),
            P(),
            P(None, "mp"),
            P("mp"),
            P(),
            P(),
            P(None, "mp"),
            P(None, "mp"),
            P("mp", None),
            P(),
            P(),
            P(),
            P(),
            P(),
            P(None, "mp"),
            P("mp"),
            P("mp", None),
            P(),
        ),
        check_vma=False,
    )
```

profile of v0, /device:TPU:0, one launch (start us, length us, event | category | flops | bytes accessed | tf_op | source)
XLA Modules:
  0.0 526.9 jit_solution(14225441652130429490)
XLA Ops:
  15.5 5.3 all-gather
  20.9 7.9 %all_gather.18 = bf16[512,512]{1,0:T(8,128)(2,1)S(1)} all-gather(bf16[256,512]{1,0:T(8,128)(2,1)S(1)} %multiply_convert_fusion.6), channel_id=1, replica_groups=mesh['dp'=16,'mp'=2] {'mp'}, dimensions={0}, use_global_device_ids=true | all-gather | bytes 786432 | tf_op jit(solution)/shard_map/all_gather | solution.py:232
  30.0 5.6 %all_gather.19 = bf16[512,256]{1,0:T(8,128)(2,1)S(1)} all-gather(bf16[256,256]{1,0:T(8,128)(2,1)S(1)} %get-tuple-element.141), channel_id=1, replica_groups=mesh['dp'=16,'mp'=2] {'mp'}, dimensions={0}, use_global_device_ids=true | all-gather | bytes 393216 | tf_op jit(solution)/shard_map/all_gather | solution.py:233
  35.6 4.3 fusion.71
  39.9 4.9 all-reduce.25
  44.8 2.1 add_multiply_fusion
  54.9 3.6 fusion.2
  61.4 7.3 %all_gather.22 = bf16[512,512]{1,0:T(8,128)(2,1)} all-gather(bf16[256,512]{1,0:T(8,128)(2,1)S(1)} %copy-done.67), channel_id=1, replica_groups=mesh['dp'=16,'mp'=2] {'mp'}, dimensions={0}, use_global_device_ids=true | all-gather | bytes 786432 | tf_op jit(solution)/shard_map/all_gather | solution.py:280
  68.8 5.3 %reduce-scatter.6.cloned.1.call-done = bf16[256,256]{1,0:T(8,128)(2,1)} async-done(((bf16[512,256]{1,0:T(8,128)(2,1)}), bf16[256,256]{1,0:T(8,128)(2,1)}) %reduce-scatter.6.cloned.1.call-update) | async-done | bytes 131088 | tf_op jit(solution)/shard_map/reduce_scatter | solution.py:254
  83.9 8.7 %all_gather.21 = bf16[512,512]{1,0:T(8,128)(2,1)S(1)} all-gather(bf16[256,512]{1,0:T(8,128)(2,1)S(1)} %add_convert_fusion.1), channel_id=1, replica_groups=mesh['dp'=16,'mp'=2] {'mp'}, dimensions={0}, use_global_device_ids=true | all-gather | bytes 786432 | tf_op jit(solution)/shard_map/all_gather | solution.py:271
  92.7 1.9 multiply_convert_fusion.3
  99.5 3.1 convolution_convert_fusion.1
  104.3 3.2 convolution_convert_fusion
  107.5 6.1 %reduce-scatter.10.cloned.1.call-done = bf16[256,512]{1,0:T(8,128)(2,1)} async-done(((bf16[512,512]{1,0:T(8,128)(2,1)}), bf16[256,512]{1,0:T(8,128)(2,1)}) %reduce-scatter.10.cloned.1.call-update) | async-done | bytes 262160 | tf_op jit(solution)/shard_map/reduce_scatter | solution.py:285
  114.9 16.1 %reduce-scatter.8.cloned.1.call-done = bf16[256,512]{1,0:T(8,128)(2,1)} async-done(((bf16[512,512]{1,0:T(8,128)(2,1)}), bf16[256,512]{1,0:T(8,128)(2,1)}) %reduce-scatter.8.cloned.1.call-update) | async-done | bytes 262160 | tf_op jit(solution)/shard_map/reduce_scatter | solution.py:274
  131.0 2.8 convert_reduce_fusion.4
  136.7 2.2 convolution_convert_fusion.7
  144.1 6.1 %all_gather.23 = bf16[512,256]{1,0:T(8,128)(2,1)S(1)} all-gather(bf16[256,256]{1,0:T(8,128)(2,1)S(1)} %get-tuple-element.82), channel_id=1, replica_groups=mesh['dp'=16,'mp'=2] {'mp'}, dimensions={0}, use_global_device_ids=true | all-gather | bytes 393216 | tf_op jit(solution)/shard_map/all_gather | solution.py:311
  150.2 11.1 %fusion.3 = (bf16[1024]{0:T(1024)(128)(2,1)}, bf16[1024]{0:T(1024)(128)(2,1)}, bf16[1024]{0:T(1024)(128)(2,1)}, bf16[1024]{0:T(1024)(128)(2,1)}, bf16[1024]{0:T(...) fusion(f32[2,256,1024]{2,1,0:T(8,128)} %copy-done.20, ...), kind=kOutput, calls=%fused_computation.10 | convolution fusion | flops 282057728 | bytes 38586368 | tf_op jit(solution)/shard_map/dot_general | solution.py:29
  161.4 2.0 pad.107
  175.8 3.5 multiply_reduce_fusion.1
  179.3 4.9 all-reduce.24
  184.3 2.9 constant_dynamic-update-slice_fusion
  188.0 3.6 fusion.72
  198.6 2.4 fusion.68
  207.8 9.2 %reduce-scatter.12.cloned.1.call-done = bf16[256,512]{1,0:T(8,128)(2,1)} async-done(((bf16[512,512]{1,0:T(8,128)(2,1)}), bf16[256,512]{1,0:T(8,128)(2,1)}) %reduce-scatter.12.cloned.1.call-update) | async-done | bytes 262160 | tf_op jit(solution)/shard_map/reduce_scatter | solution.py:329
  222.2 62.5 %all-reduce.26 = (bf16[1024]{0:T(1024)(128)(2,1)S(1)}, bf16[2,1024]{1,0:T(2,128)(2,1)S(1)}, bf16[9,1024]{1,0:T(8,128)(2,1)S(1)}, bf16[1024]{0:T(1024)(128)(2,1)S(1)}) all-reduce(bf16[1024]{0:T(1024)(128)(2,1)S(1)} %get-tuple-element.77, bf16[2,1024]{1,0:T(2,128)(2,1)S(1)} %pad_maximum_fusion.8, ...), channel_id=1, replica_groups=mesh['dp'=16,'mp'=2] {'dp'}, use_global_device_ids=true, to_apply=%region_46.47 | all-reduce | flops 13312 | bytes 53248 | tf_op jit(solution)/shard_map/psum | solution.py:375
  288.4 38.3 %all-reduce.22 = (f32[4,2,512]{2,1,0:T(2,128)}, f32[1024]{0:T(1024)}, f32[256]{0:T(256)}, f32[256]{0:T(256)}, f32[2,512]{1,0:T(2,128)}, /*index=5*/f32[512]{0:T(512)}, f32[512]{0:T(512)}) all-reduce(f32[4,2,512]{2,1,0:T(2,128)S(1)} %pad_maximum_fusion.7, ...), channel_id=1, replica_groups=mesh['dp'=16,'mp'=2] {'dp','mp'}, use_global_device_ids=true, to_apply=%region_40.41 | all-reduce | flops 7680 | bytes 61440 | tf_op jit(solution)/shard_map/psum | solution.py:383
  327.7 2.5 all-reduce.33.cloned.1.call-done
  330.3 2.9 convert_element_type.317
  337.4 173.5 %all-reduce.31.cloned.1.call-done = (f32[512,1024]{1,0:T(8,128)}, f32[3,512,256]{2,1,0:T(8,128)}, f32[512,1536]{1,0:T(8,128)}, f32[512,512]{1,0:T(8,128)}) async-done(((f32[512,1024]{1,0:T(8,128)}, f32[3,512,256]{2,1,0:T(8,128)}, f32[512,1536]{1,0:T(8,128)}, f32[512,512]{1,0:T(8,128)}), (f32[512,1024]{1,0:T(8,128)}, f32[3,512,256]{2,1,0:T(8,128)}, f32[512,1536]{1,0:T(8,128)}, ...) | async-done | bytes 7864336 | tf_op jit(solution)/shard_map/psum | solution.py:383
  510.9 3.3 copy.85
  (378 shorter events, 90.7 us)
Async XLA Ops:
  7.2 68.2 %copy-start = (bf16[512,1536]{1,0:T(8,128)(2,1)S(1)}, bf16[512,1536]{1,0:T(8,128)(2,1)}, u32[]{:S(2)}) copy-start(bf16[512,1536]{1,0:T(8,128)(2,1)} %param.36) | copy-start | bytes 4718596
  7.2 7.4 %copy-start.33 = (bf16[256,512]{1,0:T(8,128)(2,1)S(1)}, bf16[256,512]{1,0:T(8,128)(2,1)}, u32[]{:S(2)}) copy-start(bf16[256,512]{1,0:T(8,128)(2,1)} %param.22) | copy-start | bytes 786436
  7.2 66.8 %reduce-scatter.6.cloned.1.call-start = ((), (), s32[]{:S(2)}) async-start(), calls=%async_computation.5 | async-start | bytes 393216 | tf_op jit(solution)/shard_map/reduce_scatter | solution.py:254
  14.6 6.2 %copy-start.81 = (bf16[2,1024]{1,0:T(2,128)(2,1)S(1)}, bf16[2,1024]{1,0:T(2,128)(2,1)}, u32[]{:S(2)}) copy-start(bf16[2,1024]{1,0:T(2,128)(2,1)} %param.32) | copy-start | bytes 12292
  15.3 14.7 %copy-start.58 = (bf16[256,512]{1,0:T(8,128)(2,1)}, bf16[256,512]{1,0:T(8,128)(2,1)S(1)}, u32[]{:S(2)}) copy-start(bf16[256,512]{1,0:T(8,128)(2,1)S(1)} %multiply_convert_fusion.6) | copy-start | bytes 786436
  15.5 13.4 %copy-start.68 = (bf16[3,512,256]{2,1,0:T(8,128)(2,1)S(1)}, bf16[3,512,256]{2,1,0:T(8,128)(2,1)}, u32[]{:S(2)}) copy-start(bf16[3,512,256]{2,1,0:T(8,128)(2,1)} %param.30) | copy-start | bytes 2359300
  28.8 6.8 %copy-start.70 = (bf16[512,512]{1,0:T(8,128)(2,1)}, bf16[512,512]{1,0:T(8,128)(2,1)S(1)}, u32[]{:S(2)}) copy-start(bf16[512,512]{1,0:T(8,128)(2,1)S(1)} %all_gather.18) | copy-start | bytes 1572868
  51.7 6.8 %copy-start.20 = (f32[2,256,1024]{2,1,0:T(8,128)}, f32[2,256,1024]{2,1,0:T(8,128)S(1)}, u32[]{:S(2)}) copy-start(f32[2,256,1024]{2,1,0:T(8,128)S(1)} %pad.98) | copy-start | bytes 6291460
  59.5 9.2 %copy-start.82 = (bf16[2,512]{1,0:T(2,128)(2,1)S(1)}, bf16[2,512]{1,0:T(2,128)(2,1)}, u32[]{:S(2)}) copy-start(bf16[2,512]{1,0:T(2,128)(2,1)} %param.37) | copy-start | bytes 6148
  60.7 52.9 %reduce-scatter.10.cloned.1.call-start = ((), (), s32[]{:S(2)}) async-start(), calls=%async_computation.7 | async-start | bytes 786432 | tf_op jit(solution)/shard_map/reduce_scatter | solution.py:285
  82.7 10.0 %copy-start.93 = (f32[1024]{0:T(1024)S(1)}, f32[1024]{0:T(1024)}, u32[]{:S(2)}) copy-start(f32[1024]{0:T(1024)} %convert_element_type.296) | copy-start | bytes 12292
  82.7 10.0 %copy-start.101 = (bf16[512,1024]{1,0:T(8,128)(2,1)S(1)}, bf16[512,1024]{1,0:T(8,128)(2,1)}, u32[]{:S(2)}) copy-start(bf16[512,1024]{1,0:T(8,128)(2,1)} %param.40) | copy-start | bytes 3145732
  98.9 32.1 %reduce-scatter.8.cloned.1.call-start = ((), (), s32[]{:S(2)}) async-start(), calls=%async_computation.6 | async-start | bytes 786432 | tf_op jit(solution)/shard_map/reduce_scatter | solution.py:274
  104.2 97.1 %reduce-scatter.14.cloned.1.call-start = ((), (), s32[]{:S(2)}) async-start(), calls=%async_computation.9 | async-start | bytes 393216 | tf_op jit(solution)/shard_map/reduce_scatter | solution.py:332
  139.5 10.7 %copy-start.17 = (f32[2,256,1024]{2,1,0:T(8,128)S(1)}, f32[2,256,1024]{2,1,0:T(8,128)}, u32[]{:S(2)}) copy-start(f32[2,256,1024]{2,1,0:T(8,128)} %copy-done.16) | copy-start | bytes 6291460
  140.5 9.8 %copy-start.15 = (f32[2,256,1024]{2,1,0:T(8,128)S(1)}, f32[2,256,1024]{2,1,0:T(8,128)}, u32[]{:S(2)}) copy-start(f32[2,256,1024]{2,1,0:T(8,128)} %copy-done.14) | copy-start | bytes 6291460
  140.9 9.3 %copy-start.13 = (f32[2,256,1024]{2,1,0:T(8,128)S(1)}, f32[2,256,1024]{2,1,0:T(8,128)}, u32[]{:S(2)}) copy-start(f32[2,256,1024]{2,1,0:T(8,128)} %copy-done.12) | copy-start | bytes 6291460
  141.9 8.3 %copy-start.9 = (f32[2,256,1024]{2,1,0:T(8,128)S(1)}, f32[2,256,1024]{2,1,0:T(8,128)}, u32[]{:S(2)}) copy-start(f32[2,256,1024]{2,1,0:T(8,128)} %copy-done.8) | copy-start | bytes 6291460
  141.9 8.3 %copy-start.11 = (f32[2,256,1024]{2,1,0:T(8,128)S(1)}, f32[2,256,1024]{2,1,0:T(8,128)}, u32[]{:S(2)}) copy-start(f32[2,256,1024]{2,1,0:T(8,128)} %copy-done.10) | copy-start | bytes 6291460
  143.2 7.0 %copy-start.3 = (f32[512,1024]{1,0:T(8,128)S(1)}, f32[512,1024]{1,0:T(8,128)}, u32[]{:S(2)}) copy-start(f32[512,1024]{1,0:T(8,128)} %copy-done.2) | copy-start | bytes 6291460
  143.5 17.9 %copy-start.36 = (f32[256,512]{1,0:T(8,128)}, f32[256,512]{1,0:T(8,128)S(1)}, u32[]{:S(2)}) copy-start(f32[256,512]{1,0:T(8,128)S(1)} %multiply_add_fusion.1) | copy-start | bytes 1572868
  187.9 29.1 %reduce-scatter.12.cloned.1.call-start = ((), (), s32[]{:S(2)}) async-start(), calls=%async_computation.8 | async-start | bytes 786432 | tf_op jit(solution)/shard_map/reduce_scatter | solution.py:329
  194.2 136.1 %all-reduce.33.cloned.1.call-start = ((), (), s32[]{:S(2)}) async-start(), calls=%async_computation.11 | async-start | bytes 7340032 | tf_op jit(solution)/shard_map/psum | solution.py:374
  201.0 309.9 %all-reduce.31.cloned.1.call-start = ((), (), s32[]{:S(2)}) async-start(), calls=%async_computation.10 | async-start | bytes 15728640 | tf_op jit(solution)/shard_map/psum | solution.py:383
  207.8 10.9 %copy-start.32 = (f32[256,1024]{1,0:T(8,128)S(1)}, f32[256,1024]{1,0:T(8,128)}, u32[]{:S(2)}) copy-start(f32[256,1024]{1,0:T(8,128)} %copy-done.31) | copy-start | bytes 3145732
  207.8 11.0 %copy-start.37 = (f32[256,512]{1,0:T(8,128)S(1)}, f32[256,512]{1,0:T(8,128)}, u32[]{:S(2)}) copy-start(f32[256,512]{1,0:T(8,128)} %copy-done.36) | copy-start | bytes 1572868
  221.3 65.9 %copy-start.97 = (f32[512]{0:T(512)S(1)}, f32[512]{0:T(512)}, u32[]{:S(2)}) copy-start(f32[512]{0:T(512)} %get-tuple-element.40) | copy-start | bytes 6148
  221.3 65.9 %copy-start.98 = (f32[512]{0:T(512)S(1)}, f32[512]{0:T(512)}, u32[]{:S(2)}) copy-start(f32[512]{0:T(512)} %get-tuple-element.51) | copy-start | bytes 6148
  221.3 65.9 %copy-start.44 = (bf16[8,64,256]{2,1,0:T(8,128)(2,1)S(1)}, bf16[8,64,256]{2,1,0:T(8,128)(2,1)}, u32[]{:S(2)}) copy-start(bf16[8,64,256]{2,1,0:T(8,128)(2,1)} %copy-done.42) | copy-start | bytes 786436
  221.3 65.9 %copy-start.47 = (bf16[8,64,256]{2,1,0:T(8,128)(2,1)S(1)}, bf16[8,64,256]{2,1,0:T(8,128)(2,1)}, u32[]{:S(2)}) copy-start(bf16[8,64,256]{2,1,0:T(8,128)(2,1)} %copy-done.45) | copy-start | bytes 786436
  221.3 65.9 %copy-start.50 = (bf16[8,64,256]{2,1,0:T(8,128)(2,1)S(1)}, bf16[8,64,256]{2,1,0:T(8,128)(2,1)}, u32[]{:S(2)}) copy-start(bf16[8,64,256]{2,1,0:T(8,128)(2,1)} %copy-done.48) | copy-start | bytes 786436
  222.1 65.5 %copy-start.105 = (bf16[512,1024]{1,0:T(8,128)(2,1)S(1)}, bf16[512,1024]{1,0:T(8,128)(2,1)}, u32[]{:S(2)}) copy-start(bf16[512,1024]{1,0:T(8,128)(2,1)} %param.26) | copy-start | bytes 3145732
  (85 other events, 174.3 us)
Sparse Core Ops, SparseCore 0:
  60.8 13.1 reduce-scatter.5
  99.0 14.5 reduce-scatter.9
  116.4 14.5 reduce-scatter.7
  188.1 11.6 reduce-scatter.13
  202.4 14.5 reduce-scatter.11
  222.1 108.1 all-reduce.32
  337.7 173.1 all-reduce.30
where the time goes:
time: 535 us; the launch traced here: 527 us
  waiting for transfers between devices  213 us (40%)
  blocking collectives  152 us (28%)
  matrix products  54.4 us (10%)
  local copies, waits for them, and re-layouts  46.3 us (9%)
  other arithmetic  44.3 us (8%)
  between operations  16.9 us (3%)
    psum x1, waiting for transfers between devices, body(): lax.psum((grad_norms, grad_gated_weight, grad_gated_bias, grad_conv_weigh...  173 us
    psum x1, blocking collectives, body(): lax.psum(inner_set[1].astype(jnp.bfloat16), 'dp').astype(jnp.float32)  62.5 us
    psum x1, blocking collectives, body(): lax.psum((grad_norms, grad_gated_weight, grad_gated_bias, grad_conv_weigh...  38.3 us
    unnamed x225, local copies, waits for them, and re-layouts  29.7 us
    dot_general x8, matrix products, right_turned(): lax.dot_general(left, right, (((1,), (1,)), ((), ())), preferred_element_...  20.5 us
    dot_general x8, matrix products, left_turned(): lax.dot_general(left, right, (((0,), (0,)), ((), ())), preferred_element_...  16.6 us
    reduce_scatter x1, waiting for transfers between devices, body(): lax.psum_scatter(matmul(hidden_low, shrink_all).astype(jnp.bfloat16), 'mp...  16.1 us
    dot_general x8, matrix products, matmul(): return jnp.dot(left, right, preferred_element_type=jnp.float32)  12.8 us
  transfers between devices with their start and end apart: 7, of which 6 were waited for; matrix products, arithmetic and copies ran while one was open for 8% of the time, Pallas kernels for 0%

commit v1 on v0

v1 whole, which is shorter than its diff:
```python
import jax
import jax.numpy as jnp
from jax import lax
from jax.sharding import PartitionSpec as P

HEADS = 8
SEQ = 256
EPS = 1e-06
LOW = jnp.bfloat16
F32 = jnp.float32


def as_low(values):
    return values.astype(LOW)


def matmul(left, right):
    return jnp.dot(left, right, preferred_element_type=F32)


def left_turned(left, right):
    return lax.dot_general(left, right, (((0,), (0,)), ((), ())), preferred_element_type=F32)


def right_turned(left, right):
    return lax.dot_general(left, right, (((1,), (1,)), ((), ())), preferred_element_type=F32)


def shift_rows(values, offset):
    channels = values.shape[1]
    framed = values.reshape(-1, SEQ, channels)
    if offset > 0:
        framed = jnp.pad(framed[:, offset:], ((0, 0), (0, offset), (0, 0)))
    elif offset < 0:
        framed = jnp.pad(framed[:, :offset], ((0, 0), (-offset, 0), (0, 0)))
    return framed.reshape(-1, channels)


def silu_slope(values):
    sigma = jax.nn.sigmoid(values)
    return sigma * (1.0 + values * (1.0 - sigma))


def layer_norm(values, gain, bias):
    centre = jnp.mean(values, -1, keepdims=True)
    centered = values - centre
    variance = jnp.mean(centered * centered, -1, keepdims=True)
    rstd = lax.rsqrt(variance + EPS)
    normed = centered * rstd
    return (normed * gain + bias, normed, rstd)


def norm_back(grad_out, normed, rstd, gain):
    scaled = grad_out * gain
    first_mean = jnp.mean(scaled, -1, keepdims=True)
    second_mean = jnp.mean(scaled * normed, -1, keepdims=True)
    grad_in = rstd * (scaled - first_mean - normed * second_mean)
    return (grad_in, jnp.stack([jnp.sum(grad_out * normed, 0), jnp.sum(grad_out, 0)]))


def scores_of(query_heads, key_heads, keep_rows, head_size):
    row_count = query_heads.shape[0]
    scores = jnp.einsum("rqhd,rkhd->rhqk", query_heads, key_heads, preferred_element_type=F32)
    scores = scores * head_size ** (-0.5)
    return jnp.where(keep_rows.reshape(row_count, 1, 1, SEQ) > 0, scores, -1000000000.0)


def attend_forward(queries, keys, values, keep_rows):
    row_count = queries.shape[0] // SEQ
    head_size = queries.shape[1] // HEADS
    shape = (row_count, SEQ, HEADS, head_size)
    scores = scores_of(queries.reshape(shape), keys.reshape(shape), keep_rows, head_size)
    highest = jnp.max(scores, -1, keepdims=True)
    weights = jnp.exp(scores - highest)
    total = jnp.sum(weights, -1, keepdims=True)
    probs = weights / total
    mixed = jnp.einsum(
        "rhqk,rkhd->rqhd", as_low(probs), values.reshape(shape), preferred_element_type=F32
    )
    return (mixed.reshape(queries.shape), probs)


def attend_backward(queries, keys, values, probs, grad_attended):
    row_count = queries.shape[0] // SEQ
    head_size = queries.shape[1] // HEADS
    shape = (row_count, SEQ, HEADS, head_size)
    query_heads = queries.reshape(shape)
    key_heads = keys.reshape(shape)
    grad_heads = grad_attended.reshape(shape)
    probs_low = as_low(probs)
    grad_values = jnp.einsum("rhqk,rqhd->rkhd", probs_low, grad_heads, preferred_element_type=F32)
    grad_probs = jnp.einsum(
        "rqhd,rkhd->rhqk", grad_heads, values.reshape(shape), preferred_element_type=F32
    )
    weighted = jnp.sum(grad_probs * probs, -1, keepdims=True)
    grad_scores = as_low(probs * (grad_probs - weighted))
    grad_queries = jnp.einsum(
        "rhqk,rkhd->rqhd", grad_scores, key_heads, preferred_element_type=F32
    ) * head_size ** (-0.5)
    grad_keys = jnp.einsum(
        "rhqk,rqhd->rkhd", grad_scores, query_heads, preferred_element_type=F32
    ) * head_size ** (-0.5)
    flat = queries.shape
    return (grad_queries.reshape(flat), grad_keys.reshape(flat), grad_values.reshape(flat))


def swap(values, axis, bit):
    count = lax.axis_size(axis)
    return lax.ppermute(values, axis, [(at, at ^ bit) for at in range(count)])


def bit_of(axis, bit):
    return (lax.axis_index(axis) // bit) % 2


def bits_of(axis):
    bits, bit = [], 1
    while bit < lax.axis_size(axis):
        bits.append(bit)
        bit *= 2
    return bits


def add_low(first, second):
    return as_low(first.astype(F32) + second.astype(F32))


def split(values, own):
    half = values.shape[0] // 2
    mine = lax.dynamic_slice_in_dim(values, own * half, half, 0)
    other = lax.dynamic_slice_in_dim(values, (1 - own) * half, half, 0)
    return mine, other


def join(mine, other, own):
    swapped = own == 1
    return jnp.concatenate(
        [jnp.where(swapped, other, mine), jnp.where(swapped, mine, other)], 0
    )


def gather_inner(own_piece):
    core = bit_of("dp", 1)
    mine, _ = split(own_piece, core)
    halves = [mine]
    for bit in bits_of("mp"):
        halves = halves + [swap(item, "mp", bit) for item in halves]
    rest = [join(item, swap(item, "dp", 1), core) for item in halves[1:]]
    return [own_piece] + rest


def gather_small(own_piece):
    items = [own_piece]
    for bit in bits_of("mp"):
        items = items + [swap(item, "mp", bit) for item in items]
    return items


def sum_shared(values, order):
    held = []
    steps = [("dp", 1)] + order
    for axis, bit in steps[:-1]:
        own = bit_of(axis, bit)
        mine, other = split(values, own)
        values = add_low(mine, swap(other, axis, bit))
        held.append((axis, bit, own))
    axis, bit = steps[-1]
    values = add_low(values, swap(values, axis, bit))
    for axis, bit, own in reversed(held):
        values = join(values, swap(values, axis, bit), own)
    return values.astype(F32)


def sum_inner(pieces, order):
    held = []
    steps = [("dp", 1)] + order
    for axis, bit in steps[:-1]:
        if axis == "mp":
            keep_count = len(pieces) // 2
            moved = [swap(item, axis, bit) for item in pieces[keep_count:]]
            pieces = [add_low(one, two) for one, two in zip(pieces[:keep_count], moved)]
            continue
        own = bit_of(axis, bit)
        parts = [split(item, own) for item in pieces]
        pieces = [add_low(mine, swap(other, axis, bit)) for mine, other in parts]
        held.append((axis, bit, own))
    axis, bit = steps[-1]
    values = add_low(pieces[0], swap(pieces[0], axis, bit))
    for axis, bit, own in reversed(held):
        values = join(values, swap(values, axis, bit), own)
    return values.astype(F32)


def sum_small(values):
    for axis in ("dp", "mp"):
        for bit in bits_of(axis):
            values = values + swap(values, axis, bit)
    return values


def body(
    cell_input,
    lengths,
    out_grad,
    norm_params,
    gated_weight,
    gated_bias,
    left_weight,
    left_bias,
    conv_weight,
    conv_bias,
    inner_norm,
    depth_weight,
    point_weight,
    point_bias,
    project_weight,
    project_bias,
    output_weight,
    output_bias,
    expand_weight,
    expand_bias,
    shrink_weight,
    shrink_bias,
):
    width = cell_input.shape[1]
    half_width = conv_weight.shape[2]
    local = left_weight.shape[1]
    inner = local * lax.axis_size("mp")
    offset = lax.axis_index("mp") * local
    mp_bits = bits_of("mp")[::-1]
    dp_bits = bits_of("dp")[1:]
    mp_first = [("mp", bit) for bit in mp_bits] + [("dp", bit) for bit in dp_bits]
    dp_first = (
        [("dp", dp_bits[0])] + [("mp", bit) for bit in mp_bits] + [("dp", bit) for bit in dp_bits[1:]]
    )

    vectors = jnp.concatenate(
        [left_bias[None], expand_bias[None], inner_norm, depth_weight], 0
    )
    vectors = jnp.concatenate(gather_small(vectors), 1).astype(F32)
    left_bias_all, expand_bias_all = vectors[0], vectors[1]
    inner_all, depth_all = vectors[2:4], vectors[4:13]
    left_all = jnp.concatenate(gather_inner(left_weight), 1)
    point_all = jnp.concatenate(gather_inner(point_weight), 0)
    expand_all = jnp.concatenate(gather_inner(expand_weight), 1)
    shrink_all = jnp.concatenate(gather_inner(shrink_weight), 0)

    positions = jnp.arange(SEQ, dtype=jnp.int32)
    keep = (positions[None, :] < lengths[:, None]).astype(F32).reshape(-1)
    start_x = cell_input.astype(F32)
    norms = norm_params.astype(F32)
    norm_one, normed_one, rstd_one = layer_norm(start_x, norms[0, 0], norms[0, 1])
    low_one = as_low(norm_one)
    gated_pre = matmul(low_one, gated_weight) + gated_bias.astype(F32)
    values_one = gated_pre[:, :width]
    gates_one = jax.nn.sigmoid(gated_pre[:, width:])
    resid_one = start_x + values_one * gates_one
    norm_two, normed_two, rstd_two = layer_norm(resid_one, norms[1, 0], norms[1, 1])
    low_two = as_low(norm_two * keep[:, None])
    stacked = jnp.concatenate([shift_rows(low_two, -1), low_two, shift_rows(low_two, 1)], 1)
    conv_flat = conv_weight.reshape(3 * width, half_width)
    right_pre = matmul(stacked, conv_flat) + conv_bias.astype(F32)
    right_low = as_low(jax.nn.silu(right_pre))

    left_pre = matmul(low_two, left_all) + left_bias_all
    right_part = lax.dynamic_update_slice_in_dim(
        jnp.zeros((low_two.shape[0], inner), LOW), right_low, offset, 1
    )
    mixed = jax.nn.silu(left_pre) + right_part.astype(F32)
    centre = jnp.sum(mixed, 1, keepdims=True) / inner
    variance = jnp.sum(mixed * mixed, 1, keepdims=True) / inner - centre * centre
    inner_rstd = lax.rsqrt(variance + EPS)
    inner_normed = (mixed - centre) * inner_rstd
    normal_out = (inner_normed * inner_all[0] + inner_all[1]) * keep[:, None]
    depth = jnp.zeros_like(normal_out)
    for tap in range(9):
        depth = depth + shift_rows(normal_out, tap - 4) * depth_all[tap]
    depth_low = as_low(depth)
    sep = matmul(depth_low, point_all) + point_bias.astype(F32)
    resid_two = resid_one + jnp.pad(sep, ((0, 0), (0, width - half_width)))
    norm_four, normed_four, rstd_four = layer_norm(resid_two, norms[2, 0], norms[2, 1])
    low_four = as_low(norm_four)
    projected = matmul(low_four, project_weight)
    biases = project_bias.astype(F32)
    queries = as_low(projected[:, :width] + biases[0])
    keys = as_low(projected[:, width : 2 * width])
    values = as_low(projected[:, 2 * width :] + biases[1])
    attended, probs = attend_forward(queries, keys, values, keep)
    attended_low = as_low(attended)
    resid_three = resid_two + matmul(attended_low, output_weight) + output_bias.astype(F32)
    norm_five, normed_five, rstd_five = layer_norm(resid_three, norms[3, 0], norms[3, 1])
    low_five = as_low(norm_five)
    expand_pre = matmul(low_five, expand_all) + expand_bias_all
    hidden_low = as_low(jax.nn.silu(expand_pre))
    shrunk = matmul(hidden_low, shrink_all)
    cell_output = as_low(resid_three + shrunk + shrink_bias.astype(F32))

    grad_top = out_grad.astype(F32)
    grad_shrink_bias = jnp.sum(grad_top, 0)
    cols = [slice(at, at + local) for at in range(0, inner, local)]
    grad_shrink = sum_inner(
        [as_low(left_turned(hidden_low[:, col], out_grad)) for col in cols], mp_first
    )
    grad_expand_pre = as_low(right_turned(out_grad, shrink_all) * silu_slope(expand_pre))
    grad_expand_bias = jnp.sum(grad_expand_pre.astype(F32), 0)
    grad_expand = sum_inner(
        [as_low(left_turned(low_five, grad_expand_pre[:, col])) for col in cols], dp_first
    )
    grad_five = right_turned(grad_expand_pre, expand_all)
    grad_in_five, grad_norm_five = norm_back(grad_five, normed_five, rstd_five, norms[3, 0])
    grad_three = grad_top + grad_in_five
    grad_attn_low = as_low(grad_three)
    grad_output_bias = jnp.sum(grad_attn_low.astype(F32), 0)
    grad_output_weight = as_low(left_turned(attended_low, grad_attn_low))
    grad_attended = as_low(right_turned(grad_attn_low, output_weight))
    grad_queries, grad_keys, grad_values = attend_backward(
        queries, keys, values, probs, grad_attended
    )
    grad_projected = as_low(jnp.concatenate([grad_queries, grad_keys, grad_values], 1))
    grad_project_weight = as_low(left_turned(low_four, grad_projected))
    both = sum_shared(jnp.concatenate([grad_project_weight, grad_output_weight], 1), mp_first)
    grad_project_weight = both[:, : 3 * width]
    grad_output_weight = both[:, 3 * width :]
    grad_proj_float = grad_projected.astype(F32)
    grad_query_bias = jnp.sum(grad_proj_float[:, :width], 0)
    grad_value_bias = jnp.sum(grad_proj_float[:, 2 * width :], 0)
    grad_four = right_turned(grad_projected, project_weight)
    grad_in_four, grad_norm_four = norm_back(grad_four, normed_four, rstd_four, norms[2, 0])
    grad_two = grad_three + grad_in_four
    grad_sep = as_low(grad_two[:, :half_width])
    grad_point_bias = jnp.sum(grad_sep.astype(F32), 0)

    grad_point = sum_inner(
        [as_low(left_turned(depth_low[:, col], grad_sep)) for col in cols], mp_first
    )
    grad_depth = right_turned(grad_sep, point_all)
    grad_taps = jnp.stack(
        [jnp.sum(shift_rows(normal_out, tap - 4) * grad_depth, 0) for tap in range(9)]
    )
    grad_normal = jnp.zeros_like(grad_depth)
    for tap in range(9):
        grad_normal = grad_normal + shift_rows(grad_depth * depth_all[tap], 4 - tap)
    grad_normal = grad_normal * keep[:, None]
    scaled = grad_normal * inner_all[0]
    first = jnp.sum(scaled, 1, keepdims=True) / inner
    second = jnp.sum(scaled * inner_normed, 1, keepdims=True) / inner
    grad_mixed = inner_rstd * (scaled - first - inner_normed * second)
    grad_inner_gain = jnp.sum(grad_normal * inner_normed, 0)
    grad_inner_bias = jnp.sum(grad_normal, 0)
    grad_left_pre = as_low(grad_mixed * silu_slope(left_pre))
    grad_left_b = jnp.sum(grad_left_pre.astype(F32), 0)
    grad_left = sum_inner(
        [as_low(left_turned(low_two, grad_left_pre[:, col])) for col in cols], dp_first
    )
    grad_low_left = right_turned(grad_left_pre, left_all)
    grad_right = lax.dynamic_slice_in_dim(grad_mixed, offset, half_width, 1)
    grad_right_pre = as_low(grad_right * silu_slope(right_pre))
    grad_conv_bias = jnp.sum(grad_right_pre.astype(F32), 0)
    grad_conv = as_low(left_turned(stacked, grad_right_pre))
    grad_stacked = right_turned(grad_right_pre, conv_flat)
    grad_low_two = (
        grad_low_left
        + shift_rows(grad_stacked[:, :width], 1)
        + grad_stacked[:, width : 2 * width]
        + shift_rows(grad_stacked[:, 2 * width :], -1)
    )
    grad_in_two, grad_norm_two = norm_back(
        grad_low_two * keep[:, None], normed_two, rstd_two, norms[1, 0]
    )
    grad_one = grad_two + grad_in_two
    grad_gated = as_low(
        jnp.concatenate(
            [grad_one * gates_one, grad_one * values_one * gates_one * (1.0 - gates_one)], 1
        )
    )
    grad_gated_bias = jnp.sum(grad_gated.astype(F32), 0)
    grad_gated_weight = as_low(left_turned(low_one, grad_gated))
    last = sum_shared(
        jnp.concatenate(
            [grad_gated_weight] + [grad_conv[at * width : (at + 1) * width] for at in range(3)], 1
        ),
        dp_first,
    )
    grad_gated_weight = last[:, : 2 * width]
    grad_conv = jnp.stack(
        [
            last[:, 2 * width + at * half_width : 2 * width + (at + 1) * half_width]
            for at in range(3)
        ]
    )
    grad_in_one, grad_norm_one = norm_back(
        right_turned(grad_gated, gated_weight), normed_one, rstd_one, norms[0, 0]
    )
    input_grad = grad_one + grad_in_one

    wide = jnp.concatenate(
        [grad_left_b[None], grad_expand_bias[None], grad_inner_gain[None], grad_inner_bias[None], grad_taps], 0
    )
    fixed = [
        grad_norm_one.reshape(-1),
        grad_norm_two.reshape(-1),
        grad_norm_four.reshape(-1),
        grad_norm_five.reshape(-1),
        grad_gated_bias,
        grad_query_bias,
        grad_value_bias,
        grad_output_bias,
        grad_shrink_bias,
        grad_conv_bias,
        grad_point_bias,
    ]
    fixed = jnp.concatenate(fixed)
    fixed = jnp.pad(fixed, (0, -fixed.shape[0] % local)).reshape(-1, local)
    fixed_rows = fixed.shape[0]
    wide_chunks = [wide[:, col] for col in cols]
    for bit in mp_bits:
        half_count = len(wide_chunks) // 2
        moved = [swap(item, "mp", bit) for item in wide_chunks[half_count:]]
        wide_chunks = [one + two for one, two in zip(wide_chunks[:half_count], moved)]
    for bit in mp_bits:
        fixed = fixed + swap(fixed, "mp", bit)
    small = jnp.concatenate([fixed, wide_chunks[0]], 0)
    for bit in bits_of("dp"):
        small = small + swap(small, "dp", bit)
    fixed, wide = small[:fixed_rows].reshape(-1), small[fixed_rows:]
    sizes = [2 * width] * 4 + [2 * width, width, width, width, width, half_width, half_width]
    starts = [sum(sizes[:at]) for at in range(len(sizes))]
    picked = [fixed[start : start + size] for start, size in zip(starts, sizes)]
    return (
        cell_output,
        input_grad,
        fixed[: 8 * width].reshape(4, 2, width),
        grad_gated_weight,
        picked[4],
        grad_left,
        wide[0],
        grad_conv,
        picked[9],
        wide[2:4],
        wide[4:13],
        grad_point,
        picked[10],
        grad_project_weight,
        jnp.stack([picked[5], picked[6]]),
        both[:, 3 * width :],
        picked[7],
        grad_expand,
        wide[1],
        grad_shrink,
        picked[8],
    )


def solution(mesh):
    return jax.shard_map(
        body,
        mesh=mesh,
        in_specs=(
            P(("dp", "mp"), None),
            P(("dp", "mp")),
            P(("dp", "mp"), None),
            P(),
            P(),
            P(),
            P(None, "mp"),
            P("mp"),
            P(),
            P(),
            P(None, "mp"),
            P(None, "mp"),
            P("mp", None),
            P(),
            P(),
            P(),
            P(),
            P(),
            P(None, "mp"),
            P("mp"),
            P("mp", None),
            P(),
        ),
        out_specs=(
            P(("dp", "mp"), None),
            P(("dp", "mp"), None),
            P(),
            P(),
            P(),
            P(None, "mp"),
            P("mp"),
            P(),
            P(),
            P(None, "mp"),
            P(None, "mp"),
            P("mp", None),
            P(),
            P(),
            P(),
            P(),
            P(),
            P(None, "mp"),
            P("mp"),
            P("mp", None),
            P(),
        ),
        check_vma=False,
    )
```

time: 535 us -> 383 us (0.72)
  blocking collectives: 152 us -> 0 us
  waiting for transfers between devices: 213 us -> 127 us
  starting transfers between devices: 0.54 us -> 71.2 us
  other arithmetic: 44.3 us -> 69.8 us
  between operations: 16.9 us -> 4.77 us
    psum x2 -> x0, waiting for transfers between devices: 176 us -> none  [the longest x1 173 us: body(): lax.psum((grad_norms, grad_gated_weight, grad_gated_bias, grad_conv_weigh...]
    ppermute x0 -> x71, waiting for transfers between devices: none -> 127 us  [swap(): return lax.ppermute(values, axis, [(at, at ^ bit) for at in range(count)])]
    psum x4 -> x0, blocking collectives: 111 us -> none  [the longest x1 62.5 us: body(): lax.psum(inner_set[1].astype(jnp.bfloat16), 'dp').astype(jnp.float32)]
    ppermute x0 -> x71, starting transfers between devices: none -> 71.2 us  [swap(): return lax.ppermute(values, axis, [(at, at ^ bit) for at in range(count)])]
    all_gather x6 -> x0, blocking collectives: 40.9 us -> none  [the longest x1 8.72 us: body(): rows_five = lax.all_gather(low_five, 'mp', axis=0, tiled=True)]
    reduce_scatter x5 -> x0, waiting for transfers between devices: 36.8 us -> none  [the longest x1 16.1 us: body(): lax.psum_scatter(matmul(hidden_low, shrink_all).astype(jnp.bfloat16), 'mp...]
    unnamed x225 -> x418, local copies, waits for them, and re-layouts: 29.7 us -> 11.8 us
    dynamic_slice x0 -> x29, local copies, waits for them, and re-layouts: none -> 13.4 us  [the longest x25 7.21 us: split(): other = lax.dynamic_slice_in_dim(values, (1 - own) * half, half, 0)]
  transfers between devices with their start and end apart: 7 -> 71, of which waited for: 6 -> 30; matrix products, arithmetic and copies ran while one was open for 8% -> 22% of each run, Pallas kernels for 0% -> 0%
where the time goes in v1:
time: 383 us; the launch traced here: 378 us
  waiting for transfers between devices  127 us (33%)
  starting transfers between devices  71.2 us (19%)
  other arithmetic  69.8 us (18%)
  matrix products  53.7 us (14%)
  local copies, waits for them, and re-layouts  51.6 us (13%)
  between operations  4.77 us (1%)
    ppermute x71, waiting for transfers between devices, swap(): return lax.ppermute(values, axis, [(at, at ^ bit) for at in range(count)])  127 us
    ppermute x71, starting transfers between devices, swap(): return lax.ppermute(values, axis, [(at, at ^ bit) for at in range(count)])  71.2 us
    dot_general x12, matrix products, left_turned(): lax.dot_general(left, right, (((0,), (0,)), ((), ())), preferred_element_...  17.1 us
    dot_general x8, matrix products, matmul(): return jnp.dot(left, right, preferred_element_type=F32)  15 us
    convert_element_type x36, other arithmetic, as_low(): return values.astype(LOW)  14.8 us
    reduce_sum x1, other arithmetic, body(): grad_inner_gain = jnp.sum(grad_normal * inner_normed, 0)  13.7 us
    dot_general x8, matrix products, right_turned(): lax.dot_general(left, right, (((1,), (1,)), ((), ())), preferred_element_...  12.9 us
    unnamed x418, local copies, waits for them, and re-layouts  11.8 us
  transfers between devices with their start and end apart: 71, of which 30 were waited for; matrix products, arithmetic and copies ran while one was open for 22% of the time, Pallas kernels for 0%

profile of v1, /device:TPU:0, one launch (start us, length us, event | category | flops | bytes accessed | tf_op | source)
XLA Modules:
  0.0 378.3 jit_solution(10850994332377461495)
XLA Ops:
  3.1 3.0 collective-permute-start.2
  29.4 10.6 %collective-permute-done.5 = bf16[256,1024]{1,0:T(8,128)(2,1)} collective-permute-done((bf16[256,1024]{1,0:T(8,128)(2,1)}, bf16[256,1024]{1,0:T(8,128)(2,1)}, u32[]{:S(2)}, u32[]{:S(2)}) %collective-permute-start.5) | collective-permute-done | bytes 524320 | tf_op jit(solution)/shard_map/ppermute | solution.py:109
  40.0 9.8 %collective-permute-done.7 = bf16[512,512]{1,0:T(8,128)(2,1)} collective-permute-done((bf16[512,512]{1,0:T(8,128)(2,1)}, bf16[512,512]{1,0:T(8,128)(2,1)}, u32[]{:S(2)}, u32[]{:S(2)}) %collective-permute-start.7) | collective-permute-done | bytes 524320 | tf_op jit(solution)/shard_map/ppermute | solution.py:109
  52.1 7.3 %fusion.94 = (f32[256]{0:T(256)S(1)}, f32[256]{0:T(256)S(1)}, f32[256,2048]{1,0:T(8,128)S(1)}, f32[256,2048]{1,0:T(8,128)}) fusion(bf16[256,2048]{1,0:T(8,128)(2,1)} %get-tuple-element.181, f32[2048]{0:T(1024)S(1)} %bitcast.369, bf16[256,512]{1,0:T(8,128)(2,1)S(1)} %multiply_convert_fusion.5, bf16[256,1024]{1,0:T(8,128)(2,1)S(1)} %get-tuple-element.111, ...), kind=kOutput, calls=%fused_computation.422 | convolution fusion | flops 548404736 | bytes 7612416 | tf_op jit(solution)/shard_map/dot_general | solution.py:18
  63.7 3.8 %fusion.5 = bf16[256,2048]{1,0:T(8,128)(2,1)S(1)} fusion(f32[1,252,2048]{2,1,0:T(8,128)S(1)} %get-tuple-element.82, f32[1,253,2048]{2,1,0:T(8,128)S(1)} %get-tuple-element.84, f32[1,254,2048]{2,1,0:T(8,128)S(1)} %get-tuple-element.86, f32[1,255,2048]{2,1,0:T(8,128)S(1)} %get-tuple-element.88, f32[1,255,2048]{2,1,0:T(8,128)S(1)} %get-tuple-element.87, ...), kind=kLoop, calls=%fused_computation.25 | loop fusion | flops 12058624 | bytes 19852288 | tf_op jit(solution)/shard_map/convert_element_type | solution.py:14
  73.3 3.2 fusion.109
  84.7 4.8 %convert_reduce_fusion = (f32[2048]{0:T(1024)}, bf16[256,2048]{1,0:T(8,128)(2,1)S(1)}) fusion(f32[256,2048]{1,0:T(8,128)S(1)} %get-tuple-element.189, bf16[256,512]{1,0:T(8,128)(2,1)S(1)} %copy-done.42, bf16[512,512]{1,0:T(8,128)(2,1)S(1)} %get-tuple-element.107, bf16[512,512]{1,0:T(8,128)(2,1)S(1)} %get-tuple-element.106, bf16[1024,512]{1,0:T(8,128)(2,1)S(1)} %copy-done.94), kind=kOutput, calls=%fused_computation.58 | convolution fusion | flops 548927488 | bytes 5513216 | tf_op jit(solution)/shard_map/dot_general | solution.py:26
  103.0 4.5 %multiply_bitcast_fusion.7 = (f32[1,256,2048]{2,1,0:T(8,128)S(1)}, f32[1,256,2048]{2,1,0:T(8,128)}, f32[1,256,2048]{2,1,0:T(8,128)}, f32[1,256,2048]{2,1,0:T(8,1...) fusion(f32[256,2048]{1,0:T(8,128)S(1)} %fusion.65, ...), kind=kLoop, calls=%fused_computation.70 | loop fusion | flops 4194304 | bytes 18939904 | tf_op jit(solution)/shard_map/reshape | solution.py:31
  115.8 13.7 %multiply_reduce_fusion.1 = (f32[2048]{0:T(1024)}, f32[256]{0:T(256)S(1)}, f32[2048]{0:T(1024)}, f32[256]{0:T(256)S(1)}, f32[2048]{0:T(1024)}, /*index=5*/f32[20...) fusion(f32[256,2048]{1,0:T(8,128)S(1)} %copy-done.3, ...), kind=kLoop, calls=%fused_computation.57 | loop fusion | flops 20948480 | bytes 39638016 | tf_op jit(solution)/shard_map/reduce_sum | solution.py:348
  129.5 3.7 convert_reduce_fusion.1
  188.2 2.7 collective-permute-start.14
  191.7 4.8 %collective-permute-done.14 = f32[21,1024]{1,0:T(8,128)S(1)} collective-permute-done((f32[21,1024]{1,0:T(8,128)S(1)}, f32[21,1024]{1,0:T(8,128)S(1)}, u32[]{:S(2)}, u32[]{:S(2)}) %collective-permute-start.14) | collective-permute-done | bytes 86048 | tf_op jit(solution)/shard_map/ppermute | solution.py:109
  209.1 5.7 %collective-permute-done.36 = bf16[512,256]{1,0:T(8,128)(2,1)S(1)} collective-permute-done((bf16[512,256]{1,0:T(8,128)(2,1)S(1)}, bf16[512,256]{1,0:T(8,128)(2,1)S(1)}, u32[]{:S(2)}, u32[]{:S(2)}) %collective-permute-start.36) | collective-permute-done | bytes 262176 | tf_op jit(solution)/shard_map/ppermute | solution.py:109
  217.5 3.4 collective-permute-done.37
  221.8 3.6 collective-permute-done.38
  229.0 3.8 collective-permute-done.39
  234.0 3.7 collective-permute-done.40
  241.6 4.2 %collective-permute-done.41 = bf16[256,256]{1,0:T(8,128)(2,1)S(1)} collective-permute-done((bf16[256,256]{1,0:T(8,128)(2,1)S(1)}, bf16[256,256]{1,0:T(8,128)(2,1)S(1)}, u32[]{:S(2)}, u32[]{:S(2)}) %collective-permute-start.41) | collective-permute-done | bytes 131104 | tf_op jit(solution)/shard_map/ppermute | solution.py:109
  247.9 7.1 %collective-permute-done.28 = bf16[128,1024]{1,0:T(8,128)(2,1)S(1)} collective-permute-done((bf16[128,1024]{1,0:T(8,128)(2,1)S(1)}, bf16[128,1024]{1,0:T(8,128)(2,1)S(1)}, u32[]{:S(2)}, u32[]{:S(2)}) %collective-permute-start.28) | collective-permute-done | bytes 262176 | tf_op jit(solution)/shard_map/ppermute | solution.py:109
  257.8 8.4 %collective-permute-done.56 = bf16[128,1024]{1,0:T(8,128)(2,1)S(1)} collective-permute-done((bf16[128,1024]{1,0:T(8,128)(2,1)S(1)}, bf16[128,1024]{1,0:T(8,128)(2,1)S(1)}, u32[]{:S(2)}, u32[]{:S(2)}) %collective-permute-start.56) | collective-permute-done | bytes 262176 | tf_op jit(solution)/shard_map/ppermute | solution.py:109
  269.6 3.1 collective-permute-done.29
  275.1 3.0 collective-permute-start.30
  279.4 8.7 %collective-permute-done.30 = bf16[64,1024]{1,0:T(8,128)(2,1)S(1)} collective-permute-done((bf16[64,1024]{1,0:T(8,128)(2,1)S(1)}, bf16[64,1024]{1,0:T(8,128)(2,1)S(1)}, u32[]{:S(2)}, u32[]{:S(2)}) %collective-permute-start.30) | collective-permute-done | bytes 131104 | tf_op jit(solution)/shard_map/ppermute | solution.py:109
  302.9 3.9 %collective-permute-done.67 = bf16[128,512]{1,0:T(8,128)(2,1)S(1)} collective-permute-done((bf16[128,512]{1,0:T(8,128)(2,1)S(1)}, bf16[128,512]{1,0:T(8,128)(2,1)S(1)}, u32[]{:S(2)}, u32[]{:S(2)}) %collective-permute-start.67) | collective-permute-done | bytes 131104 | tf_op jit(solution)/shard_map/ppermute | solution.py:109
  310.0 2.6 collective-permute-done.68
  314.7 2.6 collective-permute-start.19
  317.4 5.0 %collective-permute-done.19 = bf16[32,1792]{1,0:T(8,128)(2,1)S(1)} collective-permute-done((bf16[32,1792]{1,0:T(8,128)(2,1)S(1)}, bf16[32,1792]{1,0:T(8,128)(2,1)S(1)}, u32[]{:S(2)}, u32[]{:S(2)}) %collective-permute-start.19) | collective-permute-done | bytes 114720 | tf_op jit(solution)/shard_map/ppermute | solution.py:109
  324.6 3.2 collective-permute-done.20
  329.2 3.1 collective-permute-start.47
  332.5 5.4 %collective-permute-done.47 = bf16[32,2048]{1,0:T(8,128)(2,1)S(1)} collective-permute-done((bf16[32,2048]{1,0:T(8,128)(2,1)S(1)}, bf16[32,2048]{1,0:T(8,128)(2,1)S(1)}, u32[]{:S(2)}, u32[]{:S(2)}) %collective-permute-start.47) | collective-permute-done | bytes 131104 | tf_op jit(solution)/shard_map/ppermute | solution.py:109
  349.1 7.9 %collective-permute-done.49 = bf16[64,2048]{1,0:T(8,128)(2,1)S(1)} collective-permute-done((bf16[64,2048]{1,0:T(8,128)(2,1)S(1)}, bf16[64,2048]{1,0:T(8,128)(2,1)S(1)}, u32[]{:S(2)}, u32[]{:S(2)}) %collective-permute-start.49) | collective-permute-done | bytes 262176 | tf_op jit(solution)/shard_map/ppermute | solution.py:109
  359.8 10.1 %collective-permute-done.50 = bf16[128,2048]{1,0:T(8,128)(2,1)S(1)} collective-permute-done((bf16[128,2048]{1,0:T(8,128)(2,1)S(1)}, bf16[128,2048]{1,0:T(8,128)(2,1)S(1)}, u32[]{:S(2)}, u32[]{:S(2)}) %collective-permute-start.50) | collective-permute-done | bytes 524320 | tf_op jit(solution)/shard_map/ppermute | solution.py:109
  (779 shorter events, 203.3 us)
Async XLA Ops:
  3.1 24.7 %collective-permute-start.2 = (bf16[13,1024]{1,0:T(8,128)(2,1)S(1)}, bf16[13,1024]{1,0:T(8,128)(2,1)S(1)}, u32[]{:S(2)}, u32[]{:S(2)}) collective-permute-start(bf16[13,1024]{1,0:T(8,128)(2,1)S(1)} %pad_maximum_fusion.30), channel_id=1, source_target_pairs={{0,1},{1,0},{2,3},{3,2},{4,5},{5,4},{6,7},{7,6},{8,9},{9,8},{10,11... | collective-permute-start | bytes 79880 | tf_op jit(solution)/shard_map/ppermute | solution.py:109
  7.9 20.8 %collective-permute-start = (bf16[256,1024]{1,0:T(8,128)(2,1)}, bf16[256,1024]{1,0:T(8,128)(2,1)}, u32[]{:S(2)}, u32[]{:S(2)}) collective-permute-start(bf16[256,1024]{1,0:T(8,128)(2,1)} %constant_dynamic-slice_fusion.28), channel_id=1, source_target_pairs={{0,1},{1,0},{2,3},{3,2},{4,5},{5,4},{6,7},{7,6},{8,9},{9,8},{10,11... | collective-permute-start | bytes 1572872 | tf_op jit(solution)/shard_map/ppermute | solution.py:109
  9.7 19.1 %collective-permute-start.3 = (bf16[512,256]{1,0:T(8,128)(2,1)}, bf16[512,256]{1,0:T(8,128)(2,1)}, u32[]{:S(2)}, u32[]{:S(2)}) collective-permute-start(bf16[512,256]{1,0:T(8,128)(2,1)} %constant_dynamic-slice_fusion.27), channel_id=1, source_target_pairs={{0,1},{1,0},{2,3},{3,2},{4,5},{5,4},{6,7},{7,6},{8,9},{9,8},{10,11... | collective-permute-start | bytes 786440 | tf_op jit(solution)/shard_map/ppermute | solution.py:109
  13.5 26.5 %collective-permute-start.5 = (bf16[256,1024]{1,0:T(8,128)(2,1)}, bf16[256,1024]{1,0:T(8,128)(2,1)}, u32[]{:S(2)}, u32[]{:S(2)}) collective-permute-start(bf16[256,1024]{1,0:T(8,128)(2,1)} %constant_dynamic-slice_fusion.26), channel_id=1, source_target_pairs={{0,1},{1,0},{2,3},{3,2},{4,5},{5,4},{6,7},{7,6},{8,9},{9,8},{10,11... | collective-permute-start | bytes 1572872 | tf_op jit(solution)/shard_map/ppermute | solution.py:109
  14.4 35.4 %collective-permute-start.7 = (bf16[512,512]{1,0:T(8,128)(2,1)}, bf16[512,512]{1,0:T(8,128)(2,1)}, u32[]{:S(2)}, u32[]{:S(2)}) collective-permute-start(bf16[512,512]{1,0:T(8,128)(2,1)} %constant_dynamic-slice_fusion.25), channel_id=1, source_target_pairs={{0,1},{1,0},{2,3},{3,2},{4,5},{5,4},{6,7},{7,6},{8,9},{9,8},{10,11... | collective-permute-start | bytes 1572872 | tf_op jit(solution)/shard_map/ppermute | solution.py:109
  28.7 21.0 %collective-permute-start.4 = (bf16[512,256]{1,0:T(8,128)(2,1)}, bf16[512,256]{1,0:T(8,128)(2,1)S(1)}, u32[]{:S(2)}, u32[]{:S(2)}) collective-permute-start(bf16[512,256]{1,0:T(8,128)(2,1)} %collective-permute-done.3), channel_id=1, source_target_pairs={{0,2},{2,0},{4,6},{6,4},{8,10},{10,8},{12,14},{14,12},{16,18},{18,... | collective-permute-start | bytes 786440 | tf_op jit(solution)/shard_map/ppermute | solution.py:109
  28.7 22.0 %collective-permute-start.1 = (bf16[256,1024]{1,0:T(8,128)(2,1)}, bf16[256,1024]{1,0:T(8,128)(2,1)S(1)}, u32[]{:S(2)}, u32[]{:S(2)}) collective-permute-start(bf16[256,1024]{1,0:T(8,128)(2,1)} %collective-permute-done), channel_id=1, source_target_pairs={{0,2},{2,0},{4,6},{6,4},{8,10},{10,8},{12,14},{14,12},{16,18},{18,... | collective-permute-start | bytes 1572872 | tf_op jit(solution)/shard_map/ppermute | solution.py:109
  40.0 39.8 %collective-permute-start.6 = (bf16[256,1024]{1,0:T(8,128)(2,1)}, bf16[256,1024]{1,0:T(8,128)(2,1)}, u32[]{:S(2)}, u32[]{:S(2)}) collective-permute-start(bf16[256,1024]{1,0:T(8,128)(2,1)} %collective-permute-done.5), channel_id=1, source_target_pairs={{0,2},{2,0},{4,6},{6,4},{8,10},{10,8},{12,14},{14,12},{16,18},{18,... | collective-permute-start | bytes 1572872 | tf_op jit(solution)/shard_map/ppermute | solution.py:109
  49.7 33.3 %collective-permute-start.8 = (bf16[512,512]{1,0:T(8,128)(2,1)}, bf16[512,512]{1,0:T(8,128)(2,1)}, u32[]{:S(2)}, u32[]{:S(2)}) collective-permute-start(bf16[512,512]{1,0:T(8,128)(2,1)} %collective-permute-done.7), channel_id=1, source_target_pairs={{0,2},{2,0},{4,6},{6,4},{8,10},{10,8},{12,14},{14,12},{16,18},{18,... | collective-permute-start | bytes 1572872 | tf_op jit(solution)/shard_map/ppermute | solution.py:109
  162.9 13.3 %collective-permute-start.10 = (f32[13,1024]{1,0:T(8,128)}, f32[13,1024]{1,0:T(8,128)}, u32[]{:S(2)}, u32[]{:S(2)}) collective-permute-start(f32[13,1024]{1,0:T(8,128)} %slice.435), channel_id=1, source_target_pairs={{0,1},{1,0},{2,3},{3,2},{4,5},{5,4},{6,7},{7,6},{8,9},{9,8},{10,11... | collective-permute-start | bytes 159752 | tf_op jit(solution)/shard_map/ppermute | solution.py:109
  168.5 71.5 %collective-permute-start.15 = (bf16[256,1792]{1,0:T(8,128)(2,1)}, bf16[256,1792]{1,0:T(8,128)(2,1)}, u32[]{:S(2)}, u32[]{:S(2)}) collective-permute-start(bf16[256,1792]{1,0:T(8,128)(2,1)} %constant_dynamic-slice_fusion.24), channel_id=1, source_target_pairs={{0,2},{2,0},{4,6},{6,4},{8,10},{10,8},{12,14},{14,12},{16,18},{18,... | collective-permute-start | bytes 2752520 | tf_op jit(solution)/shard_map/ppermute | solution.py:109
  169.5 31.2 %collective-permute-start.26 = (bf16[256,1024]{1,0:T(8,128)(2,1)}, bf16[256,1024]{1,0:T(8,128)(2,1)}, u32[]{:S(2)}, u32[]{:S(2)}) collective-permute-start(bf16[256,1024]{1,0:T(8,128)(2,1)} %constant_dynamic-slice_fusion.18), channel_id=1, source_target_pairs={{0,2},{2,0},{4,6},{6,4},{8,10},{10,8},{12,14},{14,12},{16,18},{18,... | collective-permute-start | bytes 1572872 | tf_op jit(solution)/shard_map/ppermute | solution.py:109
  170.8 32.3 %collective-permute-start.24 = (bf16[256,1024]{1,0:T(8,128)(2,1)}, bf16[256,1024]{1,0:T(8,128)(2,1)}, u32[]{:S(2)}, u32[]{:S(2)}) collective-permute-start(bf16[256,1024]{1,0:T(8,128)(2,1)} %constant_dynamic-slice_fusion.20), channel_id=1, source_target_pairs={{0,2},{2,0},{4,6},{6,4},{8,10},{10,8},{12,14},{14,12},{16,18},{18,... | collective-permute-start | bytes 1572872 | tf_op jit(solution)/shard_map/ppermute | solution.py:109
  188.2 19.2 %collective-permute-start.34 = (bf16[512,256]{1,0:T(8,128)(2,1)}, bf16[512,256]{1,0:T(8,128)(2,1)}, u32[]{:S(2)}, u32[]{:S(2)}) collective-permute-start(bf16[512,256]{1,0:T(8,128)(2,1)} %constant_dynamic-slice_fusion.15), channel_id=1, source_target_pairs={{0,2},{2,0},{4,6},{6,4},{8,10},{10,8},{12,14},{14,12},{16,18},{18,... | collective-permute-start | bytes 786440 | tf_op jit(solution)/shard_map/ppermute | solution.py:109
  203.0 63.3 %collective-permute-start.43 = (bf16[256,2048]{1,0:T(8,128)(2,1)}, bf16[256,2048]{1,0:T(8,128)(2,1)S(1)}, u32[]{:S(2)}, u32[]{:S(2)}) collective-permute-start(bf16[256,2048]{1,0:T(8,128)(2,1)} %fusion.30), channel_id=1, source_target_pairs={{0,2},{2,0},{4,6},{6,4},{8,10},{10,8},{12,14},{14,12},{16,18},{18,... | collective-permute-start | bytes 3145736 | tf_op jit(solution)/shard_map/ppermute | solution.py:109
  207.2 61.4 %collective-permute-start.62 = (bf16[512,512]{1,0:T(8,128)(2,1)S(1)}, bf16[512,512]{1,0:T(8,128)(2,1)S(1)}, u32[]{:S(2)}, u32[]{:S(2)}) collective-permute-start(bf16[512,512]{1,0:T(8,128)(2,1)S(1)} %copy-done.81), channel_id=1, source_target_pairs={{0,2},{2,0},{4,6},{6,4},{8,10},{10,8},{12,14},{14,12},{16,18},{18,... | collective-permute-start | bytes 1572872 | tf_op jit(solution)/shard_map/ppermute | solution.py:109
  207.4 19.4 %collective-permute-start.27 = (bf16[128,1024]{1,0:T(8,128)(2,1)S(1)}, bf16[128,1024]{1,0:T(8,128)(2,1)S(1)}, u32[]{:S(2)}, u32[]{:S(2)}) collective-permute-start(bf16[128,1024]{1,0:T(8,128)(2,1)S(1)} %constant_dynamic-slice_fusion.17), channel_id=1, source_target_pairs={{0,4},{2,6},{4,0},{6,2},{8,12},{10,14},{12,8},{14,10},{16,20},{18,... | collective-permute-start | bytes 786440 | tf_op jit(solution)/shard_map/ppermute | solution.py:109
  232.8 13.6 %collective-permute-start.25 = (bf16[128,1024]{1,0:T(8,128)(2,1)S(1)}, bf16[128,1024]{1,0:T(8,128)(2,1)S(1)}, u32[]{:S(2)}, u32[]{:S(2)}) collective-permute-start(bf16[128,1024]{1,0:T(8,128)(2,1)S(1)} %constant_dynamic-slice_fusion.19), channel_id=1, source_target_pairs={{0,4},{2,6},{4,0},{6,2},{8,12},{10,14},{12,8},{14,10},{16,20},{18,... | collective-permute-start | bytes 786440 | tf_op jit(solution)/shard_map/ppermute | solution.py:109
  237.7 18.0 %collective-permute-start.53 = (bf16[128,1024]{1,0:T(8,128)(2,1)S(1)}, bf16[128,1024]{1,0:T(8,128)(2,1)S(1)}, u32[]{:S(2)}, u32[]{:S(2)}) collective-permute-start(bf16[128,1024]{1,0:T(8,128)(2,1)S(1)} %constant_dynamic-slice_fusion.7), channel_id=1, source_target_pairs={{0,4},{2,6},{4,0},{6,2},{8,12},{10,14},{12,8},{14,10},{16,20},{18,... | collective-permute-start | bytes 786440 | tf_op jit(solution)/shard_map/ppermute | solution.py:109
  246.4 22.6 %collective-permute-start.64 = (bf16[512,512]{1,0:T(8,128)(2,1)S(1)}, bf16[512,512]{1,0:T(8,128)(2,1)S(1)}, u32[]{:S(2)}, u32[]{:S(2)}) collective-permute-start(bf16[512,512]{1,0:T(8,128)(2,1)S(1)} %add_convert_fusion.3), channel_id=1, source_target_pairs={{0,1},{1,0},{2,3},{3,2},{4,5},{5,4},{6,7},{7,6},{8,9},{9,8},{10,11... | collective-permute-start | bytes 1572872 | tf_op jit(solution)/shard_map/ppermute | solution.py:109
  255.7 36.6 %collective-permute-start.16 = (bf16[128,1792]{1,0:T(8,128)(2,1)S(1)}, bf16[128,1792]{1,0:T(8,128)(2,1)S(1)}, u32[]{:S(2)}, u32[]{:S(2)}) collective-permute-start(bf16[128,1792]{1,0:T(8,128)(2,1)S(1)} %constant_dynamic-slice_fusion.23), channel_id=1, source_target_pairs={{0,4},{2,6},{4,0},{6,2},{8,12},{10,14},{12,8},{14,10},{16,20},{18,... | collective-permute-start | bytes 1376264 | tf_op jit(solution)/shard_map/ppermute | solution.py:109
  268.9 31.8 %collective-permute-start.44 = (bf16[128,2048]{1,0:T(8,128)(2,1)S(1)}, bf16[128,2048]{1,0:T(8,128)(2,1)S(1)}, u32[]{:S(2)}, u32[]{:S(2)}) collective-permute-start(bf16[128,2048]{1,0:T(8,128)(2,1)S(1)} %constant_dynamic-slice_fusion.11), channel_id=1, source_target_pairs={{0,1},{1,0},{2,3},{3,2},{4,5},{5,4},{6,7},{7,6},{8,9},{9,8},{10,11... | collective-permute-start | bytes 1572872 | tf_op jit(solution)/shard_map/ppermute | solution.py:109
  272.7 18.0 %collective-permute-start.65 = (bf16[256,512]{1,0:T(8,128)(2,1)S(1)}, bf16[256,512]{1,0:T(8,128)(2,1)S(1)}, u32[]{:S(2)}, u32[]{:S(2)}) collective-permute-start(bf16[256,512]{1,0:T(8,128)(2,1)S(1)} %constant_dynamic-slice_fusion.1), channel_id=1, source_target_pairs={{0,4},{2,6},{4,0},{6,2},{8,12},{10,14},{12,8},{14,10},{16,20},{18,... | collective-permute-start | bytes 786440 | tf_op jit(solution)/shard_map/ppermute | solution.py:109
  292.5 15.0 %collective-permute-start.17 = (bf16[64,1792]{1,0:T(8,128)(2,1)S(1)}, bf16[64,1792]{1,0:T(8,128)(2,1)S(1)}, u32[]{:S(2)}, u32[]{:S(2)}) collective-permute-start(bf16[64,1792]{1,0:T(8,128)(2,1)S(1)} %constant_dynamic-slice_fusion.22), channel_id=1, source_target_pairs={{0,1},{1,0},{2,3},{3,2},{4,5},{5,4},{6,7},{7,6},{8,9},{9,8},{10,11... | collective-permute-start | bytes 688136 | tf_op jit(solution)/shard_map/ppermute | solution.py:109
  294.5 14.5 %collective-permute-start.32 = (bf16[128,1024]{1,0:T(8,128)(2,1)S(1)}, bf16[128,1024]{1,0:T(8,128)(2,1)S(1)}, u32[]{:S(2)}, u32[]{:S(2)}) collective-permute-start(bf16[128,1024]{1,0:T(8,128)(2,1)S(1)} %pad_maximum_fusion.20), channel_id=1, source_target_pairs={{0,4},{2,6},{4,0},{6,2},{8,12},{10,14},{12,8},{14,10},{16,20},{18,... | collective-permute-start | bytes 786440 | tf_op jit(solution)/shard_map/ppermute | solution.py:109
  300.9 16.4 %collective-permute-start.45 = (bf16[64,2048]{1,0:T(8,128)(2,1)S(1)}, bf16[64,2048]{1,0:T(8,128)(2,1)S(1)}, u32[]{:S(2)}, u32[]{:S(2)}) collective-permute-start(bf16[64,2048]{1,0:T(8,128)(2,1)S(1)} %constant_dynamic-slice_fusion.10), channel_id=1, source_target_pairs={{0,4},{2,6},{4,0},{6,2},{8,12},{10,14},{12,8},{14,10},{16,20},{18,... | collective-permute-start | bytes 786440 | tf_op jit(solution)/shard_map/ppermute | solution.py:109
  309.2 36.2 %collective-permute-start.33 = (bf16[256,1024]{1,0:T(8,128)(2,1)S(1)}, bf16[256,1024]{1,0:T(8,128)(2,1)S(1)}, u32[]{:S(2)}, u32[]{:S(2)}) collective-permute-start(bf16[256,1024]{1,0:T(8,128)(2,1)S(1)} %pad_maximum_fusion.11), channel_id=1, source_target_pairs={{0,2},{2,0},{4,6},{6,4},{8,10},{10,8},{12,14},{14,12},{16,18},{18,... | collective-permute-start | bytes 1572872 | tf_op jit(solution)/shard_map/ppermute | solution.py:109
  309.4 36.2 %collective-permute-start.61 = (bf16[256,1024]{1,0:T(8,128)(2,1)S(1)}, bf16[256,1024]{1,0:T(8,128)(2,1)S(1)}, u32[]{:S(2)}, u32[]{:S(2)}) collective-permute-start(bf16[256,1024]{1,0:T(8,128)(2,1)S(1)} %pad_maximum_fusion.13), channel_id=1, source_target_pairs={{0,2},{2,0},{4,6},{6,4},{8,10},{10,8},{12,14},{14,12},{16,18},{18,... | collective-permute-start | bytes 1572872 | tf_op jit(solution)/shard_map/ppermute | solution.py:109
  312.7 19.6 %collective-permute-start.69 = (bf16[256,512]{1,0:T(8,128)(2,1)S(1)}, bf16[256,512]{1,0:T(8,128)(2,1)S(1)}, u32[]{:S(2)}, u32[]{:S(2)}) collective-permute-start(bf16[256,512]{1,0:T(8,128)(2,1)S(1)} %pad_maximum_fusion.24), channel_id=1, source_target_pairs={{0,4},{2,6},{4,0},{6,2},{8,12},{10,14},{12,8},{14,10},{16,20},{18,... | collective-permute-start | bytes 786440 | tf_op jit(solution)/shard_map/ppermute | solution.py:109
  332.4 25.6 %collective-permute-start.70 = (bf16[512,512]{1,0:T(8,128)(2,1)S(1)}, bf16[512,512]{1,0:T(8,128)(2,1)S(1)}, u32[]{:S(2)}, u32[]{:S(2)}) collective-permute-start(bf16[512,512]{1,0:T(8,128)(2,1)S(1)} %pad_maximum_fusion.14), channel_id=1, source_target_pairs={{0,2},{2,0},{4,6},{6,4},{8,10},{10,8},{12,14},{14,12},{16,18},{18,... | collective-permute-start | bytes 1572872 | tf_op jit(solution)/shard_map/ppermute | solution.py:109
  338.6 19.0 %collective-permute-start.22 = (bf16[128,1792]{1,0:T(8,128)(2,1)S(1)}, bf16[128,1792]{1,0:T(8,128)(2,1)S(1)}, u32[]{:S(2)}, u32[]{:S(2)}) collective-permute-start(bf16[128,1792]{1,0:T(8,128)(2,1)S(1)} %pad_maximum_fusion.15), channel_id=1, source_target_pairs={{0,4},{2,6},{4,0},{6,2},{8,12},{10,14},{12,8},{14,10},{16,20},{18,... | collective-permute-start | bytes 1376264 | tf_op jit(solution)/shard_map/ppermute | solution.py:109
  343.1 13.9 %collective-permute-start.49 = (bf16[64,2048]{1,0:T(8,128)(2,1)S(1)}, bf16[64,2048]{1,0:T(8,128)(2,1)S(1)}, u32[]{:S(2)}, u32[]{:S(2)}) collective-permute-start(bf16[64,2048]{1,0:T(8,128)(2,1)S(1)} %pad_maximum_fusion.22), channel_id=1, source_target_pairs={{0,4},{2,6},{4,0},{6,2},{8,12},{10,14},{12,8},{14,10},{16,20},{18,... | collective-permute-start | bytes 786440 | tf_op jit(solution)/shard_map/ppermute | solution.py:109
  (240 other events, 1541.0 us)

commit v2 on v1

v2 whole, which is shorter than its diff:
```python
import jax
import jax.numpy as jnp
from jax import lax
from jax.experimental import pallas as pl
from jax.experimental.pallas import tpu as pltpu
from jax.sharding import PartitionSpec as P

HEADS = 8
SEQ = 256
EPS = 1e-06
NEGATIVE = -1000000000.0
LOW = jnp.bfloat16
F32 = jnp.float32
STEP = 64
LIMIT = 40 * 2**20


def as_low(values):
    return values.astype(LOW)


def dot(left, right):
    return jnp.dot(left, right, preferred_element_type=F32)


def dot_left(left, right):
    return lax.dot_general(left, right, (((0,), (0,)), ((), ())), preferred_element_type=F32)


def dot_right(left, right):
    return lax.dot_general(left, right, (((1,), (1,)), ((), ())), preferred_element_type=F32)


def swap(values, axis, bit):
    count = lax.axis_size(axis)
    return lax.ppermute(values, axis, [(at, at ^ bit) for at in range(count)])


def bit_of(axis, bit):
    return (lax.axis_index(axis) // bit) % 2


def bits_of(axis):
    bits, bit = [], 1
    while bit < lax.axis_size(axis):
        bits.append(bit)
        bit *= 2
    return bits


def add_low(first, second):
    return as_low(first.astype(F32) + second.astype(F32))


def split(values, own):
    half = values.shape[0] // 2
    mine = lax.dynamic_slice_in_dim(values, own * half, half, 0)
    other = lax.dynamic_slice_in_dim(values, (1 - own) * half, half, 0)
    return mine, other


def join(mine, other, own):
    swapped = own == 1
    return jnp.concatenate(
        [jnp.where(swapped, other, mine), jnp.where(swapped, mine, other)], 0
    )


def sum_shared(values, order):
    held = []
    steps = [("dp", 1)] + order
    for axis, bit in steps[:-1]:
        own = bit_of(axis, bit)
        mine, other = split(values, own)
        values = add_low(mine, swap(other, axis, bit))
        held.append((axis, bit, own))
    axis, bit = steps[-1]
    values = add_low(values, swap(values, axis, bit))
    for axis, bit, own in reversed(held):
        values = join(values, swap(values, axis, bit), own)
    return values.astype(F32)


def sum_inner(pieces, order):
    held = []
    steps = [("dp", 1)] + order
    for axis, bit in steps[:-1]:
        if axis == "mp":
            keep_count = len(pieces) // 2
            moved = [swap(item, axis, bit) for item in pieces[keep_count:]]
            pieces = [add_low(one, two) for one, two in zip(pieces[:keep_count], moved)]
            continue
        own = bit_of(axis, bit)
        parts = [split(item, own) for item in pieces]
        pieces = [add_low(mine, swap(other, axis, bit)) for mine, other in parts]
        held.append((axis, bit, own))
    axis, bit = steps[-1]
    values = add_low(pieces[0], swap(pieces[0], axis, bit))
    for axis, bit, own in reversed(held):
        values = join(values, swap(values, axis, bit), own)
    return values.astype(F32)


def sigmoid(values):
    return 0.5 * jnp.tanh(0.5 * values) + 0.5


def spans(total, step):
    return [slice(at, at + step) for at in range(0, total, step)]


def at_lane(start, size):
    return pl.ds(pl.multiple_of(start, 128), size)


def normalize(values):
    width = values.shape[1]
    centre = jnp.sum(values, -1, keepdims=True) * (1.0 / width)
    centered = values - centre
    variance = jnp.sum(centered * centered, -1, keepdims=True) * (1.0 / width)
    rstd = lax.rsqrt(variance + EPS)
    return centered * rstd, rstd


def normalize_back(grad, normed, rstd, gain):
    width = grad.shape[1]
    scaled = grad * gain
    first = jnp.sum(scaled, -1, keepdims=True) * (1.0 / width)
    second = jnp.sum(scaled * normed, -1, keepdims=True) * (1.0 / width)
    return rstd * (scaled - first - normed * second)


def columns_sum(values):
    return jnp.sum(values, 0, keepdims=True)


def low_columns_sum(values):
    ones = jnp.ones((16, values.shape[0]), LOW)
    return dot(ones, values)[0:1]


def keep_rows(info, start, rows):
    return jnp.where(
        lax.broadcasted_iota(jnp.int32, (rows, 1), 0) + start < info[2], 1.0, 0.0
    ).astype(F32)


def run(kernel, outs, ins, scratch, flops):
    specs = [pl.BlockSpec(memory_space=pltpu.SMEM)] + [
        pl.BlockSpec(memory_space=pltpu.VMEM) for _ in ins[1:]
    ]
    moved = sum(item.size * item.dtype.itemsize for item in list(ins) + list(outs))
    return pl.pallas_call(
        kernel,
        out_shape=outs,
        in_specs=specs,
        out_specs=[pl.BlockSpec(memory_space=pltpu.VMEM) for _ in outs],
        scratch_shapes=scratch,
        compiler_params=pltpu.CompilerParams(vmem_limit_bytes=LIMIT),
        cost_estimate=pl.CostEstimate(flops=flops, bytes_accessed=moved, transcendentals=0),
    )(*ins)


def shaped(shape, kind):
    return jax.ShapeDtypeStruct(shape, kind)


def pre_kernel(info, x_ref, vec, gated_w, conv_w, a1, values, gates, x1, a2, right_pre, right):
    width = x_ref.shape[1]
    for row in spans(SEQ, STEP):
        normed, _ = normalize(x_ref[row].astype(F32))
        a1[row] = as_low(normed * vec[0:1] + vec[1:2])
    for col in spans(width, 256):
        gate_col = slice(col.start + width, col.stop + width)
        value = dot(a1[...], gated_w[:, col]) + vec[8:9, col]
        gate = sigmoid(dot(a1[...], gated_w[:, gate_col]) + vec[9:10, col])
        values[:, col] = value
        gates[:, col] = gate
        x1[:, col] = x_ref[:, col].astype(F32) + value * gate
    for row in spans(SEQ, STEP):
        normed, _ = normalize(x1[row])
        kept = keep_rows(info, row.start, STEP)
        a2[row] = as_low((normed * vec[2:3] + vec[3:4]) * kept)
    rows = lax.broadcasted_iota(jnp.int32, right_pre.shape, 0)
    first = jnp.where(rows == 0, 0.0, pltpu.roll(dot(a2[...], conv_w[0]), 1, 0))
    last = jnp.where(rows == SEQ - 1, 0.0, pltpu.roll(dot(a2[...], conv_w[2]), SEQ - 1, 0))
    total = first + dot(a2[...], conv_w[1]) + last + vec[10:11, 0 : right_pre.shape[1]]
    right_pre[...] = total
    right[...] = as_low(total * sigmoid(total))


def unpack(refs, counts):
    groups, at = [], 0
    for count in counts:
        groups.append(refs[at : at + count])
        at += count
    return groups


def inner_forward_kernel(pieces, refs):
    info, refs = refs[0], refs[1:]
    (x1, a2, right, vec), left, point, wide, outs, scratch = unpack(
        refs, [4, 2 * pieces - 1, 2 * pieces - 1, pieces, 5, 6]
    )
    x2, normed_ref, slope_ref, depth, rstd_ref = outs
    mixed, total, square, centre_ref, padded, padded_two = scratch
    local = left[0].shape[1]
    inner = local * pieces
    core, offset = info[0], info[1]
    half = a2.shape[1] // 2
    near = a2[:, at_lane(core * half, half)]
    far = a2[:, at_lane((1 - core) * half, half)]
    right_rows = right[...].astype(F32)
    total[...] = jnp.zeros_like(total)
    square[...] = jnp.zeros_like(square)
    for piece in range(pieces):
        for col in spans(local, 256):
            if piece == 0:
                pre = dot(a2[...], left[0][:, col])
            else:
                pre = dot(near, left[2 * piece - 1][:, col]) + dot(far, left[2 * piece][:, col])
            pre = pre + wide[piece][0:16, col].astype(F32)[0:1]
            sigma = sigmoid(pre)
            at = piece * local + col.start
            here = slice(at, at + 256)
            slope_ref[:, here] = as_low(sigma * (1.0 + pre * (1.0 - sigma)))
            value = pre * sigma + right_rows * jnp.where(offset == at, 1.0, 0.0)
            mixed[:, here] = value
            total[...] += value[:, 0:128] + value[:, 128:256]
            squared = value * value
            square[...] += squared[:, 0:128] + squared[:, 128:256]
    centre = jnp.sum(total[...], 1, keepdims=True) * (1.0 / inner)
    variance = jnp.sum(square[...], 1, keepdims=True) * (1.0 / inner) - centre * centre
    rstd = lax.rsqrt(variance + EPS)
    centre_ref[...] = jnp.broadcast_to(centre, centre_ref.shape)
    rstd_ref[...] = jnp.broadcast_to(rstd, rstd_ref.shape)
    for pad in (padded, padded_two):
        pad[0:8] = jnp.zeros((8, 128), F32)
        pad[SEQ + 8 : SEQ + 16] = jnp.zeros((8, 128), F32)
    kept = keep_rows(info, 0, SEQ)
    for piece in range(pieces):

        def one(at, pad):
            col = at_lane(at, 128)
            here = at_lane(piece * local + at, 128)
            vectors = wide[piece][:, col].astype(F32)
            normed = (mixed[:, here] - centre_ref[...]) * rstd_ref[...]
            normed_ref[:, here] = as_low(normed)
            pad[8 : SEQ + 8] = (normed * vectors[2:3] + vectors[3:4]) * kept
            result = pad[4 : SEQ + 4] * vectors[4:5]
            for tap in range(1, 9):
                result = result + pad[4 + tap : SEQ + 4 + tap] * vectors[4 + tap : 5 + tap]
            depth[:, here] = as_low(result)

        def step(index, carry):
            one(index * 256, padded)
            one(index * 256 + 128, padded_two)
            return carry

        lax.fori_loop(0, local // 256, step, 0)
    width = x1.shape[1]
    channels = point[0].shape[1]
    sep = dot(depth[:, 0:local], point[0][...])
    rows = local // 2
    for piece in range(1, pieces):
        base = piece * local
        sep = sep + dot(depth[:, at_lane(base + core * rows, rows)], point[2 * piece - 1][...])
        sep = sep + dot(depth[:, at_lane(base + (1 - core) * rows, rows)], point[2 * piece][...])
    x2[:, 0:channels] = x1[:, 0:channels] + sep + vec[10:11, channels : 2 * channels]
    x2[:, channels:width] = x1[:, channels:width]


def masked_scores(queries, keys, valid, scale):
    return jnp.where(valid, dot_right(queries, keys) * scale, NEGATIVE)


def attention_forward_kernel(
    info, x2, vec, project_w, output_w, a4, qkv, lse, attended, x3, a5
):
    width = x2.shape[1]
    for row in spans(SEQ, STEP):
        normed, _ = normalize(x2[row])
        a4[row] = as_low(normed * vec[4:5] + vec[5:6])
    for col in spans(3 * width, 256):
        part = dot(a4[...], project_w[:, col])
        if col.start < width:
            part = part + vec[11:12, col]
        elif col.start >= 2 * width:
            part = part + vec[12:13, col.start - 2 * width : col.stop - 2 * width]
        qkv[:, col] = as_low(part)
    scale = (width // HEADS) ** (-0.5)
    lanes = lax.broadcasted_iota(jnp.int32, (SEQ, 128), 1)
    valid = lax.broadcasted_iota(jnp.int32, (SEQ, SEQ), 1) < info[2]
    logs = jnp.zeros((SEQ, 128), F32)
    for pair in range(width // 128):
        at = pair * 128
        queries = qkv[:, at : at + 128]
        keys = qkv[:, width + at : width + at + 128]
        vals = qkv[:, 2 * width + at : 2 * width + at + 128]
        mixed = []
        for side in range(2):
            mine = (lanes < 64) if side == 0 else (lanes >= 64)
            scores = masked_scores(jnp.where(mine, queries, 0), keys, valid, scale)
            highest = jnp.max(scores, -1, keepdims=True)
            weights = jnp.exp(scores - highest)
            total = jnp.sum(weights, -1, keepdims=True)
            mixed.append(dot(as_low(weights * (1.0 / total)), vals))
            logs = jnp.where(lanes == 2 * pair + side, highest + jnp.log(total), logs)
        attended[:, at : at + 128] = as_low(jnp.where(lanes < 64, mixed[0], mixed[1]))
    lse[...] = logs
    x3[...] = x2[...] + dot(attended[...], output_w[...]) + vec[13:14]
    for row in spans(SEQ, STEP):
        normed, _ = normalize(x3[row])
        a5[row] = as_low(normed * vec[6:7] + vec[7:8])


def feed_kernel(pieces, refs):
    info, refs = refs[0], refs[1:]
    (a5, x3, top, vec), expand, shrink, wide, outs, scratch = unpack(
        refs, [4, 2 * pieces - 1, 2 * pieces - 1, pieces, 8, 5]
    )
    output, shrink_keep, shrink_send, expand_keep, expand_send, dx3, fixed, grad_bias = outs
    hidden, slope, d_expand, shrunk, d_a5 = scratch
    local = expand[0].shape[1]
    width = x3.shape[1]
    half, rows = width // 2, local // 2
    core = info[0]
    near = a5[:, at_lane(core * half, half)]
    far = a5[:, at_lane((1 - core) * half, half)]
    for piece in range(pieces):
        for col in spans(local, 256):
            if piece == 0:
                pre = dot(a5[...], expand[0][:, col])
            else:
                pre = dot(near, expand[2 * piece - 1][:, col]) + dot(
                    far, expand[2 * piece][:, col]
                )
            pre = pre + wide[piece][0:16, col].astype(F32)[1:2]
            sigma = sigmoid(pre)
            here = slice(piece * local + col.start, piece * local + col.stop)
            hidden[:, here] = as_low(pre * sigma)
            slope[:, here] = sigma * (1.0 + pre * (1.0 - sigma))
    blocks = [(0, shrink[0])]
    for piece in range(1, pieces):
        blocks.append((piece * local + core * rows, shrink[2 * piece - 1]))
        blocks.append((piece * local + (1 - core) * rows, shrink[2 * piece]))
    for base, weights in blocks:
        count = weights.shape[0]
        part = dot(hidden[:, at_lane(base, count)], weights[...])
        if weights is shrink[0]:
            shrunk[...] = part
        else:
            shrunk[...] += part
        for row in spans(count, min(256, count)):
            size = row.stop - row.start
            here = at_lane(base + row.start, size)
            back = dot_right(top[...], weights[row])
            d_expand[:, here] = as_low(back * slope[:, here])
    for row in spans(SEQ, STEP):
        output[row] = as_low(x3[row] + shrunk[row] + vec[14:15])
    for piece in range(pieces):
        base = piece * local
        cols = slice(base, base + local)
        for side, shrink_out, expand_out in (
            (1 - core, shrink_send, expand_send),
            (core, shrink_keep, expand_keep),
        ):
            shrink_out[piece] = as_low(
                dot_left(hidden[:, at_lane(base + side * rows, rows)], top[...])
            )
            expand_out[piece] = as_low(
                dot_left(a5[:, at_lane(side * half, half)], d_expand[:, cols])
            )
        grad_bias[:, cols] = jnp.broadcast_to(low_columns_sum(d_expand[:, cols]), (8, local))
        if piece == 0:
            d_a5[...] = dot_right(d_expand[:, cols], expand[0][...])
        else:
            d_a5[:, at_lane(core * half, half)] += dot_right(
                d_expand[:, cols], expand[2 * piece - 1][...]
            )
            d_a5[:, at_lane((1 - core) * half, half)] += dot_right(
                d_expand[:, cols], expand[2 * piece][...]
            )
    fixed[...] = jnp.zeros_like(fixed)
    for row in spans(SEQ, STEP):
        normed, rstd = normalize(x3[row])
        grad = d_a5[row]
        dx3[row] = top[row].astype(F32) + normalize_back(grad, normed, rstd, vec[6:7])
        fixed[6:7] += columns_sum(grad * normed)
        fixed[7:8] += columns_sum(grad)
    fixed[13:14] = low_columns_sum(top[...])


def attention_backward_kernel(
    info, dx3, attended, output_w, qkv, lse, a4, project_w, x2, vec, before,
    send, keep, dx2, d_sep, fixed, d_out, d_att, d_proj
):
    width = x2.shape[1]
    half = width // 2
    core = info[0]
    fixed[...] = before[...]
    d_out[...] = as_low(dx3[...])
    d_att[...] = as_low(dot_right(d_out[...], output_w[...]))
    scale = (width // HEADS) ** (-0.5)
    lanes = lax.broadcasted_iota(jnp.int32, (SEQ, 128), 1)
    valid = lax.broadcasted_iota(jnp.int32, (SEQ, SEQ), 1) < info[2]
    for pair in range(width // 128):
        at = pair * 128
        queries = qkv[:, at : at + 128]
        keys = qkv[:, width + at : width + at + 128]
        vals = qkv[:, 2 * width + at : 2 * width + at + 128]
        grads = d_att[:, at : at + 128]
        parts = []
        for side in range(2):
            head = 2 * pair + side
            mine = (lanes < 64) if side == 0 else (lanes >= 64)
            scores = masked_scores(jnp.where(mine, queries, 0), keys, valid, scale)
            probs = jnp.exp(scores - lse[:, head : head + 1])
            d_vals = dot_left(as_low(probs), grads)
            d_probs = dot_right(jnp.where(mine, grads, 0), vals)
            weighted = jnp.sum(d_probs * probs, -1, keepdims=True)
            d_scores = as_low(probs * (d_probs - weighted))
            parts.append((dot(d_scores, keys) * scale, dot_left(d_scores, queries) * scale, d_vals))
        for kind in range(3):
            here = slice(kind * width + at, kind * width + at + 128)
            d_proj[:, here] = as_low(jnp.where(lanes < 64, parts[0][kind], parts[1][kind]))
    for side, out in ((1 - core, send), (core, keep)):
        here = at_lane(side * half, half)
        out[:, 3 * width :] = as_low(dot_left(attended[:, here], d_out[...]))
        out[:, : 3 * width] = as_low(dot_left(a4[:, here], d_proj[...]))
    fixed[12:13] = low_columns_sum(d_out[...])
    fixed[10:11] = low_columns_sum(d_proj[:, :width])
    fixed[11:12] = low_columns_sum(d_proj[:, 2 * width :])
    dx2[...] = dot_right(d_proj[...], project_w[...])
    for row in spans(SEQ, STEP):
        normed, rstd = normalize(x2[row])
        grad = dx2[row]
        dx2[row] = dx3[row] + normalize_back(grad, normed, rstd, vec[4:5])
        fixed[4:5] += columns_sum(grad * normed)
        fixed[5:6] += columns_sum(grad)
    channels = d_sep.shape[1]
    d_sep[...] = as_low(dx2[:, :channels])
    fixed[14:15, channels : 2 * channels] = low_columns_sum(d_sep[...])


def inner_backward_kernel(pieces, refs):
    info, refs = refs[0], refs[1:]
    (d_sep, depth, normed_ref, slope_ref, rstd_ref, a2, bias_before), point, left, wide, outs, scratch = unpack(
        refs, [7, 2 * pieces - 1, 2 * pieces - 1, pieces, 7, 6]
    )
    left_keep, left_send, point_keep, point_send, d_a2, d_right, grads = outs
    d_depth, padded, padded_two, d_left, first_ref, second_ref = scratch
    local = left[0].shape[1]
    inner = local * pieces
    core, offset = info[0], info[1]
    rows = local // 2
    half = a2.shape[1] // 2
    blocks = [(0, point[0])]
    for piece in range(1, pieces):
        blocks.append((piece * (local // 128) + core * (rows // 128), point[2 * piece - 1]))
        blocks.append((piece * (local // 128) + (1 - core) * (rows // 128), point[2 * piece]))
    for base, weights in blocks:
        count = weights.shape[0]
        for row in spans(count, min(256, count)):
            back = dot_right(d_sep[...], weights[row])
            for part in range((row.stop - row.start) // 128):
                d_depth[base + row.start // 128 + part, 8 : SEQ + 8] = back[
                    :, part * 128 : (part + 1) * 128
                ]
    first_ref[...] = jnp.zeros_like(first_ref)
    second_ref[...] = jnp.zeros_like(second_ref)
    for pad in (padded, padded_two):
        pad[0:8] = jnp.zeros((8, 128), F32)
        pad[SEQ + 8 : SEQ + 16] = jnp.zeros((8, 128), F32)
    grads[...] = jnp.zeros_like(grads)
    grads[1:2] = bias_before[0:1]
    kept = keep_rows(info, 0, SEQ)
    for piece in range(pieces):

        def one(at, pad):
            col = at_lane(at, 128)
            here = at_lane(piece * local + at, 128)
            index = (piece * local + at) // 128
            vectors = wide[piece][:, col].astype(F32)
            d_depth[index, 0:8] = jnp.zeros((8, 128), F32)
            d_depth[index, SEQ + 8 : SEQ + 16] = jnp.zeros((8, 128), F32)
            normed = normed_ref[:, here].astype(F32)
            pad[8 : SEQ + 8] = (normed * vectors[2:3] + vectors[3:4]) * kept
            own = d_depth[index, 8 : SEQ + 8]
            result = d_depth[index, 12 : SEQ + 12] * vectors[4:5]
            grads[4:5, here] = columns_sum(pad[4 : SEQ + 4] * own)
            for tap in range(1, 9):
                result = result + d_depth[index, 12 - tap : SEQ + 12 - tap] * vectors[4 + tap : 5 + tap]
                grads[4 + tap : 5 + tap, here] = columns_sum(pad[4 + tap : SEQ + 4 + tap] * own)
            result = result * kept
            grads[2:3, here] = columns_sum(result * normed)
            grads[3:4, here] = columns_sum(result)
            scaled = result * vectors[2:3]
            first_ref[...] += scaled
            second_ref[...] += scaled * normed
            d_depth[index, 8 : SEQ + 8] = scaled

        def step(index, carry):
            one(index * 256, padded)
            one(index * 256 + 128, padded_two)
            return carry

        lax.fori_loop(0, local // 256, step, 0)
    first_ref[...] = jnp.broadcast_to(
        jnp.sum(first_ref[...], 1, keepdims=True) * (1.0 / inner), first_ref.shape
    )
    second_ref[...] = jnp.broadcast_to(
        jnp.sum(second_ref[...], 1, keepdims=True) * (1.0 / inner), second_ref.shape
    )

    def back(index, carry):
        here = at_lane(index * 128, 128)
        normed = normed_ref[:, here].astype(F32)
        d_mixed = rstd_ref[...] * (
            d_depth[index, 8 : SEQ + 8] - first_ref[...] - normed * second_ref[...]
        )
        d_depth[index, 8 : SEQ + 8] = d_mixed
        d_left[:, here] = as_low(d_mixed * slope_ref[:, here].astype(F32))
        return carry

    lax.fori_loop(0, inner // 128, back, 0)
    for part in range(d_right.shape[1] // 128):
        d_right[:, part * 128 : (part + 1) * 128] = d_depth[offset // 128 + part, 8 : SEQ + 8]
    for piece in range(pieces):
        base = piece * local
        cols = slice(base, base + local)
        for side, left_out, point_out in (
            (1 - core, left_send, point_send),
            (core, left_keep, point_keep),
        ):
            left_out[piece] = as_low(
                dot_left(a2[:, at_lane(side * half, half)], d_left[:, cols])
            )
            point_out[piece] = as_low(
                dot_left(depth[:, at_lane(base + side * rows, rows)], d_sep[...])
            )
        grads[0:1, cols] = low_columns_sum(d_left[:, cols])
        if piece == 0:
            d_a2[...] = dot_right(d_left[:, cols], left[0][...])
        else:
            d_a2[:, at_lane(core * half, half)] += dot_right(d_left[:, cols], left[2 * piece - 1][...])
            d_a2[:, at_lane((1 - core) * half, half)] += dot_right(d_left[:, cols], left[2 * piece][...])


def last_kernel(
    info, d_a2_left, d_right, right_pre, conv_w, a2, x1, dx2, values, gates, a1, gated_w, x_ref, vec, before,
    send, keep, input_grad, fixed, shifted, d_a2, d_gated
):
    width = x1.shape[1]
    half = width // 2
    channels = right_pre.shape[1]
    core = info[0]
    fixed[...] = before[...]
    pre = right_pre[...]
    sigma = sigmoid(pre)
    low = as_low(d_right[...] * (sigma * (1.0 + pre * (1.0 - sigma))))
    fixed[14:15, 0:channels] = low_columns_sum(low)
    wide = low.astype(F32)
    rows = lax.broadcasted_iota(jnp.int32, wide.shape, 0)
    shifted[:, 0:channels] = as_low(
        jnp.where(rows == SEQ - 1, 0.0, pltpu.roll(wide, SEQ - 1, 0))
    )
    shifted[:, channels : 2 * channels] = low
    shifted[:, 2 * channels :] = as_low(jnp.where(rows == 0, 0.0, pltpu.roll(wide, 1, 0)))
    total = d_a2_left[...]
    for tap in range(3):
        total = total + dot_right(shifted[:, tap * channels : (tap + 1) * channels], conv_w[tap])
    d_a2[...] = total
    for row in spans(SEQ, STEP):
        normed, rstd = normalize(x1[row])
        grad = d_a2[row] * keep_rows(info, row.start, STEP)
        fixed[2:3] += columns_sum(grad * normed)
        fixed[3:4] += columns_sum(grad)
        dx1 = dx2[row] + normalize_back(grad, normed, rstd, vec[2:3])
        input_grad[row] = dx1
        gate = gates[row]
        scaled = dx1 * gate
        d_gated[row, 0:width] = as_low(scaled)
        d_gated[row, width:] = as_low(scaled * values[row] * (1.0 - gate))
    for side, out in ((1 - core, send), (core, keep)):
        here = at_lane(side * half, half)
        out[:, 0 : 2 * width] = as_low(dot_left(a1[:, here], d_gated[...]))
        out[:, 2 * width :] = as_low(dot_left(a2[:, here], shifted[...]))
    sums = low_columns_sum(d_gated[...])
    fixed[8:9] = sums[:, 0:width]
    fixed[9:10] = sums[:, width:]
    d_a2[...] = dot_right(d_gated[...], gated_w[...])
    for row in spans(SEQ, STEP):
        normed, rstd = normalize(x_ref[row].astype(F32))
        grad = d_a2[row]
        fixed[0:1] += columns_sum(grad * normed)
        fixed[1:2] += columns_sum(grad)
        input_grad[row] += normalize_back(grad, normed, rstd, vec[0:1])


def gather_inner(own_piece):
    core = bit_of("dp", 1)
    mine, _ = split(own_piece, core)
    halves = [mine]
    for bit in bits_of("mp"):
        halves = halves + [swap(item, "mp", bit) for item in halves]
    found = [own_piece]
    for item in halves[1:]:
        found += [item, swap(item, "dp", 1)]
    return found


def gather_small(own_piece):
    items = [own_piece]
    for bit in bits_of("mp"):
        items = items + [swap(item, "mp", bit) for item in items]
    return items


def finish_shared(mine, other, order):
    own = bit_of("dp", 1)
    values = add_low(mine, swap(other, "dp", 1))
    held = [("dp", 1, own)]
    for axis, bit in order[:-1]:
        own = bit_of(axis, bit)
        mine, other = split(values, own)
        values = add_low(mine, swap(other, axis, bit))
        held.append((axis, bit, own))
    axis, bit = order[-1]
    values = add_low(values, swap(values, axis, bit))
    for axis, bit, own in reversed(held):
        values = join(values, swap(values, axis, bit), own)
    return values.astype(F32)


def finish_inner(mine, other, order):
    values = add_low(mine, swap(other, "dp", 1))
    pieces = [values[at] for at in range(values.shape[0])]
    held = [("dp", 1, bit_of("dp", 1))]
    for axis, bit in order[:-1]:
        if axis == "mp":
            keep_count = len(pieces) // 2
            moved = [swap(item, axis, bit) for item in pieces[keep_count:]]
            pieces = [add_low(one, two) for one, two in zip(pieces[:keep_count], moved)]
            continue
        own = bit_of(axis, bit)
        parts = [split(item, own) for item in pieces]
        pieces = [add_low(mine, swap(other, axis, bit)) for mine, other in parts]
        held.append((axis, bit, own))
    axis, bit = order[-1]
    values = add_low(pieces[0], swap(pieces[0], axis, bit))
    for axis, bit, own in reversed(held):
        values = join(values, swap(values, axis, bit), own)
    return values.astype(F32)


def body(
    cell_input,
    lengths,
    out_grad,
    norm_params,
    gated_weight,
    gated_bias,
    left_weight,
    left_bias,
    conv_weight,
    conv_bias,
    inner_norm,
    depth_weight,
    point_weight,
    point_bias,
    project_weight,
    project_bias,
    output_weight,
    output_bias,
    expand_weight,
    expand_bias,
    shrink_weight,
    shrink_bias,
):
    width = cell_input.shape[1]
    channels = conv_weight.shape[2]
    local = left_weight.shape[1]
    pieces = lax.axis_size("mp")
    inner = local * pieces
    tokens = cell_input.shape[0]
    assert tokens == SEQ
    mp_bits = bits_of("mp")[::-1]
    dp_bits = bits_of("dp")[1:]
    mp_first = [("mp", bit) for bit in mp_bits] + [("dp", bit) for bit in dp_bits]
    dp_first = (
        [("dp", dp_bits[0])] + [("mp", bit) for bit in mp_bits] + [("dp", bit) for bit in dp_bits[1:]]
    )
    core = bit_of("dp", 1)
    info = jnp.stack([core, lax.axis_index("mp") * local, lengths[0]]).astype(jnp.int32)

    left = gather_inner(left_weight)
    point = gather_inner(point_weight)
    wide = gather_small(
        jnp.concatenate(
            [
                left_bias[None],
                expand_bias[None],
                inner_norm,
                depth_weight,
                jnp.zeros((3, local), LOW),
            ],
            0,
        )
    )
    expand = gather_inner(expand_weight)
    shrink = gather_inner(shrink_weight)
    vec = jnp.concatenate(
        [
            norm_params.reshape(8, width),
            gated_bias.reshape(2, width),
            jnp.concatenate([conv_bias, point_bias]).reshape(1, width),
            project_bias,
            output_bias[None],
            shrink_bias[None],
            jnp.zeros((1, width), LOW),
        ],
        0,
    ).astype(F32)

    a1, values, gates, x1, a2, right_pre, right = run(
        pre_kernel,
        [
            shaped((tokens, width), LOW),
            shaped((tokens, width), F32),
            shaped((tokens, width), F32),
            shaped((tokens, width), F32),
            shaped((tokens, width), LOW),
            shaped((tokens, channels), F32),
            shaped((tokens, channels), LOW),
        ],
        [info, cell_input, vec, gated_weight, conv_weight],
        [],
        10**9,
    )
    x2, normed, slope, depth, rstd = run(
        lambda *refs: inner_forward_kernel(pieces, refs),
        [
            shaped((tokens, width), F32),
            shaped((tokens, inner), LOW),
            shaped((tokens, inner), LOW),
            shaped((tokens, inner), LOW),
            shaped((tokens, 128), F32),
        ],
        [info, x1, a2, right, vec] + left + point + wide,
        [
            pltpu.VMEM((tokens, inner), F32),
            pltpu.VMEM((tokens, 128), F32),
            pltpu.VMEM((tokens, 128), F32),
            pltpu.VMEM((tokens, 128), F32),
            pltpu.VMEM((tokens + 16, 128), F32),
            pltpu.VMEM((tokens + 16, 128), F32),
        ],
        2 * 10**9,
    )
    a4, qkv, lse, attended, x3, a5 = run(
        attention_forward_kernel,
        [
            shaped((tokens, width), LOW),
            shaped((tokens, 3 * width), LOW),
            shaped((tokens, 128), F32),
            shaped((tokens, width), LOW),
            shaped((tokens, width), F32),
            shaped((tokens, width), LOW),
        ],
        [info, x2, vec, project_weight, output_weight],
        [],
        10**9,
    )
    cell_output, shrink_keep, shrink_send, expand_keep, expand_send, dx3, fixed, expand_sum = run(
        lambda *refs: feed_kernel(pieces, refs),
        [
            shaped((tokens, width), LOW),
            shaped((pieces, local // 2, width), LOW),
            shaped((pieces, local // 2, width), LOW),
            shaped((pieces, width // 2, local), LOW),
            shaped((pieces, width // 2, local), LOW),
            shaped((tokens, width), F32),
            shaped((16, width), F32),
            shaped((8, inner), F32),
        ],
        [info, a5, x3, out_grad, vec] + expand + shrink + wide,
        [
            pltpu.VMEM((tokens, inner), LOW),
            pltpu.VMEM((tokens, inner), F32),
            pltpu.VMEM((tokens, inner), LOW),
            pltpu.VMEM((tokens, width), F32),
            pltpu.VMEM((tokens, width), F32),
        ],
        3 * 10**9,
    )
    grad_shrink = finish_inner(shrink_keep, shrink_send, mp_first)
    grad_expand = finish_inner(expand_keep, expand_send, dp_first)
    proj_send, proj_keep, dx2, d_sep, fixed = run(
        attention_backward_kernel,
        [
            shaped((width // 2, 4 * width), LOW),
            shaped((width // 2, 4 * width), LOW),
            shaped((tokens, width), F32),
            shaped((tokens, channels), LOW),
            shaped((16, width), F32),
        ],
        [info, dx3, attended, output_weight, qkv, lse, a4, project_weight, x2, vec, fixed],
        [
            pltpu.VMEM((tokens, width), LOW),
            pltpu.VMEM((tokens, width), LOW),
            pltpu.VMEM((tokens, 3 * width), LOW),
        ],
        2 * 10**9,
    )
    both = finish_shared(proj_keep, proj_send, mp_first)
    left_keep, left_send, point_keep, point_send, d_a2, d_right, wide_sums = run(
        lambda *refs: inner_backward_kernel(pieces, refs),
        [
            shaped((pieces, width // 2, local), LOW),
            shaped((pieces, width // 2, local), LOW),
            shaped((pieces, local // 2, channels), LOW),
            shaped((pieces, local // 2, channels), LOW),
            shaped((tokens, width), F32),
            shaped((tokens, channels), F32),
            shaped((16, inner), F32),
        ],
        [info, d_sep, depth, normed, slope, rstd, a2, expand_sum] + point + left + wide,
        [
            pltpu.VMEM((inner // 128, tokens + 16, 128), F32),
            pltpu.VMEM((tokens + 16, 128), F32),
            pltpu.VMEM((tokens + 16, 128), F32),
            pltpu.VMEM((tokens, inner), LOW),
            pltpu.VMEM((tokens, 128), F32),
            pltpu.VMEM((tokens, 128), F32),
        ],
        3 * 10**9,
    )
    grad_left = finish_inner(left_keep, left_send, dp_first)
    grad_point = finish_inner(point_keep, point_send, mp_first)
    last_send, last_keep, input_grad, fixed = run(
        last_kernel,
        [
            shaped((width // 2, 2 * width + 3 * channels), LOW),
            shaped((width // 2, 2 * width + 3 * channels), LOW),
            shaped((tokens, width), F32),
            shaped((16, width), F32),
        ],
        [
            info,
            d_a2,
            d_right,
            right_pre,
            conv_weight,
            a2,
            x1,
            dx2,
            values,
            gates,
            a1,
            gated_weight,
            cell_input,
            vec,
            fixed,
        ],
        [
            pltpu.VMEM((tokens, 3 * channels), LOW),
            pltpu.VMEM((tokens, width), F32),
            pltpu.VMEM((tokens, 2 * width), LOW),
        ],
        2 * 10**9,
    )
    last = finish_shared(last_keep, last_send, dp_first)
    grad_conv = jnp.stack(
        [
            last[:, 2 * width + at * channels : 2 * width + (at + 1) * channels]
            for at in range(3)
        ]
    )

    chunks = [wide_sums[:, at : at + local] for at in range(0, inner, local)]
    for bit in mp_bits:
        count = len(chunks) // 2
        moved = [swap(item, "mp", bit) for item in chunks[count:]]
        chunks = [one + two for one, two in zip(chunks[:count], moved)]
        fixed = fixed + swap(fixed, "mp", bit)
    wide_total = chunks[0]
    for bit in bits_of("dp"):
        fixed = fixed + swap(fixed, "dp", bit)
        wide_total = wide_total + swap(wide_total, "dp", bit)
    return (
        cell_output,
        input_grad,
        fixed[0:8].reshape(4, 2, width),
        last[:, : 2 * width],
        fixed[8:10].reshape(2 * width),
        grad_left,
        wide_total[0],
        grad_conv,
        fixed[14, :channels],
        wide_total[2:4],
        wide_total[4:13],
        grad_point,
        fixed[14, channels:],
        both[:, : 3 * width],
        fixed[10:12],
        both[:, 3 * width :],
        fixed[12],
        grad_expand,
        wide_total[1],
        grad_shrink,
        fixed[13],
    )


def solution(mesh):
    return jax.shard_map(
        body,
        mesh=mesh,
        in_specs=(
            P(("dp", "mp"), None),
            P(("dp", "mp")),
            P(("dp", "mp"), None),
            P(),
            P(),
            P(),
            P(None, "mp"),
            P("mp"),
            P(),
            P(),
            P(None, "mp"),
            P(None, "mp"),
            P("mp", None),
            P(),
            P(),
            P(),
            P(),
            P(),
            P(None, "mp"),
            P("mp"),
            P("mp", None),
            P(),
        ),
        out_specs=(
            P(("dp", "mp"), None),
            P(("dp", "mp"), None),
            P(),
            P(),
            P(),
            P(None, "mp"),
            P("mp"),
            P(),
            P(),
            P(None, "mp"),
            P(None, "mp"),
            P("mp", None),
            P(),
            P(),
            P(),
            P(),
            P(),
            P(None, "mp"),
            P("mp"),
            P("mp", None),
            P(),
        ),
        check_vma=False,
    )
```

time: 383 us -> 286 us (0.75); the launches traced: 378 us -> 285 us
  matrix products: 53.7 us -> 0 us
  other arithmetic: 69.8 us -> 22 us
  Pallas kernels: 0 us -> 38.4 us
  local copies, waits for them, and re-layouts: 51.6 us -> 24.1 us
    dot_general x33 -> x0, matrix products: 50.5 us -> none  [the longest x12 17.1 us: left_turned(): lax.dot_general(left, right, (((0,), (0,)), ((), ())), preferred_element_...]
    pallas_call x0 -> x7, Pallas kernels: none -> 38.4 us  [run(): pl.pallas_call(kernel, out_shape=outs, in_specs=specs, out_specs=[pl.Bloc...]
    reduce_sum x14 -> x0, other arithmetic: 21.8 us -> none  [the longest x1 13.7 us: body(): grad_inner_gain = jnp.sum(grad_normal * inner_normed, 0)]
    slice x24 -> x12, local copies, waits for them, and re-layouts: 18.4 us -> 7.28 us  [the longest x1 1.96 us: body(): both[:, :3 * width]]
    dynamic_slice x25 -> x16, local copies, waits for them, and re-layouts: 7.21 us -> 0.38 us  [split(): other = lax.dynamic_slice_in_dim(values, (1 - own) * half, half, 0)]
    convert_element_type x36 -> x30, other arithmetic: 14.8 us -> 9.43 us  [as_low(): return values.astype(LOW)]
    reshape x3 -> x0, other arithmetic: 5.26 us -> none  [shift_rows(): framed = values.reshape(-1, SEQ, channels)]
    select_n x24 -> x19, other arithmetic: 7.74 us -> 2.87 us  [join(): jnp.where(swapped, other, mine)]
  transfers between devices with their start and end apart: 71 -> 71, of which waited for: 30 -> 27; matrix products, arithmetic and copies ran while one was open for 22% -> 11% of each run, Pallas kernels for 0% -> 4%
where the time goes in v2:
time: 286 us; the launch traced here: 285 us
  waiting for transfers between devices  128 us (45%)
  starting transfers between devices  70.3 us (25%)
  Pallas kernels  38.4 us (13%)
  local copies, waits for them, and re-layouts  24.1 us (8%)
  other arithmetic  22 us (8%)
    ppermute x71, waiting for transfers between devices, swap(): return lax.ppermute(values, axis, [(at, at ^ bit) for at in range(count)])  128 us
    ppermute x71, starting transfers between devices, swap(): return lax.ppermute(values, axis, [(at, at ^ bit) for at in range(count)])  70.3 us
    pallas_call x7, Pallas kernels, run(): pl.pallas_call(kernel, out_shape=outs, in_specs=specs, out_specs=[pl.Bloc...  38.4 us
    unnamed x75, local copies, waits for them, and re-layouts  10.1 us
    convert_element_type x30, other arithmetic, as_low(): return values.astype(LOW)  9.43 us
    convert_element_type x4, other arithmetic, finish_inner(): return values.astype(F32)  5.79 us
  transfers between devices with their start and end apart: 71, of which 27 were waited for; matrix products, arithmetic and copies ran while one was open for 11% of the time, Pallas kernels for 4%

profile of v2, /device:TPU:0, one launch (start us, length us, event | category | flops | bytes accessed | tf_op | source)
XLA Modules:
  0.0 285.4 jit_solution(7215524116940760189)
XLA Ops:
  2.9 2.9 %collective-permute-start = (bf16[256,1024]{1,0:T(8,128)(2,1)}, bf16[256,1024]{1,0:T(8,128)(2,1)}, u32[]{:S(2)}, u32[]{:S(2)}) collective-permute-start(bf16[256,1024]{1,0:T(8,128)(2,1)} %constant_dynamic-slice_fusion.15), channel_id=1, source_target_pairs={{0,1},{1,0},{2,3},{3,2},{4,5},{5,4},{6,7},{7,6},{8,9},{9,8},{10,11... | collective-permute-start | bytes 1572872 | tf_op jit(solution)/shard_map/ppermute | solution.py:36
  10.6 8.3 %collective-permute-done.refs_6_.refs_12_ = bf16[256,1024]{1,0:T(8,128)(2,1)} collective-permute-done((bf16[256,1024]{1,0:T(8,128)(2,1)}, bf16[256,1024]{1,0:T(8,128)(2,1)}, u32[]{:S(2)}, u32[]{:S(2)}) %collective-permute-start) | collective-permute-done | bytes 524320 | tf_op jit(solution)/shard_map/ppermute | solution.py:36
  19.1 2.1 collective-permute-start.4
  21.3 25.2 %collective-permute-done.2.refs_9_ = bf16[512,256]{1,0:T(8,128)(2,1)} collective-permute-done((bf16[512,256]{1,0:T(8,128)(2,1)}, bf16[512,256]{1,0:T(8,128)(2,1)}, u32[]{:S(2)}, u32[]{:S(2)}) %collective-permute-start.2) | collective-permute-done | bytes 262176 | tf_op jit(solution)/shard_map/ppermute | solution.py:36
  51.1 6.5 %shard_map.374 = (f32[256,512]{1,0:T(8,128)S(1)}, bf16[256,2048]{1,0:T(8,128)(2,1)S(1)}, bf16[256,2048]{1,0:T(8,128)(2,1)S(1)}, bf16[256,2048]{1,0:T(8,128)(2,1)S(1)}, f32[256,128]{1,0:T(8,128)S(1)}) custom-call(s32[3]{0:T(128)S(1)} %pad_add_fusion.info.refs_0_, f32[256,512]{1,0:T(8,128)S(1)} %get-tuple-element.63.refs_1_.x1, ...), custom_call_target="tpu_custom_call" | custom-call | flops 2000000000 | bytes 7962636 | tf_op jit(solution)/shard_map/pallas_call | solution.py:153
  57.7 3.0 %shard_map.375 = (bf16[256,512]{1,0:T(8,128)(2,1)S(1)}, bf16[256,1536]{1,0:T(8,128)(2,1)S(1)}, f32[256,128]{1,0:T(8,128)S(1)}, bf16[256,512]{1,0:T(8,128)(2,1)S(...) custom-call(s32[3]{0:T(128)S(1)} %pad_add_fusion.info.refs_0_, f32[256,512]{1,0:T(8,128)S(1)} %get-tuple-element.66.x2, ...), custom_call_target="tpu_custom_call" | custom-call | flops 1000000000 | bytes 4882444 | tf_op jit(solution)/shard_map/pallas_call | solution.py:153
  60.8 6.4 %shard_map.376 = (bf16[256,512]{1,0:T(8,128)(2,1)}, bf16[2,512,512]{2,1,0:T(8,128)(2,1)S(1)}, bf16[2,512,512]{2,1,0:T(8,128)(2,1)S(1)}, bf16[2,256,1024]{2,1,0:T...) custom-call(s32[3]{0:T(128)S(1)} %pad_add_fusion.info.refs_0_, ...), custom_call_target="tpu_custom_call" | custom-call | flops 3000000000 | bytes 10420236 | tf_op jit(solution)/shard_map/pallas_call | solution.py:153
  69.1 5.7 %shard_map.377 = (bf16[256,2048]{1,0:T(8,128)(2,1)S(1)}, bf16[256,2048]{1,0:T(8,128)(2,1)S(1)}, f32[256,512]{1,0:T(8,128)S(1)}, bf16[256,256]{1,0:T(8,128)(2,1)S(1)}, f32[16,512]{1,0:T(8,128)S(1)}) custom-call(s32[3]{0:T(128)S(1)} %pad_add_fusion.info.refs_0_, f32[256,512]{1,0:T(8,128)S(1)} %get-tuple-element.70.dx3, ...), custom_call_target="tpu_custom_call" | custom-call | flops 2000000000 | bytes 7438348 | tf_op jit(solution)/shard_map/pallas_call | solution.py:153
  75.8 11.5 %shard_map.378 = (bf16[2,256,1024]{2,1,0:T(8,128)(2,1)S(1)}, bf16[2,256,1024]{2,1,0:T(8,128)(2,1)S(1)}, bf16[2,512,256]{2,1,0:T(8,128)(2,1)S(1)}, bf16[2,512,256...) custom-call(s32[3]{0:T(128)S(1)} %pad_add_fusion.info.refs_0_, ...), custom_call_target="tpu_custom_call" | custom-call | flops 3000000000 | bytes 11010060 | tf_op jit(solution)/shard_map/pallas_call | solution.py:153
  89.2 3.3 %shard_map.379 = (bf16[256,1792]{1,0:T(8,128)(2,1)S(1)}, bf16[256,1792]{1,0:T(8,128)(2,1)S(1)}, f32[256,512]{1,0:T(8,128)}, f32[16,512]{1,0:T(8,128)S(1)}) custom-call(s32[3]{0:T(128)S(1)} %pad_add_fusion.info.refs_0_, f32[256,512]{1,0:T(8,128)S(1)} %get-tuple-element.82.d_a2_left, f32[256,256]{1,0:T(8,128)S(1)} %get-tuple-element.83.d_right, ...), custom_call_target="tpu_custom_call" | custom-call | flops 2000000000 | bytes 8224780 | tf_op jit(solution)/shard_map/pallas_call | solution.py:153
  101.4 2.0 collective-permute-done.11
  105.3 2.1 collective-permute-done.12
  107.4 2.8 collective-permute-start.13
  123.6 2.9 %collective-permute-start.36 = (f32[16,1024]{1,0:T(8,128)S(1)}, f32[16,1024]{1,0:T(8,128)S(1)}, u32[]{:S(2)}, u32[]{:S(2)}) collective-permute-start(f32[16,1024]{1,0:T(8,128)S(1)} %add.269), channel_id=1, source_target_pairs={{0,16},{2,18},{4,20},{6,22},{8,24},{10,26},{12,28},{14,30},{16,0},... | collective-permute-start | bytes 196616 | tf_op jit(solution)/shard_map/ppermute | solution.py:36
  133.9 3.8 %collective-permute-done.39 = bf16[256,256]{1,0:T(8,128)(2,1)S(1)} collective-permute-done((bf16[256,256]{1,0:T(8,128)(2,1)S(1)}, bf16[256,256]{1,0:T(8,128)(2,1)S(1)}, u32[]{:S(2)}, u32[]{:S(2)}) %collective-permute-start.39) | collective-permute-done | bytes 131104 | tf_op jit(solution)/shard_map/ppermute | solution.py:36
  138.1 4.2 %collective-permute-done.40 = bf16[128,256]{1,0:T(8,128)(2,1)S(1)} collective-permute-done((bf16[128,256]{1,0:T(8,128)(2,1)S(1)}, bf16[128,256]{1,0:T(8,128)(2,1)S(1)}, u32[]{:S(2)}, u32[]{:S(2)}) %collective-permute-start.40) | collective-permute-done | bytes 65568 | tf_op jit(solution)/shard_map/ppermute | solution.py:36
  143.9 2.3 collective-permute-start.41
  155.0 3.2 %collective-permute-done.42 = bf16[128,256]{1,0:T(8,128)(2,1)S(1)} collective-permute-done((bf16[128,256]{1,0:T(8,128)(2,1)S(1)}, bf16[128,256]{1,0:T(8,128)(2,1)S(1)}, u32[]{:S(2)}, u32[]{:S(2)}) %collective-permute-start.42) | collective-permute-done | bytes 65568 | tf_op jit(solution)/shard_map/ppermute | solution.py:36
  158.9 9.6 %collective-permute-done.43 = bf16[256,256]{1,0:T(8,128)(2,1)S(1)} collective-permute-done((bf16[256,256]{1,0:T(8,128)(2,1)S(1)}, bf16[256,256]{1,0:T(8,128)(2,1)S(1)}, u32[]{:S(2)}, u32[]{:S(2)}) %collective-permute-start.43) | collective-permute-done | bytes 131104 | tf_op jit(solution)/shard_map/ppermute | solution.py:36
  170.8 7.0 %collective-permute-done.56 = bf16[128,1024]{1,0:T(8,128)(2,1)S(1)} collective-permute-done((bf16[128,1024]{1,0:T(8,128)(2,1)S(1)}, bf16[128,1024]{1,0:T(8,128)(2,1)S(1)}, u32[]{:S(2)}, u32[]{:S(2)}) %collective-permute-start.56) | collective-permute-done | bytes 262176 | tf_op jit(solution)/shard_map/ppermute | solution.py:36
  183.0 14.7 %collective-permute-done.26 = bf16[128,1024]{1,0:T(8,128)(2,1)S(1)} collective-permute-done((bf16[128,1024]{1,0:T(8,128)(2,1)S(1)}, bf16[128,1024]{1,0:T(8,128)(2,1)S(1)}, u32[]{:S(2)}, u32[]{:S(2)}) %collective-permute-start.26) | collective-permute-done | bytes 262176 | tf_op jit(solution)/shard_map/ppermute | solution.py:36
  199.0 2.0 collective-permute-done.57
  210.1 3.3 %collective-permute-start.18 = (bf16[32,1792]{1,0:T(8,128)(2,1)S(1)}, bf16[32,1792]{1,0:T(8,128)(2,1)S(1)}, u32[]{:S(2)}, u32[]{:S(2)}) collective-permute-start(bf16[32,1792]{1,0:T(8,128)(2,1)S(1)} %add_convert_fusion.23), channel_id=1, source_target_pairs={{0,16},{2,18},{4,20},{6,22},{8,24},{10,26},{12,28},{14,30},{16,0},... | collective-permute-start | bytes 344072 | tf_op jit(solution)/shard_map/ppermute | solution.py:36
  213.5 3.0 %collective-permute-start.66 = (bf16[128,512]{1,0:T(8,128)(2,1)S(1)}, bf16[128,512]{1,0:T(8,128)(2,1)S(1)}, u32[]{:S(2)}, u32[]{:S(2)}) collective-permute-start(bf16[128,512]{1,0:T(8,128)(2,1)S(1)} %constant_dynamic-slice_fusion), channel_id=1, source_target_pairs={{0,8},{2,10},{4,12},{6,14},{8,0},{10,2},{12,4},{14,6},{16,24},{18,... | collective-permute-start | bytes 393224 | tf_op jit(solution)/shard_map/ppermute | solution.py:36
  216.7 2.3 collective-permute-done.59
  223.1 4.5 %collective-permute-done.19 = bf16[32,1792]{1,0:T(8,128)(2,1)S(1)} collective-permute-done((bf16[32,1792]{1,0:T(8,128)(2,1)S(1)}, bf16[32,1792]{1,0:T(8,128)(2,1)S(1)}, u32[]{:S(2)}, u32[]{:S(2)}) %collective-permute-start.19) | collective-permute-done | bytes 114720 | tf_op jit(solution)/shard_map/ppermute | solution.py:36
  227.7 2.9 %collective-permute-start.20 = (bf16[64,1792]{1,0:T(8,128)(2,1)S(1)}, bf16[64,1792]{1,0:T(8,128)(2,1)S(1)}, u32[]{:S(2)}, u32[]{:S(2)}) collective-permute-start(bf16[64,1792]{1,0:T(8,128)(2,1)S(1)} %pad_maximum_fusion.13), channel_id=1, source_target_pairs={{0,1},{1,0},{2,3},{3,2},{4,5},{5,4},{6,7},{7,6},{8,9},{9,8},{10,11... | collective-permute-start | bytes 688136 | tf_op jit(solution)/shard_map/ppermute | solution.py:36
  230.9 2.2 collective-permute-start.67
  237.8 4.6 %collective-permute-done.49 = bf16[32,2048]{1,0:T(8,128)(2,1)S(1)} collective-permute-done((bf16[32,2048]{1,0:T(8,128)(2,1)S(1)}, bf16[32,2048]{1,0:T(8,128)(2,1)S(1)}, u32[]{:S(2)}, u32[]{:S(2)}) %collective-permute-start.49) | collective-permute-done | bytes 131104 | tf_op jit(solution)/shard_map/ppermute | solution.py:36
  249.1 11.6 %collective-permute-done.69 = bf16[256,512]{1,0:T(8,128)(2,1)S(1)} collective-permute-done((bf16[256,512]{1,0:T(8,128)(2,1)S(1)}, bf16[256,512]{1,0:T(8,128)(2,1)S(1)}, u32[]{:S(2)}, u32[]{:S(2)}) %collective-permute-start.69) | collective-permute-done | bytes 262176 | tf_op jit(solution)/shard_map/ppermute | solution.py:36
  260.9 2.6 collective-permute-done.51
  267.8 7.6 %collective-permute-done.52 = bf16[128,2048]{1,0:T(8,128)(2,1)S(1)} collective-permute-done((bf16[128,2048]{1,0:T(8,128)(2,1)S(1)}, bf16[128,2048]{1,0:T(8,128)(2,1)S(1)}, u32[]{:S(2)}, u32[]{:S(2)}) %collective-permute-start.52) | collective-permute-done | bytes 524320 | tf_op jit(solution)/shard_map/ppermute | solution.py:36
  (323 shorter events, 106.4 us)
Async XLA Ops:
  2.9 16.0 %collective-permute-start = (bf16[256,1024]{1,0:T(8,128)(2,1)}, bf16[256,1024]{1,0:T(8,128)(2,1)}, u32[]{:S(2)}, u32[]{:S(2)}) collective-permute-start(bf16[256,1024]{1,0:T(8,128)(2,1)} %constant_dynamic-slice_fusion.15), channel_id=1, source_target_pairs={{0,1},{1,0},{2,3},{3,2},{4,5},{5,4},{6,7},{7,6},{8,9},{9,8},{10,11... | collective-permute-start | bytes 1572872 | tf_op jit(solution)/shard_map/ppermute | solution.py:36
  6.9 39.6 %collective-permute-start.5 = (bf16[256,1024]{1,0:T(8,128)(2,1)S(1)}, bf16[256,1024]{1,0:T(8,128)(2,1)}, u32[]{:S(2)}, u32[]{:S(2)}) collective-permute-start(bf16[256,1024]{1,0:T(8,128)(2,1)S(1)} %constant_dynamic-slice_fusion.13), channel_id=1, source_target_pairs={{0,1},{1,0},{2,3},{3,2},{4,5},{5,4},{6,7},{7,6},{8,9},{9,8},{10,11... | collective-permute-start | bytes 1572872 | tf_op jit(solution)/shard_map/ppermute | solution.py:36
  7.8 39.2 %collective-permute-start.7 = (bf16[512,512]{1,0:T(8,128)(2,1)}, bf16[512,512]{1,0:T(8,128)(2,1)}, u32[]{:S(2)}, u32[]{:S(2)}) collective-permute-start(bf16[512,512]{1,0:T(8,128)(2,1)} %constant_dynamic-slice_fusion.12), channel_id=1, source_target_pairs={{0,1},{1,0},{2,3},{3,2},{4,5},{5,4},{6,7},{7,6},{8,9},{9,8},{10,11... | collective-permute-start | bytes 1572872 | tf_op jit(solution)/shard_map/ppermute | solution.py:36
  10.5 35.9 %collective-permute-start.2 = (bf16[512,256]{1,0:T(8,128)(2,1)}, bf16[512,256]{1,0:T(8,128)(2,1)}, u32[]{:S(2)}, u32[]{:S(2)}) collective-permute-start(bf16[512,256]{1,0:T(8,128)(2,1)} %constant_dynamic-slice_fusion.14), channel_id=1, source_target_pairs={{0,1},{1,0},{2,3},{3,2},{4,5},{5,4},{6,7},{7,6},{8,9},{9,8},{10,11... | collective-permute-start | bytes 786440 | tf_op jit(solution)/shard_map/ppermute | solution.py:36
  18.9 32.2 %collective-permute-start.1 = (bf16[256,1024]{1,0:T(8,128)(2,1)}, bf16[256,1024]{1,0:T(8,128)(2,1)}, u32[]{:S(2)}, u32[]{:S(2)}) collective-permute-start(bf16[256,1024]{1,0:T(8,128)(2,1)} %collective-permute-done.refs_6_.refs_12_), channel_id=1, source_target_pairs={{0,2},{2,0},{4,6},{6,4},{8,10},{10,8},{12,14},{14,12},{16,18},{18,... | collective-permute-start | bytes 1572872 | tf_op jit(solution)/shard_map/ppermute | solution.py:36
  19.1 31.9 %collective-permute-start.4 = (bf16[16,1024]{1,0:T(8,128)(2,1)S(1)}, bf16[16,1024]{1,0:T(8,128)(2,1)S(1)}, u32[]{:S(2)}, u32[]{:S(2)}) collective-permute-start(bf16[16,1024]{1,0:T(8,128)(2,1)S(1)} %concatenate.71.refs_11_.refs_14_), channel_id=1, source_target_pairs={{0,1},{1,0},{2,3},{3,2},{4,5},{5,4},{6,7},{7,6},{8,9},{9,8},{10,11... | collective-permute-start | bytes 98312 | tf_op jit(solution)/shard_map/ppermute | solution.py:36
  46.5 14.3 %collective-permute-start.6 = (bf16[256,1024]{1,0:T(8,128)(2,1)}, bf16[256,1024]{1,0:T(8,128)(2,1)}, u32[]{:S(2)}, u32[]{:S(2)}) collective-permute-start(bf16[256,1024]{1,0:T(8,128)(2,1)} %collective-permute-done.5.refs_6_), channel_id=1, source_target_pairs={{0,2},{2,0},{4,6},{6,4},{8,10},{10,8},{12,14},{14,12},{16,18},{18,... | collective-permute-start | bytes 1572872 | tf_op jit(solution)/shard_map/ppermute | solution.py:36
  98.3 20.0 %collective-permute-start.37 = (bf16[2,512,256]{2,1,0:T(8,128)(2,1)}, bf16[2,512,256]{2,1,0:T(8,128)(2,1)}, u32[]{:S(2)}, u32[]{:S(2)}) collective-permute-start(bf16[2,512,256]{2,1,0:T(8,128)(2,1)} %get-tuple-element.98), channel_id=1, source_target_pairs={{0,2},{2,0},{4,6},{6,4},{8,10},{10,8},{12,14},{14,12},{16,18},{18,... | collective-permute-start | bytes 1572872 | tf_op jit(solution)/shard_map/ppermute | solution.py:36
  110.2 33.7 %collective-permute-start.63 = (bf16[2,512,512]{2,1,0:T(8,128)(2,1)}, bf16[2,512,512]{2,1,0:T(8,128)(2,1)}, u32[]{:S(2)}, u32[]{:S(2)}) collective-permute-start(bf16[2,512,512]{2,1,0:T(8,128)(2,1)} %copy-done.17), channel_id=1, source_target_pairs={{0,2},{2,0},{4,6},{6,4},{8,10},{10,8},{12,14},{14,12},{16,18},{18,... | collective-permute-start | bytes 3145736 | tf_op jit(solution)/shard_map/ppermute | solution.py:36
  110.2 37.6 %collective-permute-start.23 = (bf16[2,256,1024]{2,1,0:T(8,128)(2,1)}, bf16[2,256,1024]{2,1,0:T(8,128)(2,1)}, u32[]{:S(2)}, u32[]{:S(2)}) collective-permute-start(bf16[2,256,1024]{2,1,0:T(8,128)(2,1)} %copy-done.18), channel_id=1, source_target_pairs={{0,2},{2,0},{4,6},{6,4},{8,10},{10,8},{12,14},{14,12},{16,18},{18,... | collective-permute-start | bytes 3145736 | tf_op jit(solution)/shard_map/ppermute | solution.py:36
  110.8 39.8 %collective-permute-start.54 = (bf16[2,256,1024]{2,1,0:T(8,128)(2,1)}, bf16[2,256,1024]{2,1,0:T(8,128)(2,1)}, u32[]{:S(2)}, u32[]{:S(2)}) collective-permute-start(bf16[2,256,1024]{2,1,0:T(8,128)(2,1)} %copy-done.16), channel_id=1, source_target_pairs={{0,2},{2,0},{4,6},{6,4},{8,10},{10,8},{12,14},{14,12},{16,18},{18,... | collective-permute-start | bytes 3145736 | tf_op jit(solution)/shard_map/ppermute | solution.py:36
  137.7 16.2 %collective-permute-start.45 = (bf16[256,2048]{1,0:T(8,128)(2,1)}, bf16[256,2048]{1,0:T(8,128)(2,1)S(1)}, u32[]{:S(2)}, u32[]{:S(2)}) collective-permute-start(bf16[256,2048]{1,0:T(8,128)(2,1)} %copy-done.15), channel_id=1, source_target_pairs={{0,2},{2,0},{4,6},{6,4},{8,10},{10,8},{12,14},{14,12},{16,18},{18,... | collective-permute-start | bytes 3145736 | tf_op jit(solution)/shard_map/ppermute | solution.py:36
  142.4 35.9 %collective-permute-start.15 = (bf16[128,1792]{1,0:T(8,128)(2,1)S(1)}, bf16[128,1792]{1,0:T(8,128)(2,1)S(1)}, u32[]{:S(2)}, u32[]{:S(2)}) collective-permute-start(bf16[128,1792]{1,0:T(8,128)(2,1)S(1)} %constant_dynamic-slice_fusion.11), channel_id=1, source_target_pairs={{0,4},{2,6},{4,0},{6,2},{8,12},{10,14},{12,8},{14,10},{16,20},{18,... | collective-permute-start | bytes 1376264 | tf_op jit(solution)/shard_map/ppermute | solution.py:36
  147.9 54.3 %collective-permute-start.64 = (bf16[512,512]{1,0:T(8,128)(2,1)S(1)}, bf16[512,512]{1,0:T(8,128)(2,1)S(1)}, u32[]{:S(2)}, u32[]{:S(2)}) collective-permute-start(bf16[512,512]{1,0:T(8,128)(2,1)S(1)} %slice_bitcast_fusion), channel_id=1, source_target_pairs={{0,1},{1,0},{2,3},{3,2},{4,5},{5,4},{6,7},{7,6},{8,9},{9,8},{10,11... | collective-permute-start | bytes 1572872 | tf_op jit(solution)/shard_map/ppermute | solution.py:36
  150.0 32.7 %collective-permute-start.24 = (bf16[128,1024]{1,0:T(8,128)(2,1)S(1)}, bf16[128,1024]{1,0:T(8,128)(2,1)S(1)}, u32[]{:S(2)}, u32[]{:S(2)}) collective-permute-start(bf16[128,1024]{1,0:T(8,128)(2,1)S(1)} %dynamic-slice_bitcast_fusion.3), channel_id=1, source_target_pairs={{0,4},{2,6},{4,0},{6,2},{8,12},{10,14},{12,8},{14,10},{16,20},{18,... | collective-permute-start | bytes 786440 | tf_op jit(solution)/shard_map/ppermute | solution.py:36
  150.6 19.5 %collective-permute-start.25 = (bf16[128,1024]{1,0:T(8,128)(2,1)S(1)}, bf16[128,1024]{1,0:T(8,128)(2,1)S(1)}, u32[]{:S(2)}, u32[]{:S(2)}) collective-permute-start(bf16[128,1024]{1,0:T(8,128)(2,1)S(1)} %dynamic-slice_bitcast_fusion.2), channel_id=1, source_target_pairs={{0,4},{2,6},{4,0},{6,2},{8,12},{10,14},{12,8},{14,10},{16,20},{18,... | collective-permute-start | bytes 786440 | tf_op jit(solution)/shard_map/ppermute | solution.py:36
  170.2 27.7 %collective-permute-start.55 = (bf16[128,1024]{1,0:T(8,128)(2,1)S(1)}, bf16[128,1024]{1,0:T(8,128)(2,1)S(1)}, u32[]{:S(2)}, u32[]{:S(2)}) collective-permute-start(bf16[128,1024]{1,0:T(8,128)(2,1)S(1)} %dynamic-slice_bitcast_fusion.1), channel_id=1, source_target_pairs={{0,4},{2,6},{4,0},{6,2},{8,12},{10,14},{12,8},{14,10},{16,20},{18,... | collective-permute-start | bytes 786440 | tf_op jit(solution)/shard_map/ppermute | solution.py:36
  177.8 26.2 %collective-permute-start.46 = (bf16[128,2048]{1,0:T(8,128)(2,1)S(1)}, bf16[128,2048]{1,0:T(8,128)(2,1)S(1)}, u32[]{:S(2)}, u32[]{:S(2)}) collective-permute-start(bf16[128,2048]{1,0:T(8,128)(2,1)S(1)} %constant_dynamic-slice_fusion.5), channel_id=1, source_target_pairs={{0,1},{1,0},{2,3},{3,2},{4,5},{5,4},{6,7},{7,6},{8,9},{9,8},{10,11... | collective-permute-start | bytes 1572872 | tf_op jit(solution)/shard_map/ppermute | solution.py:36
  179.9 17.8 %collective-permute-start.26 = (bf16[128,1024]{1,0:T(8,128)(2,1)S(1)}, bf16[128,1024]{1,0:T(8,128)(2,1)S(1)}, u32[]{:S(2)}, u32[]{:S(2)}) collective-permute-start(bf16[128,1024]{1,0:T(8,128)(2,1)S(1)} %fusion.4), channel_id=1, source_target_pairs={{0,1},{1,0},{2,3},{3,2},{4,5},{5,4},{6,7},{7,6},{8,9},{9,8},{10,11... | collective-permute-start | bytes 786440 | tf_op jit(solution)/shard_map/ppermute | solution.py:36
  182.7 18.4 %collective-permute-start.57 = (bf16[128,1024]{1,0:T(8,128)(2,1)S(1)}, bf16[128,1024]{1,0:T(8,128)(2,1)S(1)}, u32[]{:S(2)}, u32[]{:S(2)}) collective-permute-start(bf16[128,1024]{1,0:T(8,128)(2,1)S(1)} %fusion.1), channel_id=1, source_target_pairs={{0,1},{1,0},{2,3},{3,2},{4,5},{5,4},{6,7},{7,6},{8,9},{9,8},{10,11... | collective-permute-start | bytes 786440 | tf_op jit(solution)/shard_map/ppermute | solution.py:36
  204.1 14.9 %collective-permute-start.47 = (bf16[64,2048]{1,0:T(8,128)(2,1)S(1)}, bf16[64,2048]{1,0:T(8,128)(2,1)S(1)}, u32[]{:S(2)}, u32[]{:S(2)}) collective-permute-start(bf16[64,2048]{1,0:T(8,128)(2,1)S(1)} %constant_dynamic-slice_fusion.4), channel_id=1, source_target_pairs={{0,4},{2,6},{4,0},{6,2},{8,12},{10,14},{12,8},{14,10},{16,20},{18,... | collective-permute-start | bytes 786440 | tf_op jit(solution)/shard_map/ppermute | solution.py:36
  213.5 17.1 %collective-permute-start.66 = (bf16[128,512]{1,0:T(8,128)(2,1)S(1)}, bf16[128,512]{1,0:T(8,128)(2,1)S(1)}, u32[]{:S(2)}, u32[]{:S(2)}) collective-permute-start(bf16[128,512]{1,0:T(8,128)(2,1)S(1)} %constant_dynamic-slice_fusion), channel_id=1, source_target_pairs={{0,8},{2,10},{4,12},{6,14},{8,0},{10,2},{12,4},{14,6},{16,24},{18,... | collective-permute-start | bytes 393224 | tf_op jit(solution)/shard_map/ppermute | solution.py:36
  216.6 16.6 %collective-permute-start.29 = (bf16[64,1024]{1,0:T(8,128)(2,1)S(1)}, bf16[64,1024]{1,0:T(8,128)(2,1)S(1)}, u32[]{:S(2)}, u32[]{:S(2)}) collective-permute-start(bf16[64,1024]{1,0:T(8,128)(2,1)S(1)} %add_convert_fusion.20), channel_id=1, source_target_pairs={{0,8},{2,10},{4,12},{6,14},{8,0},{10,2},{12,4},{14,6},{16,24},{18,... | collective-permute-start | bytes 393224 | tf_op jit(solution)/shard_map/ppermute | solution.py:36
  219.0 15.8 %collective-permute-start.60 = (bf16[64,1024]{1,0:T(8,128)(2,1)S(1)}, bf16[64,1024]{1,0:T(8,128)(2,1)S(1)}, u32[]{:S(2)}, u32[]{:S(2)}) collective-permute-start(bf16[64,1024]{1,0:T(8,128)(2,1)S(1)} %add_convert_fusion.15), channel_id=1, source_target_pairs={{0,8},{2,10},{4,12},{6,14},{8,0},{10,2},{12,4},{14,6},{16,24},{18,... | collective-permute-start | bytes 393224 | tf_op jit(solution)/shard_map/ppermute | solution.py:36
  221.3 14.1 %collective-permute-start.48 = (bf16[32,2048]{1,0:T(8,128)(2,1)S(1)}, bf16[32,2048]{1,0:T(8,128)(2,1)S(1)}, u32[]{:S(2)}, u32[]{:S(2)}) collective-permute-start(bf16[32,2048]{1,0:T(8,128)(2,1)S(1)} %constant_dynamic-slice_fusion.3), channel_id=1, source_target_pairs={{0,8},{2,10},{4,12},{6,14},{8,0},{10,2},{12,4},{14,6},{16,24},{18,... | collective-permute-start | bytes 393224 | tf_op jit(solution)/shard_map/ppermute | solution.py:36
  227.7 14.8 %collective-permute-start.20 = (bf16[64,1792]{1,0:T(8,128)(2,1)S(1)}, bf16[64,1792]{1,0:T(8,128)(2,1)S(1)}, u32[]{:S(2)}, u32[]{:S(2)}) collective-permute-start(bf16[64,1792]{1,0:T(8,128)(2,1)S(1)} %pad_maximum_fusion.13), channel_id=1, source_target_pairs={{0,1},{1,0},{2,3},{3,2},{4,5},{5,4},{6,7},{7,6},{8,9},{9,8},{10,11... | collective-permute-start | bytes 688136 | tf_op jit(solution)/shard_map/ppermute | solution.py:36
  242.6 21.1 %collective-permute-start.21 = (bf16[128,1792]{1,0:T(8,128)(2,1)S(1)}, bf16[128,1792]{1,0:T(8,128)(2,1)S(1)}, u32[]{:S(2)}, u32[]{:S(2)}) collective-permute-start(bf16[128,1792]{1,0:T(8,128)(2,1)S(1)} %pad_maximum_fusion.7), channel_id=1, source_target_pairs={{0,4},{2,6},{4,0},{6,2},{8,12},{10,14},{12,8},{14,10},{16,20},{18,... | collective-permute-start | bytes 1376264 | tf_op jit(solution)/shard_map/ppermute | solution.py:36
  244.3 16.4 %collective-permute-start.69 = (bf16[256,512]{1,0:T(8,128)(2,1)S(1)}, bf16[256,512]{1,0:T(8,128)(2,1)S(1)}, u32[]{:S(2)}, u32[]{:S(2)}) collective-permute-start(bf16[256,512]{1,0:T(8,128)(2,1)S(1)} %pad_maximum_fusion.12), channel_id=1, source_target_pairs={{0,4},{2,6},{4,0},{6,2},{8,12},{10,14},{12,8},{14,10},{16,20},{18,... | collective-permute-start | bytes 786440 | tf_op jit(solution)/shard_map/ppermute | solution.py:36
  245.5 18.6 %collective-permute-start.31 = (bf16[256,1024]{1,0:T(8,128)(2,1)S(1)}, bf16[256,1024]{1,0:T(8,128)(2,1)S(1)}, u32[]{:S(2)}, u32[]{:S(2)}) collective-permute-start(bf16[256,1024]{1,0:T(8,128)(2,1)S(1)} %pad_maximum_fusion.3), channel_id=1, source_target_pairs={{0,2},{2,0},{4,6},{6,4},{8,10},{10,8},{12,14},{14,12},{16,18},{18,... | collective-permute-start | bytes 1572872 | tf_op jit(solution)/shard_map/ppermute | solution.py:36
  245.7 18.3 %collective-permute-start.62 = (bf16[256,1024]{1,0:T(8,128)(2,1)S(1)}, bf16[256,1024]{1,0:T(8,128)(2,1)S(1)}, u32[]{:S(2)}, u32[]{:S(2)}) collective-permute-start(bf16[256,1024]{1,0:T(8,128)(2,1)S(1)} %pad_maximum_fusion.5), channel_id=1, source_target_pairs={{0,2},{2,0},{4,6},{6,4},{8,10},{10,8},{12,14},{14,12},{16,18},{18,... | collective-permute-start | bytes 1572872 | tf_op jit(solution)/shard_map/ppermute | solution.py:36
  247.5 16.0 %collective-permute-start.51 = (bf16[64,2048]{1,0:T(8,128)(2,1)S(1)}, bf16[64,2048]{1,0:T(8,128)(2,1)S(1)}, u32[]{:S(2)}, u32[]{:S(2)}) collective-permute-start(bf16[64,2048]{1,0:T(8,128)(2,1)S(1)} %pad_maximum_fusion.10), channel_id=1, source_target_pairs={{0,4},{2,6},{4,0},{6,2},{8,12},{10,14},{12,8},{14,10},{16,20},{18,... | collective-permute-start | bytes 786440 | tf_op jit(solution)/shard_map/ppermute | solution.py:36
  260.8 15.1 %collective-permute-start.70 = (bf16[512,512]{1,0:T(8,128)(2,1)S(1)}, bf16[512,512]{1,0:T(8,128)(2,1)S(1)}, u32[]{:S(2)}, u32[]{:S(2)}) collective-permute-start(bf16[512,512]{1,0:T(8,128)(2,1)S(1)} %pad_maximum_fusion.6), channel_id=1, source_target_pairs={{0,2},{2,0},{4,6},{6,4},{8,10},{10,8},{12,14},{14,12},{16,18},{18,... | collective-permute-start | bytes 1572872 | tf_op jit(solution)/shard_map/ppermute | solution.py:36
  (76 other events, 921.9 us)

commit v3 on v2

--- a/solution.py
+++ b/solution.py
@@ -13,6 +13,8 @@
 F32 = jnp.float32
 STEP = 64
 LIMIT = 40 * 2**20
+SCALE = 4
+ADV = 20 * 10**9
 
 
 def as_low(values):
@@ -145,20 +147,47 @@
     ).astype(F32)
 
 
-def run(kernel, outs, ins, scratch, flops):
-    specs = [pl.BlockSpec(memory_space=pltpu.SMEM)] + [
-        pl.BlockSpec(memory_space=pltpu.VMEM) for _ in ins[1:]
-    ]
-    moved = sum(item.size * item.dtype.itemsize for item in list(ins) + list(outs))
-    return pl.pallas_call(
-        kernel,
-        out_shape=outs,
-        in_specs=specs,
-        out_specs=[pl.BlockSpec(memory_space=pltpu.VMEM) for _ in outs],
-        scratch_shapes=scratch,
-        compiler_params=pltpu.CompilerParams(vmem_limit_bytes=LIMIT),
-        cost_estimate=pl.CostEstimate(flops=flops, bytes_accessed=moved, transcendentals=0),
-    )(*ins)
+class Chain:
+    def __init__(self):
+        self.link = None
+
+    def run(self, kernel, outs, ins, scratch, flops):
+        specs = [pl.BlockSpec(memory_space=pltpu.SMEM)] + [
+            pl.BlockSpec(memory_space=pltpu.VMEM) for _ in ins[1:]
+        ]
+        count = len(ins)
+        moved = sum(item.size * item.dtype.itemsize for item in list(ins) + list(outs))
+        ins = list(ins)
+        linked = self.link is not None
+        if linked:
+            ins.append(self.link)
+            specs.append(pl.BlockSpec(memory_space=pl.ANY))
+
+        def call(*refs):
+            kernel(*(refs[:count] + refs[count + 1 :] if linked else refs))
+
+        results = pl.pallas_call(
+            call,
+            out_shape=outs,
+            in_specs=specs,
+            out_specs=[pl.BlockSpec(memory_space=pltpu.VMEM) for _ in outs],
+            scratch_shapes=scratch,
+            compiler_params=pltpu.CompilerParams(vmem_limit_bytes=LIMIT),
+            cost_estimate=pl.CostEstimate(flops=flops, bytes_accessed=moved + flops // 50, transcendentals=0),
+        )(*ins)
+        self.link = results[-1]
+        return results
+
+
+def put(out, first, count, offset, values):
+    rows = values.shape[0] // count
+    low = as_low(values)
+    for quarter in range(count):
+        for part in range(values.shape[1] // 256):
+            at = offset + part * rows
+            out[first + quarter, at : at + rows] = low[
+                quarter * rows : (quarter + 1) * rows, part * 256 : (part + 1) * 256
+            ]
 
 
 def shaped(shape, kind):
@@ -197,29 +226,44 @@
     return groups
 
 
-def inner_forward_kernel(pieces, refs):
+def assemble(target, blocks, code):
+    rows = blocks[0].shape[0]
+    for at, block in enumerate(blocks):
+        spot = jnp.bitwise_xor(code, at) if at else code
+        target[pl.ds(pl.multiple_of(spot * rows, 16), rows)] = block[...]
+
+
+def code_of(info, count):
+    return info[0] if count == 2 else info[0] * 2 + info[4]
+
+
+def code_z(info, count):
+    return info[0] if count == 2 else info[0] * 2 + info[5]
+
+
+def group_blocks(refs, pieces):
+    count = len(refs) // (pieces - 1)
+    return [refs[at : at + count] for at in range(0, len(refs), count)]
+
+
+def inner_forward_kernel(pieces, sizes, refs):
     info, refs = refs[0], refs[1:]
-    (x1, a2, right, vec), left, point, wide, outs, scratch = unpack(
-        refs, [4, 2 * pieces - 1, 2 * pieces - 1, pieces, 5, 6]
-    )
-    x2, normed_ref, slope_ref, depth, rstd_ref = outs
+    (a2, right, left), left_in, wide, outs, scratch = unpack(refs, [3, sizes[0], pieces, 5, 6])
+    normed_ref, slope_ref, depth, rstd_ref, left_rest = outs
     mixed, total, square, centre_ref, padded, padded_two = scratch
-    local = left[0].shape[1]
+    local = left.shape[1]
     inner = local * pieces
-    core, offset = info[0], info[1]
-    half = a2.shape[1] // 2
-    near = a2[:, at_lane(core * half, half)]
-    far = a2[:, at_lane((1 - core) * half, half)]
+    offset = info[1]
     right_rows = right[...].astype(F32)
     total[...] = jnp.zeros_like(total)
     square[...] = jnp.zeros_like(square)
     for piece in range(pieces):
+        if piece:
+            blocks = group_blocks(left_in, pieces)[piece - 1]
+            assemble(left_rest.at[piece - 1], blocks, code_of(info, len(blocks)))
         for col in spans(local, 256):
-            if piece == 0:
-                pre = dot(a2[...], left[0][:, col])
-            else:
-                pre = dot(near, left[2 * piece - 1][:, col]) + dot(far, left[2 * piece][:, col])
-            pre = pre + wide[piece][0:16, col].astype(F32)[0:1]
+            weights = left[:, col] if piece == 0 else left_rest[piece - 1, :, col]
+            pre = dot(a2[...], weights) + wide[piece][0:16, col].astype(F32)[0:1]
             sigma = sigmoid(pre)
             at = piece * local + col.start
             here = slice(at, at + 256)
@@ -258,26 +302,26 @@
             return carry
 
         lax.fori_loop(0, local // 256, step, 0)
-    width = x1.shape[1]
-    channels = point[0].shape[1]
-    sep = dot(depth[:, 0:local], point[0][...])
-    rows = local // 2
+
+
+def masked_scores(queries, keys, valid, scale):
+    return jnp.where(valid, dot_right(queries, keys) * scale, NEGATIVE)
+
+
+def attention_forward_kernel(pieces, sizes, refs):
+    (info, x1, depth, point, vec, project_w, output_w), point_in, outs = unpack(
+        refs, [7, sizes[1], 8]
+    )
+    x2, a4, qkv, lse, attended, x3, a5, point_rest = outs
+    width = x2.shape[1]
+    local, channels = point.shape
+    sep = dot(depth[:, 0:local], point[...])
     for piece in range(1, pieces):
-        base = piece * local
-        sep = sep + dot(depth[:, at_lane(base + core * rows, rows)], point[2 * piece - 1][...])
-        sep = sep + dot(depth[:, at_lane(base + (1 - core) * rows, rows)], point[2 * piece][...])
+        blocks = group_blocks(point_in, pieces)[piece - 1]
+        assemble(point_rest.at[piece - 1], blocks, code_of(info, len(blocks)))
+        sep = sep + dot(depth[:, piece * local : (piece + 1) * local], point_rest[piece - 1])
     x2[:, 0:channels] = x1[:, 0:channels] + sep + vec[10:11, channels : 2 * channels]
     x2[:, channels:width] = x1[:, channels:width]
-
-
-def masked_scores(queries, keys, valid, scale):
-    return jnp.where(valid, dot_right(queries, keys) * scale, NEGATIVE)
-
-
-def attention_forward_kernel(
-    info, x2, vec, project_w, output_w, a4, qkv, lse, attended, x3, a5
-):
-    width = x2.shape[1]
     for row in spans(SEQ, STEP):
         normed, _ = normalize(x2[row])
         a4[row] = as_low(normed * vec[4:5] + vec[5:6])
@@ -314,73 +358,73 @@
         a5[row] = as_low(normed * vec[6:7] + vec[7:8])
 
 
-def feed_kernel(pieces, refs):
+def feed_kernel(pieces, sizes, refs):
     info, refs = refs[0], refs[1:]
-    (a5, x3, top, vec), expand, shrink, wide, outs, scratch = unpack(
-        refs, [4, 2 * pieces - 1, 2 * pieces - 1, pieces, 8, 5]
-    )
-    output, shrink_keep, shrink_send, expand_keep, expand_send, dx3, fixed, grad_bias = outs
-    hidden, slope, d_expand, shrunk, d_a5 = scratch
-    local = expand[0].shape[1]
-    width = x3.shape[1]
-    half, rows = width // 2, local // 2
-    core = info[0]
-    near = a5[:, at_lane(core * half, half)]
-    far = a5[:, at_lane((1 - core) * half, half)]
+    (a5, top, expand), expand_in, wide, outs = unpack(refs, [3, sizes[2], pieces, 5])
+    hidden, slope, keep, send, expand_rest = outs
+    local = expand.shape[1]
+    core, rows = info[0], local // 2
     for piece in range(pieces):
+        if piece:
+            blocks = group_blocks(expand_in, pieces)[piece - 1]
+            assemble(expand_rest.at[piece - 1], blocks, code_of(info, len(blocks)))
         for col in spans(local, 256):
-            if piece == 0:
-                pre = dot(a5[...], expand[0][:, col])
-            else:
-                pre = dot(near, expand[2 * piece - 1][:, col]) + dot(
-                    far, expand[2 * piece][:, col]
-                )
-            pre = pre + wide[piece][0:16, col].astype(F32)[1:2]
+            weights = expand[:, col] if piece == 0 else expand_rest[piece - 1, :, col]
+            pre = dot(a5[...], weights) + wide[piece][0:16, col].astype(F32)[1:2]
             sigma = sigmoid(pre)
             here = slice(piece * local + col.start, piece * local + col.stop)
             hidden[:, here] = as_low(pre * sigma)
-            slope[:, here] = sigma * (1.0 + pre * (1.0 - sigma))
-    blocks = [(0, shrink[0])]
-    for piece in range(1, pieces):
-        blocks.append((piece * local + core * rows, shrink[2 * piece - 1]))
-        blocks.append((piece * local + (1 - core) * rows, shrink[2 * piece]))
-    for base, weights in blocks:
-        count = weights.shape[0]
-        part = dot(hidden[:, at_lane(base, count)], weights[...])
-        if weights is shrink[0]:
+            slope[:, here] = as_low(sigma * (1.0 + pre * (1.0 - sigma)))
+    for piece in range(pieces):
+        for side, out in ((1 - core, send), (core, keep)):
+            put(
+                out,
+                2 * piece,
+                2,
+                0,
+                dot_left(hidden[:, at_lane(piece * local + side * rows, rows)], top[...]),
+            )
+
+
+def feed_back_kernel(pieces, sizes, refs):
+    info, refs = refs[0], refs[1:]
+    (a5, x3, top, vec, hidden, slope, expand, expand_rest, shrink), shrink_in, outs, scratch = unpack(
+        refs, [9, sizes[3], 6, 4]
+    )
+    output, keep, send, dx3, fixed, grad_bias = outs
+    d_expand, shrunk, d_a5, shrink_rest = scratch
+    local = expand.shape[1]
+    half = x3.shape[1] // 2
+    core = info[0]
+    for piece in range(pieces):
+        base = piece * local
+        if piece:
+            blocks = group_blocks(shrink_in, pieces)[piece - 1]
+            assemble(shrink_rest.at[piece - 1], blocks, code_z(info, len(blocks)))
+        weights = shrink if piece == 0 else shrink_rest.at[piece - 1]
+        part = dot(hidden[:, base : base + local], weights[...])
+        if piece == 0:
             shrunk[...] = part
         else:
             shrunk[...] += part
-        for row in spans(count, min(256, count)):
-            size = row.stop - row.start
-            here = at_lane(base + row.start, size)
-            back = dot_right(top[...], weights[row])
-            d_expand[:, here] = as_low(back * slope[:, here])
+        for row in spans(local, 256):
+            here = slice(base + row.start, base + row.stop)
+            d_expand[:, here] = as_low(
+                dot_right(top[...], weights[row]) * slope[:, here].astype(F32)
+            )
     for row in spans(SEQ, STEP):
         output[row] = as_low(x3[row] + shrunk[row] + vec[14:15])
     for piece in range(pieces):
-        base = piece * local
-        cols = slice(base, base + local)
-        for side, shrink_out, expand_out in (
-            (1 - core, shrink_send, expand_send),
-            (core, shrink_keep, expand_keep),
-        ):
-            shrink_out[piece] = as_low(
-                dot_left(hidden[:, at_lane(base + side * rows, rows)], top[...])
-            )
-            expand_out[piece] = as_low(
-                dot_left(a5[:, at_lane(side * half, half)], d_expand[:, cols])
-            )
+        cols = slice(piece * local, (piece + 1) * local)
+        for side, out in ((1 - core, send), (core, keep)):
+            grad = dot_left(a5[:, at_lane(side * half, half)], d_expand[:, cols])
+            put(out, 2 * piece, 2, 0, grad)
         grad_bias[:, cols] = jnp.broadcast_to(low_columns_sum(d_expand[:, cols]), (8, local))
+        weights = expand[...] if piece == 0 else expand_rest[piece - 1]
         if piece == 0:
-            d_a5[...] = dot_right(d_expand[:, cols], expand[0][...])
+            d_a5[...] = dot_right(d_expand[:, cols], weights)
         else:
-            d_a5[:, at_lane(core * half, half)] += dot_right(
-                d_expand[:, cols], expand[2 * piece - 1][...]
-            )
-            d_a5[:, at_lane((1 - core) * half, half)] += dot_right(
-                d_expand[:, cols], expand[2 * piece][...]
-            )
+            d_a5[...] += dot_right(d_expand[:, cols], weights)
     fixed[...] = jnp.zeros_like(fixed)
     for row in spans(SEQ, STEP):
         normed, rstd = normalize(x3[row])
@@ -426,8 +470,8 @@
             d_proj[:, here] = as_low(jnp.where(lanes < 64, parts[0][kind], parts[1][kind]))
     for side, out in ((1 - core, send), (core, keep)):
         here = at_lane(side * half, half)
-        out[:, 3 * width :] = as_low(dot_left(attended[:, here], d_out[...]))
-        out[:, : 3 * width] = as_low(dot_left(a4[:, here], d_proj[...]))
+        put(out, 0, 4, 0, dot_left(a4[:, here], d_proj[...]))
+        put(out, 0, 4, 3 * width * half // 1024, dot_left(attended[:, here], d_out[...]))
     fixed[12:13] = low_columns_sum(d_out[...])
     fixed[10:11] = low_columns_sum(d_proj[:, :width])
     fixed[11:12] = low_columns_sum(d_proj[:, 2 * width :])
@@ -445,28 +489,26 @@
 
 def inner_backward_kernel(pieces, refs):
     info, refs = refs[0], refs[1:]
-    (d_sep, depth, normed_ref, slope_ref, rstd_ref, a2, bias_before), point, left, wide, outs, scratch = unpack(
-        refs, [7, 2 * pieces - 1, 2 * pieces - 1, pieces, 7, 6]
-    )
-    left_keep, left_send, point_keep, point_send, d_a2, d_right, grads = outs
+    (
+        (d_sep, depth, normed_ref, slope_ref, rstd_ref, a2, bias_before, point, point_rest, left, left_rest),
+        wide,
+        outs,
+        scratch,
+    ) = unpack(refs, [11, pieces, 5, 6])
+    keep, send, d_a2, d_right, grads = outs
     d_depth, padded, padded_two, d_left, first_ref, second_ref = scratch
-    local = left[0].shape[1]
+    local = left.shape[1]
     inner = local * pieces
     core, offset = info[0], info[1]
     rows = local // 2
     half = a2.shape[1] // 2
-    blocks = [(0, point[0])]
-    for piece in range(1, pieces):
-        blocks.append((piece * (local // 128) + core * (rows // 128), point[2 * piece - 1]))
-        blocks.append((piece * (local // 128) + (1 - core) * (rows // 128), point[2 * piece]))
-    for base, weights in blocks:
-        count = weights.shape[0]
-        for row in spans(count, min(256, count)):
+    for piece in range(pieces):
+        weights = point if piece == 0 else point_rest.at[piece - 1]
+        for row in spans(local, 256):
             back = dot_right(d_sep[...], weights[row])
-            for part in range((row.stop - row.start) // 128):
-                d_depth[base + row.start // 128 + part, 8 : SEQ + 8] = back[
-                    :, part * 128 : (part + 1) * 128
-                ]
+            index = (piece * local + row.start) // 128
+            d_depth[index, 8 : SEQ + 8] = back[:, 0:128]
+            d_depth[index + 1, 8 : SEQ + 8] = back[:, 128:256]
     first_ref[...] = jnp.zeros_like(first_ref)
     second_ref[...] = jnp.zeros_like(second_ref)
     for pad in (padded, padded_two):
@@ -529,27 +571,21 @@
     for piece in range(pieces):
         base = piece * local
         cols = slice(base, base + local)
-        for side, left_out, point_out in (
-            (1 - core, left_send, point_send),
-            (core, left_keep, point_keep),
-        ):
-            left_out[piece] = as_low(
-                dot_left(a2[:, at_lane(side * half, half)], d_left[:, cols])
-            )
-            point_out[piece] = as_low(
-                dot_left(depth[:, at_lane(base + side * rows, rows)], d_sep[...])
-            )
+        for side, out in ((1 - core, send), (core, keep)):
+            grad = dot_left(a2[:, at_lane(side * half, half)], d_left[:, cols])
+            put(out, 2 * piece, 2, 0, grad)
+            grad = dot_left(depth[:, at_lane(base + side * rows, rows)], d_sep[...])
+            put(out, 2 * piece, 2, half * local // 512, grad)
         grads[0:1, cols] = low_columns_sum(d_left[:, cols])
         if piece == 0:
-            d_a2[...] = dot_right(d_left[:, cols], left[0][...])
+            d_a2[...] = dot_right(d_left[:, cols], left[...])
         else:
-            d_a2[:, at_lane(core * half, half)] += dot_right(d_left[:, cols], left[2 * piece - 1][...])
-            d_a2[:, at_lane((1 - core) * half, half)] += dot_right(d_left[:, cols], left[2 * piece][...])
+            d_a2[...] += dot_right(d_left[:, cols], left_rest[piece - 1])
 
 
 def last_kernel(
-    info, d_a2_left, d_right, right_pre, conv_w, a2, x1, dx2, values, gates, a1, gated_w, x_ref, vec, before,
-    send, keep, input_grad, fixed, shifted, d_a2, d_gated
+    info, d_a2_left, d_right, right_pre, conv_w, a2, x1, dx2, values, gates, a1, gated_w, x_ref, vec, before, wide_sums,
+    send, keep, input_grad, fixed, shifted, d_a2, d_gated, rows_ref
 ):
     width = x1.shape[1]
     half = width // 2
@@ -584,8 +620,8 @@
         d_gated[row, width:] = as_low(scaled * values[row] * (1.0 - gate))
     for side, out in ((1 - core, send), (core, keep)):
         here = at_lane(side * half, half)
-        out[:, 0 : 2 * width] = as_low(dot_left(a1[:, here], d_gated[...]))
-        out[:, 2 * width :] = as_low(dot_left(a2[:, here], shifted[...]))
+        put(out, 0, 4, 0, dot_left(a1[:, here], d_gated[...]))
+        put(out, 0, 4, half * width // 512, dot_left(a2[:, here], shifted[...]))
     sums = low_columns_sum(d_gated[...])
     fixed[8:9] = sums[:, 0:width]
     fixed[9:10] = sums[:, width:]
@@ -596,18 +632,241 @@
         fixed[0:1] += columns_sum(grad * normed)
         fixed[1:2] += columns_sum(grad)
         input_grad[row] += normalize_back(grad, normed, rstd, vec[0:1])
-
-
-def gather_inner(own_piece):
-    core = bit_of("dp", 1)
-    mine, _ = split(own_piece, core)
-    halves = [mine]
-    for bit in bits_of("mp"):
-        halves = halves + [swap(item, "mp", bit) for item in halves]
-    found = [own_piece]
-    for item in halves[1:]:
-        found += [item, swap(item, "dp", 1)]
-    return found
+    pack_small(info, wide_sums, fixed, send, keep, rows_ref)
+
+
+def pack_small(info, wide, fixed, send, keep, rows_ref):
+    if rows_ref is None:
+        return
+    pieces = lax.axis_size("mp")
+    local = wide.shape[1] // pieces
+    parts = local // 256
+    rows_ref[...] = jnp.zeros_like(rows_ref)
+    for piece in range(pieces):
+        owner = jnp.bitwise_xor(info[1] // local, piece)
+        for part in range(parts):
+            spot = pl.multiple_of((owner * parts + part) * 16, 16)
+            at = piece * local + part * 256
+            rows_ref[pl.ds(spot, 16)] = wide[:, at : at + 256]
+    base = wide.shape[1] // 16
+    for part in range(fixed.shape[1] // 256):
+        rows_ref[base + part * 16 : base + (part + 1) * 16] = fixed[:, part * 256 : (part + 1) * 256]
+    count = rows_ref.shape[0] // 2
+    offset = send.shape[1] - count // 4
+    for side, out in ((1 - info[0], send), (info[0], keep)):
+        put(out, 0, 4, offset, rows_ref[pl.ds(pl.multiple_of(side * count, 16), count)])
+
+
+def cut_kernel(parts, counts, refs):
+    info, ins, outs, sems = refs[0], refs[1 : parts + 1], refs[parts + 1 : -1], refs[-1]
+    copies = []
+    for at, (source, target) in enumerate(zip(ins, outs)):
+        rows = target.shape[0]
+        code = (info[0], code_of(info, 4), code_z(info, 4))[counts[at]]
+        here = pl.ds(pl.multiple_of(code * rows, 16), rows)
+        copies.append(pltpu.make_async_copy(source.at[here], target, sems.at[at]))
+    for copy in copies:
+        copy.start()
+    for copy in copies:
+        copy.wait()
+
+
+def cut(info, arrays, counts):
+    outs = [
+        shaped((item.shape[0] // (2 if kind == 0 else 4), item.shape[1]), item.dtype)
+        for item, kind in zip(arrays, counts)
+    ]
+    return pl.pallas_call(
+        lambda *refs: cut_kernel(len(arrays), counts, refs),
+        out_shape=outs,
+        in_specs=[pl.BlockSpec(memory_space=pltpu.SMEM)]
+        + [pl.BlockSpec(memory_space=pl.ANY) for _ in arrays],
+        out_specs=[pl.BlockSpec(memory_space=pltpu.VMEM) for _ in arrays],
+        scratch_shapes=[pltpu.SemaphoreType.DMA((len(arrays),))],
+    )(info, *arrays)
+
+
+def flat_swap(values, partner):
+    count = lax.axis_size("dp") * lax.axis_size("mp")
+    return lax.ppermute(values, ("dp", "mp"), [(at, partner(at)) for at in range(count)])
+
+
+PARTNERS = {
+    "core": lambda at: at ^ 2,
+    "first": lambda at: at ^ (4 if at & 2 else 1),
+    "second": lambda at: at ^ (1 if at & 2 else 4),
+    "x": lambda at: at ^ 1,
+    "y": lambda at: at ^ 4,
+    "near": lambda at: at ^ 8,
+    "far": lambda at: at ^ 16,
+}
+INNER_STEPS = [
+    ("quarter", "first"),
+    ("half_mix", "second"),
+    ("half_near", "near"),
+    ("sum", "far"),
+    ("sum", "near"),
+    ("join_near", "y"),
+    ("join_y", "core"),
+    ("final", None),
+]
+SHARED_STEPS = [
+    ("quarter", "first"),
+    ("half_mix", "second"),
+    ("half_near", "near"),
+    ("sum", "far"),
+    ("sum", "near"),
+    ("join_near", "second"),
+    ("join_mix", "first"),
+    ("spread", "core"),
+    ("final", None),
+]
+
+
+PLAN = "ab d c ab d c ab cd b a cd ep a c d p e c d p c d d d".split()
+
+
+class Stream:
+    def __init__(self, inner, mine, other, parts):
+        self.inner = inner
+        self.mine = mine
+        self.flight = flat_swap(other, PARTNERS["core"])
+        self.steps = list(INNER_STEPS if inner else SHARED_STEPS)
+        self.parts = parts
+
+
+def advance_kernel(jobs, refs):
+    info, refs = refs[0], refs[1:]
+    core, y, near = info[0], info[4], info[5]
+    ins, outs = list(refs[: 2 * len(jobs)]), list(refs[2 * len(jobs) :])
+    for inner, step, parts in jobs:
+        mine, flight = ins.pop(0), ins.pop(0)
+        x = 0 if inner else info[3]
+        mix = core * x + (1 - core) * y
+
+        def added(spot):
+            return as_low(mine[spot].astype(F32) + flight[spot].astype(F32))
+
+        if step == "quarter":
+            keep, send = outs.pop(0), outs.pop(0)
+            for at in range(2):
+                send[at] = added(core * (2 * at + 1 - y) + (1 - core) * (2 * (1 - x) + at))
+                keep[at] = added(core * (2 * at + y) + (1 - core) * (2 * x + at))
+        elif step == "half_mix":
+            keep, send = outs.pop(0), outs.pop(0)
+            send[0] = added(1 - mix)
+            keep[0] = added(mix)
+        elif step == "half_near":
+            keep, send = outs.pop(0), outs.pop(0)
+            rows = keep.shape[1]
+            for out, side in ((send, 1 - near), (keep, near)):
+                here = pl.ds(pl.multiple_of(side * rows, 16), rows)
+                out[0] = as_low(mine[0, here].astype(F32) + flight[0, here].astype(F32))
+        elif step == "sum":
+            outs.pop(0)[0] = added(0)
+        elif step == "join_near":
+            out = outs.pop(0)
+            rows = mine.shape[1]
+            out[0, pl.ds(pl.multiple_of(near * rows, 16), rows)] = mine[0]
+            out[0, pl.ds(pl.multiple_of((1 - near) * rows, 16), rows)] = flight[0]
+        elif step in ("join_y", "join_mix"):
+            out = outs.pop(0)
+            side = y if step == "join_y" else mix
+            out[side] = mine[0]
+            out[1 - side] = flight[0]
+        elif step == "spread":
+            out = outs.pop(0)
+            for at in range(2):
+                out[core * (2 * at + y) + (1 - core) * (2 * x + at)] = mine[at]
+                out[core * (2 * at + 1 - y) + (1 - core) * (2 * (1 - x) + at)] = flight[at]
+        else:
+            for offset, rows, shape in parts:
+                out = outs.pop(0)
+                columns = shape[-1] // 256
+                for source, side in ((mine, core), (flight, 1 - core)):
+                    for quarter in range(mine.shape[0]):
+                        spot = (side * mine.shape[0] + quarter) * rows
+                        here = pl.ds(pl.multiple_of(spot, 16), rows)
+                        for part in range(columns * (shape[0] if len(shape) == 3 else 1)):
+                            at = offset + part * rows
+                            block = source[quarter, at : at + rows].astype(F32)
+                            if len(shape) == 3:
+                                out[part, here] = block
+                            else:
+                                out[here, part * 256 : (part + 1) * 256] = block
+
+
+def advance(chain, info, streams):
+    jobs, ins, outs = [], [info], []
+    for stream in streams:
+        step = stream.steps[0][0]
+        jobs.append((stream.inner, step, stream.parts))
+        ins += [stream.mine, stream.flight]
+        lead, rows, columns = stream.mine.shape
+        if step in ("quarter", "half_mix"):
+            outs += [shaped((lead // 2, rows, columns), LOW)] * 2
+        elif step == "half_near":
+            outs += [shaped((lead, rows // 2, columns), LOW)] * 2
+        elif step == "sum":
+            outs.append(shaped((lead, rows, columns), LOW))
+        elif step == "join_near":
+            outs.append(shaped((lead, rows * 2, columns), LOW))
+        elif step == "final":
+            outs += [shaped(shape, F32) for _, _, shape in stream.parts]
+        else:
+            outs.append(shaped((lead * 2, rows, columns), LOW))
+    results = list(chain.run(lambda *refs: advance_kernel(jobs, refs), outs, ins, [], ADV))
+    for stream in streams:
+        step, partner = stream.steps.pop(0)
+        if step == "final":
+            stream.mine = [results.pop(0) for _ in stream.parts]
+            continue
+        stream.mine = results.pop(0)
+        if step in ("quarter", "half_mix", "half_near"):
+            stream.flight = flat_swap(results.pop(0), PARTNERS[partner])
+        else:
+            stream.flight = flat_swap(stream.mine, PARTNERS[partner])
+
+
+def opened(packed, first, count, offset, rows, columns):
+    parts = [
+        packed[first : first + count, offset + at * rows : offset + (at + 1) * rows]
+        for at in range(columns // 256)
+    ]
+    return jnp.concatenate(parts, 2).reshape(count * rows, columns)
+
+
+def small_kernel(info, total, wide, fixed):
+    local = wide.shape[1]
+    parts = local // 256
+    for part in range(parts):
+        spot = pl.multiple_of((info[1] // local * parts + part) * 16, 16)
+        wide[:, part * 256 : (part + 1) * 256] = total[pl.ds(spot, 16)]
+    base = local * 2 // 16
+    for part in range(fixed.shape[1] // 256):
+        fixed[:, part * 256 : (part + 1) * 256] = total[base + part * 16 : base + (part + 1) * 16]
+
+
+class Weights:
+    def __init__(self, piece, kind):
+        pieces = [piece]
+        for bit in bits_of("mp"):
+            pieces = pieces + [swap(item, "mp", bit) for item in pieces]
+        self.blocks = [[item] for item in pieces[1:]]
+        self.kind = kind
+
+    def hop(self, after):
+        for blocks in self.blocks:
+            item, _ = lax.optimization_barrier((blocks[0], after))
+            blocks[0] = item
+            blocks.append(swap(item, "dp", (2, 4)[self.kind - 1]))
+
+    def share(self, after):
+        found = []
+        for blocks in self.blocks:
+            held = [lax.optimization_barrier((item, after))[0] for item in blocks]
+            found += held + [swap(item, "dp", 1) for item in held]
+        return found
 
 
 def gather_small(own_piece):
@@ -685,17 +944,32 @@
     inner = local * pieces
     tokens = cell_input.shape[0]
     assert tokens == SEQ
+    tuned = lax.axis_size("dp") == 16 and pieces == 2
     mp_bits = bits_of("mp")[::-1]
     dp_bits = bits_of("dp")[1:]
     mp_first = [("mp", bit) for bit in mp_bits] + [("dp", bit) for bit in dp_bits]
-    dp_first = (
-        [("dp", dp_bits[0])] + [("mp", bit) for bit in mp_bits] + [("dp", bit) for bit in dp_bits[1:]]
-    )
     core = bit_of("dp", 1)
-    info = jnp.stack([core, lax.axis_index("mp") * local, lengths[0]]).astype(jnp.int32)
-
-    left = gather_inner(left_weight)
-    point = gather_inner(point_weight)
+    info = jnp.stack(
+        [
+            core,
+            lax.axis_index("mp") * local,
+            lengths[0],
+            lax.axis_index("mp") % 2,
+            bit_of("dp", 2),
+            bit_of("dp", 4),
+        ]
+    ).astype(jnp.int32)
+    chain = Chain()
+
+    def inner_rows(size):
+        return (2 * pieces, size // 1024, 256)
+
+
+    kinds = (0, 1, 1, 2)
+    owned = (left_weight, point_weight, expand_weight, shrink_weight)
+    cuts = cut(info, owned, kinds)
+    chain.link = cuts[-1]
+    left, point, expand, shrink = [Weights(part, kind) for part, kind in zip(cuts, kinds)]
     wide = gather_small(
         jnp.concatenate(
             [
@@ -708,8 +982,7 @@
             0,
         )
     )
-    expand = gather_inner(expand_weight)
-    shrink = gather_inner(shrink_weight)
+    sizes = [(pieces - 1) * (2 if kind == 0 else 4) for kind in kinds]
     vec = jnp.concatenate(
         [
             norm_params.reshape(8, width),
@@ -723,7 +996,7 @@
         0,
     ).astype(F32)
 
-    a1, values, gates, x1, a2, right_pre, right = run(
+    a1, values, gates, x1, a2, right_pre, right = chain.run(
         pre_kernel,
         [
             shaped((tokens, width), LOW),
@@ -736,18 +1009,20 @@
         ],
         [info, cell_input, vec, gated_weight, conv_weight],
         [],
-        10**9,
-    )
-    x2, normed, slope, depth, rstd = run(
-        lambda *refs: inner_forward_kernel(pieces, refs),
-        [
-            shaped((tokens, width), F32),
+        int(2.2e9 * SCALE),
+    )
+    left_blocks = left.share(right)
+    point.hop(right)
+    normed, slope, depth, rstd, left_rest = chain.run(
+        lambda *refs: inner_forward_kernel(pieces, sizes, refs),
+        [
             shaped((tokens, inner), LOW),
             shaped((tokens, inner), LOW),
             shaped((tokens, inner), LOW),
             shaped((tokens, 128), F32),
+            shaped((pieces - 1, width, local), LOW),
         ],
-        [info, x1, a2, right, vec] + left + point + wide,
+        [info, a2, right, left_weight] + left_blocks + wide,
         [
             pltpu.VMEM((tokens, inner), F32),
             pltpu.VMEM((tokens, 128), F32),
@@ -756,51 +1031,72 @@
             pltpu.VMEM((tokens + 16, 128), F32),
             pltpu.VMEM((tokens + 16, 128), F32),
         ],
-        2 * 10**9,
-    )
-    a4, qkv, lse, attended, x3, a5 = run(
-        attention_forward_kernel,
-        [
+        int(6.5e9 * SCALE),
+    )
+    point_blocks = point.share(rstd)
+    expand.hop(rstd)
+    x2, a4, qkv, lse, attended, x3, a5, point_rest = chain.run(
+        lambda *refs: attention_forward_kernel(pieces, sizes, refs),
+        [
+            shaped((tokens, width), F32),
             shaped((tokens, width), LOW),
             shaped((tokens, 3 * width), LOW),
             shaped((tokens, 128), F32),
             shaped((tokens, width), LOW),
             shaped((tokens, width), F32),
             shaped((tokens, width), LOW),
+            shaped((pieces - 1, local, channels), LOW),
         ],
-        [info, x2, vec, project_weight, output_weight],
+        [info, x1, depth, point_weight, vec, project_weight, output_weight] + point_blocks,
         [],
-        10**9,
-    )
-    cell_output, shrink_keep, shrink_send, expand_keep, expand_send, dx3, fixed, expand_sum = run(
-        lambda *refs: feed_kernel(pieces, refs),
+        int(4.4e9 * SCALE),
+    )
+    expand_blocks = expand.share(a5)
+    shrink.hop(a5)
+    hidden, feed_slope, shrink_keep, shrink_send, expand_rest = chain.run(
+        lambda *refs: feed_kernel(pieces, sizes, refs),
+        [
+            shaped((tokens, inner), LOW),
+            shaped((tokens, inner), LOW),
+            shaped(inner_rows(local * width), LOW),
+            shaped(inner_rows(local * width), LOW),
+            shaped((pieces - 1, width, local), LOW),
+        ],
+        [info, a5, out_grad, expand_weight] + expand_blocks + wide,
+        [],
+        int(3.4e9 * SCALE),
+    )
+    if tuned:
+        shr = Stream(True, shrink_keep, shrink_send, [(0, local // 4, (local, width))])
+    shrink_blocks = shrink.share(hidden)
+    cell_output, expand_keep, expand_send, dx3, fixed, expand_sum = chain.run(
+        lambda *refs: feed_back_kernel(pieces, sizes, refs),
         [
             shaped((tokens, width), LOW),
-            shaped((pieces, local // 2, width), LOW),
-            shaped((pieces, local // 2, width), LOW),
-            shaped((pieces, width // 2, local), LOW),
-            shaped((pieces, width // 2, local), LOW),
+            shaped(inner_rows(local * width), LOW),
+            shaped(inner_rows(local * width), LOW),
             shaped((tokens, width), F32),
             shaped((16, width), F32),
             shaped((8, inner), F32),
         ],
-        [info, a5, x3, out_grad, vec] + expand + shrink + wide,
-        [
-            pltpu.VMEM((tokens, inner), LOW),
-            pltpu.VMEM((tokens, inner), F32),
+        [info, a5, x3, out_grad, vec, hidden, feed_slope, expand_weight, expand_rest, shrink_weight]
+        + shrink_blocks,
+        [
             pltpu.VMEM((tokens, inner), LOW),
             pltpu.VMEM((tokens, width), F32),
             pltpu.VMEM((tokens, width), F32),
+            pltpu.VMEM((pieces - 1, local, width), LOW),
         ],
-        3 * 10**9,
-    )
-    grad_shrink = finish_inner(shrink_keep, shrink_send, mp_first)
-    grad_expand = finish_inner(expand_keep, expand_send, dp_first)
-    proj_send, proj_keep, dx2, d_sep, fixed = run(
+        int(4.6e9 * SCALE),
+    )
+    if tuned:
+        exp = Stream(True, expand_keep, expand_send, [(0, width // 4, (width, local))])
+        advance(chain, info, [shr])
+    proj_send, proj_keep, dx2, d_sep, fixed = chain.run(
         attention_backward_kernel,
         [
-            shaped((width // 2, 4 * width), LOW),
-            shaped((width // 2, 4 * width), LOW),
+            shaped((4, width * width // 512, 256), LOW),
+            shaped((4, width * width // 512, 256), LOW),
             shaped((tokens, width), F32),
             shaped((tokens, channels), LOW),
             shaped((16, width), F32),
@@ -811,21 +1107,44 @@
             pltpu.VMEM((tokens, width), LOW),
             pltpu.VMEM((tokens, 3 * width), LOW),
         ],
-        2 * 10**9,
-    )
-    both = finish_shared(proj_keep, proj_send, mp_first)
-    left_keep, left_send, point_keep, point_send, d_a2, d_right, wide_sums = run(
+        int(6.7e9 * SCALE),
+    )
+    if tuned:
+        pro = Stream(
+            False,
+            proj_keep,
+            proj_send,
+            [
+                (0, width // 8, (width, 3 * width)),
+                (3 * width * width // 2048, width // 8, (width, width)),
+            ],
+        )
+        advance(chain, info, [exp, shr])
+        advance(chain, info, [pro])
+    left_keep, left_send, d_a2, d_right, wide_sums = chain.run(
         lambda *refs: inner_backward_kernel(pieces, refs),
         [
-            shaped((pieces, width // 2, local), LOW),
-            shaped((pieces, width // 2, local), LOW),
-            shaped((pieces, local // 2, channels), LOW),
-            shaped((pieces, local // 2, channels), LOW),
+            shaped(inner_rows(local * (width + channels)), LOW),
+            shaped(inner_rows(local * (width + channels)), LOW),
             shaped((tokens, width), F32),
             shaped((tokens, channels), F32),
             shaped((16, inner), F32),
         ],
-        [info, d_sep, depth, normed, slope, rstd, a2, expand_sum] + point + left + wide,
+        [
+            info,
+            d_sep,
+            depth,
+            normed,
+            slope,
+            rstd,
+            a2,
+            expand_sum,
+            point_weight,
+            point_rest,
+            left_weight,
+            left_rest,
+        ]
+        + wide,
         [
             pltpu.VMEM((inner // 128, tokens + 16, 128), F32),
             pltpu.VMEM((tokens + 16, 128), F32),
@@ -834,15 +1153,26 @@
             pltpu.VMEM((tokens, 128), F32),
             pltpu.VMEM((tokens, 128), F32),
         ],
-        3 * 10**9,
-    )
-    grad_left = finish_inner(left_keep, left_send, dp_first)
-    grad_point = finish_inner(point_keep, point_send, mp_first)
-    last_send, last_keep, input_grad, fixed = run(
-        last_kernel,
-        [
-            shaped((width // 2, 2 * width + 3 * channels), LOW),
-            shaped((width // 2, 2 * width + 3 * channels), LOW),
+        int(11.5e9 * SCALE),
+    )
+    if tuned:
+        lef = Stream(
+            True,
+            left_keep,
+            left_send,
+            [
+                (0, width // 4, (width, local)),
+                (width * local // 1024, local // 4, (local, channels)),
+            ],
+        )
+        advance(chain, info, [shr, exp, pro])
+    small = 32 if tuned else 0
+    last_rows = width * (2 * width + 3 * channels) // 2048 + small
+    last_send, last_keep, input_grad, fixed = chain.run(
+        last_kernel if tuned else lambda *refs: last_kernel(*refs, None),
+        [
+            shaped((4, last_rows, 256), LOW),
+            shaped((4, last_rows, 256), LOW),
             shaped((tokens, width), F32),
             shaped((16, width), F32),
         ],
@@ -862,37 +1192,79 @@
             cell_input,
             vec,
             fixed,
+            wide_sums,
         ],
         [
             pltpu.VMEM((tokens, 3 * channels), LOW),
             pltpu.VMEM((tokens, width), F32),
             pltpu.VMEM((tokens, 2 * width), LOW),
-        ],
-        2 * 10**9,
-    )
-    last = finish_shared(last_keep, last_send, dp_first)
-    grad_conv = jnp.stack(
-        [
-            last[:, 2 * width + at * channels : 2 * width + (at + 1) * channels]
-            for at in range(3)
         ]
-    )
-
-    chunks = [wide_sums[:, at : at + local] for at in range(0, inner, local)]
-    for bit in mp_bits:
-        count = len(chunks) // 2
-        moved = [swap(item, "mp", bit) for item in chunks[count:]]
-        chunks = [one + two for one, two in zip(chunks[:count], moved)]
-        fixed = fixed + swap(fixed, "mp", bit)
-    wide_total = chunks[0]
-    for bit in bits_of("dp"):
-        fixed = fixed + swap(fixed, "dp", bit)
-        wide_total = wide_total + swap(wide_total, "dp", bit)
+        + ([pltpu.VMEM((8 * small, 256), F32)] if tuned else []),
+        int(4.0e9 * SCALE),
+    )
+    if tuned:
+        lat = Stream(
+            False,
+            last_keep,
+            last_send,
+            [
+                (0, width // 8, (width, 2 * width)),
+                (width * width // 1024, width // 8, (3, width, channels)),
+                (last_rows - small, small, (8 * small, 256)),
+            ],
+        )
+        advance(chain, info, [lef])
+        groups = {"a": [shr], "b": [exp, pro], "e": [exp], "p": [pro], "c": [lef], "d": [lat]}
+        for names in PLAN:
+            advance(chain, info, [item for name in names for item in groups[name]])
+        wide_total, fixed = chain.run(
+            small_kernel,
+            [shaped((16, local), F32), shaped((16, width), F32)],
+            [info, lat.mine[2]],
+            [],
+            10**6,
+        )
+        (grad_shrink,), (grad_expand,), (grad_left, grad_point) = shr.mine, exp.mine, lef.mine
+        (grad_proj, grad_out), (grad_gated, grad_conv, _) = pro.mine, lat.mine
+    else:
+
+        def whole(keep, send, offset, rows, columns):
+            both = [
+                jnp.stack([opened(item, 2 * at, 2, offset, rows, columns) for at in range(pieces)])
+                for item in (keep, send)
+            ]
+            return finish_inner(both[0], both[1], mp_first)
+
+        def shared(keep, send, offset, rows, columns):
+            both = [opened(item, 0, 4, offset, rows, columns) for item in (keep, send)]
+            return finish_shared(both[0], both[1], mp_first)
+
+        eighth = width // 8
+        grad_shrink = whole(shrink_keep, shrink_send, 0, local // 4, width)
+        grad_expand = whole(expand_keep, expand_send, 0, width // 4, local)
+        grad_left = whole(left_keep, left_send, 0, width // 4, local)
+        grad_point = whole(left_keep, left_send, width * local // 1024, local // 4, channels)
+        grad_proj = shared(proj_keep, proj_send, 0, eighth, 3 * width)
+        grad_out = shared(proj_keep, proj_send, 6 * eighth, eighth, width)
+        grad_gated = shared(last_keep, last_send, 0, eighth, 2 * width)
+        grad_conv = jnp.stack(
+            [shared(last_keep, last_send, (4 + at) * eighth, eighth, channels) for at in range(3)]
+        )
+        chunks = [wide_sums[:, at : at + local] for at in range(0, inner, local)]
+        for bit in mp_bits:
+            count = len(chunks) // 2
+            moved = [swap(item, "mp", bit) for item in chunks[count:]]
+            chunks = [one + two for one, two in zip(chunks[:count], moved)]
+            fixed = fixed + swap(fixed, "mp", bit)
+        wide_total = chunks[0]
+        for bit in bits_of("dp"):
+            fixed = fixed + swap(fixed, "dp", bit)
+            wide_total = wide_total + swap(wide_total, "dp", bit)
     return (
         cell_output,
         input_grad,
         fixed[0:8].reshape(4, 2, width),
-        last[:, : 2 * width],
+        grad_gated,
         fixed[8:10].reshape(2 * width),
         grad_left,
         wide_total[0],
@@ -902,9 +1274,9 @@
         wide_total[4:13],
         grad_point,
         fixed[14, channels:],
-        both[:, : 3 * width],
+        grad_proj,
         fixed[10:12],
-        both[:, 3 * width :],
+        grad_out,
         fixed[12],
         grad_expand,
         wide_total[1],

time: 286 us -> 201 us (0.70)
  waiting for transfers between devices: 128 us -> 57.9 us
  Pallas kernels: 38.4 us -> 68.7 us
  other arithmetic: 22 us -> 0.02 us
  starting transfers between devices: 70.3 us -> 49.8 us
    ppermute x71 -> x15, waiting for transfers between devices: 128 us -> 13.8 us  [swap(): return lax.ppermute(values, axis, [(at, at ^ bit) for at in range(count)])]
    ppermute x71 -> x15, starting transfers between devices: 70.3 us -> 13.3 us  [swap(): return lax.ppermute(values, axis, [(at, at ^ bit) for at in range(count)])]
    ppermute x0 -> x42, waiting for transfers between devices: none -> 44.1 us  [flat_swap(): lax.ppermute(values, ('dp', 'mp'), [(at, partner(at)) for at in range(cou...]
    ppermute x0 -> x42, starting transfers between devices: none -> 36.5 us  [flat_swap(): lax.ppermute(values, ('dp', 'mp'), [(at, partner(at)) for at in range(cou...]
    pallas_call x7 -> x39, Pallas kernels: 38.4 us -> 68.7 us  [the longest x38 65.6 us: run(): pl.pallas_call(call, out_shape=outs, in_specs=specs, out_specs=[pl.BlockS...]
    convert_element_type x36 -> x0, other arithmetic: 16 us -> none  [the longest x30 9.43 us: as_low(): return values.astype(LOW)]
    unnamed x75 -> x107, local copies, waits for them, and re-layouts: 10.1 us -> 17 us
    dynamic_slice x20 -> x0, local copies, waits for them, and re-layouts: 5.03 us -> none  [the longest x4 4.65 us: split(): mine = lax.dynamic_slice_in_dim(values, own * half, half, 0)]
  transfers between devices with their start and end apart: 71 -> 57, of which waited for: 27 -> 22; matrix products, arithmetic and copies ran while one was open for 11% -> 0% of each run, Pallas kernels for 4% -> 30%
where the time goes in v3:
time: 201 us
  Pallas kernels  68.7 us (34%)
  waiting for transfers between devices  57.9 us (29%)
  starting transfers between devices  49.8 us (25%)
  local copies, waits for them, and re-layouts  22.1 us (11%)
  between operations  2.34 us (1%)
    pallas_call x38, Pallas kernels, run(): pl.pallas_call(call, out_shape=outs, in_specs=specs, out_specs=[pl.BlockS...  65.6 us
    ppermute x42, waiting for transfers between devices, flat_swap(): lax.ppermute(values, ('dp', 'mp'), [(at, partner(at)) for at in range(cou...  44.1 us
    ppermute x42, starting transfers between devices, flat_swap(): lax.ppermute(values, ('dp', 'mp'), [(at, partner(at)) for at in range(cou...  36.5 us
    unnamed x107, local copies, waits for them, and re-layouts  17 us
    ppermute x15, waiting for transfers between devices, swap(): return lax.ppermute(values, axis, [(at, at ^ bit) for at in range(count)])  13.8 us
    ppermute x15, starting transfers between devices, swap(): return lax.ppermute(values, axis, [(at, at ^ bit) for at in range(count)])  13.3 us
  transfers between devices with their start and end apart: 57, of which 22 were waited for; matrix products, arithmetic and copies ran while one was open for 0% of the time, Pallas kernels for 30%

profile of v3, /device:TPU:0, one launch (start us, length us, event | category | flops | bytes accessed | tf_op | source)
XLA Modules:
  0.0 200.9 jit_solution(14754184691572980788)
XLA Ops:
  2.2 3.1 %shard_map.373 = (bf16[256,1024]{1,0:T(8,128)(2,1)}, bf16[256,256]{1,0:T(8,128)(2,1)}, bf16[128,1024]{1,0:T(8,128)(2,1)}, bf16[256,512]{1,0:T(8,128)(2,1)}) custom-call(s32[6]{0:T(128)} %stack.23.refs_0_, bf16[512,1024]{1,0:T(8,128)(2,1)} %refs_10_.1, bf16[1024,256]{1,0:T(8,128)(2,1)} %refs_8_.1, bf16[512,1024]{1,0:T(8,128)(2,1)} %refs_7_.2, ...), custom_call_target="tpu_custom_call" | custom-call | tf_op jit(solution)/shard_map/pallas_call | solution.py:679
  5.3 3.0 %collective-permute-start = (bf16[256,1024]{1,0:T(8,128)(2,1)}, bf16[256,1024]{1,0:T(8,128)(2,1)S(1)}, u32[]{:S(2)}, u32[]{:S(2)}) collective-permute-start(bf16[256,1024]{1,0:T(8,128)(2,1)} %get-tuple-element.137), channel_id=1, source_target_pairs={{0,1},{1,0},{2,3},{3,2},{4,5},{5,4},{6,7},{7,6},{8,9},{9,8},{10,11... | collective-permute-start | bytes 1572872 | tf_op jit(solution)/shard_map/ppermute | solution.py:38
  17.5 2.9 %collective-permute-done.refs_4_ = bf16[256,1024]{1,0:T(8,128)(2,1)S(1)} collective-permute-done((bf16[256,1024]{1,0:T(8,128)(2,1)}, bf16[256,1024]{1,0:T(8,128)(2,1)S(1)}, u32[]{:S(2)}, u32[]{:S(2)}) %collective-permute-start) | collective-permute-done | bytes 524320 | tf_op jit(solution)/shard_map/ppermute | solution.py:38
  24.5 2.5 %collective-permute-done.3.refs_7_ = bf16[256,256]{1,0:T(8,128)(2,1)} collective-permute-done((bf16[256,256]{1,0:T(8,128)(2,1)}, bf16[256,256]{1,0:T(8,128)(2,1)}, u32[]{:S(2)}, u32[]{:S(2)}) %collective-permute-start.3) | collective-permute-done | bytes 131104 | tf_op jit(solution)/shard_map/ppermute | solution.py:38
  30.7 5.6 %shard_map.375 = (bf16[256,2048]{1,0:T(8,128)(2,1)S(1)}, bf16[256,2048]{1,0:T(8,128)(2,1)S(1)}, bf16[256,2048]{1,0:T(8,128)(2,1)S(1)}, f32[256,128]{1,0:T(8,128)S(1)}, bf16[1,512,1024]{2,1,0:T(8,128)(2,1)S(1)}) custom-call(s32[6]{0:T(128)S(1)} %copy-done.4, bf16[256,512]{1,0:T(8,128)(2,1)S(1)} %copy-done.28, bf16[256,256]{1,0:T(8,128)(2,1)S(1)} %copy-done.37, ...), custom_call_target="tpu_custom_call" | custom-call | flops 25999998976 | bytes 526881312 | tf_op jit(solution)/shard_map/pallas_call | solution.py:169
  39.9 4.2 %shard_map.376 = (f32[256,512]{1,0:T(8,128)S(1)}, bf16[256,512]{1,0:T(8,128)(2,1)S(1)}, bf16[256,1536]{1,0:T(8,128)(2,1)S(1)}, f32[256,128]{1,0:T(8,128)S(1)}, b...) custom-call(s32[6]{0:T(128)S(1)} %copy-done.4, ...), custom_call_target="tpu_custom_call" | custom-call | flops 17600000000 | bytes 360028192 | tf_op jit(solution)/shard_map/pallas_call | solution.py:169
  45.0 2.3 %collective-permute-done.8.refs_5_ = bf16[128,1024]{1,0:T(8,128)(2,1)S(1)} collective-permute-done((bf16[128,1024]{1,0:T(8,128)(2,1)S(1)}, bf16[128,1024]{1,0:T(8,128)(2,1)S(1)}, u32[]{:S(2)}, u32[]{:S(2)}) %collective-permute-start.8) | collective-permute-done | bytes 262176 | tf_op jit(solution)/shard_map/ppermute | solution.py:38
  48.9 2.5 %shard_map.377 = (bf16[256,2048]{1,0:T(8,128)(2,1)S(1)}, bf16[256,2048]{1,0:T(8,128)(2,1)S(1)}, bf16[4,512,256]{2,1,0:T(8,128)(2,1)S(1)}, bf16[4,512,256]{2,1,0:T(8,128)(2,1)S(1)}, bf16[1,512,1024]{2,1,0:T(8,128)(2,1)S(1)}) custom-call(s32[6]{0:T(128)S(1)} %copy-done.4, bf16[256,512]{1,0:T(8,128)(2,1)S(1)} %get-tuple-element.146.refs_1_, ...), custom_call_target="tpu_custom_call" | custom-call | flops 13600000000 | bytes 279929888 | tf_op jit(solution)/shard_map/pallas_call | solution.py:169
  51.4 4.6 %collective-permute-done.12.refs_11_ = bf16[256,512]{1,0:T(8,128)(2,1)S(1)} collective-permute-done((bf16[256,512]{1,0:T(8,128)(2,1)S(1)}, bf16[256,512]{1,0:T(8,128)(2,1)S(1)}, u32[]{:S(2)}, u32[]{:S(2)}) %collective-permute-start.12) | collective-permute-done | bytes 262176 | tf_op jit(solution)/shard_map/ppermute | solution.py:38
  57.9 3.9 %shard_map.378 = (bf16[256,512]{1,0:T(8,128)(2,1)}, bf16[4,512,256]{2,1,0:T(8,128)(2,1)S(1)}, bf16[4,512,256]{2,1,0:T(8,128)(2,1)S(1)}, f32[256,512]{1,0:T(8,128...) custom-call(s32[6]{0:T(128)S(1)} %copy-done.4, bf16[256,512]{1,0:T(8,128)(2,1)S(1)} %get-tuple-element.146.refs_1_, ...), custom_call_target="tpu_custom_call" | custom-call | flops 18400000000 | bytes 378354720 | tf_op jit(solution)/shard_map/pallas_call | solution.py:169
  63.4 5.9 %shard_map.380 = (bf16[4,512,256]{2,1,0:T(8,128)(2,1)S(1)}, bf16[4,512,256]{2,1,0:T(8,128)(2,1)S(1)}, f32[256,512]{1,0:T(8,128)S(1)}, bf16[256,256]{1,0:T(8,128)(2,1)S(1)}, f32[16,512]{1,0:T(8,128)S(1)}) custom-call(s32[6]{0:T(128)S(1)} %copy-done.4, f32[256,512]{1,0:T(8,128)S(1)} %get-tuple-element.160.refs_1_, ...), custom_call_target="tpu_custom_call" | custom-call | flops 26800001024 | bytes 543438336 | tf_op jit(solution)/shard_map/pallas_call | solution.py:169
  69.5 2.5 %collective-permute-done.18.refs_4_ = bf16[2,512,256]{2,1,0:T(8,128)(2,1)S(1)} collective-permute-done((bf16[2,512,256]{2,1,0:T(8,128)(2,1)S(1)}, bf16[2,512,256]{2,1,0:T(8,128)(2,1)S(1)}, u32[]{:S(2)}, u32[]{:S(2)}) %collective-permute-start.18) | collective-permute-done | bytes 524320 | tf_op jit(solution)/shard_map/ppermute | solution.py:691
  76.5 9.8 %shard_map.383 = (bf16[4,768,256]{2,1,0:T(8,128)(2,1)S(1)}, bf16[4,768,256]{2,1,0:T(8,128)(2,1)S(1)}, f32[256,512]{1,0:T(8,128)S(1)}, f32[256,256]{1,0:T(8,128)S(1)}, f32[16,2048]{1,0:T(8,128)S(1)}) custom-call(s32[6]{0:T(128)S(1)} %copy-done.4, bf16[256,256]{1,0:T(8,128)(2,1)S(1)} %get-tuple-element.171.refs_1_, ...), custom_call_target="tpu_custom_call" | custom-call | flops 46000001024 | bytes 931010048 | tf_op jit(solution)/shard_map/pallas_call | solution.py:169
  86.4 2.7 %collective-permute-done.21.refs_6_ = bf16[2,512,256]{2,1,0:T(8,128)(2,1)S(1)} collective-permute-done((bf16[2,512,256]{2,1,0:T(8,128)(2,1)S(1)}, bf16[2,512,256]{2,1,0:T(8,128)(2,1)S(1)}, u32[]{:S(2)}, u32[]{:S(2)}) %collective-permute-start.21) | collective-permute-done | bytes 524320 | tf_op jit(solution)/shard_map/ppermute | solution.py:691
  93.8 3.3 %shard_map.385 = (bf16[4,480,256]{2,1,0:T(8,128)(2,1)S(1)}, bf16[4,480,256]{2,1,0:T(8,128)(2,1)S(1)}, f32[256,512]{1,0:T(8,128)}, f32[16,512]{1,0:T(8,128)S(1)}) custom-call(s32[6]{0:T(128)S(1)} %copy-done.4, f32[256,512]{1,0:T(8,128)S(1)} %get-tuple-element.182.refs_1_, f32[256,256]{1,0:T(8,128)S(1)} %get-tuple-element.183.refs_2_, ...), custom_call_target="tpu_custom_call" | custom-call | flops 16000000000 | bytes 328486944 | tf_op jit(solution)/shard_map/pallas_call | solution.py:169
  98.8 2.1 %collective-permute-done.27.refs_6_ = bf16[1,512,256]{2,1,0:T(8,128)(2,1)S(1)} collective-permute-done((bf16[1,512,256]{2,1,0:T(8,128)(2,1)S(1)}, bf16[1,512,256]{2,1,0:T(8,128)(2,1)S(1)}, u32[]{:S(2)}, u32[]{:S(2)}) %collective-permute-start.27) | collective-permute-done | bytes 262176 | tf_op jit(solution)/shard_map/ppermute | solution.py:691
  103.7 2.6 %collective-permute-start.30 = (bf16[1,256,256]{2,1,0:T(8,128)(2,1)S(1)}, bf16[1,256,256]{2,1,0:T(8,128)(2,1)S(1)}, u32[]{:S(2)}, u32[]{:S(2)}) collective-permute-start(bf16[1,256,256]{2,1,0:T(8,128)(2,1)S(1)} %get-tuple-element.213.refs_1_), channel_id=1, source_target_pairs={{0,16},{1,17},{2,18},{3,19},{4,20},{5,21},{6,22},{7,23},{8,24},{9,... | collective-permute-start | bytes 393224 | tf_op jit(solution)/shard_map/ppermute | solution.py:691
  107.7 2.4 %collective-permute-done.23.refs_2_ = bf16[2,768,256]{2,1,0:T(8,128)(2,1)S(1)} collective-permute-done((bf16[2,768,256]{2,1,0:T(8,128)(2,1)S(1)}, bf16[2,768,256]{2,1,0:T(8,128)(2,1)S(1)}, u32[]{:S(2)}, u32[]{:S(2)}) %collective-permute-start.23) | collective-permute-done | bytes 786464 | tf_op jit(solution)/shard_map/ppermute | solution.py:691
  112.3 2.7 %collective-permute-start.35 = (bf16[1,256,256]{2,1,0:T(8,128)(2,1)S(1)}, bf16[1,256,256]{2,1,0:T(8,128)(2,1)S(1)}, u32[]{:S(2)}, u32[]{:S(2)}) collective-permute-start(bf16[1,256,256]{2,1,0:T(8,128)(2,1)S(1)} %get-tuple-element.222.refs_1_), channel_id=1, source_target_pairs={{0,8},{1,9},{2,10},{3,11},{4,12},{5,13},{6,14},{7,15},{8,0},{9,1},... | collective-permute-start | bytes 393224 | tf_op jit(solution)/shard_map/ppermute | solution.py:691
  115.4 2.5 %collective-permute-start.37 = (bf16[1,256,256]{2,1,0:T(8,128)(2,1)S(1)}, bf16[1,256,256]{2,1,0:T(8,128)(2,1)S(1)}, u32[]{:S(2)}, u32[]{:S(2)}) collective-permute-start(bf16[1,256,256]{2,1,0:T(8,128)(2,1)S(1)} %get-tuple-element.217.refs_3_.refs_5_), channel_id=1, source_target_pairs={{0,16},{1,17},{2,18},{3,19},{4,20},{5,21},{6,22},{7,23},{8,24},{9,... | collective-permute-start | bytes 393224 | tf_op jit(solution)/shard_map/ppermute | solution.py:691
  121.3 4.7 %collective-permute-done.36.refs_4_ = bf16[1,256,256]{2,1,0:T(8,128)(2,1)S(1)} collective-permute-done((bf16[1,256,256]{2,1,0:T(8,128)(2,1)S(1)}, bf16[1,256,256]{2,1,0:T(8,128)(2,1)S(1)}, u32[]{:S(2)}, u32[]{:S(2)}) %collective-permute-start.36) | collective-permute-done | bytes 131104 | tf_op jit(solution)/shard_map/ppermute | solution.py:691
  132.0 3.5 %collective-permute-start.38 = (bf16[1,384,256]{2,1,0:T(8,128)(2,1)S(1)}, bf16[1,384,256]{2,1,0:T(8,128)(2,1)S(1)}, u32[]{:S(2)}, u32[]{:S(2)}) collective-permute-start(bf16[1,384,256]{2,1,0:T(8,128)(2,1)S(1)} %get-tuple-element.225.refs_1_), channel_id=1, source_target_pairs={{0,16},{1,17},{2,18},{3,19},{4,20},{5,21},{6,22},{7,23},{8,24},{9,... | collective-permute-start | bytes 589832 | tf_op jit(solution)/shard_map/ppermute | solution.py:691
  135.5 6.1 %collective-permute-done.42.refs_4_ = bf16[1,256,256]{2,1,0:T(8,128)(2,1)S(1)} collective-permute-done((bf16[1,256,256]{2,1,0:T(8,128)(2,1)S(1)}, bf16[1,256,256]{2,1,0:T(8,128)(2,1)S(1)}, u32[]{:S(2)}, u32[]{:S(2)}) %collective-permute-start.42) | collective-permute-done | bytes 131104 | tf_op jit(solution)/shard_map/ppermute | solution.py:691
  145.6 2.0 %collective-permute-start.44 = (bf16[1,384,256]{2,1,0:T(8,128)(2,1)S(1)}, bf16[1,384,256]{2,1,0:T(8,128)(2,1)S(1)}, u32[]{:S(2)}, u32[]{:S(2)}) collective-permute-start(bf16[1,384,256]{2,1,0:T(8,128)(2,1)S(1)} %get-tuple-element.232.refs_1_), channel_id=1, source_target_pairs={{0,8},{1,9},{2,10},{3,11},{4,12},{5,13},{6,14},{7,15},{8,0},{9,1},... | collective-permute-start | bytes 589832 | tf_op jit(solution)/shard_map/ppermute | solution.py:691
  148.6 2.8 %collective-permute-done.47.refs_4_ = bf16[1,512,256]{2,1,0:T(8,128)(2,1)S(1)} collective-permute-done((bf16[1,512,256]{2,1,0:T(8,128)(2,1)S(1)}, bf16[1,512,256]{2,1,0:T(8,128)(2,1)S(1)}, u32[]{:S(2)}, u32[]{:S(2)}) %collective-permute-start.47) | collective-permute-done | bytes 262176 | tf_op jit(solution)/shard_map/ppermute | solution.py:691
  158.9 2.4 %collective-permute-done.51.refs_2_ = bf16[2,512,256]{2,1,0:T(8,128)(2,1)S(1)} collective-permute-done((bf16[2,512,256]{2,1,0:T(8,128)(2,1)S(1)}, bf16[2,512,256]{2,1,0:T(8,128)(2,1)S(1)}, u32[]{:S(2)}, u32[]{:S(2)}) %collective-permute-start.51) | collective-permute-done | bytes 524320 | tf_op jit(solution)/shard_map/ppermute | solution.py:691
  164.0 5.2 %collective-permute-done.49.refs_2_ = bf16[1,768,256]{2,1,0:T(8,128)(2,1)S(1)} collective-permute-done((bf16[1,768,256]{2,1,0:T(8,128)(2,1)S(1)}, bf16[1,768,256]{2,1,0:T(8,128)(2,1)S(1)}, u32[]{:S(2)}, u32[]{:S(2)}) %collective-permute-start.49) | collective-permute-done | bytes 393248 | tf_op jit(solution)/shard_map/ppermute | solution.py:691
  172.5 2.8 %shard_map.406 = (f32[512,1536]{1,0:T(8,128)}, f32[512,512]{1,0:T(8,128)}) custom-call(s32[6]{0:T(128)S(1)} %copy-done.4, bf16[4,512,256]{2,1,0:T(8,128)(2,1)S(1)} %shard_map.402.refs_3_.refs_1_, bf16[4,512,256]{2,1,0:T(8,128)(2,1)S(1)} %collective-permute-done.54.refs_2_, bf16[1,480,256]{2,1,0:T(8,128)(2,1)S(1)} %shard_map.405.refs_3_.refs_1_), custom_call_target="tpu_custom_call" | custom-call | flops 20000000000 | bytes 406291488 | tf_op jit(solution)/shard_map/pallas_call | solution.py:169
  176.6 2.4 %shard_map.407 = (f32[512,1024]{1,0:T(8,128)}, f32[1024,256]{1,0:T(8,128)}) custom-call(s32[6]{0:T(128)S(1)} %copy-done.4, bf16[2,768,256]{2,1,0:T(8,128)(2,1)S(1)} %shard_map.404.refs_3_.refs_1_, bf16[2,768,256]{2,1,0:T(8,128)(2,1)S(1)} %collective-permute-done.53.refs_2_, f32[512,512]{1,0:T(8,128)S(1)} %copy-done.16), custom_call_target="tpu_custom_call" | custom-call | flops 20000000000 | bytes 404718624 | tf_op jit(solution)/shard_map/pallas_call | solution.py:169
  182.5 7.2 %collective-permute-done.55.refs_2_ = bf16[2,480,256]{2,1,0:T(8,128)(2,1)S(1)} collective-permute-done((bf16[2,480,256]{2,1,0:T(8,128)(2,1)S(1)}, bf16[2,480,256]{2,1,0:T(8,128)(2,1)S(1)}, u32[]{:S(2)}, u32[]{:S(2)}) %collective-permute-start.55) | collective-permute-done | bytes 491552 | tf_op jit(solution)/shard_map/ppermute | solution.py:691
  190.7 2.2 %collective-permute-done.56.refs_2_ = bf16[4,480,256]{2,1,0:T(8,128)(2,1)S(1)} collective-permute-done((bf16[4,480,256]{2,1,0:T(8,128)(2,1)S(1)}, bf16[4,480,256]{2,1,0:T(8,128)(2,1)S(1)}, u32[]{:S(2)}, u32[]{:S(2)}) %collective-permute-start.56) | collective-permute-done | bytes 983072 | tf_op jit(solution)/shard_map/ppermute | solution.py:691
  192.9 2.6 %shard_map.410 = (f32[512,1024]{1,0:T(8,128)}, f32[3,512,256]{2,1,0:T(8,128)}, f32[256,256]{1,0:T(8,128)S(1)}) custom-call(s32[6]{0:T(128)S(1)} %copy-done.4, bf16[4,480,256]{2,1,0:T(8,128)(2,1)S(1)} %shard_map.409.refs_1_.refs_3_, bf16[4,480,256]{2,1,0:T(8,128)(2,1)S(1)} %collective-permute-done.56.refs_2_, bf16[4,480,256]{2,1,0:T(8,128)(2,1)S(1)} %shard_map.409.refs_1_.refs_3_), custom_call_target="tpu_custom_call" | custom-call | flops 20000000000 | bytes 405898272 | tf_op jit(solution)/shard_map/pallas_call | solution.py:169
  (250 shorter events, 83.5 us)
Async XLA Ops:
  5.3 15.1 %collective-permute-start = (bf16[256,1024]{1,0:T(8,128)(2,1)}, bf16[256,1024]{1,0:T(8,128)(2,1)S(1)}, u32[]{:S(2)}, u32[]{:S(2)}) collective-permute-start(bf16[256,1024]{1,0:T(8,128)(2,1)} %get-tuple-element.137), channel_id=1, source_target_pairs={{0,1},{1,0},{2,3},{3,2},{4,5},{5,4},{6,7},{7,6},{8,9},{9,8},{10,11... | collective-permute-start | bytes 1572872 | tf_op jit(solution)/shard_map/ppermute | solution.py:38
  22.8 16.5 %collective-permute-start.7 = (bf16[128,1024]{1,0:T(8,128)(2,1)}, bf16[128,1024]{1,0:T(8,128)(2,1)S(1)}, u32[]{:S(2)}, u32[]{:S(2)}) collective-permute-start(bf16[128,1024]{1,0:T(8,128)(2,1)} %get-tuple-element.148), channel_id=1, source_target_pairs={{0,1},{1,0},{2,3},{3,2},{4,5},{5,4},{6,7},{7,6},{8,9},{9,8},{10,11... | collective-permute-start | bytes 786440 | tf_op jit(solution)/shard_map/ppermute | solution.py:38
  27.0 10.3 %collective-permute-start.4 = (bf16[256,256]{1,0:T(8,128)(2,1)}, bf16[256,256]{1,0:T(8,128)(2,1)S(1)}, u32[]{:S(2)}, u32[]{:S(2)}) collective-permute-start(bf16[256,256]{1,0:T(8,128)(2,1)} %collective-permute-done.3.refs_7_), channel_id=1, source_target_pairs={{0,4},{2,6},{4,0},{6,2},{8,12},{10,14},{12,8},{14,10},{16,20},{18,... | collective-permute-start | bytes 393224 | tf_op jit(solution)/shard_map/ppermute | solution.py:38
  37.8 9.5 %collective-permute-start.11 = (bf16[256,512]{1,0:T(8,128)(2,1)S(1)}, bf16[256,512]{1,0:T(8,128)(2,1)S(1)}, u32[]{:S(2)}, u32[]{:S(2)}) collective-permute-start(bf16[256,512]{1,0:T(8,128)(2,1)S(1)} %copy-done.13), channel_id=1, source_target_pairs={{0,1},{1,0},{2,3},{3,2},{4,5},{5,4},{6,7},{7,6},{8,9},{9,8},{10,11... | collective-permute-start | bytes 786440 | tf_op jit(solution)/shard_map/ppermute | solution.py:38
  62.8 9.2 %collective-permute-start.18 = (bf16[2,512,256]{2,1,0:T(8,128)(2,1)S(1)}, bf16[2,512,256]{2,1,0:T(8,128)(2,1)S(1)}, u32[]{:S(2)}, u32[]{:S(2)}) collective-permute-start(bf16[2,512,256]{2,1,0:T(8,128)(2,1)S(1)} %get-tuple-element.170.refs_11_), channel_id=1, source_target_pairs={{0,1},{1,0},{2,6},{3,7},{4,5},{5,4},{6,2},{7,3},{8,9},{9,8},{10,14... | collective-permute-start | bytes 1572872 | tf_op jit(solution)/shard_map/ppermute | solution.py:691
  73.0 13.5 %collective-permute-start.19 = (bf16[1,512,256]{2,1,0:T(8,128)(2,1)S(1)}, bf16[1,512,256]{2,1,0:T(8,128)(2,1)S(1)}, u32[]{:S(2)}, u32[]{:S(2)}) collective-permute-start(bf16[1,512,256]{2,1,0:T(8,128)(2,1)S(1)} %get-tuple-element.180.refs_3_), channel_id=1, source_target_pairs={{0,4},{1,5},{2,3},{3,2},{4,0},{5,1},{6,7},{7,6},{8,12},{9,13},{10,... | collective-permute-start | bytes 786440 | tf_op jit(solution)/shard_map/ppermute | solution.py:691
  73.6 12.8 %collective-permute-start.20 = (bf16[2,512,256]{2,1,0:T(8,128)(2,1)S(1)}, bf16[2,512,256]{2,1,0:T(8,128)(2,1)S(1)}, u32[]{:S(2)}, u32[]{:S(2)}) collective-permute-start(bf16[2,512,256]{2,1,0:T(8,128)(2,1)S(1)} %get-tuple-element.192), channel_id=1, source_target_pairs={{0,1},{1,0},{2,6},{3,7},{4,5},{5,4},{6,2},{7,3},{8,9},{9,8},{10,14... | collective-permute-start | bytes 1572872 | tf_op jit(solution)/shard_map/ppermute | solution.py:691
  75.0 14.2 %collective-permute-start.21 = (bf16[2,512,256]{2,1,0:T(8,128)(2,1)S(1)}, bf16[2,512,256]{2,1,0:T(8,128)(2,1)S(1)}, u32[]{:S(2)}, u32[]{:S(2)}) collective-permute-start(bf16[2,512,256]{2,1,0:T(8,128)(2,1)S(1)} %get-tuple-element.181.refs_14_), channel_id=1, source_target_pairs={{0,1},{1,0},{2,6},{3,7},{4,5},{5,4},{6,2},{7,3},{8,9},{9,8},{10,14... | collective-permute-start | bytes 1572872 | tf_op jit(solution)/shard_map/ppermute | solution.py:691
  86.3 10.8 %collective-permute-start.22 = (bf16[4,768,256]{2,1,0:T(8,128)(2,1)S(1)}, bf16[4,768,256]{2,1,0:T(8,128)(2,1)S(1)}, u32[]{:S(2)}, u32[]{:S(2)}) collective-permute-start(bf16[4,768,256]{2,1,0:T(8,128)(2,1)S(1)} %get-tuple-element.197), channel_id=1, source_target_pairs={{0,2},{1,3},{2,0},{3,1},{4,6},{5,7},{6,4},{7,5},{8,10},{9,11},{10,... | collective-permute-start | bytes 4718600 | tf_op jit(solution)/shard_map/ppermute | solution.py:691
  97.1 9.2 %collective-permute-start.24 = (bf16[4,480,256]{2,1,0:T(8,128)(2,1)S(1)}, bf16[4,480,256]{2,1,0:T(8,128)(2,1)S(1)}, u32[]{:S(2)}, u32[]{:S(2)}) collective-permute-start(bf16[4,480,256]{2,1,0:T(8,128)(2,1)S(1)} %get-tuple-element.202), channel_id=1, source_target_pairs={{0,2},{1,3},{2,0},{3,1},{4,6},{5,7},{6,4},{7,5},{8,10},{9,11},{10,... | collective-permute-start | bytes 2949128 | tf_op jit(solution)/shard_map/ppermute | solution.py:691
  98.0 12.1 %collective-permute-start.23 = (bf16[2,768,256]{2,1,0:T(8,128)(2,1)S(1)}, bf16[2,768,256]{2,1,0:T(8,128)(2,1)S(1)}, u32[]{:S(2)}, u32[]{:S(2)}) collective-permute-start(bf16[2,768,256]{2,1,0:T(8,128)(2,1)S(1)} %get-tuple-element.200.refs_7_), channel_id=1, source_target_pairs={{0,1},{1,0},{2,6},{3,7},{4,5},{5,4},{6,2},{7,3},{8,9},{9,8},{10,14... | collective-permute-start | bytes 2359304 | tf_op jit(solution)/shard_map/ppermute | solution.py:691
  101.6 10.0 %collective-permute-start.31 = (bf16[1,256,256]{2,1,0:T(8,128)(2,1)S(1)}, bf16[1,256,256]{2,1,0:T(8,128)(2,1)S(1)}, u32[]{:S(2)}, u32[]{:S(2)}) collective-permute-start(bf16[1,256,256]{2,1,0:T(8,128)(2,1)S(1)} %get-tuple-element.215), channel_id=1, source_target_pairs={{0,8},{1,9},{2,10},{3,11},{4,12},{5,13},{6,14},{7,15},{8,0},{9,1},... | collective-permute-start | bytes 393224 | tf_op jit(solution)/shard_map/ppermute | solution.py:691
  102.1 9.5 %collective-permute-start.32 = (bf16[1,256,256]{2,1,0:T(8,128)(2,1)S(1)}, bf16[1,256,256]{2,1,0:T(8,128)(2,1)S(1)}, u32[]{:S(2)}, u32[]{:S(2)}) collective-permute-start(bf16[1,256,256]{2,1,0:T(8,128)(2,1)S(1)} %get-tuple-element.208.refs_3_), channel_id=1, source_target_pairs={{0,8},{1,9},{2,10},{3,11},{4,12},{5,13},{6,14},{7,15},{8,0},{9,1},... | collective-permute-start | bytes 393224 | tf_op jit(solution)/shard_map/ppermute | solution.py:691
  107.0 11.7 %collective-permute-start.29 = (bf16[2,480,256]{2,1,0:T(8,128)(2,1)S(1)}, bf16[2,480,256]{2,1,0:T(8,128)(2,1)S(1)}, u32[]{:S(2)}, u32[]{:S(2)}) collective-permute-start(bf16[2,480,256]{2,1,0:T(8,128)(2,1)S(1)} %get-tuple-element.209.refs_3_), channel_id=1, source_target_pairs={{0,1},{1,0},{2,6},{3,7},{4,5},{5,4},{6,2},{7,3},{8,9},{9,8},{10,14... | collective-permute-start | bytes 1474568 | tf_op jit(solution)/shard_map/ppermute | solution.py:691
  110.8 9.3 %collective-permute-start.28 = (bf16[1,768,256]{2,1,0:T(8,128)(2,1)S(1)}, bf16[1,768,256]{2,1,0:T(8,128)(2,1)S(1)}, u32[]{:S(2)}, u32[]{:S(2)}) collective-permute-start(bf16[1,768,256]{2,1,0:T(8,128)(2,1)S(1)} %get-tuple-element.211.refs_7_), channel_id=1, source_target_pairs={{0,4},{1,5},{2,3},{3,2},{4,0},{5,1},{6,7},{7,6},{8,12},{9,13},{10,... | collective-permute-start | bytes 1179656 | tf_op jit(solution)/shard_map/ppermute | solution.py:691
  112.3 9.0 %collective-permute-start.35 = (bf16[1,256,256]{2,1,0:T(8,128)(2,1)S(1)}, bf16[1,256,256]{2,1,0:T(8,128)(2,1)S(1)}, u32[]{:S(2)}, u32[]{:S(2)}) collective-permute-start(bf16[1,256,256]{2,1,0:T(8,128)(2,1)S(1)} %get-tuple-element.222.refs_1_), channel_id=1, source_target_pairs={{0,8},{1,9},{2,10},{3,11},{4,12},{5,13},{6,14},{7,15},{8,0},{9,1},... | collective-permute-start | bytes 393224 | tf_op jit(solution)/shard_map/ppermute | solution.py:691
  114.9 11.1 %collective-permute-start.36 = (bf16[1,256,256]{2,1,0:T(8,128)(2,1)S(1)}, bf16[1,256,256]{2,1,0:T(8,128)(2,1)S(1)}, u32[]{:S(2)}, u32[]{:S(2)}) collective-permute-start(bf16[1,256,256]{2,1,0:T(8,128)(2,1)S(1)} %get-tuple-element.223.refs_3_), channel_id=1, source_target_pairs={{0,16},{1,17},{2,18},{3,19},{4,20},{5,21},{6,22},{7,23},{8,24},{9,... | collective-permute-start | bytes 393224 | tf_op jit(solution)/shard_map/ppermute | solution.py:691
  115.4 12.0 %collective-permute-start.37 = (bf16[1,256,256]{2,1,0:T(8,128)(2,1)S(1)}, bf16[1,256,256]{2,1,0:T(8,128)(2,1)S(1)}, u32[]{:S(2)}, u32[]{:S(2)}) collective-permute-start(bf16[1,256,256]{2,1,0:T(8,128)(2,1)S(1)} %get-tuple-element.217.refs_3_.refs_5_), channel_id=1, source_target_pairs={{0,16},{1,17},{2,18},{3,19},{4,20},{5,21},{6,22},{7,23},{8,24},{9,... | collective-permute-start | bytes 393224 | tf_op jit(solution)/shard_map/ppermute | solution.py:691
  119.4 11.4 %collective-permute-start.34 = (bf16[1,480,256]{2,1,0:T(8,128)(2,1)S(1)}, bf16[1,480,256]{2,1,0:T(8,128)(2,1)S(1)}, u32[]{:S(2)}, u32[]{:S(2)}) collective-permute-start(bf16[1,480,256]{2,1,0:T(8,128)(2,1)S(1)} %get-tuple-element.218.refs_3_), channel_id=1, source_target_pairs={{0,4},{1,5},{2,3},{3,2},{4,0},{5,1},{6,7},{7,6},{8,12},{9,13},{10,... | collective-permute-start | bytes 737288 | tf_op jit(solution)/shard_map/ppermute | solution.py:691
  120.7 10.6 %collective-permute-start.33 = (bf16[1,384,256]{2,1,0:T(8,128)(2,1)S(1)}, bf16[1,384,256]{2,1,0:T(8,128)(2,1)S(1)}, u32[]{:S(2)}, u32[]{:S(2)}) collective-permute-start(bf16[1,384,256]{2,1,0:T(8,128)(2,1)S(1)} %get-tuple-element.220.refs_7_), channel_id=1, source_target_pairs={{0,8},{1,9},{2,10},{3,11},{4,12},{5,13},{6,14},{7,15},{8,0},{9,1},... | collective-permute-start | bytes 589832 | tf_op jit(solution)/shard_map/ppermute | solution.py:691
  128.1 13.4 %collective-permute-start.42 = (bf16[1,256,256]{2,1,0:T(8,128)(2,1)S(1)}, bf16[1,256,256]{2,1,0:T(8,128)(2,1)S(1)}, u32[]{:S(2)}, u32[]{:S(2)}) collective-permute-start(bf16[1,256,256]{2,1,0:T(8,128)(2,1)S(1)} %get-tuple-element.224.refs_5_.refs_3_), channel_id=1, source_target_pairs={{0,8},{1,9},{2,10},{3,11},{4,12},{5,13},{6,14},{7,15},{8,0},{9,1},... | collective-permute-start | bytes 393224 | tf_op jit(solution)/shard_map/ppermute | solution.py:691
  130.1 14.1 %collective-permute-start.40 = (bf16[1,512,256]{2,1,0:T(8,128)(2,1)S(1)}, bf16[1,512,256]{2,1,0:T(8,128)(2,1)S(1)}, u32[]{:S(2)}, u32[]{:S(2)}) collective-permute-start(bf16[1,512,256]{2,1,0:T(8,128)(2,1)S(1)} %get-tuple-element.228.refs_1_), channel_id=1, source_target_pairs={{0,4},{1,5},{2,6},{3,7},{4,0},{5,1},{6,2},{7,3},{8,12},{9,13},{10,... | collective-permute-start | bytes 786440 | tf_op jit(solution)/shard_map/ppermute | solution.py:691
  131.9 13.0 %collective-permute-start.39 = (bf16[1,240,256]{2,1,0:T(8,128)(2,1)S(1)}, bf16[1,240,256]{2,1,0:T(8,128)(2,1)S(1)}, u32[]{:S(2)}, u32[]{:S(2)}) collective-permute-start(bf16[1,240,256]{2,1,0:T(8,128)(2,1)S(1)} %get-tuple-element.227.refs_5_), channel_id=1, source_target_pairs={{0,8},{1,9},{2,10},{3,11},{4,12},{5,13},{6,14},{7,15},{8,0},{9,1},... | collective-permute-start | bytes 368648 | tf_op jit(solution)/shard_map/ppermute | solution.py:691
  132.0 12.9 %collective-permute-start.38 = (bf16[1,384,256]{2,1,0:T(8,128)(2,1)S(1)}, bf16[1,384,256]{2,1,0:T(8,128)(2,1)S(1)}, u32[]{:S(2)}, u32[]{:S(2)}) collective-permute-start(bf16[1,384,256]{2,1,0:T(8,128)(2,1)S(1)} %get-tuple-element.225.refs_1_), channel_id=1, source_target_pairs={{0,16},{1,17},{2,18},{3,19},{4,20},{5,21},{6,22},{7,23},{8,24},{9,... | collective-permute-start | bytes 589832 | tf_op jit(solution)/shard_map/ppermute | solution.py:691
  144.8 9.0 %collective-permute-start.45 = (bf16[2,512,256]{2,1,0:T(8,128)(2,1)S(1)}, bf16[2,512,256]{2,1,0:T(8,128)(2,1)S(1)}, u32[]{:S(2)}, u32[]{:S(2)}) collective-permute-start(bf16[2,512,256]{2,1,0:T(8,128)(2,1)S(1)} %shard_map.396.refs_5_.refs_1_), channel_id=1, source_target_pairs={{0,2},{1,3},{2,0},{3,1},{4,6},{5,7},{6,4},{7,5},{8,10},{9,11},{10,... | collective-permute-start | bytes 1572872 | tf_op jit(solution)/shard_map/ppermute | solution.py:691
  145.5 12.5 %collective-permute-start.43 = (bf16[1,240,256]{2,1,0:T(8,128)(2,1)S(1)}, bf16[1,240,256]{2,1,0:T(8,128)(2,1)S(1)}, u32[]{:S(2)}, u32[]{:S(2)}) collective-permute-start(bf16[1,240,256]{2,1,0:T(8,128)(2,1)S(1)} %get-tuple-element.231.refs_5_.refs_1_), channel_id=1, source_target_pairs={{0,16},{1,17},{2,18},{3,19},{4,20},{5,21},{6,22},{7,23},{8,24},{9,... | collective-permute-start | bytes 368648 | tf_op jit(solution)/shard_map/ppermute | solution.py:691
  145.6 10.2 %collective-permute-start.44 = (bf16[1,384,256]{2,1,0:T(8,128)(2,1)S(1)}, bf16[1,384,256]{2,1,0:T(8,128)(2,1)S(1)}, u32[]{:S(2)}, u32[]{:S(2)}) collective-permute-start(bf16[1,384,256]{2,1,0:T(8,128)(2,1)S(1)} %get-tuple-element.232.refs_1_), channel_id=1, source_target_pairs={{0,8},{1,9},{2,10},{3,11},{4,12},{5,13},{6,14},{7,15},{8,0},{9,1},... | collective-permute-start | bytes 589832 | tf_op jit(solution)/shard_map/ppermute | solution.py:691
  152.0 10.0 %collective-permute-start.50 = (bf16[2,512,256]{2,1,0:T(8,128)(2,1)S(1)}, bf16[2,512,256]{2,1,0:T(8,128)(2,1)S(1)}, u32[]{:S(2)}, u32[]{:S(2)}) collective-permute-start(bf16[2,512,256]{2,1,0:T(8,128)(2,1)S(1)} %get-tuple-element.235.refs_1_), channel_id=1, source_target_pairs={{0,2},{1,3},{2,0},{3,1},{4,6},{5,7},{6,4},{7,5},{8,10},{9,11},{10,... | collective-permute-start | bytes 1572872 | tf_op jit(solution)/shard_map/ppermute | solution.py:691
  152.1 9.2 %collective-permute-start.51 = (bf16[2,512,256]{2,1,0:T(8,128)(2,1)S(1)}, bf16[2,512,256]{2,1,0:T(8,128)(2,1)S(1)}, u32[]{:S(2)}, u32[]{:S(2)}) collective-permute-start(bf16[2,512,256]{2,1,0:T(8,128)(2,1)S(1)} %get-tuple-element.234.refs_3_.refs_1_), channel_id=1, source_target_pairs={{0,1},{1,0},{2,6},{3,7},{4,5},{5,4},{6,2},{7,3},{8,9},{9,8},{10,14... | collective-permute-start | bytes 1572872 | tf_op jit(solution)/shard_map/ppermute | solution.py:691
  158.0 11.2 %collective-permute-start.49 = (bf16[1,768,256]{2,1,0:T(8,128)(2,1)S(1)}, bf16[1,768,256]{2,1,0:T(8,128)(2,1)S(1)}, u32[]{:S(2)}, u32[]{:S(2)}) collective-permute-start(bf16[1,768,256]{2,1,0:T(8,128)(2,1)S(1)} %shard_map.400.refs_3_.refs_1_), channel_id=1, source_target_pairs={{0,4},{1,5},{2,6},{3,7},{4,0},{5,1},{6,2},{7,3},{8,12},{9,13},{10,... | collective-permute-start | bytes 1179656 | tf_op jit(solution)/shard_map/ppermute | solution.py:691
  158.7 12.8 %collective-permute-start.48 = (bf16[1,240,256]{2,1,0:T(8,128)(2,1)S(1)}, bf16[1,240,256]{2,1,0:T(8,128)(2,1)S(1)}, u32[]{:S(2)}, u32[]{:S(2)}) collective-permute-start(bf16[1,240,256]{2,1,0:T(8,128)(2,1)S(1)} %shard_map.401.refs_3_.refs_1_), channel_id=1, source_target_pairs={{0,8},{1,9},{2,10},{3,11},{4,12},{5,13},{6,14},{7,15},{8,0},{9,1},... | collective-permute-start | bytes 368648 | tf_op jit(solution)/shard_map/ppermute | solution.py:691
  161.9 10.6 %collective-permute-start.54 = (bf16[4,512,256]{2,1,0:T(8,128)(2,1)S(1)}, bf16[4,512,256]{2,1,0:T(8,128)(2,1)S(1)}, u32[]{:S(2)}, u32[]{:S(2)}) collective-permute-start(bf16[4,512,256]{2,1,0:T(8,128)(2,1)S(1)} %shard_map.402.refs_3_.refs_1_), channel_id=1, source_target_pairs={{0,2},{1,3},{2,0},{3,1},{4,6},{5,7},{6,4},{7,5},{8,10},{9,11},{10,... | collective-permute-start | bytes 3145736 | tf_op jit(solution)/shard_map/ppermute | solution.py:691
  (78 other events, 426.2 us)

commit v4 on v3

--- a/solution.py
+++ b/solution.py
@@ -12,8 +12,9 @@
 LOW = jnp.bfloat16
 F32 = jnp.float32
 STEP = 64
-LIMIT = 40 * 2**20
+LIMIT = 24 * 2**20
 SCALE = 4
+EARLY = 0.001
 ADV = 20 * 10**9
 
 
@@ -151,7 +152,7 @@
     def __init__(self):
         self.link = None
 
-    def run(self, kernel, outs, ins, scratch, flops):
+    def run(self, kernel, outs, ins, scratch, flops, placed=0):
         specs = [pl.BlockSpec(memory_space=pltpu.SMEM)] + [
             pl.BlockSpec(memory_space=pltpu.VMEM) for _ in ins[1:]
         ]
@@ -170,12 +171,15 @@
             call,
             out_shape=outs,
             in_specs=specs,
-            out_specs=[pl.BlockSpec(memory_space=pltpu.VMEM) for _ in outs],
+            out_specs=[
+                pl.BlockSpec(memory_space=pltpu.HBM if at < placed else pltpu.VMEM)
+                for at in range(len(outs))
+            ],
             scratch_shapes=scratch,
             compiler_params=pltpu.CompilerParams(vmem_limit_bytes=LIMIT),
             cost_estimate=pl.CostEstimate(flops=flops, bytes_accessed=moved + flops // 50, transcendentals=0),
         )(*ins)
-        self.link = results[-1]
+        self.link = min(results, key=lambda item: item.size)
         return results
 
 
@@ -194,8 +198,20 @@
     return jax.ShapeDtypeStruct(shape, kind)
 
 
-def pre_kernel(info, x_ref, vec, gated_w, conv_w, a1, values, gates, x1, a2, right_pre, right):
+def pre_kernel(
+    info, x_ref, gated_w, conv_w, norms, gated_b, conv_b, point_b, project_b, output_b, shrink_b,
+    a1, values, gates, x1, a2, right_pre, vec, right
+):
     width = x_ref.shape[1]
+    channels = right.shape[1]
+    vec[...] = jnp.zeros_like(vec)
+    for at in range(4):
+        vec[2 * at : 2 * at + 2] = norms[at].astype(F32)
+    for row, item in ((8, gated_b.at[0:width]), (9, gated_b.at[width:]), (13, output_b), (14, shrink_b)):
+        vec[row : row + 1] = item[...].astype(F32).reshape(1, width)
+    vec[10:11, 0:channels] = conv_b[...].astype(F32).reshape(1, channels)
+    vec[10:11, channels:] = point_b[...].astype(F32).reshape(1, channels)
+    vec[11:13] = project_b[...].astype(F32)
     for row in spans(SEQ, STEP):
         normed, _ = normalize(x_ref[row].astype(F32))
         a1[row] = as_low(normed * vec[0:1] + vec[1:2])
@@ -226,44 +242,56 @@
     return groups
 
 
-def assemble(target, blocks, code):
-    rows = blocks[0].shape[0]
-    for at, block in enumerate(blocks):
-        spot = jnp.bitwise_xor(code, at) if at else code
-        target[pl.ds(pl.multiple_of(spot * rows, 16), rows)] = block[...]
-
-
-def code_of(info, count):
-    return info[0] if count == 2 else info[0] * 2 + info[4]
-
-
-def code_z(info, count):
-    return info[0] if count == 2 else info[0] * 2 + info[5]
-
-
-def group_blocks(refs, pieces):
-    count = len(refs) // (pieces - 1)
-    return [refs[at : at + count] for at in range(0, len(refs), count)]
-
-
-def inner_forward_kernel(pieces, sizes, refs):
+def places(info, count):
+    core, y, near = info[0], info[4], info[5]
+    if count == 2:
+        return [core, 1 - core]
+    mine = (1 - core) * y + core * near
+    theirs = (1 - core) * near + core * y
+    return [2 * core + mine, 2 * core + 1 - mine, 2 - 2 * core + theirs, 3 - 2 * core - theirs]
+
+
+def assemble(info, target, blocks, offset):
+    rows = target.shape[0] // len(blocks)
+    for spot, block in zip(places(info, len(blocks)), blocks):
+        here = pl.ds(pl.multiple_of(spot * rows, 16), rows)
+        for part in range(target.shape[1] // 256):
+            at = offset + part * rows
+            target[here, part * 256 : (part + 1) * 256] = block[at : at + rows]
+
+
+def vectors_of(own, blocks, per_piece, offset):
+    found = [(own, 0)]
+    for at in range(0, len(blocks), per_piece):
+        found.append((blocks[at], offset))
+    return found
+
+
+def rows_of(vectors, index, lanes):
+    ref, offset = vectors
+    return ref[pl.ds(pl.multiple_of(offset + index * 16, 16), 16), lanes].astype(F32)
+
+
+def inner_forward_kernel(pieces, per, refs):
     info, refs = refs[0], refs[1:]
-    (a2, right, left), left_in, wide, outs, scratch = unpack(refs, [3, sizes[0], pieces, 5, 6])
+    (a2, right, left, own), packed, outs, scratch = unpack(refs, [4, per * (pieces - 1), 5, 6])
     normed_ref, slope_ref, depth, rstd_ref, left_rest = outs
     mixed, total, square, centre_ref, padded, padded_two = scratch
     local = left.shape[1]
     inner = local * pieces
     offset = info[1]
+    skipped = a2.shape[1] * local // (256 * per) + local // per
+    wide = vectors_of(own, packed, per, skipped)
     right_rows = right[...].astype(F32)
     total[...] = jnp.zeros_like(total)
     square[...] = jnp.zeros_like(square)
     for piece in range(pieces):
         if piece:
-            blocks = group_blocks(left_in, pieces)[piece - 1]
-            assemble(left_rest.at[piece - 1], blocks, code_of(info, len(blocks)))
+            assemble(info, left_rest.at[piece - 1], packed[(piece - 1) * per : piece * per], 0)
         for col in spans(local, 256):
             weights = left[:, col] if piece == 0 else left_rest[piece - 1, :, col]
-            pre = dot(a2[...], weights) + wide[piece][0:16, col].astype(F32)[0:1]
+            pre = dot(a2[...], weights)
+            pre = pre + rows_of(wide[piece], col.start // 256, slice(0, 256))[0:1]
             sigma = sigmoid(pre)
             at = piece * local + col.start
             here = slice(at, at + 256)
@@ -284,10 +312,9 @@
     kept = keep_rows(info, 0, SEQ)
     for piece in range(pieces):
 
-        def one(at, pad):
-            col = at_lane(at, 128)
-            here = at_lane(piece * local + at, 128)
-            vectors = wide[piece][:, col].astype(F32)
+        def one(index, part, pad):
+            here = at_lane(piece * local + index * 256 + part, 128)
+            vectors = rows_of(wide[piece], index, slice(part, part + 128))
             normed = (mixed[:, here] - centre_ref[...]) * rstd_ref[...]
             normed_ref[:, here] = as_low(normed)
             pad[8 : SEQ + 8] = (normed * vectors[2:3] + vectors[3:4]) * kept
@@ -297,8 +324,8 @@
             depth[:, here] = as_low(result)
 
         def step(index, carry):
-            one(index * 256, padded)
-            one(index * 256 + 128, padded_two)
+            one(index, 0, padded)
+            one(index, 128, padded_two)
             return carry
 
         lax.fori_loop(0, local // 256, step, 0)
@@ -308,17 +335,17 @@
     return jnp.where(valid, dot_right(queries, keys) * scale, NEGATIVE)
 
 
-def attention_forward_kernel(pieces, sizes, refs):
-    (info, x1, depth, point, vec, project_w, output_w), point_in, outs = unpack(
-        refs, [7, sizes[1], 8]
+def attention_forward_kernel(pieces, per, refs):
+    (info, x1, depth, point, vec, project_w, output_w), packed, outs = unpack(
+        refs, [7, per * (pieces - 1), 8]
     )
     x2, a4, qkv, lse, attended, x3, a5, point_rest = outs
     width = x2.shape[1]
     local, channels = point.shape
     sep = dot(depth[:, 0:local], point[...])
     for piece in range(1, pieces):
-        blocks = group_blocks(point_in, pieces)[piece - 1]
-        assemble(point_rest.at[piece - 1], blocks, code_of(info, len(blocks)))
+        blocks = packed[(piece - 1) * per : piece * per]
+        assemble(info, point_rest.at[piece - 1], blocks, width * local // (256 * per))
         sep = sep + dot(depth[:, piece * local : (piece + 1) * local], point_rest[piece - 1])
     x2[:, 0:channels] = x1[:, 0:channels] + sep + vec[10:11, channels : 2 * channels]
     x2[:, channels:width] = x1[:, channels:width]
@@ -358,49 +385,33 @@
         a5[row] = as_low(normed * vec[6:7] + vec[7:8])
 
 
-def feed_kernel(pieces, sizes, refs):
+def feed_kernel(pieces, per, refs):
     info, refs = refs[0], refs[1:]
-    (a5, top, expand), expand_in, wide, outs = unpack(refs, [3, sizes[2], pieces, 5])
-    hidden, slope, keep, send, expand_rest = outs
+    (a5, x3, top, vec, expand, shrink, own), first, packed, outs, scratch = unpack(
+        refs, [7, per * (pieces - 1), per * (pieces - 1), 6, 7]
+    )
+    output, keep, send, dx3, fixed, grad_bias = outs
+    hidden, slope, d_expand, shrunk, d_a5, expand_rest, shrink_rest = scratch
     local = expand.shape[1]
-    core, rows = info[0], local // 2
+    width = x3.shape[1]
+    half, rows = width // 2, local // 2
+    core = info[0]
+    wide = vectors_of(own, first, per, width * local // (256 * per) + local // per)
     for piece in range(pieces):
         if piece:
-            blocks = group_blocks(expand_in, pieces)[piece - 1]
-            assemble(expand_rest.at[piece - 1], blocks, code_of(info, len(blocks)))
+            blocks = packed[(piece - 1) * per : piece * per]
+            assemble(info, expand_rest.at[piece - 1], blocks, 0)
+            assemble(info, shrink_rest.at[piece - 1], blocks, width * local // (256 * per))
         for col in spans(local, 256):
             weights = expand[:, col] if piece == 0 else expand_rest[piece - 1, :, col]
-            pre = dot(a5[...], weights) + wide[piece][0:16, col].astype(F32)[1:2]
+            pre = dot(a5[...], weights)
+            pre = pre + rows_of(wide[piece], col.start // 256, slice(0, 256))[1:2]
             sigma = sigmoid(pre)
             here = slice(piece * local + col.start, piece * local + col.stop)
             hidden[:, here] = as_low(pre * sigma)
-            slope[:, here] = as_low(sigma * (1.0 + pre * (1.0 - sigma)))
-    for piece in range(pieces):
-        for side, out in ((1 - core, send), (core, keep)):
-            put(
-                out,
-                2 * piece,
-                2,
-                0,
-                dot_left(hidden[:, at_lane(piece * local + side * rows, rows)], top[...]),
-            )
-
-
-def feed_back_kernel(pieces, sizes, refs):
-    info, refs = refs[0], refs[1:]
-    (a5, x3, top, vec, hidden, slope, expand, expand_rest, shrink), shrink_in, outs, scratch = unpack(
-        refs, [9, sizes[3], 6, 4]
-    )
-    output, keep, send, dx3, fixed, grad_bias = outs
-    d_expand, shrunk, d_a5, shrink_rest = scratch
-    local = expand.shape[1]
-    half = x3.shape[1] // 2
-    core = info[0]
+            slope[:, here] = sigma * (1.0 + pre * (1.0 - sigma))
     for piece in range(pieces):
         base = piece * local
-        if piece:
-            blocks = group_blocks(shrink_in, pieces)[piece - 1]
-            assemble(shrink_rest.at[piece - 1], blocks, code_z(info, len(blocks)))
         weights = shrink if piece == 0 else shrink_rest.at[piece - 1]
         part = dot(hidden[:, base : base + local], weights[...])
         if piece == 0:
@@ -409,22 +420,22 @@
             shrunk[...] += part
         for row in spans(local, 256):
             here = slice(base + row.start, base + row.stop)
-            d_expand[:, here] = as_low(
-                dot_right(top[...], weights[row]) * slope[:, here].astype(F32)
-            )
+            d_expand[:, here] = as_low(dot_right(top[...], weights[row]) * slope[:, here])
     for row in spans(SEQ, STEP):
         output[row] = as_low(x3[row] + shrunk[row] + vec[14:15])
     for piece in range(pieces):
-        cols = slice(piece * local, (piece + 1) * local)
+        base = piece * local
+        cols = slice(base, base + local)
         for side, out in ((1 - core, send), (core, keep)):
+            grad = dot_left(hidden[:, at_lane(base + side * rows, rows)], top[...])
+            put(out, 2 * piece, 2, 0, grad)
             grad = dot_left(a5[:, at_lane(side * half, half)], d_expand[:, cols])
-            put(out, 2 * piece, 2, 0, grad)
+            put(out, 2 * piece, 2, width * local // 1024, grad)
         grad_bias[:, cols] = jnp.broadcast_to(low_columns_sum(d_expand[:, cols]), (8, local))
-        weights = expand[...] if piece == 0 else expand_rest[piece - 1]
         if piece == 0:
-            d_a5[...] = dot_right(d_expand[:, cols], weights)
+            d_a5[...] = dot_right(d_expand[:, cols], expand[...])
         else:
-            d_a5[...] += dot_right(d_expand[:, cols], weights)
+            d_a5[...] += dot_right(d_expand[:, cols], expand_rest[piece - 1])
     fixed[...] = jnp.zeros_like(fixed)
     for row in spans(SEQ, STEP):
         normed, rstd = normalize(x3[row])
@@ -487,14 +498,15 @@
     fixed[14:15, channels : 2 * channels] = low_columns_sum(d_sep[...])
 
 
-def inner_backward_kernel(pieces, refs):
+def inner_backward_kernel(pieces, per, refs):
     info, refs = refs[0], refs[1:]
     (
-        (d_sep, depth, normed_ref, slope_ref, rstd_ref, a2, bias_before, point, point_rest, left, left_rest),
-        wide,
+        (d_sep, depth, normed_ref, slope_ref, rstd_ref, a2, bias_before, point, point_rest),
+        (left, left_rest, own),
+        packed,
         outs,
         scratch,
-    ) = unpack(refs, [11, pieces, 5, 6])
+    ) = unpack(refs, [9, 3, per * (pieces - 1), 5, 6])
     keep, send, d_a2, d_right, grads = outs
     d_depth, padded, padded_two, d_left, first_ref, second_ref = scratch
     local = left.shape[1]
@@ -502,6 +514,7 @@
     core, offset = info[0], info[1]
     rows = local // 2
     half = a2.shape[1] // 2
+    wide = vectors_of(own, packed, per, a2.shape[1] * local // (256 * per) + local // per)
     for piece in range(pieces):
         weights = point if piece == 0 else point_rest.at[piece - 1]
         for row in spans(local, 256):
@@ -519,11 +532,10 @@
     kept = keep_rows(info, 0, SEQ)
     for piece in range(pieces):
 
-        def one(at, pad):
-            col = at_lane(at, 128)
-            here = at_lane(piece * local + at, 128)
-            index = (piece * local + at) // 128
-            vectors = wide[piece][:, col].astype(F32)
+        def one(pair, part, pad):
+            here = at_lane(piece * local + pair * 256 + part, 128)
+            index = piece * (local // 128) + 2 * pair + part // 128
+            vectors = rows_of(wide[piece], pair, slice(part, part + 128))
             d_depth[index, 0:8] = jnp.zeros((8, 128), F32)
             d_depth[index, SEQ + 8 : SEQ + 16] = jnp.zeros((8, 128), F32)
             normed = normed_ref[:, here].astype(F32)
@@ -543,8 +555,8 @@
             d_depth[index, 8 : SEQ + 8] = scaled
 
         def step(index, carry):
-            one(index * 256, padded)
-            one(index * 256 + 128, padded_two)
+            one(index, 0, padded)
+            one(index, 128, padded_two)
             return carry
 
         lax.fori_loop(0, local // 256, step, 0)
@@ -657,33 +669,75 @@
         put(out, 0, 4, offset, rows_ref[pl.ds(pl.multiple_of(side * count, 16), count)])
 
 
-def cut_kernel(parts, counts, refs):
-    info, ins, outs, sems = refs[0], refs[1 : parts + 1], refs[parts + 1 : -1], refs[-1]
-    copies = []
-    for at, (source, target) in enumerate(zip(ins, outs)):
-        rows = target.shape[0]
-        code = (info[0], code_of(info, 4), code_z(info, 4))[counts[at]]
-        here = pl.ds(pl.multiple_of(code * rows, 16), rows)
-        copies.append(pltpu.make_async_copy(source.at[here], target, sems.at[at]))
-    for copy in copies:
-        copy.start()
-    for copy in copies:
-        copy.wait()
-
-
-def cut(info, arrays, counts):
-    outs = [
-        shaped((item.shape[0] // (2 if kind == 0 else 4), item.shape[1]), item.dtype)
-        for item, kind in zip(arrays, counts)
-    ]
+def own_place(count):
+    core = lax.axis_index("dp") % 2
+    if count == 2:
+        return core
+    y = lax.axis_index("dp") // 2 % 2
+    near = lax.axis_index("dp") // 4 % 2
+    return 2 * core + (1 - core) * y + core * near
+
+
+def cut(weights, vectors, per, link):
+    shapes = [(item.shape[0] // per, item.shape[1]) for item in weights]
+    total = sum(rows * columns // 256 for rows, columns in shapes)
+    local = weights[0].shape[1]
+    small = local // 16 if vectors else 0
+    chained = [] if link is None else [link]
+
+    def kernel(*refs):
+        refs = list(refs)
+        sources = [refs.pop(0) for _ in weights]
+        small_in = [refs.pop(0) for _ in vectors]
+        for _ in chained:
+            refs.pop(0)
+        packed = refs.pop(0)
+        own = refs.pop(0) if vectors else None
+        blocks = [refs.pop(0) for _ in weights]
+        sems = refs.pop(0)
+        held = refs.pop(0)
+        held[...] = jnp.zeros_like(held)
+        place = own_place(per)
+        copies = []
+        for at, (source, block) in enumerate(zip(sources, blocks)):
+            rows = block.shape[0]
+            here = pl.ds(pl.multiple_of(place * rows, 16), rows)
+            copies.append(pltpu.make_async_copy(source.at[here], block, sems.at[at]))
+        for copy in copies:
+            copy.start()
+        if vectors:
+            for part in range(local // 256):
+                lanes = slice(part * 256, (part + 1) * 256)
+                row = 0
+                for item in small_in:
+                    count = item.shape[0] if len(item.shape) == 2 else 1
+                    held[row : row + count] = item[..., lanes].astype(F32).reshape(count, 256)
+                    row += count
+                chunk = as_low(held[...])
+                own[part * 16 : (part + 1) * 16] = chunk
+                packed[total + part * 16 : total + (part + 1) * 16] = chunk
+        for copy in copies:
+            copy.wait()
+        offset = 0
+        for block in blocks:
+            rows, columns = block.shape
+            for part in range(columns // 256):
+                packed[offset : offset + rows] = block[:, part * 256 : (part + 1) * 256]
+                offset += rows
+
+    outs = [shaped((total + small, 256), LOW)]
+    if vectors:
+        outs.append(shaped((small, 256), LOW))
     return pl.pallas_call(
-        lambda *refs: cut_kernel(len(arrays), counts, refs),
+        kernel,
         out_shape=outs,
-        in_specs=[pl.BlockSpec(memory_space=pltpu.SMEM)]
-        + [pl.BlockSpec(memory_space=pl.ANY) for _ in arrays],
-        out_specs=[pl.BlockSpec(memory_space=pltpu.VMEM) for _ in arrays],
-        scratch_shapes=[pltpu.SemaphoreType.DMA((len(arrays),))],
-    )(info, *arrays)
+        in_specs=[pl.BlockSpec(memory_space=pl.ANY) for _ in weights]
+        + [pl.BlockSpec(memory_space=pltpu.VMEM) for _ in vectors]
+        + [pl.BlockSpec(memory_space=pl.ANY) for _ in chained],
+        out_specs=[pl.BlockSpec(memory_space=pltpu.VMEM) for _ in outs],
+        scratch_shapes=[pltpu.VMEM(shape, LOW) for shape in shapes]
+        + [pltpu.SemaphoreType.DMA((len(weights),)), pltpu.VMEM((16, 256), F32)],
+    )(*weights, *vectors, *chained)
 
 
 def flat_swap(values, partner):
@@ -699,6 +753,7 @@
     "y": lambda at: at ^ 4,
     "near": lambda at: at ^ 8,
     "far": lambda at: at ^ 16,
+    "hop": lambda at: at ^ (8 if at & 2 else 4),
 }
 INNER_STEPS = [
     ("quarter", "first"),
@@ -723,7 +778,40 @@
 ]
 
 
-PLAN = "ab d c ab d c ab cd b a cd ep a c d p e c d p c d d d".split()
+PLAN = (
+    "p",
+    "a",
+    "d",
+    "p",
+    "a",
+    "d",
+    "p",
+    "c",
+    "d",
+    "p",
+    "a",
+    "c",
+    "d",
+    "a",
+    "c",
+    "d",
+    "p",
+    "c",
+    "d",
+    "p",
+    "d",
+    "c",
+    "p",
+    "a",
+    "d",
+    "c",
+    "!d",
+    "p",
+    "!a",
+    "!p",
+    "c",
+    "!c",
+)
 
 
 class Stream:
@@ -779,21 +867,85 @@
             for at in range(2):
                 out[core * (2 * at + y) + (1 - core) * (2 * x + at)] = mine[at]
                 out[core * (2 * at + 1 - y) + (1 - core) * (2 * (1 - x) + at)] = flight[at]
-        else:
-            for offset, rows, shape in parts:
-                out = outs.pop(0)
-                columns = shape[-1] // 256
-                for source, side in ((mine, core), (flight, 1 - core)):
-                    for quarter in range(mine.shape[0]):
-                        spot = (side * mine.shape[0] + quarter) * rows
-                        here = pl.ds(pl.multiple_of(spot, 16), rows)
-                        for part in range(columns * (shape[0] if len(shape) == 3 else 1)):
-                            at = offset + part * rows
-                            block = source[quarter, at : at + rows].astype(F32)
-                            if len(shape) == 3:
-                                out[part, here] = block
-                            else:
-                                out[here, part * 256 : (part + 1) * 256] = block
+
+
+def finish_kernel(parts, small, refs):
+    info, mine, flight, refs = refs[0], refs[1], refs[2], list(refs[3:])
+    core = info[0]
+    outs = [refs.pop(0) for _ in parts]
+    smalls = [refs.pop(0) for _ in range(11)] if small else []
+    link = refs.pop(0)
+    link[...] = jnp.zeros_like(link)
+    held = [refs.pop(0) for _ in parts]
+    sems = refs.pop(0)
+    copies = []
+    for at, (offset, rows, shape) in enumerate(parts):
+        target = held[at]
+        for source, side in ((mine, core), (flight, 1 - core)):
+            for quarter in range(mine.shape[0]):
+                spot = (side * mine.shape[0] + quarter) * rows
+                here = pl.ds(pl.multiple_of(spot, 16), rows)
+                for part in range(shape[-1] // 256 * (shape[0] if len(shape) == 3 else 1)):
+                    row = offset + part * rows
+                    block = source[quarter, row : row + rows].astype(F32)
+                    if len(shape) == 3:
+                        target[part, here] = block
+                    else:
+                        target[here, part * 256 : (part + 1) * 256] = block
+        copies.append(pltpu.make_async_copy(target, outs[at], sems.at[at]))
+        copies[-1].start()
+    if small:
+        total = refs.pop(0)
+        offset, rows = small
+        for source, side in ((mine, core), (flight, 1 - core)):
+            for quarter in range(mine.shape[0]):
+                spot = (side * mine.shape[0] + quarter) * rows
+                total[pl.ds(pl.multiple_of(spot, 16), rows)] = source[
+                    quarter, offset : offset + rows
+                ].astype(F32)
+        norm, gated, left, conv, inner, depth, point, project, output, expand, shrink = smalls
+        local, width = left.shape[-1], output.shape[-1]
+        for part in range(local // 256):
+            lanes = slice(part * 256, (part + 1) * 256)
+            spot = (info[1] // local * (local // 256) + part) * 16
+            block = total[pl.ds(pl.multiple_of(spot, 16), 16)]
+            left[:, lanes] = block[0:1]
+            expand[:, lanes] = block[1:2]
+            inner[:, lanes] = block[2:4]
+            depth[:, lanes] = block[4:13]
+        for part in range(width // 256):
+            lanes = slice(part * 256, (part + 1) * 256)
+            base = local * 2 // 16 + part * 16
+            block = total[base : base + 16]
+            for at in range(4):
+                norm[at, :, lanes] = block[2 * at : 2 * at + 2]
+            gated[:, lanes] = block[8:9]
+            gated[:, width + part * 256 : width + (part + 1) * 256] = block[9:10]
+            project[:, lanes] = block[10:12]
+            output[:, lanes] = block[12:13]
+            shrink[:, lanes] = block[13:14]
+            (conv if part == 0 else point)[...] = block[14:15]
+    for copy in copies:
+        copy.wait()
+
+
+def finish(chain, info, stream, small):
+    parts = stream.parts
+    shapes = [shaped(shape, F32) for _, _, shape in parts]
+    scratch = [pltpu.VMEM(shape, F32) for _, _, shape in parts]
+    scratch.append(pltpu.SemaphoreType.DMA((len(parts),)))
+    names = []
+    if small:
+        scratch.append(pltpu.VMEM((256, 256), F32))
+        names = [shaped(shape, F32) for shape in small[1]]
+    stream.mine = chain.run(
+        lambda *refs: finish_kernel(parts, small[0] if small else None, refs),
+        shapes + names + [shaped((8, 128), F32)],
+        [info, stream.mine, stream.flight],
+        scratch,
+        ADV,
+        len(parts),
+    )
 
 
 def advance(chain, info, streams):
@@ -811,16 +963,11 @@
             outs.append(shaped((lead, rows, columns), LOW))
         elif step == "join_near":
             outs.append(shaped((lead, rows * 2, columns), LOW))
-        elif step == "final":
-            outs += [shaped(shape, F32) for _, _, shape in stream.parts]
         else:
             outs.append(shaped((lead * 2, rows, columns), LOW))
     results = list(chain.run(lambda *refs: advance_kernel(jobs, refs), outs, ins, [], ADV))
     for stream in streams:
         step, partner = stream.steps.pop(0)
-        if step == "final":
-            stream.mine = [results.pop(0) for _ in stream.parts]
-            continue
         stream.mine = results.pop(0)
         if step in ("quarter", "half_mix", "half_near"):
             stream.flight = flat_swap(results.pop(0), PARTNERS[partner])
@@ -836,30 +983,19 @@
     return jnp.concatenate(parts, 2).reshape(count * rows, columns)
 
 
-def small_kernel(info, total, wide, fixed):
-    local = wide.shape[1]
-    parts = local // 256
-    for part in range(parts):
-        spot = pl.multiple_of((info[1] // local * parts + part) * 16, 16)
-        wide[:, part * 256 : (part + 1) * 256] = total[pl.ds(spot, 16)]
-    base = local * 2 // 16
-    for part in range(fixed.shape[1] // 256):
-        fixed[:, part * 256 : (part + 1) * 256] = total[base + part * 16 : base + (part + 1) * 16]
-
-
 class Weights:
-    def __init__(self, piece, kind):
-        pieces = [piece]
+    def __init__(self, packed, per):
+        pieces = [packed]
         for bit in bits_of("mp"):
             pieces = pieces + [swap(item, "mp", bit) for item in pieces]
         self.blocks = [[item] for item in pieces[1:]]
-        self.kind = kind
+        self.per = per
 
     def hop(self, after):
-        for blocks in self.blocks:
-            item, _ = lax.optimization_barrier((blocks[0], after))
-            blocks[0] = item
-            blocks.append(swap(item, "dp", (2, 4)[self.kind - 1]))
+        if self.per == 4:
+            for blocks in self.blocks:
+                blocks[0], _ = lax.optimization_barrier((blocks[0], after))
+                blocks.append(flat_swap(blocks[0], PARTNERS["hop"]))
 
     def share(self, after):
         found = []
@@ -867,13 +1003,6 @@
             held = [lax.optimization_barrier((item, after))[0] for item in blocks]
             found += held + [swap(item, "dp", 1) for item in held]
         return found
-
-
-def gather_small(own_piece):
-    items = [own_piece]
-    for bit in bits_of("mp"):
-        items = items + [swap(item, "mp", bit) for item in items]
-    return items
 
 
 def finish_shared(mine, other, order):
@@ -965,38 +1094,14 @@
         return (2 * pieces, size // 1024, 256)
 
 
-    kinds = (0, 1, 1, 2)
-    owned = (left_weight, point_weight, expand_weight, shrink_weight)
-    cuts = cut(info, owned, kinds)
-    chain.link = cuts[-1]
-    left, point, expand, shrink = [Weights(part, kind) for part, kind in zip(cuts, kinds)]
-    wide = gather_small(
-        jnp.concatenate(
-            [
-                left_bias[None],
-                expand_bias[None],
-                inner_norm,
-                depth_weight,
-                jnp.zeros((3, local), LOW),
-            ],
-            0,
-        )
-    )
-    sizes = [(pieces - 1) * (2 if kind == 0 else 4) for kind in kinds]
-    vec = jnp.concatenate(
-        [
-            norm_params.reshape(8, width),
-            gated_bias.reshape(2, width),
-            jnp.concatenate([conv_bias, point_bias]).reshape(1, width),
-            project_bias,
-            output_bias[None],
-            shrink_bias[None],
-            jnp.zeros((1, width), LOW),
-        ],
-        0,
-    ).astype(F32)
-
-    a1, values, gates, x1, a2, right_pre, right = chain.run(
+    per = 4 if tuned else 2
+    vectors = [left_bias, expand_bias, inner_norm, depth_weight]
+    packed, own = cut([left_weight, point_weight], vectors, per, None)
+    early = Weights(packed, per)
+    (packed,) = cut([expand_weight, shrink_weight], [], per, own)
+    late = Weights(packed, per)
+    chain.link = packed
+    a1, values, gates, x1, a2, right_pre, vec, right = chain.run(
         pre_kernel,
         [
             shaped((tokens, width), LOW),
@@ -1005,16 +1110,29 @@
             shaped((tokens, width), F32),
             shaped((tokens, width), LOW),
             shaped((tokens, channels), F32),
+            shaped((16, width), F32),
             shaped((tokens, channels), LOW),
         ],
-        [info, cell_input, vec, gated_weight, conv_weight],
+        [
+            info,
+            cell_input,
+            gated_weight,
+            conv_weight,
+            norm_params,
+            gated_bias,
+            conv_bias,
+            point_bias,
+            project_bias,
+            output_bias,
+            shrink_bias,
+        ],
         [],
-        int(2.2e9 * SCALE),
-    )
-    left_blocks = left.share(right)
-    point.hop(right)
+        int(2.2e9 * EARLY),
+    )
+    early.hop(right)
+    early_blocks = early.share(right)
     normed, slope, depth, rstd, left_rest = chain.run(
-        lambda *refs: inner_forward_kernel(pieces, sizes, refs),
+        lambda *refs: inner_forward_kernel(pieces, per, refs),
         [
             shaped((tokens, inner), LOW),
             shaped((tokens, inner), LOW),
@@ -1022,7 +1140,7 @@
             shaped((tokens, 128), F32),
             shaped((pieces - 1, width, local), LOW),
         ],
-        [info, a2, right, left_weight] + left_blocks + wide,
+        [info, a2, right, left_weight, own] + early_blocks,
         [
             pltpu.VMEM((tokens, inner), F32),
             pltpu.VMEM((tokens, 128), F32),
@@ -1031,12 +1149,11 @@
             pltpu.VMEM((tokens + 16, 128), F32),
             pltpu.VMEM((tokens + 16, 128), F32),
         ],
-        int(6.5e9 * SCALE),
-    )
-    point_blocks = point.share(rstd)
-    expand.hop(rstd)
+        int(6.5e9 * EARLY),
+    )
+    late.hop(rstd)
     x2, a4, qkv, lse, attended, x3, a5, point_rest = chain.run(
-        lambda *refs: attention_forward_kernel(pieces, sizes, refs),
+        lambda *refs: attention_forward_kernel(pieces, per, refs),
         [
             shaped((tokens, width), F32),
             shaped((tokens, width), LOW),
@@ -1047,51 +1164,46 @@
             shaped((tokens, width), LOW),
             shaped((pieces - 1, local, channels), LOW),
         ],
-        [info, x1, depth, point_weight, vec, project_weight, output_weight] + point_blocks,
+        [info, x1, depth, point_weight, vec, project_weight, output_weight]
+        + early_blocks,
         [],
-        int(4.4e9 * SCALE),
-    )
-    expand_blocks = expand.share(a5)
-    shrink.hop(a5)
-    hidden, feed_slope, shrink_keep, shrink_send, expand_rest = chain.run(
-        lambda *refs: feed_kernel(pieces, sizes, refs),
-        [
-            shaped((tokens, inner), LOW),
-            shaped((tokens, inner), LOW),
-            shaped(inner_rows(local * width), LOW),
-            shaped(inner_rows(local * width), LOW),
-            shaped((pieces - 1, width, local), LOW),
-        ],
-        [info, a5, out_grad, expand_weight] + expand_blocks + wide,
-        [],
-        int(3.4e9 * SCALE),
-    )
-    if tuned:
-        shr = Stream(True, shrink_keep, shrink_send, [(0, local // 4, (local, width))])
-    shrink_blocks = shrink.share(hidden)
-    cell_output, expand_keep, expand_send, dx3, fixed, expand_sum = chain.run(
-        lambda *refs: feed_back_kernel(pieces, sizes, refs),
+        int(4.4e9 * EARLY),
+    )
+    late_blocks = late.share(a5)
+    cell_output, feed_keep, feed_send, dx3, fixed, expand_sum = chain.run(
+        lambda *refs: feed_kernel(pieces, per, refs),
         [
             shaped((tokens, width), LOW),
-            shaped(inner_rows(local * width), LOW),
-            shaped(inner_rows(local * width), LOW),
+            shaped(inner_rows(2 * local * width), LOW),
+            shaped(inner_rows(2 * local * width), LOW),
             shaped((tokens, width), F32),
             shaped((16, width), F32),
             shaped((8, inner), F32),
         ],
-        [info, a5, x3, out_grad, vec, hidden, feed_slope, expand_weight, expand_rest, shrink_weight]
-        + shrink_blocks,
-        [
+        [info, a5, x3, out_grad, vec, expand_weight, shrink_weight, own]
+        + early_blocks
+        + late_blocks,
+        [
+            pltpu.VMEM((tokens, inner), LOW),
+            pltpu.VMEM((tokens, inner), F32),
             pltpu.VMEM((tokens, inner), LOW),
             pltpu.VMEM((tokens, width), F32),
             pltpu.VMEM((tokens, width), F32),
+            pltpu.VMEM((pieces - 1, width, local), LOW),
             pltpu.VMEM((pieces - 1, local, width), LOW),
         ],
-        int(4.6e9 * SCALE),
+        int(8e9 * SCALE),
     )
     if tuned:
-        exp = Stream(True, expand_keep, expand_send, [(0, width // 4, (width, local))])
-        advance(chain, info, [shr])
+        fee = Stream(
+            True,
+            feed_keep,
+            feed_send,
+            [
+                (0, local // 4, (local, width)),
+                (width * local // 1024, width // 4, (width, local)),
+            ],
+        )
     proj_send, proj_keep, dx2, d_sep, fixed = chain.run(
         attention_backward_kernel,
         [
@@ -1119,10 +1231,9 @@
                 (3 * width * width // 2048, width // 8, (width, width)),
             ],
         )
-        advance(chain, info, [exp, shr])
-        advance(chain, info, [pro])
+        advance(chain, info, [fee])
     left_keep, left_send, d_a2, d_right, wide_sums = chain.run(
-        lambda *refs: inner_backward_kernel(pieces, refs),
+        lambda *refs: inner_backward_kernel(pieces, per, refs),
         [
             shaped(inner_rows(local * (width + channels)), LOW),
             shaped(inner_rows(local * (width + channels)), LOW),
@@ -1143,8 +1254,9 @@
             point_rest,
             left_weight,
             left_rest,
+            own,
         ]
-        + wide,
+        + early_blocks,
         [
             pltpu.VMEM((inner // 128, tokens + 16, 128), F32),
             pltpu.VMEM((tokens + 16, 128), F32),
@@ -1165,7 +1277,7 @@
                 (width * local // 1024, local // 4, (local, channels)),
             ],
         )
-        advance(chain, info, [shr, exp, pro])
+        advance(chain, info, [fee])
     small = 32 if tuned else 0
     last_rows = width * (2 * width + 3 * channels) // 2048 + small
     last_send, last_keep, input_grad, fixed = chain.run(
@@ -1210,22 +1322,34 @@
             [
                 (0, width // 8, (width, 2 * width)),
                 (width * width // 1024, width // 8, (3, width, channels)),
-                (last_rows - small, small, (8 * small, 256)),
             ],
         )
-        advance(chain, info, [lef])
-        groups = {"a": [shr], "b": [exp, pro], "e": [exp], "p": [pro], "c": [lef], "d": [lat]}
+        groups = {"a": [fee], "p": [pro], "c": [lef], "d": [lat]}
+        small_shapes = [
+            (4, 2, width),
+            (1, 2 * width),
+            (1, local),
+            (1, channels),
+            (2, local),
+            (9, local),
+            (1, channels),
+            (2, width),
+            (1, width),
+            (1, local),
+            (1, width),
+        ]
+        small_part = ((last_rows - small, small), small_shapes)
         for names in PLAN:
-            advance(chain, info, [item for name in names for item in groups[name]])
-        wide_total, fixed = chain.run(
-            small_kernel,
-            [shaped((16, local), F32), shaped((16, width), F32)],
-            [info, lat.mine[2]],
-            [],
-            10**6,
-        )
-        (grad_shrink,), (grad_expand,), (grad_left, grad_point) = shr.mine, exp.mine, lef.mine
-        (grad_proj, grad_out), (grad_gated, grad_conv, _) = pro.mine, lat.mine
+            if names[0] == "!":
+                stream = groups[names[1]][0]
+                finish(chain, info, stream, small_part if names == "!d" else None)
+            else:
+                advance(chain, info, [groups[name][0] for name in names])
+        (grad_shrink, grad_expand, _), (grad_left, grad_point, _) = fee.mine, lef.mine
+        (grad_proj, grad_out, _), (grad_gated, grad_conv) = pro.mine, lat.mine[:2]
+        smalls = [
+            item.reshape(-1) if item.shape[0] == 1 else item for item in lat.mine[2:-1]
+        ]
     else:
 
         def whole(keep, send, offset, rows, columns):
@@ -1240,8 +1364,10 @@
             return finish_shared(both[0], both[1], mp_first)
 
         eighth = width // 8
-        grad_shrink = whole(shrink_keep, shrink_send, 0, local // 4, width)
-        grad_expand = whole(expand_keep, expand_send, 0, width // 4, local)
+        grad_shrink = whole(feed_keep, feed_send, 0, local // 4, width)
+        grad_expand = whole(
+            feed_keep, feed_send, width * local // 1024, width // 4, local
+        )
         grad_left = whole(left_keep, left_send, 0, width // 4, local)
         grad_point = whole(left_keep, left_send, width * local // 1024, local // 4, channels)
         grad_proj = shared(proj_keep, proj_send, 0, eighth, 3 * width)
@@ -1260,28 +1386,41 @@
         for bit in bits_of("dp"):
             fixed = fixed + swap(fixed, "dp", bit)
             wide_total = wide_total + swap(wide_total, "dp", bit)
+        smalls = [
+            fixed[0:8].reshape(4, 2, width),
+            fixed[8:10].reshape(2 * width),
+            wide_total[0],
+            fixed[14, :channels],
+            wide_total[2:4],
+            wide_total[4:13],
+            fixed[14, channels:],
+            fixed[10:12],
+            fixed[12],
+            wide_total[1],
+            fixed[13],
+        ]
     return (
         cell_output,
         input_grad,
-        fixed[0:8].reshape(4, 2, width),
+        smalls[0],
         grad_gated,
-        fixed[8:10].reshape(2 * width),
+        smalls[1],
         grad_left,
-        wide_total[0],
+        smalls[2],
         grad_conv,
-        fixed[14, :channels],
-        wide_total[2:4],
-        wide_total[4:13],
+        smalls[3],
+        smalls[4],
+        smalls[5],
         grad_point,
-        fixed[14, channels:],
+        smalls[6],
         grad_proj,
-        fixed[10:12],
+        smalls[7],
         grad_out,
-        fixed[12],
+        smalls[8],
         grad_expand,
-        wide_total[1],
+        smalls[9],
         grad_shrink,
-        fixed[13],
+        smalls[10],
     )
 
 

time: 201 us -> 181 us (0.900)
  local copies, waits for them, and re-layouts: 22.1 us -> 2.84 us
  waiting for transfers between devices: 57.9 us -> 50 us
  Pallas kernels: 68.7 us -> 73.9 us
    unnamed x107 -> x42, local copies, waits for them, and re-layouts: 17 us -> 2.75 us
    ppermute x42 -> x36, starting transfers between devices: 36.5 us -> 47.2 us  [flat_swap(): lax.ppermute(values, ('dp', 'mp'), [(at, partner(at)) for at in range(cou...]
    ppermute x15 -> x6, starting transfers between devices: 13.3 us -> 4.57 us  [swap(): return lax.ppermute(values, axis, [(at, at ^ bit) for at in range(count)])]
    ppermute x15 -> x6, waiting for transfers between devices: 13.8 us -> 6.95 us  [swap(): return lax.ppermute(values, axis, [(at, at ^ bit) for at in range(count)])]
    slice x7 -> x0, local copies, waits for them, and re-layouts: 3.59 us -> none  [the longest x1 0.64 us: body(): wide_total[4:13]]
    pallas_call x38 -> x41, Pallas kernels: 65.6 us -> 69.2 us  [run(): pl.pallas_call(call, out_shape=outs, in_specs=specs, out_specs=[pl.BlockS...]
    pallas_call x1 -> x2, Pallas kernels: 3.06 us -> 4.68 us  [cut(): pl.pallas_call(kernel, out_shape=outs, in_specs=[pl.BlockSpec(memory_spac...]
    ppermute x42 -> x36, waiting for transfers between devices: 44.1 us -> 43 us  [flat_swap(): lax.ppermute(values, ('dp', 'mp'), [(at, partner(at)) for at in range(cou...]
  transfers between devices with their start and end apart: 57 -> 42, of which waited for: 22 -> 17; matrix products, arithmetic and copies ran while one was open for 0% -> 0% of each run, Pallas kernels for 30% -> 34%
where the time goes in v4:
time: 181 us
  Pallas kernels  73.9 us (41%)
  starting transfers between devices  51.8 us (29%)
  waiting for transfers between devices  50 us (28%)
  local copies, waits for them, and re-layouts  2.84 us (2%)
  between operations  2.12 us (1%)
    pallas_call x41, Pallas kernels, run(): pl.pallas_call(call, out_shape=outs, in_specs=specs, out_specs=[pl.BlockS...  69.2 us
    ppermute x36, starting transfers between devices, flat_swap(): lax.ppermute(values, ('dp', 'mp'), [(at, partner(at)) for at in range(cou...  47.2 us
    ppermute x36, waiting for transfers between devices, flat_swap(): lax.ppermute(values, ('dp', 'mp'), [(at, partner(at)) for at in range(cou...  43 us
    ppermute x6, waiting for transfers between devices, swap(): return lax.ppermute(values, axis, [(at, at ^ bit) for at in range(count)])  6.95 us
    pallas_call x2, Pallas kernels, cut(): pl.pallas_call(kernel, out_shape=outs, in_specs=[pl.BlockSpec(memory_spac...  4.68 us
    ppermute x6, starting transfers between devices, swap(): return lax.ppermute(values, axis, [(at, at ^ bit) for at in range(count)])  4.57 us
  transfers between devices with their start and end apart: 42, of which 17 were waited for; matrix products, arithmetic and copies ran while one was open for 0% of the time, Pallas kernels for 34%

profile of v4, /device:TPU:0, one launch (start us, length us, event | category | flops | bytes accessed | tf_op | source)
XLA Modules:
  0.0 180.6 jit_solution(12010529511189257920)
XLA Ops:
  0.8 2.7 %shard_map.373 = (bf16[832,256]{1,0:T(8,128)(2,1)}, bf16[64,256]{1,0:T(8,128)(2,1)}) custom-call(bf16[512,1024]{1,0:T(8,128)(2,1)} %refs_10_.3, bf16[1024,256]{1,0:T(8,128)(2,1)} %refs_8_.3, bf16[1024]{0:T(1024)(128)(2,1)} %refs_2_.2, bf16[1024]{0:T(1024)(128)(2,1)} %refs_3_.6, bf16[2,1024]{1,0:T(2,128)(2,1)} %refs_4_.3, bf16[9,1024]{1,0:T(8,128)(2,1)} %refs_5_.4), custom_call_target="tpu_custom_call" | custom-call | tf_op jit(solution)/shard_map/pallas_call | solution.py:731
  3.5 3.0 %collective-permute-start = (bf16[832,256]{1,0:T(8,128)(2,1)}, bf16[832,256]{1,0:T(8,128)(2,1)S(1)}, u32[]{:S(2)}, u32[]{:S(2)}) collective-permute-start(bf16[832,256]{1,0:T(8,128)(2,1)} %get-tuple-element.119), channel_id=1, source_target_pairs={{0,1},{1,0},{2,3},{3,2},{4,5},{5,4},{6,7},{7,6},{8,9},{9,8},{10,11... | collective-permute-start | bytes 1277960 | tf_op jit(solution)/shard_map/ppermute | solution.py:39
  7.2 2.0 %shard_map.374.refs_11_ = bf16[1024,256]{1,0:T(8,128)(2,1)} custom-call(bf16[512,1024]{1,0:T(8,128)(2,1)} %refs_5_.7, bf16[1024,512]{1,0:T(8,128)(2,1)} %refs_6_.5, bf16[64,256]{1,0:T(8,128)(2,1)} %get-tuple-element.115.refs_2_.refs_4_.refs_7_.refs_12_), custom_call_target="tpu_custom_call" | custom-call | tf_op jit(solution)/shard_map/pallas_call | solution.py:731
  13.2 3.3 %collective-permute-done.refs_5_.refs_7_.refs_8_.refs_13_ = bf16[832,256]{1,0:T(8,128)(2,1)S(1)} collective-permute-done((bf16[832,256]{1,0:T(8,128)(2,1)}, bf16[832,256]{1,0:T(8,128)(2,1)S(1)}, u32[]{:S(2)}, u32[]{:S(2)}) %collective-permute-start) | collective-permute-done | bytes 426016 | tf_op jit(solution)/shard_map/ppermute | solution.py:39
  19.8 4.9 %collective-permute-done.1.refs_6_.refs_8_.refs_9_.refs_14_ = bf16[832,256]{1,0:T(8,128)(2,1)S(1)} collective-permute-done((bf16[832,256]{1,0:T(8,128)(2,1)S(1)}, bf16[832,256]{1,0:T(8,128)(2,1)S(1)}, u32[]{:S(2)}, u32[]{:S(2)}) %collective-permute-start.1) | collective-permute-done | bytes 426016 | tf_op jit(solution)/shard_map/ppermute | solution.py:745
  26.4 5.0 %shard_map.376 = (bf16[256,2048]{1,0:T(8,128)(2,1)S(1)}, bf16[256,2048]{1,0:T(8,128)(2,1)S(1)}, bf16[256,2048]{1,0:T(8,128)(2,1)S(1)}, f32[256,128]{1,0:T(8,128)S(1)}, bf16[1,512,1024]{2,1,0:T(8,128)(2,1)S(1)}) custom-call(s32[6]{0:T(128)S(1)} %stack.23.refs_0_, bf16[256,512]{1,0:T(8,128)(2,1)S(1)} %get-tuple-element.117.refs_1_.refs_6_.refs_5_, ...), custom_call_target="tpu_custom_call" | custom-call | flops 6500000 | bytes 7633896 | tf_op jit(solution)/shard_map/pallas_call | solution.py:170
  33.3 3.8 %shard_map.377 = (f32[256,512]{1,0:T(8,128)S(1)}, bf16[256,512]{1,0:T(8,128)(2,1)S(1)}, bf16[256,1536]{1,0:T(8,128)(2,1)S(1)}, f32[256,128]{1,0:T(8,128)S(1)}, b...) custom-call(s32[6]{0:T(128)S(1)} %stack.23.refs_0_, ...), custom_call_target="tpu_custom_call" | custom-call | flops 4400000 | bytes 9295832 | tf_op jit(solution)/shard_map/pallas_call | solution.py:170
  37.2 3.5 %collective-permute-done.5.refs_13_ = bf16[1024,256]{1,0:T(8,128)(2,1)S(1)} collective-permute-done((bf16[1024,256]{1,0:T(8,128)(2,1)S(1)}, bf16[1024,256]{1,0:T(8,128)(2,1)S(1)}, u32[]{:S(2)}, u32[]{:S(2)}) %collective-permute-start.5) | collective-permute-done | bytes 524320 | tf_op jit(solution)/shard_map/ppermute | solution.py:745
  42.6 5.6 %shard_map.378 = (bf16[256,512]{1,0:T(8,128)(2,1)}, bf16[4,1024,256]{2,1,0:T(8,128)(2,1)S(1)}, bf16[4,1024,256]{2,1,0:T(8,128)(2,1)S(1)}, f32[256,512]{1,0:T(8,1...) custom-call(s32[6]{0:T(128)S(1)} %stack.23.refs_0_, bf16[256,512]{1,0:T(8,128)(2,1)S(1)} %get-tuple-element.126.refs_1_, ...), custom_call_target="tpu_custom_call" | custom-call | flops 32000000000 | bytes 652091392 | tf_op jit(solution)/shard_map/pallas_call | solution.py:170
  48.3 5.7 %shard_map.379 = (bf16[4,512,256]{2,1,0:T(8,128)(2,1)S(1)}, bf16[4,512,256]{2,1,0:T(8,128)(2,1)S(1)}, f32[256,512]{1,0:T(8,128)S(1)}, bf16[256,256]{1,0:T(8,128)(2,1)S(1)}, f32[16,512]{1,0:T(8,128)S(1)}) custom-call(s32[6]{0:T(128)S(1)} %stack.23.refs_0_, f32[256,512]{1,0:T(8,128)S(1)} %get-tuple-element.133.refs_1_, ...), custom_call_target="tpu_custom_call" | custom-call | flops 26800001024 | bytes 543438336 | tf_op jit(solution)/shard_map/pallas_call | solution.py:170
  57.2 10.4 %shard_map.381 = (bf16[4,768,256]{2,1,0:T(8,128)(2,1)S(1)}, bf16[4,768,256]{2,1,0:T(8,128)(2,1)}, f32[256,512]{1,0:T(8,128)S(1)}, f32[256,256]{1,0:T(8,128)S(1)}, f32[16,2048]{1,0:T(8,128)S(1)}) custom-call(s32[6]{0:T(128)S(1)} %stack.23.refs_0_, bf16[256,256]{1,0:T(8,128)(2,1)S(1)} %get-tuple-element.139.refs_1_, ...), custom_call_target="tpu_custom_call" | custom-call | flops 46000001024 | bytes 932681216 | tf_op jit(solution)/shard_map/pallas_call | solution.py:170
  67.7 2.6 %collective-permute-done.9.refs_2_ = bf16[2,1024,256]{2,1,0:T(8,128)(2,1)S(1)} collective-permute-done((bf16[2,1024,256]{2,1,0:T(8,128)(2,1)S(1)}, bf16[2,1024,256]{2,1,0:T(8,128)(2,1)S(1)}, u32[]{:S(2)}, u32[]{:S(2)}) %collective-permute-start.9) | collective-permute-done | bytes 1048608 | tf_op jit(solution)/shard_map/ppermute | solution.py:745
  72.9 3.4 %shard_map.383 = (bf16[4,480,256]{2,1,0:T(8,128)(2,1)S(1)}, bf16[4,480,256]{2,1,0:T(8,128)(2,1)S(1)}, f32[256,512]{1,0:T(8,128)}, f32[16,512]{1,0:T(8,128)S(1)}) custom-call(s32[6]{0:T(128)S(1)} %stack.23.refs_0_, f32[256,512]{1,0:T(8,128)S(1)} %get-tuple-element.149.refs_1_, f32[256,256]{1,0:T(8,128)S(1)} %get-tuple-element.150.refs_2_, ...), custom_call_target="tpu_custom_call" | custom-call | flops 16000000000 | bytes 328486944 | tf_op jit(solution)/shard_map/pallas_call | solution.py:170
  78.7 3.3 %collective-permute-done.11.refs_2_ = bf16[1,1024,256]{2,1,0:T(8,128)(2,1)S(1)} collective-permute-done((bf16[1,1024,256]{2,1,0:T(8,128)(2,1)S(1)}, bf16[1,1024,256]{2,1,0:T(8,128)(2,1)S(1)}, u32[]{:S(2)}, u32[]{:S(2)}) %collective-permute-start.11) | collective-permute-done | bytes 524320 | tf_op jit(solution)/shard_map/ppermute | solution.py:745
  82.6 2.1 %collective-permute-start.14 = (bf16[1,512,256]{2,1,0:T(8,128)(2,1)S(1)}, bf16[1,512,256]{2,1,0:T(8,128)(2,1)S(1)}, u32[]{:S(2)}, u32[]{:S(2)}) collective-permute-start(bf16[1,512,256]{2,1,0:T(8,128)(2,1)S(1)} %get-tuple-element.170), channel_id=1, source_target_pairs={{0,8},{1,9},{2,10},{3,11},{4,12},{5,13},{6,14},{7,15},{8,0},{9,1},... | collective-permute-start | bytes 786440 | tf_op jit(solution)/shard_map/ppermute | solution.py:745
  87.8 2.5 %collective-permute-start.13 = (bf16[2,480,256]{2,1,0:T(8,128)(2,1)S(1)}, bf16[2,480,256]{2,1,0:T(8,128)(2,1)S(1)}, u32[]{:S(2)}, u32[]{:S(2)}) collective-permute-start(bf16[2,480,256]{2,1,0:T(8,128)(2,1)S(1)} %get-tuple-element.169), channel_id=1, source_target_pairs={{0,1},{1,0},{2,6},{3,7},{4,5},{5,4},{6,2},{7,3},{8,9},{9,8},{10,14... | collective-permute-start | bytes 1474568 | tf_op jit(solution)/shard_map/ppermute | solution.py:745
  90.9 2.6 %collective-permute-start.21 = (bf16[1,512,256]{2,1,0:T(8,128)(2,1)S(1)}, bf16[1,512,256]{2,1,0:T(8,128)(2,1)S(1)}, u32[]{:S(2)}, u32[]{:S(2)}) collective-permute-start(bf16[1,512,256]{2,1,0:T(8,128)(2,1)S(1)} %shard_map.388.refs_3_.refs_1_), channel_id=1, source_target_pairs={{0,16},{1,17},{2,18},{3,19},{4,20},{5,21},{6,22},{7,23},{8,24},{9,... | collective-permute-start | bytes 786440 | tf_op jit(solution)/shard_map/ppermute | solution.py:745
  93.5 4.0 %collective-permute-done.13.refs_2_ = bf16[2,480,256]{2,1,0:T(8,128)(2,1)S(1)} collective-permute-done((bf16[2,480,256]{2,1,0:T(8,128)(2,1)S(1)}, bf16[2,480,256]{2,1,0:T(8,128)(2,1)S(1)}, u32[]{:S(2)}, u32[]{:S(2)}) %collective-permute-start.13) | collective-permute-done | bytes 491552 | tf_op jit(solution)/shard_map/ppermute | solution.py:745
  105.3 2.0 %collective-permute-done.16.refs_2_ = bf16[1,480,256]{2,1,0:T(8,128)(2,1)S(1)} collective-permute-done((bf16[1,480,256]{2,1,0:T(8,128)(2,1)S(1)}, bf16[1,480,256]{2,1,0:T(8,128)(2,1)S(1)}, u32[]{:S(2)}, u32[]{:S(2)}) %collective-permute-start.16) | collective-permute-done | bytes 245792 | tf_op jit(solution)/shard_map/ppermute | solution.py:745
  108.6 3.1 %collective-permute-start.28 = (bf16[1,256,256]{2,1,0:T(8,128)(2,1)S(1)}, bf16[1,256,256]{2,1,0:T(8,128)(2,1)S(1)}, u32[]{:S(2)}, u32[]{:S(2)}) collective-permute-start(bf16[1,256,256]{2,1,0:T(8,128)(2,1)S(1)} %shard_map.393.refs_3_.refs_1_), channel_id=1, source_target_pairs={{0,16},{1,17},{2,18},{3,19},{4,20},{5,21},{6,22},{7,23},{8,24},{9,... | collective-permute-start | bytes 393224 | tf_op jit(solution)/shard_map/ppermute | solution.py:745
  117.1 2.6 %collective-permute-start.23 = (bf16[1,240,256]{2,1,0:T(8,128)(2,1)S(1)}, bf16[1,240,256]{2,1,0:T(8,128)(2,1)S(1)}, u32[]{:S(2)}, u32[]{:S(2)}) collective-permute-start(bf16[1,240,256]{2,1,0:T(8,128)(2,1)S(1)} %shard_map.396.refs_3_.refs_1_), channel_id=1, source_target_pairs={{0,16},{1,17},{2,18},{3,19},{4,20},{5,21},{6,22},{7,23},{8,24},{9,... | collective-permute-start | bytes 368648 | tf_op jit(solution)/shard_map/ppermute | solution.py:745
  120.5 2.2 %collective-permute-done.25.refs_2_ = bf16[1,512,256]{2,1,0:T(8,128)(2,1)S(1)} collective-permute-done((bf16[1,512,256]{2,1,0:T(8,128)(2,1)S(1)}, bf16[1,512,256]{2,1,0:T(8,128)(2,1)S(1)}, u32[]{:S(2)}, u32[]{:S(2)}) %collective-permute-start.25) | collective-permute-done | bytes 262176 | tf_op jit(solution)/shard_map/ppermute | solution.py:745
  124.3 4.7 %collective-permute-done.24.refs_2_ = bf16[1,768,256]{2,1,0:T(8,128)(2,1)S(1)} collective-permute-done((bf16[1,768,256]{2,1,0:T(8,128)(2,1)S(1)}, bf16[1,768,256]{2,1,0:T(8,128)(2,1)S(1)}, u32[]{:S(2)}, u32[]{:S(2)}) %collective-permute-start.24) | collective-permute-done | bytes 393248 | tf_op jit(solution)/shard_map/ppermute | solution.py:745
  134.7 3.9 %collective-permute-done.27.refs_2_ = bf16[1,384,256]{2,1,0:T(8,128)(2,1)S(1)} collective-permute-done((bf16[1,384,256]{2,1,0:T(8,128)(2,1)S(1)}, bf16[1,384,256]{2,1,0:T(8,128)(2,1)S(1)}, u32[]{:S(2)}, u32[]{:S(2)}) %collective-permute-start.27) | collective-permute-done | bytes 196640 | tf_op jit(solution)/shard_map/ppermute | solution.py:745
  143.2 5.7 %collective-permute-done.29.refs_2_ = bf16[1,480,256]{2,1,0:T(8,128)(2,1)S(1)} collective-permute-done((bf16[1,480,256]{2,1,0:T(8,128)(2,1)S(1)}, bf16[1,480,256]{2,1,0:T(8,128)(2,1)S(1)}, u32[]{:S(2)}, u32[]{:S(2)}) %collective-permute-start.29) | collective-permute-done | bytes 245792 | tf_op jit(solution)/shard_map/ppermute | solution.py:745
  149.5 3.6 %collective-permute-start.31 = (bf16[2,480,256]{2,1,0:T(8,128)(2,1)S(1)}, bf16[2,480,256]{2,1,0:T(8,128)(2,1)S(1)}, u32[]{:S(2)}, u32[]{:S(2)}) collective-permute-start(bf16[2,480,256]{2,1,0:T(8,128)(2,1)S(1)} %shard_map.404.refs_3_.refs_1_), channel_id=1, source_target_pairs={{0,1},{1,0},{2,6},{3,7},{4,5},{5,4},{6,2},{7,3},{8,9},{9,8},{10,14... | collective-permute-start | bytes 1474568 | tf_op jit(solution)/shard_map/ppermute | solution.py:745
  155.6 3.1 %collective-permute-start.38 = (bf16[2,512,256]{2,1,0:T(8,128)(2,1)S(1)}, bf16[2,512,256]{2,1,0:T(8,128)(2,1)S(1)}, u32[]{:S(2)}, u32[]{:S(2)}) collective-permute-start(bf16[2,512,256]{2,1,0:T(8,128)(2,1)S(1)} %shard_map.406.refs_3_.refs_1_), channel_id=1, source_target_pairs={{0,1},{1,0},{2,6},{3,7},{4,5},{5,4},{6,2},{7,3},{8,9},{9,8},{10,14... | collective-permute-start | bytes 1572872 | tf_op jit(solution)/shard_map/ppermute | solution.py:745
  164.2 3.2 %shard_map.410 = (f32[512,1024]{1,0:T(8,128)}, f32[3,512,256]{2,1,0:T(8,128)}, f32[4,2,512]{2,1,0:T(2,128)}, f32[1,1024]{1,0:T(1,128)}, f32[1,1024]{1,0:T(1,128)...) custom-call(s32[6]{0:T(128)S(1)} %stack.23.refs_0_, ...), custom_call_target="tpu_custom_call" | custom-call | flops 20000000000 | bytes 405724192 | tf_op jit(solution)/shard_map/pallas_call | solution.py:170
  168.9 2.8 %shard_map.412 = (f32[1024,512]{1,0:T(8,128)}, f32[512,1024]{1,0:T(8,128)}, f32[8,128]{1,0:T(8,128)S(1)}) custom-call(s32[6]{0:T(128)S(1)} %stack.23.refs_0_, bf16[2,1024,256]{2,1,0:T(8,128)(2,1)S(1)} %shard_map.407.refs_3_.refs_1_, bf16[2,1024,256]{2,1,0:T(8,128)(2,1)S(1)} %collective-permute-done.40.refs_2_, ...), custom_call_target="tpu_custom_call" | custom-call | flops 20000000000 | bytes 406295584 | tf_op jit(solution)/shard_map/pallas_call | solution.py:170
  171.7 2.8 %shard_map.413 = (f32[512,1536]{1,0:T(8,128)}, f32[512,512]{1,0:T(8,128)}, f32[8,128]{1,0:T(8,128)S(1)}) custom-call(s32[6]{0:T(128)S(1)} %stack.23.refs_0_, bf16[4,512,256]{2,1,0:T(8,128)(2,1)S(1)} %shard_map.411.refs_3_.refs_1_, bf16[4,512,256]{2,1,0:T(8,128)(2,1)S(1)} %collective-permute-done.39.refs_2_, f32[8,128]{1,0:T(8,128)S(1)} %get-tuple-element.192.refs_3_), custom_call_target="tpu_custom_call" | custom-call | flops 20000000000 | bytes 406295584 | tf_op jit(solution)/shard_map/pallas_call | solution.py:170
  175.6 1.9 %collective-permute-done.41.refs_2_ = bf16[2,768,256]{2,1,0:T(8,128)(2,1)S(1)} collective-permute-done((bf16[2,768,256]{2,1,0:T(8,128)(2,1)S(1)}, bf16[2,768,256]{2,1,0:T(8,128)(2,1)S(1)}, u32[]{:S(2)}, u32[]{:S(2)}) %collective-permute-start.41) | collective-permute-done | bytes 786464 | tf_op jit(solution)/shard_map/ppermute | solution.py:745
  177.5 3.0 %shard_map.415 = (f32[512,1024]{1,0:T(8,128)}, f32[1024,256]{1,0:T(8,128)}, f32[8,128]{1,0:T(8,128)}) custom-call(s32[6]{0:T(128)S(1)} %stack.23.refs_0_, bf16[2,768,256]{2,1,0:T(8,128)(2,1)S(1)} %shard_map.414.refs_1_.refs_3_, bf16[2,768,256]{2,1,0:T(8,128)(2,1)S(1)} %collective-permute-done.41.refs_2_, bf16[2,768,256]{2,1,0:T(8,128)(2,1)S(1)} %shard_map.414.refs_1_.refs_3_), custom_call_target="tpu_custom_call" | custom-call | flops 20000000000 | bytes 404722720 | tf_op jit(solution)/shard_map/pallas_call | solution.py:170
  (138 shorter events, 63.5 us)
Async XLA Ops:
  3.5 13.0 %collective-permute-start = (bf16[832,256]{1,0:T(8,128)(2,1)}, bf16[832,256]{1,0:T(8,128)(2,1)S(1)}, u32[]{:S(2)}, u32[]{:S(2)}) collective-permute-start(bf16[832,256]{1,0:T(8,128)(2,1)} %get-tuple-element.119), channel_id=1, source_target_pairs={{0,1},{1,0},{2,3},{3,2},{4,5},{5,4},{6,7},{7,6},{8,9},{9,8},{10,11... | collective-permute-start | bytes 1277960 | tf_op jit(solution)/shard_map/ppermute | solution.py:39
  16.5 8.1 %collective-permute-start.1 = (bf16[832,256]{1,0:T(8,128)(2,1)S(1)}, bf16[832,256]{1,0:T(8,128)(2,1)S(1)}, u32[]{:S(2)}, u32[]{:S(2)}) collective-permute-start(bf16[832,256]{1,0:T(8,128)(2,1)S(1)} %collective-permute-done.refs_5_.refs_7_.refs_8_.refs_13_), channel_id=1, source_target_pairs={{0,4},{1,5},{2,10},{3,11},{4,0},{5,1},{6,14},{7,15},{8,12},{9,13},... | collective-permute-start | bytes 1277960 | tf_op jit(solution)/shard_map/ppermute | solution.py:745
  18.3 13.2 %collective-permute-start.4 = (bf16[1024,256]{1,0:T(8,128)(2,1)S(1)}, bf16[1024,256]{1,0:T(8,128)(2,1)S(1)}, u32[]{:S(2)}, u32[]{:S(2)}) collective-permute-start(bf16[1024,256]{1,0:T(8,128)(2,1)S(1)} %copy-done.2), channel_id=1, source_target_pairs={{0,1},{1,0},{2,3},{3,2},{4,5},{5,4},{6,7},{7,6},{8,9},{9,8},{10,11... | collective-permute-start | bytes 1572872 | tf_op jit(solution)/shard_map/ppermute | solution.py:39
  31.4 9.2 %collective-permute-start.5 = (bf16[1024,256]{1,0:T(8,128)(2,1)S(1)}, bf16[1024,256]{1,0:T(8,128)(2,1)S(1)}, u32[]{:S(2)}, u32[]{:S(2)}) collective-permute-start(bf16[1024,256]{1,0:T(8,128)(2,1)S(1)} %collective-permute-done.4.refs_12_), channel_id=1, source_target_pairs={{0,4},{1,5},{2,10},{3,11},{4,0},{5,1},{6,14},{7,15},{8,12},{9,13},... | collective-permute-start | bytes 1572872 | tf_op jit(solution)/shard_map/ppermute | solution.py:745
  54.0 22.3 %collective-permute-start.12 = (bf16[4,512,256]{2,1,0:T(8,128)(2,1)S(1)}, bf16[4,512,256]{2,1,0:T(8,128)(2,1)S(1)}, u32[]{:S(2)}, u32[]{:S(2)}) collective-permute-start(bf16[4,512,256]{2,1,0:T(8,128)(2,1)S(1)} %get-tuple-element.164), channel_id=1, source_target_pairs={{0,2},{1,3},{2,0},{3,1},{4,6},{5,7},{6,4},{7,5},{8,10},{9,11},{10,... | collective-permute-start | bytes 3145736 | tf_op jit(solution)/shard_map/ppermute | solution.py:745
  55.4 14.9 %collective-permute-start.9 = (bf16[2,1024,256]{2,1,0:T(8,128)(2,1)S(1)}, bf16[2,1024,256]{2,1,0:T(8,128)(2,1)S(1)}, u32[]{:S(2)}, u32[]{:S(2)}) collective-permute-start(bf16[2,1024,256]{2,1,0:T(8,128)(2,1)S(1)} %get-tuple-element.157), channel_id=1, source_target_pairs={{0,1},{1,0},{2,6},{3,7},{4,5},{5,4},{6,2},{7,3},{8,9},{9,8},{10,14... | collective-permute-start | bytes 3145736 | tf_op jit(solution)/shard_map/ppermute | solution.py:745
  67.7 34.3 %collective-permute-start.17 = (bf16[4,768,256]{2,1,0:T(8,128)(2,1)}, bf16[4,768,256]{2,1,0:T(8,128)(2,1)}, u32[]{:S(2)}, u32[]{:S(2)}) collective-permute-start(bf16[4,768,256]{2,1,0:T(8,128)(2,1)} %get-tuple-element.176), channel_id=1, source_target_pairs={{0,2},{1,3},{2,0},{3,1},{4,6},{5,7},{6,4},{7,5},{8,10},{9,11},{10,... | collective-permute-start | bytes 4718600 | tf_op jit(solution)/shard_map/ppermute | solution.py:745
  71.1 10.8 %collective-permute-start.11 = (bf16[1,1024,256]{2,1,0:T(8,128)(2,1)S(1)}, bf16[1,1024,256]{2,1,0:T(8,128)(2,1)S(1)}, u32[]{:S(2)}, u32[]{:S(2)}) collective-permute-start(bf16[1,1024,256]{2,1,0:T(8,128)(2,1)S(1)} %get-tuple-element.162), channel_id=1, source_target_pairs={{0,4},{1,5},{2,3},{3,2},{4,0},{5,1},{6,7},{7,6},{8,12},{9,13},{10,... | collective-permute-start | bytes 1572872 | tf_op jit(solution)/shard_map/ppermute | solution.py:745
  77.1 9.2 %collective-permute-start.15 = (bf16[2,512,256]{2,1,0:T(8,128)(2,1)S(1)}, bf16[2,512,256]{2,1,0:T(8,128)(2,1)S(1)}, u32[]{:S(2)}, u32[]{:S(2)}) collective-permute-start(bf16[2,512,256]{2,1,0:T(8,128)(2,1)S(1)} %get-tuple-element.171), channel_id=1, source_target_pairs={{0,1},{1,0},{2,6},{3,7},{4,5},{5,4},{6,2},{7,3},{8,9},{9,8},{10,14... | collective-permute-start | bytes 1572872 | tf_op jit(solution)/shard_map/ppermute | solution.py:745
  82.6 7.7 %collective-permute-start.14 = (bf16[1,512,256]{2,1,0:T(8,128)(2,1)S(1)}, bf16[1,512,256]{2,1,0:T(8,128)(2,1)S(1)}, u32[]{:S(2)}, u32[]{:S(2)}) collective-permute-start(bf16[1,512,256]{2,1,0:T(8,128)(2,1)S(1)} %get-tuple-element.170), channel_id=1, source_target_pairs={{0,8},{1,9},{2,10},{3,11},{4,12},{5,13},{6,14},{7,15},{8,0},{9,1},... | collective-permute-start | bytes 786440 | tf_op jit(solution)/shard_map/ppermute | solution.py:745
  87.0 11.1 %collective-permute-start.18 = (bf16[1,512,256]{2,1,0:T(8,128)(2,1)S(1)}, bf16[1,512,256]{2,1,0:T(8,128)(2,1)S(1)}, u32[]{:S(2)}, u32[]{:S(2)}) collective-permute-start(bf16[1,512,256]{2,1,0:T(8,128)(2,1)S(1)} %get-tuple-element.177), channel_id=1, source_target_pairs={{0,4},{1,5},{2,3},{3,2},{4,0},{5,1},{6,7},{7,6},{8,12},{9,13},{10,... | collective-permute-start | bytes 786440 | tf_op jit(solution)/shard_map/ppermute | solution.py:745
  87.8 9.7 %collective-permute-start.13 = (bf16[2,480,256]{2,1,0:T(8,128)(2,1)S(1)}, bf16[2,480,256]{2,1,0:T(8,128)(2,1)S(1)}, u32[]{:S(2)}, u32[]{:S(2)}) collective-permute-start(bf16[2,480,256]{2,1,0:T(8,128)(2,1)S(1)} %get-tuple-element.169), channel_id=1, source_target_pairs={{0,1},{1,0},{2,6},{3,7},{4,5},{5,4},{6,2},{7,3},{8,9},{9,8},{10,14... | collective-permute-start | bytes 1474568 | tf_op jit(solution)/shard_map/ppermute | solution.py:745
  90.9 20.8 %collective-permute-start.21 = (bf16[1,512,256]{2,1,0:T(8,128)(2,1)S(1)}, bf16[1,512,256]{2,1,0:T(8,128)(2,1)S(1)}, u32[]{:S(2)}, u32[]{:S(2)}) collective-permute-start(bf16[1,512,256]{2,1,0:T(8,128)(2,1)S(1)} %shard_map.388.refs_3_.refs_1_), channel_id=1, source_target_pairs={{0,16},{1,17},{2,18},{3,19},{4,20},{5,21},{6,22},{7,23},{8,24},{9,... | collective-permute-start | bytes 786440 | tf_op jit(solution)/shard_map/ppermute | solution.py:745
  98.8 9.2 %collective-permute-start.22 = (bf16[1,256,256]{2,1,0:T(8,128)(2,1)S(1)}, bf16[1,256,256]{2,1,0:T(8,128)(2,1)S(1)}, u32[]{:S(2)}, u32[]{:S(2)}) collective-permute-start(bf16[1,256,256]{2,1,0:T(8,128)(2,1)S(1)} %get-tuple-element.183), channel_id=1, source_target_pairs={{0,8},{1,9},{2,10},{3,11},{4,12},{5,13},{6,14},{7,15},{8,0},{9,1},... | collective-permute-start | bytes 393224 | tf_op jit(solution)/shard_map/ppermute | solution.py:745
  103.7 12.1 %collective-permute-start.20 = (bf16[2,768,256]{2,1,0:T(8,128)(2,1)S(1)}, bf16[2,768,256]{2,1,0:T(8,128)(2,1)S(1)}, u32[]{:S(2)}, u32[]{:S(2)}) collective-permute-start(bf16[2,768,256]{2,1,0:T(8,128)(2,1)S(1)} %get-tuple-element.182), channel_id=1, source_target_pairs={{0,1},{1,0},{2,6},{3,7},{4,5},{5,4},{6,2},{7,3},{8,9},{9,8},{10,14... | collective-permute-start | bytes 2359304 | tf_op jit(solution)/shard_map/ppermute | solution.py:745
  107.9 8.6 %collective-permute-start.19 = (bf16[1,240,256]{2,1,0:T(8,128)(2,1)S(1)}, bf16[1,240,256]{2,1,0:T(8,128)(2,1)S(1)}, u32[]{:S(2)}, u32[]{:S(2)}) collective-permute-start(bf16[1,240,256]{2,1,0:T(8,128)(2,1)S(1)} %get-tuple-element.181), channel_id=1, source_target_pairs={{0,8},{1,9},{2,10},{3,11},{4,12},{5,13},{6,14},{7,15},{8,0},{9,1},... | collective-permute-start | bytes 368648 | tf_op jit(solution)/shard_map/ppermute | solution.py:745
  108.6 23.8 %collective-permute-start.28 = (bf16[1,256,256]{2,1,0:T(8,128)(2,1)S(1)}, bf16[1,256,256]{2,1,0:T(8,128)(2,1)S(1)}, u32[]{:S(2)}, u32[]{:S(2)}) collective-permute-start(bf16[1,256,256]{2,1,0:T(8,128)(2,1)S(1)} %shard_map.393.refs_3_.refs_1_), channel_id=1, source_target_pairs={{0,16},{1,17},{2,18},{3,19},{4,20},{5,21},{6,22},{7,23},{8,24},{9,... | collective-permute-start | bytes 393224 | tf_op jit(solution)/shard_map/ppermute | solution.py:745
  112.2 10.5 %collective-permute-start.25 = (bf16[1,512,256]{2,1,0:T(8,128)(2,1)S(1)}, bf16[1,512,256]{2,1,0:T(8,128)(2,1)S(1)}, u32[]{:S(2)}, u32[]{:S(2)}) collective-permute-start(bf16[1,512,256]{2,1,0:T(8,128)(2,1)S(1)} %shard_map.394.refs_3_.refs_1_), channel_id=1, source_target_pairs={{0,8},{1,9},{2,10},{3,11},{4,12},{5,13},{6,14},{7,15},{8,0},{9,1},... | collective-permute-start | bytes 786440 | tf_op jit(solution)/shard_map/ppermute | solution.py:745
  117.1 12.6 %collective-permute-start.23 = (bf16[1,240,256]{2,1,0:T(8,128)(2,1)S(1)}, bf16[1,240,256]{2,1,0:T(8,128)(2,1)S(1)}, u32[]{:S(2)}, u32[]{:S(2)}) collective-permute-start(bf16[1,240,256]{2,1,0:T(8,128)(2,1)S(1)} %shard_map.396.refs_3_.refs_1_), channel_id=1, source_target_pairs={{0,16},{1,17},{2,18},{3,19},{4,20},{5,21},{6,22},{7,23},{8,24},{9,... | collective-permute-start | bytes 368648 | tf_op jit(solution)/shard_map/ppermute | solution.py:745
  119.7 9.3 %collective-permute-start.24 = (bf16[1,768,256]{2,1,0:T(8,128)(2,1)S(1)}, bf16[1,768,256]{2,1,0:T(8,128)(2,1)S(1)}, u32[]{:S(2)}, u32[]{:S(2)}) collective-permute-start(bf16[1,768,256]{2,1,0:T(8,128)(2,1)S(1)} %get-tuple-element.185), channel_id=1, source_target_pairs={{0,4},{1,5},{2,3},{3,2},{4,0},{5,1},{6,7},{7,6},{8,12},{9,13},{10,... | collective-permute-start | bytes 1179656 | tf_op jit(solution)/shard_map/ppermute | solution.py:745
  124.1 34.6 %collective-permute-start.32 = (bf16[1,1024,256]{2,1,0:T(8,128)(2,1)}, bf16[1,1024,256]{2,1,0:T(8,128)(2,1)}, u32[]{:S(2)}, u32[]{:S(2)}) collective-permute-start(bf16[1,1024,256]{2,1,0:T(8,128)(2,1)} %shard_map.397.refs_3_.refs_1_), channel_id=1, source_target_pairs={{0,4},{1,5},{2,6},{3,7},{4,0},{5,1},{6,2},{7,3},{8,12},{9,13},{10,... | collective-permute-start | bytes 1572872 | tf_op jit(solution)/shard_map/ppermute | solution.py:745
  130.3 9.2 %collective-permute-start.26 = (bf16[1,240,256]{2,1,0:T(8,128)(2,1)S(1)}, bf16[1,240,256]{2,1,0:T(8,128)(2,1)S(1)}, u32[]{:S(2)}, u32[]{:S(2)}) collective-permute-start(bf16[1,240,256]{2,1,0:T(8,128)(2,1)S(1)} %shard_map.399.refs_3_.refs_1_), channel_id=1, source_target_pairs={{0,8},{1,9},{2,10},{3,11},{4,12},{5,13},{6,14},{7,15},{8,0},{9,1},... | collective-permute-start | bytes 368648 | tf_op jit(solution)/shard_map/ppermute | solution.py:745
  132.0 6.6 %collective-permute-start.27 = (bf16[1,384,256]{2,1,0:T(8,128)(2,1)S(1)}, bf16[1,384,256]{2,1,0:T(8,128)(2,1)S(1)}, u32[]{:S(2)}, u32[]{:S(2)}) collective-permute-start(bf16[1,384,256]{2,1,0:T(8,128)(2,1)S(1)} %get-tuple-element.187), channel_id=1, source_target_pairs={{0,8},{1,9},{2,10},{3,11},{4,12},{5,13},{6,14},{7,15},{8,0},{9,1},... | collective-permute-start | bytes 589832 | tf_op jit(solution)/shard_map/ppermute | solution.py:745
  133.0 8.4 %collective-permute-start.30 = (bf16[1,256,256]{2,1,0:T(8,128)(2,1)S(1)}, bf16[1,256,256]{2,1,0:T(8,128)(2,1)S(1)}, u32[]{:S(2)}, u32[]{:S(2)}) collective-permute-start(bf16[1,256,256]{2,1,0:T(8,128)(2,1)S(1)} %shard_map.400.refs_3_.refs_1_), channel_id=1, source_target_pairs={{0,8},{1,9},{2,10},{3,11},{4,12},{5,13},{6,14},{7,15},{8,0},{9,1},... | collective-permute-start | bytes 393224 | tf_op jit(solution)/shard_map/ppermute | solution.py:745
  139.2 13.9 %collective-permute-start.34 = (bf16[1,384,256]{2,1,0:T(8,128)(2,1)S(1)}, bf16[1,384,256]{2,1,0:T(8,128)(2,1)S(1)}, u32[]{:S(2)}, u32[]{:S(2)}) collective-permute-start(bf16[1,384,256]{2,1,0:T(8,128)(2,1)S(1)} %shard_map.401.refs_3_.refs_1_), channel_id=1, source_target_pairs={{0,16},{1,17},{2,18},{3,19},{4,20},{5,21},{6,22},{7,23},{8,24},{9,... | collective-permute-start | bytes 589832 | tf_op jit(solution)/shard_map/ppermute | solution.py:745
  140.1 8.9 %collective-permute-start.29 = (bf16[1,480,256]{2,1,0:T(8,128)(2,1)S(1)}, bf16[1,480,256]{2,1,0:T(8,128)(2,1)S(1)}, u32[]{:S(2)}, u32[]{:S(2)}) collective-permute-start(bf16[1,480,256]{2,1,0:T(8,128)(2,1)S(1)} %shard_map.402.refs_3_.refs_1_), channel_id=1, source_target_pairs={{0,4},{1,5},{2,3},{3,2},{4,0},{5,1},{6,7},{7,6},{8,12},{9,13},{10,... | collective-permute-start | bytes 737288 | tf_op jit(solution)/shard_map/ppermute | solution.py:745
  141.9 13.1 %collective-permute-start.33 = (bf16[1,512,256]{2,1,0:T(8,128)(2,1)S(1)}, bf16[1,512,256]{2,1,0:T(8,128)(2,1)S(1)}, u32[]{:S(2)}, u32[]{:S(2)}) collective-permute-start(bf16[1,512,256]{2,1,0:T(8,128)(2,1)S(1)} %shard_map.403.refs_3_.refs_1_), channel_id=1, source_target_pairs={{0,4},{1,5},{2,3},{3,2},{4,0},{5,1},{6,7},{7,6},{8,12},{9,13},{10,... | collective-permute-start | bytes 786440 | tf_op jit(solution)/shard_map/ppermute | solution.py:745
  149.5 10.6 %collective-permute-start.31 = (bf16[2,480,256]{2,1,0:T(8,128)(2,1)S(1)}, bf16[2,480,256]{2,1,0:T(8,128)(2,1)S(1)}, u32[]{:S(2)}, u32[]{:S(2)}) collective-permute-start(bf16[2,480,256]{2,1,0:T(8,128)(2,1)S(1)} %shard_map.404.refs_3_.refs_1_), channel_id=1, source_target_pairs={{0,1},{1,0},{2,6},{3,7},{4,5},{5,4},{6,2},{7,3},{8,9},{9,8},{10,14... | collective-permute-start | bytes 1474568 | tf_op jit(solution)/shard_map/ppermute | solution.py:745
  153.7 7.6 %collective-permute-start.36 = (bf16[1,384,256]{2,1,0:T(8,128)(2,1)S(1)}, bf16[1,384,256]{2,1,0:T(8,128)(2,1)S(1)}, u32[]{:S(2)}, u32[]{:S(2)}) collective-permute-start(bf16[1,384,256]{2,1,0:T(8,128)(2,1)S(1)} %shard_map.405.refs_3_.refs_1_), channel_id=1, source_target_pairs={{0,8},{1,9},{2,10},{3,11},{4,12},{5,13},{6,14},{7,15},{8,0},{9,1},... | collective-permute-start | bytes 589832 | tf_op jit(solution)/shard_map/ppermute | solution.py:745
  155.6 11.8 %collective-permute-start.38 = (bf16[2,512,256]{2,1,0:T(8,128)(2,1)S(1)}, bf16[2,512,256]{2,1,0:T(8,128)(2,1)S(1)}, u32[]{:S(2)}, u32[]{:S(2)}) collective-permute-start(bf16[2,512,256]{2,1,0:T(8,128)(2,1)S(1)} %shard_map.406.refs_3_.refs_1_), channel_id=1, source_target_pairs={{0,1},{1,0},{2,6},{3,7},{4,5},{5,4},{6,2},{7,3},{8,9},{9,8},{10,14... | collective-permute-start | bytes 1572872 | tf_op jit(solution)/shard_map/ppermute | solution.py:745
  160.0 8.8 %collective-permute-start.40 = (bf16[2,1024,256]{2,1,0:T(8,128)(2,1)S(1)}, bf16[2,1024,256]{2,1,0:T(8,128)(2,1)S(1)}, u32[]{:S(2)}, u32[]{:S(2)}) collective-permute-start(bf16[2,1024,256]{2,1,0:T(8,128)(2,1)S(1)} %shard_map.407.refs_3_.refs_1_), channel_id=1, source_target_pairs={{0,2},{1,3},{2,0},{3,1},{4,6},{5,7},{6,4},{7,5},{8,10},{9,11},{10,... | collective-permute-start | bytes 3145736 | tf_op jit(solution)/shard_map/ppermute | solution.py:745
  161.9 12.6 %collective-permute-start.37 = (bf16[1,768,256]{2,1,0:T(8,128)(2,1)S(1)}, bf16[1,768,256]{2,1,0:T(8,128)(2,1)S(1)}, u32[]{:S(2)}, u32[]{:S(2)}) collective-permute-start(bf16[1,768,256]{2,1,0:T(8,128)(2,1)S(1)} %shard_map.409.refs_3_.refs_1_), channel_id=1, source_target_pairs={{0,4},{1,5},{2,6},{3,7},{4,0},{5,1},{6,2},{7,3},{8,12},{9,13},{10,... | collective-permute-start | bytes 1179656 | tf_op jit(solution)/shard_map/ppermute | solution.py:745
  (31 other events, 248.9 us)

commit v5 on v4

--- a/solution.py
+++ b/solution.py
@@ -137,35 +137,40 @@
     return jnp.sum(values, 0, keepdims=True)
 
 
+def eighths_sum(values):
+    return jnp.sum(values.reshape(-1, 8, values.shape[1]), 0)
+
+
 def low_columns_sum(values):
     ones = jnp.ones((16, values.shape[0]), LOW)
     return dot(ones, values)[0:1]
 
 
-def keep_rows(info, start, rows):
-    return jnp.where(
-        lax.broadcasted_iota(jnp.int32, (rows, 1), 0) + start < info[2], 1.0, 0.0
-    ).astype(F32)
+def place(local):
+    dp, mp = lax.axis_index("dp"), lax.axis_index("mp")
+    return dp % 2, mp * local, None, mp % 2, dp // 2 % 2, dp // 4 % 2
 
 
 class Chain:
-    def __init__(self):
+    def __init__(self, local):
         self.link = None
+        self.local = local
 
     def run(self, kernel, outs, ins, scratch, flops, placed=0):
-        specs = [pl.BlockSpec(memory_space=pltpu.SMEM)] + [
-            pl.BlockSpec(memory_space=pltpu.VMEM) for _ in ins[1:]
+        ins = list(ins)
+        specs = [
+            pl.BlockSpec(memory_space=pltpu.SMEM if item.dtype == jnp.int32 else pltpu.VMEM)
+            for item in ins
         ]
         count = len(ins)
-        moved = sum(item.size * item.dtype.itemsize for item in list(ins) + list(outs))
-        ins = list(ins)
+        moved = sum(item.size * item.dtype.itemsize for item in ins + list(outs))
         linked = self.link is not None
         if linked:
             ins.append(self.link)
             specs.append(pl.BlockSpec(memory_space=pl.ANY))
 
         def call(*refs):
-            kernel(*(refs[:count] + refs[count + 1 :] if linked else refs))
+            kernel(place(self.local), *(refs[:count] + refs[count + 1 :] if linked else refs))
 
         results = pl.pallas_call(
             call,
@@ -177,7 +182,9 @@
             ],
             scratch_shapes=scratch,
             compiler_params=pltpu.CompilerParams(vmem_limit_bytes=LIMIT),
-            cost_estimate=pl.CostEstimate(flops=flops, bytes_accessed=moved + flops // 50, transcendentals=0),
+            cost_estimate=pl.CostEstimate(
+                flops=flops, bytes_accessed=moved + flops // 50, transcendentals=0
+            ),
         )(*ins)
         self.link = min(results, key=lambda item: item.size)
         return results
@@ -199,11 +206,15 @@
 
 
 def pre_kernel(
-    info, x_ref, gated_w, conv_w, norms, gated_b, conv_b, point_b, project_b, output_b, shrink_b,
-    a1, values, gates, x1, a2, right_pre, vec, right
+    info, lengths, x_ref, gated_w, conv_w, norms, gated_b, conv_b, point_b, project_b, output_b, shrink_b,
+    a1, values, gates, x1, a2, right_pre, vec, kept, valid, right
 ):
     width = x_ref.shape[1]
     channels = right.shape[1]
+    length = lengths[0]
+    for ref, axis in ((kept, 0), (valid, 1)):
+        spots = lax.broadcasted_iota(jnp.int32, ref.shape, axis)
+        ref[...] = jnp.where(spots < length, 1.0, 0.0).astype(F32)
     vec[...] = jnp.zeros_like(vec)
     for at in range(4):
         vec[2 * at : 2 * at + 2] = norms[at].astype(F32)
@@ -224,8 +235,7 @@
         x1[:, col] = x_ref[:, col].astype(F32) + value * gate
     for row in spans(SEQ, STEP):
         normed, _ = normalize(x1[row])
-        kept = keep_rows(info, row.start, STEP)
-        a2[row] = as_low((normed * vec[2:3] + vec[3:4]) * kept)
+        a2[row] = as_low((normed * vec[2:3] + vec[3:4]) * kept[row, 0:1])
     rows = lax.broadcasted_iota(jnp.int32, right_pre.shape, 0)
     first = jnp.where(rows == 0, 0.0, pltpu.roll(dot(a2[...], conv_w[0]), 1, 0))
     last = jnp.where(rows == SEQ - 1, 0.0, pltpu.roll(dot(a2[...], conv_w[2]), SEQ - 1, 0))
@@ -274,7 +284,9 @@
 
 def inner_forward_kernel(pieces, per, refs):
     info, refs = refs[0], refs[1:]
-    (a2, right, left, own), packed, outs, scratch = unpack(refs, [4, per * (pieces - 1), 5, 6])
+    (a2, right, left, own, keep), packed, outs, scratch = unpack(
+        refs, [5, per * (pieces - 1), 5, 6]
+    )
     normed_ref, slope_ref, depth, rstd_ref, left_rest = outs
     mixed, total, square, centre_ref, padded, padded_two = scratch
     local = left.shape[1]
@@ -309,7 +321,7 @@
     for pad in (padded, padded_two):
         pad[0:8] = jnp.zeros((8, 128), F32)
         pad[SEQ + 8 : SEQ + 16] = jnp.zeros((8, 128), F32)
-    kept = keep_rows(info, 0, SEQ)
+    kept = keep[:, 0:1]
     for piece in range(pieces):
 
         def one(index, part, pad):
@@ -336,8 +348,8 @@
 
 
 def attention_forward_kernel(pieces, per, refs):
-    (info, x1, depth, point, vec, project_w, output_w), packed, outs = unpack(
-        refs, [7, per * (pieces - 1), 8]
+    (info, x1, depth, point, vec, project_w, output_w, mask), packed, outs = unpack(
+        refs, [8, per * (pieces - 1), 8]
     )
     x2, a4, qkv, lse, attended, x3, a5, point_rest = outs
     width = x2.shape[1]
@@ -361,7 +373,7 @@
         qkv[:, col] = as_low(part)
     scale = (width // HEADS) ** (-0.5)
     lanes = lax.broadcasted_iota(jnp.int32, (SEQ, 128), 1)
-    valid = lax.broadcasted_iota(jnp.int32, (SEQ, SEQ), 1) < info[2]
+    valid = jnp.broadcast_to(mask[0:1], (SEQ, SEQ)) > 0.5
     logs = jnp.zeros((SEQ, 128), F32)
     for pair in range(width // 128):
         at = pair * 128
@@ -385,57 +397,65 @@
         a5[row] = as_low(normed * vec[6:7] + vec[7:8])
 
 
+def feed_piece(a5, top, expand, shrink, vectors, hidden, slope, d_expand):
+    local = expand.shape[1]
+    for col in spans(local, 256):
+        pre = dot(a5[...], expand[:, col])
+        pre = pre + rows_of(vectors, col.start // 256, slice(0, 256))[1:2]
+        sigma = sigmoid(pre)
+        hidden[:, col] = as_low(pre * sigma)
+        slope[:, col] = sigma * (1.0 + pre * (1.0 - sigma))
+    part = dot(hidden[...], shrink[...])
+    for row in spans(local, 256):
+        d_expand[:, row] = as_low(dot_right(top[...], shrink[row]) * slope[:, row])
+    return part
+
+
+def feed_grads(core, a5, top, hidden, d_expand, keep, send, first):
+    local = hidden.shape[1]
+    half, rows = a5.shape[1] // 2, local // 2
+    for side, out in ((1 - core, send), (core, keep)):
+        put(out, first, 2, 0, dot_left(hidden[:, at_lane(side * rows, rows)], top[...]))
+        grad = dot_left(a5[:, at_lane(side * half, half)], d_expand[...])
+        put(out, first, 2, a5.shape[1] * local // 1024, grad)
+
+
+def feed_own_kernel(
+    info, a5, top, expand, shrink, own, keep, send, shrunk, d_a5, grad_bias, hidden, slope, d_expand
+):
+    shrunk[...] = feed_piece(a5, top, expand, shrink, (own, 0), hidden, slope, d_expand)
+    feed_grads(info[0], a5, top, hidden, d_expand, keep, send, 0)
+    grad_bias[...] = jnp.broadcast_to(low_columns_sum(d_expand[...]), grad_bias.shape)
+    d_a5[...] = dot_right(d_expand[...], expand[...])
+
+
 def feed_kernel(pieces, per, refs):
     info, refs = refs[0], refs[1:]
-    (a5, x3, top, vec, expand, shrink, own), first, packed, outs, scratch = unpack(
-        refs, [7, per * (pieces - 1), per * (pieces - 1), 6, 7]
+    (a5, x3, top, vec, keep_own, send_own, shrunk_own, d_a5_own, bias_own), first, packed, outs, scratch = unpack(
+        refs, [9, per * (pieces - 1), per * (pieces - 1), 6, 7]
     )
     output, keep, send, dx3, fixed, grad_bias = outs
-    hidden, slope, d_expand, shrunk, d_a5, expand_rest, shrink_rest = scratch
-    local = expand.shape[1]
-    width = x3.shape[1]
-    half, rows = width // 2, local // 2
-    core = info[0]
-    wide = vectors_of(own, first, per, width * local // (256 * per) + local // per)
-    for piece in range(pieces):
-        if piece:
-            blocks = packed[(piece - 1) * per : piece * per]
-            assemble(info, expand_rest.at[piece - 1], blocks, 0)
-            assemble(info, shrink_rest.at[piece - 1], blocks, width * local // (256 * per))
-        for col in spans(local, 256):
-            weights = expand[:, col] if piece == 0 else expand_rest[piece - 1, :, col]
-            pre = dot(a5[...], weights)
-            pre = pre + rows_of(wide[piece], col.start // 256, slice(0, 256))[1:2]
-            sigma = sigmoid(pre)
-            here = slice(piece * local + col.start, piece * local + col.stop)
-            hidden[:, here] = as_low(pre * sigma)
-            slope[:, here] = sigma * (1.0 + pre * (1.0 - sigma))
-    for piece in range(pieces):
-        base = piece * local
-        weights = shrink if piece == 0 else shrink_rest.at[piece - 1]
-        part = dot(hidden[:, base : base + local], weights[...])
-        if piece == 0:
-            shrunk[...] = part
-        else:
-            shrunk[...] += part
-        for row in spans(local, 256):
-            here = slice(base + row.start, base + row.stop)
-            d_expand[:, here] = as_low(dot_right(top[...], weights[row]) * slope[:, here])
+    hidden, slope, d_expand, shrunk, d_a5, expand, shrink = scratch
+    local, width = shrink.shape
+    wide = vectors_of(None, first, per, width * local // (256 * per) + local // per)
+    keep[0:2] = keep_own[...]
+    send[0:2] = send_own[...]
+    shrunk[...] = shrunk_own[...]
+    d_a5[...] = d_a5_own[...]
+    grad_bias[:, 0:local] = bias_own[...]
+    for piece in range(1, pieces):
+        blocks = packed[(piece - 1) * per : piece * per]
+        assemble(info, expand, blocks, 0)
+        assemble(info, shrink, blocks, width * local // (256 * per))
+        shrunk[...] += feed_piece(
+            a5, top, expand, shrink, wide[piece], hidden, slope, d_expand
+        )
+        feed_grads(info[0], a5, top, hidden, d_expand, keep, send, 2 * piece)
+        cols = slice(piece * local, (piece + 1) * local)
+        grad_bias[:, cols] = jnp.broadcast_to(low_columns_sum(d_expand[...]), (8, local))
+        d_a5[...] += dot_right(d_expand[...], expand[...])
     for row in spans(SEQ, STEP):
         output[row] = as_low(x3[row] + shrunk[row] + vec[14:15])
-    for piece in range(pieces):
-        base = piece * local
-        cols = slice(base, base + local)
-        for side, out in ((1 - core, send), (core, keep)):
-            grad = dot_left(hidden[:, at_lane(base + side * rows, rows)], top[...])
-            put(out, 2 * piece, 2, 0, grad)
-            grad = dot_left(a5[:, at_lane(side * half, half)], d_expand[:, cols])
-            put(out, 2 * piece, 2, width * local // 1024, grad)
-        grad_bias[:, cols] = jnp.broadcast_to(low_columns_sum(d_expand[:, cols]), (8, local))
-        if piece == 0:
-            d_a5[...] = dot_right(d_expand[:, cols], expand[...])
-        else:
-            d_a5[...] += dot_right(d_expand[:, cols], expand_rest[piece - 1])
     fixed[...] = jnp.zeros_like(fixed)
     for row in spans(SEQ, STEP):
         normed, rstd = normalize(x3[row])
@@ -447,7 +467,7 @@
 
 
 def attention_backward_kernel(
-    info, dx3, attended, output_w, qkv, lse, a4, project_w, x2, vec, before,
+    info, dx3, attended, output_w, qkv, lse, a4, project_w, x2, vec, mask, before,
     send, keep, dx2, d_sep, fixed, d_out, d_att, d_proj
 ):
     width = x2.shape[1]
@@ -458,7 +478,7 @@
     d_att[...] = as_low(dot_right(d_out[...], output_w[...]))
     scale = (width // HEADS) ** (-0.5)
     lanes = lax.broadcasted_iota(jnp.int32, (SEQ, 128), 1)
-    valid = lax.broadcasted_iota(jnp.int32, (SEQ, SEQ), 1) < info[2]
+    valid = jnp.broadcast_to(mask[0:1], (SEQ, SEQ)) > 0.5
     for pair in range(width // 128):
         at = pair * 128
         queries = qkv[:, at : at + 128]
@@ -502,13 +522,13 @@
     info, refs = refs[0], refs[1:]
     (
         (d_sep, depth, normed_ref, slope_ref, rstd_ref, a2, bias_before, point, point_rest),
-        (left, left_rest, own),
+        (left, left_rest, own, keep_mask),
         packed,
         outs,
         scratch,
-    ) = unpack(refs, [9, 3, per * (pieces - 1), 5, 6])
+    ) = unpack(refs, [9, 4, per * (pieces - 1), 5, 7])
     keep, send, d_a2, d_right, grads = outs
-    d_depth, padded, padded_two, d_left, first_ref, second_ref = scratch
+    d_depth, padded, padded_two, d_left, first_ref, second_ref, sums = scratch
     local = left.shape[1]
     inner = local * pieces
     core, offset = info[0], info[1]
@@ -520,8 +540,8 @@
         for row in spans(local, 256):
             back = dot_right(d_sep[...], weights[row])
             index = (piece * local + row.start) // 128
-            d_depth[index, 8 : SEQ + 8] = back[:, 0:128]
-            d_depth[index + 1, 8 : SEQ + 8] = back[:, 128:256]
+            d_depth[index] = back[:, 0:128]
+            d_depth[index + 1] = back[:, 128:256]
     first_ref[...] = jnp.zeros_like(first_ref)
     second_ref[...] = jnp.zeros_like(second_ref)
     for pad in (padded, padded_two):
@@ -529,30 +549,29 @@
         pad[SEQ + 8 : SEQ + 16] = jnp.zeros((8, 128), F32)
     grads[...] = jnp.zeros_like(grads)
     grads[1:2] = bias_before[0:1]
-    kept = keep_rows(info, 0, SEQ)
+    kept = keep_mask[:, 0:1]
     for piece in range(pieces):
 
         def one(pair, part, pad):
             here = at_lane(piece * local + pair * 256 + part, 128)
             index = piece * (local // 128) + 2 * pair + part // 128
             vectors = rows_of(wide[piece], pair, slice(part, part + 128))
-            d_depth[index, 0:8] = jnp.zeros((8, 128), F32)
-            d_depth[index, SEQ + 8 : SEQ + 16] = jnp.zeros((8, 128), F32)
             normed = normed_ref[:, here].astype(F32)
-            pad[8 : SEQ + 8] = (normed * vectors[2:3] + vectors[3:4]) * kept
-            own = d_depth[index, 8 : SEQ + 8]
-            result = d_depth[index, 12 : SEQ + 12] * vectors[4:5]
-            grads[4:5, here] = columns_sum(pad[4 : SEQ + 4] * own)
+            normal = (normed * vectors[2:3] + vectors[3:4]) * kept
+            pad[8 : SEQ + 8] = d_depth[index]
+            result = pad[12 : SEQ + 12] * vectors[4:5]
+            sums[2, :, here] = eighths_sum(normal * pad[12 : SEQ + 12])
             for tap in range(1, 9):
-                result = result + d_depth[index, 12 - tap : SEQ + 12 - tap] * vectors[4 + tap : 5 + tap]
-                grads[4 + tap : 5 + tap, here] = columns_sum(pad[4 + tap : SEQ + 4 + tap] * own)
+                shifted = pad[12 - tap : SEQ + 12 - tap]
+                result = result + shifted * vectors[4 + tap : 5 + tap]
+                sums[2 + tap, :, here] = eighths_sum(normal * shifted)
             result = result * kept
-            grads[2:3, here] = columns_sum(result * normed)
-            grads[3:4, here] = columns_sum(result)
+            sums[0, :, here] = eighths_sum(result * normed)
+            sums[1, :, here] = eighths_sum(result)
             scaled = result * vectors[2:3]
             first_ref[...] += scaled
             second_ref[...] += scaled * normed
-            d_depth[index, 8 : SEQ + 8] = scaled
+            d_depth[index] = scaled
 
         def step(index, carry):
             one(index, 0, padded)
@@ -560,6 +579,8 @@
             return carry
 
         lax.fori_loop(0, local // 256, step, 0)
+    for col in spans(inner, 512):
+        grads[2:13, col] = jnp.sum(sums[:, :, col], 1)
     first_ref[...] = jnp.broadcast_to(
         jnp.sum(first_ref[...], 1, keepdims=True) * (1.0 / inner), first_ref.shape
     )
@@ -571,15 +592,15 @@
         here = at_lane(index * 128, 128)
         normed = normed_ref[:, here].astype(F32)
         d_mixed = rstd_ref[...] * (
-            d_depth[index, 8 : SEQ + 8] - first_ref[...] - normed * second_ref[...]
+            d_depth[index] - first_ref[...] - normed * second_ref[...]
         )
-        d_depth[index, 8 : SEQ + 8] = d_mixed
+        d_depth[index] = d_mixed
         d_left[:, here] = as_low(d_mixed * slope_ref[:, here].astype(F32))
         return carry
 
     lax.fori_loop(0, inner // 128, back, 0)
     for part in range(d_right.shape[1] // 128):
-        d_right[:, part * 128 : (part + 1) * 128] = d_depth[offset // 128 + part, 8 : SEQ + 8]
+        d_right[:, part * 128 : (part + 1) * 128] = d_depth[offset // 128 + part]
     for piece in range(pieces):
         base = piece * local
         cols = slice(base, base + local)
@@ -596,7 +617,7 @@
 
 
 def last_kernel(
-    info, d_a2_left, d_right, right_pre, conv_w, a2, x1, dx2, values, gates, a1, gated_w, x_ref, vec, before, wide_sums,
+    info, d_a2_left, d_right, right_pre, conv_w, a2, x1, dx2, values, gates, a1, gated_w, x_ref, vec, kept, before, wide_sums,
     send, keep, input_grad, fixed, shifted, d_a2, d_gated, rows_ref
 ):
     width = x1.shape[1]
@@ -621,7 +642,7 @@
     d_a2[...] = total
     for row in spans(SEQ, STEP):
         normed, rstd = normalize(x1[row])
-        grad = d_a2[row] * keep_rows(info, row.start, STEP)
+        grad = d_a2[row] * kept[row, 0:1]
         fixed[2:3] += columns_sum(grad * normed)
         fixed[3:4] += columns_sum(grad)
         dx1 = dx2[row] + normalize_back(grad, normed, rstd, vec[2:3])
@@ -879,21 +900,25 @@
     held = [refs.pop(0) for _ in parts]
     sems = refs.pop(0)
     copies = []
+    quarters = mine.shape[0]
     for at, (offset, rows, shape) in enumerate(parts):
-        target = held[at]
-        for source, side in ((mine, core), (flight, 1 - core)):
-            for quarter in range(mine.shape[0]):
-                spot = (side * mine.shape[0] + quarter) * rows
-                here = pl.ds(pl.multiple_of(spot, 16), rows)
-                for part in range(shape[-1] // 256 * (shape[0] if len(shape) == 3 else 1)):
+        target, columns, deep = held[at], shape[-1] // 256, len(shape) == 3
+        for half, (source, side) in enumerate(((mine, core), (flight, 1 - core))):
+            for quarter in range(quarters):
+                here = slice(quarter * rows, (quarter + 1) * rows)
+                for part in range(columns * (shape[0] if deep else 1)):
                     row = offset + part * rows
                     block = source[quarter, row : row + rows].astype(F32)
-                    if len(shape) == 3:
-                        target[part, here] = block
+                    if deep:
+                        target[half, part, here] = block
                     else:
-                        target[here, part * 256 : (part + 1) * 256] = block
-        copies.append(pltpu.make_async_copy(target, outs[at], sems.at[at]))
-        copies[-1].start()
+                        target[half, here, part * 256 : (part + 1) * 256] = block
+            spot = pl.ds(pl.multiple_of(side * quarters * rows, 16), quarters * rows)
+            spot = (slice(None), spot) if deep else (spot,)
+            copies.append(
+                pltpu.make_async_copy(target.at[half], outs[at].at[spot], sems.at[len(copies)])
+            )
+            copies[-1].start()
     if small:
         total = refs.pop(0)
         offset, rows = small
@@ -929,11 +954,13 @@
         copy.wait()
 
 
-def finish(chain, info, stream, small):
+def finish(chain, stream, small):
     parts = stream.parts
     shapes = [shaped(shape, F32) for _, _, shape in parts]
-    scratch = [pltpu.VMEM(shape, F32) for _, _, shape in parts]
-    scratch.append(pltpu.SemaphoreType.DMA((len(parts),)))
+    scratch = [
+        pltpu.VMEM((2,) + shape[:-2] + (shape[-2] // 2, shape[-1]), F32) for _, _, shape in parts
+    ]
+    scratch.append(pltpu.SemaphoreType.DMA((2 * len(parts),)))
     names = []
     if small:
         scratch.append(pltpu.VMEM((256, 256), F32))
@@ -941,15 +968,15 @@
     stream.mine = chain.run(
         lambda *refs: finish_kernel(parts, small[0] if small else None, refs),
         shapes + names + [shaped((8, 128), F32)],
-        [info, stream.mine, stream.flight],
+        [stream.mine, stream.flight],
         scratch,
         ADV,
         len(parts),
     )
 
 
-def advance(chain, info, streams):
-    jobs, ins, outs = [], [info], []
+def advance(chain, streams):
+    jobs, ins, outs = [], [], []
     for stream in streams:
         step = stream.steps[0][0]
         jobs.append((stream.inner, step, stream.parts))
@@ -1078,17 +1105,7 @@
     dp_bits = bits_of("dp")[1:]
     mp_first = [("mp", bit) for bit in mp_bits] + [("dp", bit) for bit in dp_bits]
     core = bit_of("dp", 1)
-    info = jnp.stack(
-        [
-            core,
-            lax.axis_index("mp") * local,
-            lengths[0],
-            lax.axis_index("mp") % 2,
-            bit_of("dp", 2),
-            bit_of("dp", 4),
-        ]
-    ).astype(jnp.int32)
-    chain = Chain()
+    chain = Chain(local)
 
     def inner_rows(size):
         return (2 * pieces, size // 1024, 256)
@@ -1101,7 +1118,7 @@
     (packed,) = cut([expand_weight, shrink_weight], [], per, own)
     late = Weights(packed, per)
     chain.link = packed
-    a1, values, gates, x1, a2, right_pre, vec, right = chain.run(
+    a1, values, gates, x1, a2, right_pre, vec, kept, valid, right = chain.run(
         pre_kernel,
         [
             shaped((tokens, width), LOW),
@@ -1111,10 +1128,12 @@
             shaped((tokens, width), LOW),
             shaped((tokens, channels), F32),
             shaped((16, width), F32),
+            shaped((tokens, 128), F32),
+            shaped((8, tokens), F32),
             shaped((tokens, channels), LOW),
         ],
         [
-            info,
+            lengths,
             cell_input,
             gated_weight,
             conv_weight,
@@ -1140,7 +1159,7 @@
             shaped((tokens, 128), F32),
             shaped((pieces - 1, width, local), LOW),
         ],
-        [info, a2, right, left_weight, own] + early_blocks,
+        [a2, right, left_weight, own, kept] + early_blocks,
         [
             pltpu.VMEM((tokens, inner), F32),
             pltpu.VMEM((tokens, 128), F32),
@@ -1164,12 +1183,29 @@
             shaped((tokens, width), LOW),
             shaped((pieces - 1, local, channels), LOW),
         ],
-        [info, x1, depth, point_weight, vec, project_weight, output_weight]
+        [x1, depth, point_weight, vec, project_weight, output_weight, valid]
         + early_blocks,
         [],
         int(4.4e9 * EARLY),
     )
-    late_blocks = late.share(a5)
+    keep_own, send_own, shrunk_own, d_a5_own, bias_own = chain.run(
+        feed_own_kernel,
+        [
+            shaped((2, 2 * local * width // 1024, 256), LOW),
+            shaped((2, 2 * local * width // 1024, 256), LOW),
+            shaped((tokens, width), F32),
+            shaped((tokens, width), F32),
+            shaped((8, local), F32),
+        ],
+        [a5, out_grad, expand_weight, shrink_weight, own],
+        [
+            pltpu.VMEM((tokens, local), LOW),
+            pltpu.VMEM((tokens, local), F32),
+            pltpu.VMEM((tokens, local), LOW),
+        ],
+        int(3e9 * EARLY),
+    )
+    late_blocks = late.share(bias_own)
     cell_output, feed_keep, feed_send, dx3, fixed, expand_sum = chain.run(
         lambda *refs: feed_kernel(pieces, per, refs),
         [
@@ -1180,17 +1216,17 @@
             shaped((16, width), F32),
             shaped((8, inner), F32),
         ],
-        [info, a5, x3, out_grad, vec, expand_weight, shrink_weight, own]
+        [a5, x3, out_grad, vec, keep_own, send_own, shrunk_own, d_a5_own, bias_own]
         + early_blocks
         + late_blocks,
         [
-            pltpu.VMEM((tokens, inner), LOW),
-            pltpu.VMEM((tokens, inner), F32),
-            pltpu.VMEM((tokens, inner), LOW),
+            pltpu.VMEM((tokens, local), LOW),
+            pltpu.VMEM((tokens, local), F32),
+            pltpu.VMEM((tokens, local), LOW),
             pltpu.VMEM((tokens, width), F32),
             pltpu.VMEM((tokens, width), F32),
-            pltpu.VMEM((pieces - 1, width, local), LOW),
-            pltpu.VMEM((pieces - 1, local, width), LOW),
+            pltpu.VMEM((width, local), LOW),
+            pltpu.VMEM((local, width), LOW),
         ],
         int(8e9 * SCALE),
     )
@@ -1213,7 +1249,7 @@
             shaped((tokens, channels), LOW),
             shaped((16, width), F32),
         ],
-        [info, dx3, attended, output_weight, qkv, lse, a4, project_weight, x2, vec, fixed],
+        [dx3, attended, output_weight, qkv, lse, a4, project_weight, x2, vec, valid, fixed],
         [
             pltpu.VMEM((tokens, width), LOW),
             pltpu.VMEM((tokens, width), LOW),
@@ -1231,7 +1267,7 @@
                 (3 * width * width // 2048, width // 8, (width, width)),
             ],
         )
-        advance(chain, info, [fee])
+        advance(chain, [fee])
     left_keep, left_send, d_a2, d_right, wide_sums = chain.run(
         lambda *refs: inner_backward_kernel(pieces, per, refs),
         [
@@ -1242,7 +1278,6 @@
             shaped((16, inner), F32),
         ],
         [
-            info,
             d_sep,
             depth,
             normed,
@@ -1255,15 +1290,17 @@
             left_weight,
             left_rest,
             own,
+            kept,
         ]
         + early_blocks,
         [
-            pltpu.VMEM((inner // 128, tokens + 16, 128), F32),
+            pltpu.VMEM((inner // 128, tokens, 128), F32),
             pltpu.VMEM((tokens + 16, 128), F32),
             pltpu.VMEM((tokens + 16, 128), F32),
             pltpu.VMEM((tokens, inner), LOW),
             pltpu.VMEM((tokens, 128), F32),
             pltpu.VMEM((tokens, 128), F32),
+            pltpu.VMEM((11, 8, inner), F32),
         ],
         int(11.5e9 * SCALE),
     )
@@ -1277,7 +1314,7 @@
                 (width * local // 1024, local // 4, (local, channels)),
             ],
         )
-        advance(chain, info, [fee])
+        advance(chain, [fee])
     small = 32 if tuned else 0
     last_rows = width * (2 * width + 3 * channels) // 2048 + small
     last_send, last_keep, input_grad, fixed = chain.run(
@@ -1289,7 +1326,6 @@
             shaped((16, width), F32),
         ],
         [
-            info,
             d_a2,
             d_right,
             right_pre,
@@ -1303,6 +1339,7 @@
             gated_weight,
             cell_input,
             vec,
+            kept,
             fixed,
             wide_sums,
         ],
@@ -1342,9 +1379,9 @@
         for names in PLAN:
             if names[0] == "!":
                 stream = groups[names[1]][0]
-                finish(chain, info, stream, small_part if names == "!d" else None)
+                finish(chain, stream, small_part if names == "!d" else None)
             else:
-                advance(chain, info, [groups[name][0] for name in names])
+                advance(chain, [groups[name][0] for name in names])
         (grad_shrink, grad_expand, _), (grad_left, grad_point, _) = fee.mine, lef.mine
         (grad_proj, grad_out, _), (grad_gated, grad_conv) = pro.mine, lat.mine[:2]
         smalls = [

time: 181 us -> 169 us (0.934)
  Pallas kernels: 73.9 us -> 51.1 us
  waiting for transfers between devices: 50 us -> 56.5 us
  starting transfers between devices: 51.8 us -> 56.5 us
    pallas_call x41 -> x42, Pallas kernels: 69.2 us -> 46.4 us  [run(): pl.pallas_call(call, out_shape=outs, in_specs=specs, out_specs=[pl.BlockS...]
    ppermute x36, waiting for transfers between devices: 43 us -> 48.9 us  [flat_swap(): lax.ppermute(values, ('dp', 'mp'), [(at, partner(at)) for at in range(cou...]
    ppermute x36, starting transfers between devices: 47.2 us -> 52 us  [flat_swap(): lax.ppermute(values, ('dp', 'mp'), [(at, partner(at)) for at in range(cou...]
  transfers between devices with their start and end apart: 42 -> 42, of which waited for: 17 -> 21; matrix products, arithmetic and copies ran while one was open for 0% -> 0% of each run, Pallas kernels for 34% -> 25%
where the time goes in v5:
time: 169 us
  starting transfers between devices  56.5 us (33%)
  waiting for transfers between devices  56.5 us (33%)
  Pallas kernels  51.1 us (30%)
  local copies, waits for them, and re-layouts  2.76 us (2%)
  between operations  2.07 us (1%)
    ppermute x36, starting transfers between devices, flat_swap(): lax.ppermute(values, ('dp', 'mp'), [(at, partner(at)) for at in range(cou...  52 us
    ppermute x36, waiting for transfers between devices, flat_swap(): lax.ppermute(values, ('dp', 'mp'), [(at, partner(at)) for at in range(cou...  48.9 us
    pallas_call x42, Pallas kernels, run(): pl.pallas_call(call, out_shape=outs, in_specs=specs, out_specs=[pl.BlockS...  46.4 us
    ppermute x6, waiting for transfers between devices, swap(): return lax.ppermute(values, axis, [(at, at ^ bit) for at in range(count)])  7.67 us
    pallas_call x2, Pallas kernels, cut(): pl.pallas_call(kernel, out_shape=outs, in_specs=[pl.BlockSpec(memory_spac...  4.68 us
    ppermute x6, starting transfers between devices, swap(): return lax.ppermute(values, axis, [(at, at ^ bit) for at in range(count)])  4.57 us
  transfers between devices with their start and end apart: 42, of which 21 were waited for; matrix products, arithmetic and copies ran while one was open for 0% of the time, Pallas kernels for 25%

profile of v5, /device:TPU:0, one launch (start us, length us, event | category | flops | bytes accessed | tf_op | source)
XLA Modules:
  0.0 169.0 jit_solution(9173612636087564293)
XLA Ops:
  0.8 2.7 %shard_map.373 = (bf16[832,256]{1,0:T(8,128)(2,1)}, bf16[64,256]{1,0:T(8,128)(2,1)}) custom-call(bf16[512,1024]{1,0:T(8,128)(2,1)} %refs_9_.3, bf16[1024,256]{1,0:T(8,128)(2,1)} %refs_7_.3, bf16[1024]{0:T(1024)(128)(2,1)} %refs_2_.7, bf16[1024]{0:T(1024)(128)(2,1)} %refs_3_.4, bf16[2,1024]{1,0:T(2,128)(2,1)} %refs_4_.3, bf16[9,1024]{1,0:T(8,128)(2,1)} %refs_5_.3), custom_call_target="tpu_custom_call" | custom-call | tf_op jit(solution)/shard_map/pallas_call | solution.py:752
  3.5 3.0 %collective-permute-start = (bf16[832,256]{1,0:T(8,128)(2,1)}, bf16[832,256]{1,0:T(8,128)(2,1)S(1)}, u32[]{:S(2)}, u32[]{:S(2)}) collective-permute-start(bf16[832,256]{1,0:T(8,128)(2,1)} %get-tuple-element.127), channel_id=1, source_target_pairs={{0,1},{1,0},{2,3},{3,2},{4,5},{5,4},{6,7},{7,6},{8,9},{9,8},{10,11... | collective-permute-start | bytes 1277960 | tf_op jit(solution)/shard_map/ppermute | solution.py:39
  12.6 3.9 %collective-permute-done.refs_5_.refs_7_.refs_9_.refs_13_ = bf16[832,256]{1,0:T(8,128)(2,1)S(1)} collective-permute-done((bf16[832,256]{1,0:T(8,128)(2,1)}, bf16[832,256]{1,0:T(8,128)(2,1)S(1)}, u32[]{:S(2)}, u32[]{:S(2)}) %collective-permute-start) | collective-permute-done | bytes 426016 | tf_op jit(solution)/shard_map/ppermute | solution.py:39
  19.8 4.9 %collective-permute-done.1.refs_6_.refs_8_.refs_10_.refs_14_ = bf16[832,256]{1,0:T(8,128)(2,1)S(1)} collective-permute-done((bf16[832,256]{1,0:T(8,128)(2,1)S(1)}, bf16[832,256]{1,0:T(8,128)(2,1)S(1)}, u32[]{:S(2)}, u32[]{:S(2)}) %collective-permute-start.1) | collective-permute-done | bytes 426016 | tf_op jit(solution)/shard_map/ppermute | solution.py:766
  26.4 4.3 %shard_map.376 = (bf16[256,2048]{1,0:T(8,128)(2,1)S(1)}, bf16[256,2048]{1,0:T(8,128)(2,1)S(1)}, bf16[256,2048]{1,0:T(8,128)(2,1)S(1)}, f32[256,128]{1,0:T(8,128)S(1)}, bf16[1,512,1024]{2,1,0:T(8,128)(2,1)S(1)}) custom-call(bf16[256,512]{1,0:T(8,128)(2,1)S(1)} %get-tuple-element.124.refs_0_.refs_5_.refs_4_, bf16[256,256]{1,0:T(8,128)(2,1)S(1)} %get-tuple-element.125.refs_1_, ...), custom_call_target="tpu_custom_call" | custom-call | flops 6500000 | bytes 7764944 | tf_op jit(solution)/shard_map/pallas_call | solution.py:175
  32.6 3.2 %shard_map.377 = (f32[256,512]{1,0:T(8,128)S(1)}, bf16[256,512]{1,0:T(8,128)(2,1)S(1)}, bf16[256,1536]{1,0:T(8,128)(2,1)S(1)}, f32[256,128]{1,0:T(8,128)S(1)}, b...) custom-call(f32[256,512]{1,0:T(8,128)S(1)} %get-tuple-element.123.re, ...), custom_call_target="tpu_custom_call" | custom-call | flops 4400000 | bytes 9304000 | tf_op jit(solution)/shard_map/pallas_call | solution.py:175
  35.9 2.1 %shard_map.378 = (bf16[2,1024,256]{2,1,0:T(8,128)(2,1)S(1)}, bf16[2,1024,256]{2,1,0:T(8,128)(2,1)S(1)}, f32[256,512]{1,0:T(8,128)S(1)}, f32[256,512]{1,0:T(8,128)S(1)}, f32[8,1024]{1,0:T(8,128)S(1)}) custom-call(bf16[256,512]{1,0:T(8,128)(2,1)S(1)} %get-tuple-element.135.refs_0_, bf16[256,512]{1,0:T(8,128)(2,1)S(1)} %copy-done.14, ...), custom_call_target="tpu_custom_call" | custom-call | flops 3000000 | bytes 5892704 | tf_op jit(solution)/shard_map/pallas_call | solution.py:175
  41.9 3.2 %shard_map.379 = (bf16[256,512]{1,0:T(8,128)(2,1)}, bf16[4,1024,256]{2,1,0:T(8,128)(2,1)S(1)}, bf16[4,1024,256]{2,1,0:T(8,128)(2,1)S(1)}, f32[256,512]{1,0:T(8,1...) custom-call(bf16[256,512]{1,0:T(8,128)(2,1)S(1)} %get-tuple-element.135.refs_0_, ...), custom_call_target="tpu_custom_call" | custom-call | flops 32000000000 | bytes 653139968 | tf_op jit(solution)/shard_map/pallas_call | solution.py:175
  45.2 5.1 %shard_map.380 = (bf16[4,512,256]{2,1,0:T(8,128)(2,1)S(1)}, bf16[4,512,256]{2,1,0:T(8,128)(2,1)S(1)}, f32[256,512]{1,0:T(8,128)S(1)}, bf16[256,256]{1,0:T(8,128)(2,1)S(1)}, f32[16,512]{1,0:T(8,128)S(1)}) custom-call(f32[256,512]{1,0:T(8,128)S(1)} %get-tuple-element.147.refs_0_, bf16[256,512]{1,0:T(8,128)(2,1)S(1)} %get-tuple-element.148.refs_1_, ...), custom_call_target="tpu_custom_call" | custom-call | flops 26800001024 | bytes 543446528 | tf_op jit(solution)/shard_map/pallas_call | solution.py:175
  53.2 8.3 %shard_map.382 = (bf16[4,768,256]{2,1,0:T(8,128)(2,1)S(1)}, bf16[4,768,256]{2,1,0:T(8,128)(2,1)}, f32[256,512]{1,0:T(8,128)S(1)}, f32[256,256]{1,0:T(8,128)S(1)}, f32[16,2048]{1,0:T(8,128)S(1)}) custom-call(bf16[256,256]{1,0:T(8,128)(2,1)S(1)} %get-tuple-element.153.refs_0_, bf16[256,2048]{1,0:T(8,128)(2,1)S(1)} %get-tuple-element.132.refs_1_, ...), custom_call_target="tpu_custom_call" | custom-call | flops 46000001024 | bytes 932812288 | tf_op jit(solution)/shard_map/pallas_call | solution.py:175
  61.4 4.8 %collective-permute-done.9.refs_1_ = bf16[2,1024,256]{2,1,0:T(8,128)(2,1)S(1)} collective-permute-done((bf16[2,1024,256]{2,1,0:T(8,128)(2,1)S(1)}, bf16[2,1024,256]{2,1,0:T(8,128)(2,1)S(1)}, u32[]{:S(2)}, u32[]{:S(2)}) %collective-permute-start.9) | collective-permute-done | bytes 1048608 | tf_op jit(solution)/shard_map/ppermute | solution.py:766
  68.3 2.8 %shard_map.384 = (bf16[4,480,256]{2,1,0:T(8,128)(2,1)S(1)}, bf16[4,480,256]{2,1,0:T(8,128)(2,1)S(1)}, f32[256,512]{1,0:T(8,128)}, f32[16,512]{1,0:T(8,128)S(1)}) custom-call(f32[256,512]{1,0:T(8,128)S(1)} %get-tuple-element.163.refs_0_, f32[256,256]{1,0:T(8,128)S(1)} %get-tuple-element.164.refs_1_, f32[256,256]{1,0:T(8,128)S(1)} %get-tuple-element.165.refs_2_, ...), custom_call_target="tpu_custom_call" | custom-call | flops 16000000000 | bytes 328617984 | tf_op jit(solution)/shard_map/pallas_call | solution.py:175
  73.0 5.5 %collective-permute-done.11.refs_1_ = bf16[1,1024,256]{2,1,0:T(8,128)(2,1)S(1)} collective-permute-done((bf16[1,1024,256]{2,1,0:T(8,128)(2,1)S(1)}, bf16[1,1024,256]{2,1,0:T(8,128)(2,1)S(1)}, u32[]{:S(2)}, u32[]{:S(2)}) %collective-permute-start.11) | collective-permute-done | bytes 524320 | tf_op jit(solution)/shard_map/ppermute | solution.py:766
  78.6 2.1 %collective-permute-start.14 = (bf16[1,512,256]{2,1,0:T(8,128)(2,1)S(1)}, bf16[1,512,256]{2,1,0:T(8,128)(2,1)S(1)}, u32[]{:S(2)}, u32[]{:S(2)}) collective-permute-start(bf16[1,512,256]{2,1,0:T(8,128)(2,1)S(1)} %get-tuple-element.184), channel_id=1, source_target_pairs={{0,8},{1,9},{2,10},{3,11},{4,12},{5,13},{6,14},{7,15},{8,0},{9,1},... | collective-permute-start | bytes 786440 | tf_op jit(solution)/shard_map/ppermute | solution.py:766
  85.1 3.1 %collective-permute-start.21 = (bf16[1,512,256]{2,1,0:T(8,128)(2,1)S(1)}, bf16[1,512,256]{2,1,0:T(8,128)(2,1)S(1)}, u32[]{:S(2)}, u32[]{:S(2)}) collective-permute-start(bf16[1,512,256]{2,1,0:T(8,128)(2,1)S(1)} %shard_map.389.refs_2_.refs_0_), channel_id=1, source_target_pairs={{0,16},{1,17},{2,18},{3,19},{4,20},{5,21},{6,22},{7,23},{8,24},{9,... | collective-permute-start | bytes 786440 | tf_op jit(solution)/shard_map/ppermute | solution.py:766
  88.2 3.9 %collective-permute-done.13.refs_1_ = bf16[2,480,256]{2,1,0:T(8,128)(2,1)S(1)} collective-permute-done((bf16[2,480,256]{2,1,0:T(8,128)(2,1)S(1)}, bf16[2,480,256]{2,1,0:T(8,128)(2,1)S(1)}, u32[]{:S(2)}, u32[]{:S(2)}) %collective-permute-start.13) | collective-permute-done | bytes 491552 | tf_op jit(solution)/shard_map/ppermute | solution.py:766
  101.8 2.2 %collective-permute-start.28 = (bf16[1,256,256]{2,1,0:T(8,128)(2,1)S(1)}, bf16[1,256,256]{2,1,0:T(8,128)(2,1)S(1)}, u32[]{:S(2)}, u32[]{:S(2)}) collective-permute-start(bf16[1,256,256]{2,1,0:T(8,128)(2,1)S(1)} %shard_map.394.refs_2_.refs_0_), channel_id=1, source_target_pairs={{0,16},{1,17},{2,18},{3,19},{4,20},{5,21},{6,22},{7,23},{8,24},{9,... | collective-permute-start | bytes 393224 | tf_op jit(solution)/shard_map/ppermute | solution.py:766
  104.1 2.0 %collective-permute-start.25 = (bf16[1,512,256]{2,1,0:T(8,128)(2,1)S(1)}, bf16[1,512,256]{2,1,0:T(8,128)(2,1)S(1)}, u32[]{:S(2)}, u32[]{:S(2)}) collective-permute-start(bf16[1,512,256]{2,1,0:T(8,128)(2,1)S(1)} %shard_map.395.refs_2_.refs_0_), channel_id=1, source_target_pairs={{0,8},{1,9},{2,10},{3,11},{4,12},{5,13},{6,14},{7,15},{8,0},{9,1},... | collective-permute-start | bytes 786440 | tf_op jit(solution)/shard_map/ppermute | solution.py:766
  106.1 3.4 %collective-permute-done.20.refs_1_ = bf16[2,768,256]{2,1,0:T(8,128)(2,1)S(1)} collective-permute-done((bf16[2,768,256]{2,1,0:T(8,128)(2,1)S(1)}, bf16[2,768,256]{2,1,0:T(8,128)(2,1)S(1)}, u32[]{:S(2)}, u32[]{:S(2)}) %collective-permute-start.20) | collective-permute-done | bytes 786464 | tf_op jit(solution)/shard_map/ppermute | solution.py:766
  109.7 2.7 %collective-permute-start.23 = (bf16[1,240,256]{2,1,0:T(8,128)(2,1)S(1)}, bf16[1,240,256]{2,1,0:T(8,128)(2,1)S(1)}, u32[]{:S(2)}, u32[]{:S(2)}) collective-permute-start(bf16[1,240,256]{2,1,0:T(8,128)(2,1)S(1)} %shard_map.397.refs_2_.refs_0_), channel_id=1, source_target_pairs={{0,16},{1,17},{2,18},{3,19},{4,20},{5,21},{6,22},{7,23},{8,24},{9,... | collective-permute-start | bytes 368648 | tf_op jit(solution)/shard_map/ppermute | solution.py:766
  112.9 4.0 %collective-permute-done.25.refs_1_ = bf16[1,512,256]{2,1,0:T(8,128)(2,1)S(1)} collective-permute-done((bf16[1,512,256]{2,1,0:T(8,128)(2,1)S(1)}, bf16[1,512,256]{2,1,0:T(8,128)(2,1)S(1)}, u32[]{:S(2)}, u32[]{:S(2)}) %collective-permute-start.25) | collective-permute-done | bytes 262176 | tf_op jit(solution)/shard_map/ppermute | solution.py:766
  124.6 5.5 %collective-permute-done.27.refs_1_ = bf16[1,384,256]{2,1,0:T(8,128)(2,1)S(1)} collective-permute-done((bf16[1,384,256]{2,1,0:T(8,128)(2,1)S(1)}, bf16[1,384,256]{2,1,0:T(8,128)(2,1)S(1)}, u32[]{:S(2)}, u32[]{:S(2)}) %collective-permute-start.27) | collective-permute-done | bytes 196640 | tf_op jit(solution)/shard_map/ppermute | solution.py:766
  130.8 2.2 %collective-permute-start.29 = (bf16[1,480,256]{2,1,0:T(8,128)(2,1)S(1)}, bf16[1,480,256]{2,1,0:T(8,128)(2,1)S(1)}, u32[]{:S(2)}, u32[]{:S(2)}) collective-permute-start(bf16[1,480,256]{2,1,0:T(8,128)(2,1)S(1)} %shard_map.403.refs_2_.refs_0_), channel_id=1, source_target_pairs={{0,4},{1,5},{2,3},{3,2},{4,0},{5,1},{6,7},{7,6},{8,12},{9,13},{10,... | collective-permute-start | bytes 737288 | tf_op jit(solution)/shard_map/ppermute | solution.py:766
  133.8 6.0 %collective-permute-done.29.refs_1_ = bf16[1,480,256]{2,1,0:T(8,128)(2,1)S(1)} collective-permute-done((bf16[1,480,256]{2,1,0:T(8,128)(2,1)S(1)}, bf16[1,480,256]{2,1,0:T(8,128)(2,1)S(1)}, u32[]{:S(2)}, u32[]{:S(2)}) %collective-permute-start.29) | collective-permute-done | bytes 245792 | tf_op jit(solution)/shard_map/ppermute | solution.py:766
  139.9 4.8 %collective-permute-start.31 = (bf16[2,480,256]{2,1,0:T(8,128)(2,1)S(1)}, bf16[2,480,256]{2,1,0:T(8,128)(2,1)S(1)}, u32[]{:S(2)}, u32[]{:S(2)}) collective-permute-start(bf16[2,480,256]{2,1,0:T(8,128)(2,1)S(1)} %shard_map.405.refs_2_.refs_0_), channel_id=1, source_target_pairs={{0,1},{1,0},{2,6},{3,7},{4,5},{5,4},{6,2},{7,3},{8,9},{9,8},{10,14... | collective-permute-start | bytes 1474568 | tf_op jit(solution)/shard_map/ppermute | solution.py:766
  145.5 4.8 %collective-permute-start.38 = (bf16[2,512,256]{2,1,0:T(8,128)(2,1)S(1)}, bf16[2,512,256]{2,1,0:T(8,128)(2,1)S(1)}, u32[]{:S(2)}, u32[]{:S(2)}) collective-permute-start(bf16[2,512,256]{2,1,0:T(8,128)(2,1)S(1)} %shard_map.407.refs_2_.refs_0_), channel_id=1, source_target_pairs={{0,1},{1,0},{2,6},{3,7},{4,5},{5,4},{6,2},{7,3},{8,9},{9,8},{10,14... | collective-permute-start | bytes 1572872 | tf_op jit(solution)/shard_map/ppermute | solution.py:766
  152.4 2.1 %collective-permute-start.37 = (bf16[1,768,256]{2,1,0:T(8,128)(2,1)S(1)}, bf16[1,768,256]{2,1,0:T(8,128)(2,1)S(1)}, u32[]{:S(2)}, u32[]{:S(2)}) collective-permute-start(bf16[1,768,256]{2,1,0:T(8,128)(2,1)S(1)} %shard_map.410.refs_2_.refs_0_), channel_id=1, source_target_pairs={{0,4},{1,5},{2,6},{3,7},{4,0},{5,1},{6,2},{7,3},{8,12},{9,13},{10,... | collective-permute-start | bytes 1179656 | tf_op jit(solution)/shard_map/ppermute | solution.py:766
  155.8 2.6 %shard_map.411 = (f32[512,1024]{1,0:T(8,128)}, f32[3,512,256]{2,1,0:T(8,128)}, f32[4,2,512]{2,1,0:T(2,128)}, f32[1,1024]{1,0:T(1,128)}, f32[1,1024]{1,0:T(1,128)...) custom-call(bf16[4,480,256]{2,1,0:T(8,128)(2,1)S(1)} %shard_map.409., ...), custom_call_target="tpu_custom_call" | custom-call | flops 20000000000 | bytes 405724160 | tf_op jit(solution)/shard_map/pallas_call | solution.py:175
  159.4 2.1 %shard_map.413 = (f32[1024,512]{1,0:T(8,128)}, f32[512,1024]{1,0:T(8,128)}, f32[8,128]{1,0:T(8,128)S(1)}) custom-call(bf16[2,1024,256]{2,1,0:T(8,128)(2,1)S(1)} %shard_map.408.refs_2_.refs_0_, bf16[2,1024,256]{2,1,0:T(8,128)(2,1)S(1)} %collective-permute-done.40.refs_1_, bf16[4,512,256]{2,1,0:T(8,128)(2,1)S(1)} %shard_map.412.refs_2_.refs_0_), custom_call_target="tpu_custom_call" | custom-call | flops 20000000000 | bytes 406295552 | tf_op jit(solution)/shard_map/pallas_call | solution.py:175
  161.9 2.1 %shard_map.414 = (f32[512,1536]{1,0:T(8,128)}, f32[512,512]{1,0:T(8,128)}, f32[8,128]{1,0:T(8,128)S(1)}) custom-call(bf16[4,512,256]{2,1,0:T(8,128)(2,1)S(1)} %shard_map.412.refs_2_.refs_0_, bf16[4,512,256]{2,1,0:T(8,128)(2,1)S(1)} %collective-permute-done.39.refs_1_, f32[8,128]{1,0:T(8,128)S(1)} %get-tuple-element.206.refs_2_), custom_call_target="tpu_custom_call" | custom-call | flops 20000000000 | bytes 406295552 | tf_op jit(solution)/shard_map/pallas_call | solution.py:175
  164.3 2.1 %collective-permute-done.41.refs_1_ = bf16[2,768,256]{2,1,0:T(8,128)(2,1)S(1)} collective-permute-done((bf16[2,768,256]{2,1,0:T(8,128)(2,1)S(1)}, bf16[2,768,256]{2,1,0:T(8,128)(2,1)S(1)}, u32[]{:S(2)}, u32[]{:S(2)}) %collective-permute-start.41) | collective-permute-done | bytes 786464 | tf_op jit(solution)/shard_map/ppermute | solution.py:766
  166.5 2.4 %shard_map.416 = (f32[512,1024]{1,0:T(8,128)}, f32[1024,256]{1,0:T(8,128)}, f32[8,128]{1,0:T(8,128)}) custom-call(bf16[2,768,256]{2,1,0:T(8,128)(2,1)S(1)} %shard_map.415.refs_0_.refs_2_, bf16[2,768,256]{2,1,0:T(8,128)(2,1)S(1)} %collective-permute-done.41.refs_1_, bf16[2,768,256]{2,1,0:T(8,128)(2,1)S(1)} %shard_map.415.refs_0_.refs_2_), custom_call_target="tpu_custom_call" | custom-call | flops 20000000000 | bytes 404722688 | tf_op jit(solution)/shard_map/pallas_call | solution.py:175
  (142 shorter events, 53.0 us)
Async XLA Ops:
  3.5 13.0 %collective-permute-start = (bf16[832,256]{1,0:T(8,128)(2,1)}, bf16[832,256]{1,0:T(8,128)(2,1)S(1)}, u32[]{:S(2)}, u32[]{:S(2)}) collective-permute-start(bf16[832,256]{1,0:T(8,128)(2,1)} %get-tuple-element.127), channel_id=1, source_target_pairs={{0,1},{1,0},{2,3},{3,2},{4,5},{5,4},{6,7},{7,6},{8,9},{9,8},{10,11... | collective-permute-start | bytes 1277960 | tf_op jit(solution)/shard_map/ppermute | solution.py:39
  16.5 8.1 %collective-permute-start.1 = (bf16[832,256]{1,0:T(8,128)(2,1)S(1)}, bf16[832,256]{1,0:T(8,128)(2,1)S(1)}, u32[]{:S(2)}, u32[]{:S(2)}) collective-permute-start(bf16[832,256]{1,0:T(8,128)(2,1)S(1)} %collective-permute-done.refs_5_.refs_7_.refs_9_.refs_13_), channel_id=1, source_target_pairs={{0,4},{1,5},{2,10},{3,11},{4,0},{5,1},{6,14},{7,15},{8,12},{9,13},... | collective-permute-start | bytes 1277960 | tf_op jit(solution)/shard_map/ppermute | solution.py:766
  18.3 12.6 %collective-permute-start.4 = (bf16[1024,256]{1,0:T(8,128)(2,1)S(1)}, bf16[1024,256]{1,0:T(8,128)(2,1)S(1)}, u32[]{:S(2)}, u32[]{:S(2)}) collective-permute-start(bf16[1024,256]{1,0:T(8,128)(2,1)S(1)} %copy-done.4), channel_id=1, source_target_pairs={{0,1},{1,0},{2,3},{3,2},{4,5},{5,4},{6,7},{7,6},{8,9},{9,8},{10,11... | collective-permute-start | bytes 1572872 | tf_op jit(solution)/shard_map/ppermute | solution.py:39
  30.8 9.2 %collective-permute-start.5 = (bf16[1024,256]{1,0:T(8,128)(2,1)S(1)}, bf16[1024,256]{1,0:T(8,128)(2,1)S(1)}, u32[]{:S(2)}, u32[]{:S(2)}) collective-permute-start(bf16[1024,256]{1,0:T(8,128)(2,1)S(1)} %collective-permute-done.4.refs_13_), channel_id=1, source_target_pairs={{0,4},{1,5},{2,10},{3,11},{4,0},{5,1},{6,14},{7,15},{8,12},{9,13},... | collective-permute-start | bytes 1572872 | tf_op jit(solution)/shard_map/ppermute | solution.py:766
  50.3 20.8 %collective-permute-start.12 = (bf16[4,512,256]{2,1,0:T(8,128)(2,1)S(1)}, bf16[4,512,256]{2,1,0:T(8,128)(2,1)S(1)}, u32[]{:S(2)}, u32[]{:S(2)}) collective-permute-start(bf16[4,512,256]{2,1,0:T(8,128)(2,1)S(1)} %get-tuple-element.178), channel_id=1, source_target_pairs={{0,2},{1,3},{2,0},{3,1},{4,6},{5,7},{6,4},{7,5},{8,10},{9,11},{10,... | collective-permute-start | bytes 3145736 | tf_op jit(solution)/shard_map/ppermute | solution.py:766
  51.4 14.9 %collective-permute-start.9 = (bf16[2,1024,256]{2,1,0:T(8,128)(2,1)S(1)}, bf16[2,1024,256]{2,1,0:T(8,128)(2,1)S(1)}, u32[]{:S(2)}, u32[]{:S(2)}) collective-permute-start(bf16[2,1024,256]{2,1,0:T(8,128)(2,1)S(1)} %get-tuple-element.171), channel_id=1, source_target_pairs={{0,1},{1,0},{2,6},{3,7},{4,5},{5,4},{6,2},{7,3},{8,9},{9,8},{10,14... | collective-permute-start | bytes 3145736 | tf_op jit(solution)/shard_map/ppermute | solution.py:766
  61.4 34.2 %collective-permute-start.17 = (bf16[4,768,256]{2,1,0:T(8,128)(2,1)}, bf16[4,768,256]{2,1,0:T(8,128)(2,1)}, u32[]{:S(2)}, u32[]{:S(2)}) collective-permute-start(bf16[4,768,256]{2,1,0:T(8,128)(2,1)} %get-tuple-element.190), channel_id=1, source_target_pairs={{0,2},{1,3},{2,0},{3,1},{4,6},{5,7},{6,4},{7,5},{8,10},{9,11},{10,... | collective-permute-start | bytes 4718600 | tf_op jit(solution)/shard_map/ppermute | solution.py:766
  66.5 12.0 %collective-permute-start.11 = (bf16[1,1024,256]{2,1,0:T(8,128)(2,1)S(1)}, bf16[1,1024,256]{2,1,0:T(8,128)(2,1)S(1)}, u32[]{:S(2)}, u32[]{:S(2)}) collective-permute-start(bf16[1,1024,256]{2,1,0:T(8,128)(2,1)S(1)} %get-tuple-element.176), channel_id=1, source_target_pairs={{0,4},{1,5},{2,3},{3,2},{4,0},{5,1},{6,7},{7,6},{8,12},{9,13},{10,... | collective-permute-start | bytes 1572872 | tf_op jit(solution)/shard_map/ppermute | solution.py:766
  71.4 9.5 %collective-permute-start.15 = (bf16[2,512,256]{2,1,0:T(8,128)(2,1)S(1)}, bf16[2,512,256]{2,1,0:T(8,128)(2,1)S(1)}, u32[]{:S(2)}, u32[]{:S(2)}) collective-permute-start(bf16[2,512,256]{2,1,0:T(8,128)(2,1)S(1)} %get-tuple-element.185), channel_id=1, source_target_pairs={{0,1},{1,0},{2,6},{3,7},{4,5},{5,4},{6,2},{7,3},{8,9},{9,8},{10,14... | collective-permute-start | bytes 1572872 | tf_op jit(solution)/shard_map/ppermute | solution.py:766
  72.9 7.7 %collective-permute-start.10 = (bf16[4,480,256]{2,1,0:T(8,128)(2,1)S(1)}, bf16[4,480,256]{2,1,0:T(8,128)(2,1)S(1)}, u32[]{:S(2)}, u32[]{:S(2)}) collective-permute-start(bf16[4,480,256]{2,1,0:T(8,128)(2,1)S(1)} %get-tuple-element.175), channel_id=1, source_target_pairs={{0,2},{1,3},{2,0},{3,1},{4,6},{5,7},{6,4},{7,5},{8,10},{9,11},{10,... | collective-permute-start | bytes 2949128 | tf_op jit(solution)/shard_map/ppermute | solution.py:766
  81.1 11.1 %collective-permute-start.18 = (bf16[1,512,256]{2,1,0:T(8,128)(2,1)S(1)}, bf16[1,512,256]{2,1,0:T(8,128)(2,1)S(1)}, u32[]{:S(2)}, u32[]{:S(2)}) collective-permute-start(bf16[1,512,256]{2,1,0:T(8,128)(2,1)S(1)} %get-tuple-element.191), channel_id=1, source_target_pairs={{0,4},{1,5},{2,3},{3,2},{4,0},{5,1},{6,7},{7,6},{8,12},{9,13},{10,... | collective-permute-start | bytes 786440 | tf_op jit(solution)/shard_map/ppermute | solution.py:766
  82.7 9.4 %collective-permute-start.13 = (bf16[2,480,256]{2,1,0:T(8,128)(2,1)S(1)}, bf16[2,480,256]{2,1,0:T(8,128)(2,1)S(1)}, u32[]{:S(2)}, u32[]{:S(2)}) collective-permute-start(bf16[2,480,256]{2,1,0:T(8,128)(2,1)S(1)} %get-tuple-element.183), channel_id=1, source_target_pairs={{0,1},{1,0},{2,6},{3,7},{4,5},{5,4},{6,2},{7,3},{8,9},{9,8},{10,14... | collective-permute-start | bytes 1474568 | tf_op jit(solution)/shard_map/ppermute | solution.py:766
  85.1 18.9 %collective-permute-start.21 = (bf16[1,512,256]{2,1,0:T(8,128)(2,1)S(1)}, bf16[1,512,256]{2,1,0:T(8,128)(2,1)S(1)}, u32[]{:S(2)}, u32[]{:S(2)}) collective-permute-start(bf16[1,512,256]{2,1,0:T(8,128)(2,1)S(1)} %shard_map.389.refs_2_.refs_0_), channel_id=1, source_target_pairs={{0,16},{1,17},{2,18},{3,19},{4,20},{5,21},{6,22},{7,23},{8,24},{9,... | collective-permute-start | bytes 786440 | tf_op jit(solution)/shard_map/ppermute | solution.py:766
  92.3 9.4 %collective-permute-start.22 = (bf16[1,256,256]{2,1,0:T(8,128)(2,1)S(1)}, bf16[1,256,256]{2,1,0:T(8,128)(2,1)S(1)}, u32[]{:S(2)}, u32[]{:S(2)}) collective-permute-start(bf16[1,256,256]{2,1,0:T(8,128)(2,1)S(1)} %get-tuple-element.197), channel_id=1, source_target_pairs={{0,8},{1,9},{2,10},{3,11},{4,12},{5,13},{6,14},{7,15},{8,0},{9,1},... | collective-permute-start | bytes 393224 | tf_op jit(solution)/shard_map/ppermute | solution.py:766
  97.5 12.1 %collective-permute-start.20 = (bf16[2,768,256]{2,1,0:T(8,128)(2,1)S(1)}, bf16[2,768,256]{2,1,0:T(8,128)(2,1)S(1)}, u32[]{:S(2)}, u32[]{:S(2)}) collective-permute-start(bf16[2,768,256]{2,1,0:T(8,128)(2,1)S(1)} %get-tuple-element.196), channel_id=1, source_target_pairs={{0,1},{1,0},{2,6},{3,7},{4,5},{5,4},{6,2},{7,3},{8,9},{9,8},{10,14... | collective-permute-start | bytes 2359304 | tf_op jit(solution)/shard_map/ppermute | solution.py:766
  100.9 8.8 %collective-permute-start.19 = (bf16[1,240,256]{2,1,0:T(8,128)(2,1)S(1)}, bf16[1,240,256]{2,1,0:T(8,128)(2,1)S(1)}, u32[]{:S(2)}, u32[]{:S(2)}) collective-permute-start(bf16[1,240,256]{2,1,0:T(8,128)(2,1)S(1)} %get-tuple-element.195), channel_id=1, source_target_pairs={{0,8},{1,9},{2,10},{3,11},{4,12},{5,13},{6,14},{7,15},{8,0},{9,1},... | collective-permute-start | bytes 368648 | tf_op jit(solution)/shard_map/ppermute | solution.py:766
  101.8 20.9 %collective-permute-start.28 = (bf16[1,256,256]{2,1,0:T(8,128)(2,1)S(1)}, bf16[1,256,256]{2,1,0:T(8,128)(2,1)S(1)}, u32[]{:S(2)}, u32[]{:S(2)}) collective-permute-start(bf16[1,256,256]{2,1,0:T(8,128)(2,1)S(1)} %shard_map.394.refs_2_.refs_0_), channel_id=1, source_target_pairs={{0,16},{1,17},{2,18},{3,19},{4,20},{5,21},{6,22},{7,23},{8,24},{9,... | collective-permute-start | bytes 393224 | tf_op jit(solution)/shard_map/ppermute | solution.py:766
  104.1 12.8 %collective-permute-start.25 = (bf16[1,512,256]{2,1,0:T(8,128)(2,1)S(1)}, bf16[1,512,256]{2,1,0:T(8,128)(2,1)S(1)}, u32[]{:S(2)}, u32[]{:S(2)}) collective-permute-start(bf16[1,512,256]{2,1,0:T(8,128)(2,1)S(1)} %shard_map.395.refs_2_.refs_0_), channel_id=1, source_target_pairs={{0,8},{1,9},{2,10},{3,11},{4,12},{5,13},{6,14},{7,15},{8,0},{9,1},... | collective-permute-start | bytes 786440 | tf_op jit(solution)/shard_map/ppermute | solution.py:766
  109.7 10.8 %collective-permute-start.23 = (bf16[1,240,256]{2,1,0:T(8,128)(2,1)S(1)}, bf16[1,240,256]{2,1,0:T(8,128)(2,1)S(1)}, u32[]{:S(2)}, u32[]{:S(2)}) collective-permute-start(bf16[1,240,256]{2,1,0:T(8,128)(2,1)S(1)} %shard_map.397.refs_2_.refs_0_), channel_id=1, source_target_pairs={{0,16},{1,17},{2,18},{3,19},{4,20},{5,21},{6,22},{7,23},{8,24},{9,... | collective-permute-start | bytes 368648 | tf_op jit(solution)/shard_map/ppermute | solution.py:766
  112.4 8.1 %collective-permute-start.24 = (bf16[1,768,256]{2,1,0:T(8,128)(2,1)S(1)}, bf16[1,768,256]{2,1,0:T(8,128)(2,1)S(1)}, u32[]{:S(2)}, u32[]{:S(2)}) collective-permute-start(bf16[1,768,256]{2,1,0:T(8,128)(2,1)S(1)} %get-tuple-element.199), channel_id=1, source_target_pairs={{0,4},{1,5},{2,3},{3,2},{4,0},{5,1},{6,7},{7,6},{8,12},{9,13},{10,... | collective-permute-start | bytes 1179656 | tf_op jit(solution)/shard_map/ppermute | solution.py:766
  117.8 32.6 %collective-permute-start.32 = (bf16[1,1024,256]{2,1,0:T(8,128)(2,1)}, bf16[1,1024,256]{2,1,0:T(8,128)(2,1)}, u32[]{:S(2)}, u32[]{:S(2)}) collective-permute-start(bf16[1,1024,256]{2,1,0:T(8,128)(2,1)} %shard_map.398.refs_2_.refs_0_), channel_id=1, source_target_pairs={{0,4},{1,5},{2,6},{3,7},{4,0},{5,1},{6,2},{7,3},{8,12},{9,13},{10,... | collective-permute-start | bytes 1572872 | tf_op jit(solution)/shard_map/ppermute | solution.py:766
  120.6 10.2 %collective-permute-start.26 = (bf16[1,240,256]{2,1,0:T(8,128)(2,1)S(1)}, bf16[1,240,256]{2,1,0:T(8,128)(2,1)S(1)}, u32[]{:S(2)}, u32[]{:S(2)}) collective-permute-start(bf16[1,240,256]{2,1,0:T(8,128)(2,1)S(1)} %shard_map.400.refs_2_.refs_0_), channel_id=1, source_target_pairs={{0,8},{1,9},{2,10},{3,11},{4,12},{5,13},{6,14},{7,15},{8,0},{9,1},... | collective-permute-start | bytes 368648 | tf_op jit(solution)/shard_map/ppermute | solution.py:766
  122.5 7.6 %collective-permute-start.27 = (bf16[1,384,256]{2,1,0:T(8,128)(2,1)S(1)}, bf16[1,384,256]{2,1,0:T(8,128)(2,1)S(1)}, u32[]{:S(2)}, u32[]{:S(2)}) collective-permute-start(bf16[1,384,256]{2,1,0:T(8,128)(2,1)S(1)} %get-tuple-element.201), channel_id=1, source_target_pairs={{0,8},{1,9},{2,10},{3,11},{4,12},{5,13},{6,14},{7,15},{8,0},{9,1},... | collective-permute-start | bytes 589832 | tf_op jit(solution)/shard_map/ppermute | solution.py:766
  122.7 10.4 %collective-permute-start.30 = (bf16[1,256,256]{2,1,0:T(8,128)(2,1)S(1)}, bf16[1,256,256]{2,1,0:T(8,128)(2,1)S(1)}, u32[]{:S(2)}, u32[]{:S(2)}) collective-permute-start(bf16[1,256,256]{2,1,0:T(8,128)(2,1)S(1)} %shard_map.401.refs_2_.refs_0_), channel_id=1, source_target_pairs={{0,8},{1,9},{2,10},{3,11},{4,12},{5,13},{6,14},{7,15},{8,0},{9,1},... | collective-permute-start | bytes 393224 | tf_op jit(solution)/shard_map/ppermute | solution.py:766
  130.2 14.6 %collective-permute-start.34 = (bf16[1,384,256]{2,1,0:T(8,128)(2,1)S(1)}, bf16[1,384,256]{2,1,0:T(8,128)(2,1)S(1)}, u32[]{:S(2)}, u32[]{:S(2)}) collective-permute-start(bf16[1,384,256]{2,1,0:T(8,128)(2,1)S(1)} %shard_map.402.refs_2_.refs_0_), channel_id=1, source_target_pairs={{0,16},{1,17},{2,18},{3,19},{4,20},{5,21},{6,22},{7,23},{8,24},{9,... | collective-permute-start | bytes 589832 | tf_op jit(solution)/shard_map/ppermute | solution.py:766
  130.8 9.0 %collective-permute-start.29 = (bf16[1,480,256]{2,1,0:T(8,128)(2,1)S(1)}, bf16[1,480,256]{2,1,0:T(8,128)(2,1)S(1)}, u32[]{:S(2)}, u32[]{:S(2)}) collective-permute-start(bf16[1,480,256]{2,1,0:T(8,128)(2,1)S(1)} %shard_map.403.refs_2_.refs_0_), channel_id=1, source_target_pairs={{0,4},{1,5},{2,3},{3,2},{4,0},{5,1},{6,7},{7,6},{8,12},{9,13},{10,... | collective-permute-start | bytes 737288 | tf_op jit(solution)/shard_map/ppermute | solution.py:766
  133.1 12.3 %collective-permute-start.33 = (bf16[1,512,256]{2,1,0:T(8,128)(2,1)S(1)}, bf16[1,512,256]{2,1,0:T(8,128)(2,1)S(1)}, u32[]{:S(2)}, u32[]{:S(2)}) collective-permute-start(bf16[1,512,256]{2,1,0:T(8,128)(2,1)S(1)} %shard_map.404.refs_2_.refs_0_), channel_id=1, source_target_pairs={{0,4},{1,5},{2,3},{3,2},{4,0},{5,1},{6,7},{7,6},{8,12},{9,13},{10,... | collective-permute-start | bytes 786440 | tf_op jit(solution)/shard_map/ppermute | solution.py:766
  139.9 11.8 %collective-permute-start.31 = (bf16[2,480,256]{2,1,0:T(8,128)(2,1)S(1)}, bf16[2,480,256]{2,1,0:T(8,128)(2,1)S(1)}, u32[]{:S(2)}, u32[]{:S(2)}) collective-permute-start(bf16[2,480,256]{2,1,0:T(8,128)(2,1)S(1)} %shard_map.405.refs_2_.refs_0_), channel_id=1, source_target_pairs={{0,1},{1,0},{2,6},{3,7},{4,5},{5,4},{6,2},{7,3},{8,9},{9,8},{10,14... | collective-permute-start | bytes 1474568 | tf_op jit(solution)/shard_map/ppermute | solution.py:766
  144.8 7.6 %collective-permute-start.36 = (bf16[1,384,256]{2,1,0:T(8,128)(2,1)S(1)}, bf16[1,384,256]{2,1,0:T(8,128)(2,1)S(1)}, u32[]{:S(2)}, u32[]{:S(2)}) collective-permute-start(bf16[1,384,256]{2,1,0:T(8,128)(2,1)S(1)} %shard_map.406.refs_2_.refs_0_), channel_id=1, source_target_pairs={{0,8},{1,9},{2,10},{3,11},{4,12},{5,13},{6,14},{7,15},{8,0},{9,1},... | collective-permute-start | bytes 589832 | tf_op jit(solution)/shard_map/ppermute | solution.py:766
  145.5 12.9 %collective-permute-start.38 = (bf16[2,512,256]{2,1,0:T(8,128)(2,1)S(1)}, bf16[2,512,256]{2,1,0:T(8,128)(2,1)S(1)}, u32[]{:S(2)}, u32[]{:S(2)}) collective-permute-start(bf16[2,512,256]{2,1,0:T(8,128)(2,1)S(1)} %shard_map.407.refs_2_.refs_0_), channel_id=1, source_target_pairs={{0,1},{1,0},{2,6},{3,7},{4,5},{5,4},{6,2},{7,3},{8,9},{9,8},{10,14... | collective-permute-start | bytes 1572872 | tf_op jit(solution)/shard_map/ppermute | solution.py:766
  151.6 7.7 %collective-permute-start.40 = (bf16[2,1024,256]{2,1,0:T(8,128)(2,1)S(1)}, bf16[2,1024,256]{2,1,0:T(8,128)(2,1)S(1)}, u32[]{:S(2)}, u32[]{:S(2)}) collective-permute-start(bf16[2,1024,256]{2,1,0:T(8,128)(2,1)S(1)} %shard_map.408.refs_2_.refs_0_), channel_id=1, source_target_pairs={{0,2},{1,3},{2,0},{3,1},{4,6},{5,7},{6,4},{7,5},{8,10},{9,11},{10,... | collective-permute-start | bytes 3145736 | tf_op jit(solution)/shard_map/ppermute | solution.py:766
  152.4 11.6 %collective-permute-start.37 = (bf16[1,768,256]{2,1,0:T(8,128)(2,1)S(1)}, bf16[1,768,256]{2,1,0:T(8,128)(2,1)S(1)}, u32[]{:S(2)}, u32[]{:S(2)}) collective-permute-start(bf16[1,768,256]{2,1,0:T(8,128)(2,1)S(1)} %shard_map.410.refs_2_.refs_0_), channel_id=1, source_target_pairs={{0,4},{1,5},{2,6},{3,7},{4,0},{5,1},{6,2},{7,3},{8,12},{9,13},{10,... | collective-permute-start | bytes 1179656 | tf_op jit(solution)/shard_map/ppermute | solution.py:766
  (33 other events, 253.1 us)

commit v6 on v5

--- a/solution.py
+++ b/solution.py
@@ -206,8 +206,8 @@
 
 
 def pre_kernel(
-    info, lengths, x_ref, gated_w, conv_w, norms, gated_b, conv_b, point_b, project_b, output_b, shrink_b,
-    a1, values, gates, x1, a2, right_pre, vec, kept, valid, right
+    info, lengths, left, own, x_ref, gated_w, conv_w, norms, gated_b, conv_b, point_b, project_b, output_b, shrink_b,
+    a1, values, gates, x1, a2, right_pre, vec, kept, valid, mixed, slope, total_ref, square, right
 ):
     width = x_ref.shape[1]
     channels = right.shape[1]
@@ -242,6 +242,10 @@
     total = first + dot(a2[...], conv_w[1]) + last + vec[10:11, 0 : right_pre.shape[1]]
     right_pre[...] = total
     right[...] = as_low(total * sigmoid(total))
+    total_ref[...] = jnp.zeros_like(total_ref)
+    square[...] = jnp.zeros_like(square)
+    right_rows = right[...].astype(F32)
+    left_piece(a2, left, (own, 0), right_rows, info[1], 0, mixed, slope, total_ref, square)
 
 
 def unpack(refs, counts):
@@ -282,37 +286,43 @@
     return ref[pl.ds(pl.multiple_of(offset + index * 16, 16), 16), lanes].astype(F32)
 
 
+def left_piece(a2, left, vectors, right_rows, offset, base, mixed, slope, total, square):
+    local = left.shape[1]
+    for col in spans(local, 256):
+        pre = dot(a2[...], left[:, col])
+        pre = pre + rows_of(vectors, col.start // 256, slice(0, 256))[0:1]
+        sigma = sigmoid(pre)
+        at = base + col.start
+        slope[:, at : at + 256] = as_low(sigma * (1.0 + pre * (1.0 - sigma)))
+        value = pre * sigma + right_rows * jnp.where(offset == at, 1.0, 0.0)
+        mixed[:, col] = value
+        total[...] += value[:, 0:128] + value[:, 128:256]
+        squared = value * value
+        square[...] += squared[:, 0:128] + squared[:, 128:256]
+
+
 def inner_forward_kernel(pieces, per, refs):
     info, refs = refs[0], refs[1:]
-    (a2, right, left, own, keep), packed, outs, scratch = unpack(
-        refs, [5, per * (pieces - 1), 5, 6]
+    (a2, right, mixed_own, slope_own, total_own, square_own, own, keep), packed, outs, scratch = unpack(
+        refs, [8, per * (pieces - 1), 5, 6]
     )
     normed_ref, slope_ref, depth, rstd_ref, left_rest = outs
     mixed, total, square, centre_ref, padded, padded_two = scratch
-    local = left.shape[1]
+    local = mixed_own.shape[1]
     inner = local * pieces
-    offset = info[1]
     skipped = a2.shape[1] * local // (256 * per) + local // per
     wide = vectors_of(own, packed, per, skipped)
     right_rows = right[...].astype(F32)
-    total[...] = jnp.zeros_like(total)
-    square[...] = jnp.zeros_like(square)
-    for piece in range(pieces):
-        if piece:
-            assemble(info, left_rest.at[piece - 1], packed[(piece - 1) * per : piece * per], 0)
-        for col in spans(local, 256):
-            weights = left[:, col] if piece == 0 else left_rest[piece - 1, :, col]
-            pre = dot(a2[...], weights)
-            pre = pre + rows_of(wide[piece], col.start // 256, slice(0, 256))[0:1]
-            sigma = sigmoid(pre)
-            at = piece * local + col.start
-            here = slice(at, at + 256)
-            slope_ref[:, here] = as_low(sigma * (1.0 + pre * (1.0 - sigma)))
-            value = pre * sigma + right_rows * jnp.where(offset == at, 1.0, 0.0)
-            mixed[:, here] = value
-            total[...] += value[:, 0:128] + value[:, 128:256]
-            squared = value * value
-            square[...] += squared[:, 0:128] + squared[:, 128:256]
+    total[...] = total_own[...]
+    square[...] = square_own[...]
+    slope_ref[:, 0:local] = slope_own[...]
+    for piece in range(1, pieces):
+        rest = left_rest.at[piece - 1]
+        assemble(info, rest, packed[(piece - 1) * per : piece * per], 0)
+        left_piece(
+            a2, rest, wide[piece], right_rows, info[1], piece * local,
+            mixed.at[piece - 1], slope_ref, total, square,
+        )
     centre = jnp.sum(total[...], 1, keepdims=True) * (1.0 / inner)
     variance = jnp.sum(square[...], 1, keepdims=True) * (1.0 / inner) - centre * centre
     rstd = lax.rsqrt(variance + EPS)
@@ -327,7 +337,9 @@
         def one(index, part, pad):
             here = at_lane(piece * local + index * 256 + part, 128)
             vectors = rows_of(wide[piece], index, slice(part, part + 128))
-            normed = (mixed[:, here] - centre_ref[...]) * rstd_ref[...]
+            source = mixed_own if piece == 0 else mixed.at[piece - 1]
+            value = source[:, at_lane(index * 256 + part, 128)]
+            normed = (value - centre_ref[...]) * rstd_ref[...]
             normed_ref[:, here] = as_low(normed)
             pad[8 : SEQ + 8] = (normed * vectors[2:3] + vectors[3:4]) * kept
             result = pad[4 : SEQ + 4] * vectors[4:5]
@@ -467,13 +479,9 @@
 
 
 def attention_backward_kernel(
-    info, dx3, attended, output_w, qkv, lse, a4, project_w, x2, vec, mask, before,
-    send, keep, dx2, d_sep, fixed, d_out, d_att, d_proj
+    info, dx3, attended, output_w, qkv, lse, mask, d_out, d_proj, d_att
 ):
-    width = x2.shape[1]
-    half = width // 2
-    core = info[0]
-    fixed[...] = before[...]
+    width = dx3.shape[1]
     d_out[...] = as_low(dx3[...])
     d_att[...] = as_low(dot_right(d_out[...], output_w[...]))
     scale = (width // HEADS) ** (-0.5)
@@ -499,6 +507,15 @@
         for kind in range(3):
             here = slice(kind * width + at, kind * width + at + 128)
             d_proj[:, here] = as_low(jnp.where(lanes < 64, parts[0][kind], parts[1][kind]))
+
+
+def project_backward_kernel(
+    info, dx3, attended, a4, d_out, d_proj, project_w, x2, vec, before, send, keep, dx2, d_sep, fixed
+):
+    width = x2.shape[1]
+    half = width // 2
+    core = info[0]
+    fixed[...] = before[...]
     for side, out in ((1 - core, send), (core, keep)):
         here = at_lane(side * half, half)
         put(out, 0, 4, 0, dot_left(a4[:, here], d_proj[...]))
@@ -714,19 +731,23 @@
             refs.pop(0)
         packed = refs.pop(0)
         own = refs.pop(0) if vectors else None
-        blocks = [refs.pop(0) for _ in weights]
-        sems = refs.pop(0)
-        held = refs.pop(0)
-        held[...] = jnp.zeros_like(held)
+        sems, held = refs
         place = own_place(per)
         copies = []
-        for at, (source, block) in enumerate(zip(sources, blocks)):
-            rows = block.shape[0]
+        offset = 0
+        for source, (rows, columns) in zip(sources, shapes):
             here = pl.ds(pl.multiple_of(place * rows, 16), rows)
-            copies.append(pltpu.make_async_copy(source.at[here], block, sems.at[at]))
-        for copy in copies:
-            copy.start()
+            for part in range(columns // 256):
+                copy = pltpu.make_async_copy(
+                    source.at[here, pl.ds(part * 256, 256)],
+                    packed.at[pl.ds(offset, rows)],
+                    sems.at[len(copies)],
+                )
+                copy.start()
+                copies.append(copy)
+                offset += rows
         if vectors:
+            held[...] = jnp.zeros_like(held)
             for part in range(local // 256):
                 lanes = slice(part * 256, (part + 1) * 256)
                 row = 0
@@ -739,12 +760,6 @@
                 packed[total + part * 16 : total + (part + 1) * 16] = chunk
         for copy in copies:
             copy.wait()
-        offset = 0
-        for block in blocks:
-            rows, columns = block.shape
-            for part in range(columns // 256):
-                packed[offset : offset + rows] = block[:, part * 256 : (part + 1) * 256]
-                offset += rows
 
     outs = [shaped((total + small, 256), LOW)]
     if vectors:
@@ -756,8 +771,10 @@
         + [pl.BlockSpec(memory_space=pltpu.VMEM) for _ in vectors]
         + [pl.BlockSpec(memory_space=pl.ANY) for _ in chained],
         out_specs=[pl.BlockSpec(memory_space=pltpu.VMEM) for _ in outs],
-        scratch_shapes=[pltpu.VMEM(shape, LOW) for shape in shapes]
-        + [pltpu.SemaphoreType.DMA((len(weights),)), pltpu.VMEM((16, 256), F32)],
+        scratch_shapes=[
+            pltpu.SemaphoreType.DMA((sum(columns // 256 for _, columns in shapes),)),
+            pltpu.VMEM((16, 256), F32),
+        ],
     )(*weights, *vectors, *chained)
 
 
@@ -806,15 +823,13 @@
     "p",
     "a",
     "d",
-    "p",
     "c",
     "d",
     "p",
     "a",
     "c",
     "d",
-    "a",
-    "c",
+    "ac",
     "d",
     "p",
     "c",
@@ -1118,7 +1133,7 @@
     (packed,) = cut([expand_weight, shrink_weight], [], per, own)
     late = Weights(packed, per)
     chain.link = packed
-    a1, values, gates, x1, a2, right_pre, vec, kept, valid, right = chain.run(
+    a1, values, gates, x1, a2, right_pre, vec, kept, valid, *parts, right = chain.run(
         pre_kernel,
         [
             shaped((tokens, width), LOW),
@@ -1130,10 +1145,16 @@
             shaped((16, width), F32),
             shaped((tokens, 128), F32),
             shaped((8, tokens), F32),
+            shaped((tokens, local), F32),
+            shaped((tokens, local), LOW),
+            shaped((tokens, 128), F32),
+            shaped((tokens, 128), F32),
             shaped((tokens, channels), LOW),
         ],
         [
             lengths,
+            left_weight,
+            own,
             cell_input,
             gated_weight,
             conv_weight,
@@ -1159,9 +1180,9 @@
             shaped((tokens, 128), F32),
             shaped((pieces - 1, width, local), LOW),
         ],
-        [a2, right, left_weight, own, kept] + early_blocks,
+        [a2, right, *parts, own, kept] + early_blocks,
         [
-            pltpu.VMEM((tokens, inner), F32),
+            pltpu.VMEM((pieces - 1, tokens, local), F32),
             pltpu.VMEM((tokens, 128), F32),
             pltpu.VMEM((tokens, 128), F32),
             pltpu.VMEM((tokens, 128), F32),
@@ -1240,8 +1261,17 @@
                 (width * local // 1024, width // 4, (width, local)),
             ],
         )
+    d_out, d_proj = chain.run(
+        attention_backward_kernel,
+        [shaped((tokens, width), LOW), shaped((tokens, 3 * width), LOW)],
+        [dx3, attended, output_weight, qkv, lse, valid],
+        [pltpu.VMEM((tokens, width), LOW)],
+        int(5e9 * SCALE),
+    )
+    if tuned:
+        advance(chain, [fee])
     proj_send, proj_keep, dx2, d_sep, fixed = chain.run(
-        attention_backward_kernel,
+        project_backward_kernel,
         [
             shaped((4, width * width // 512, 256), LOW),
             shaped((4, width * width // 512, 256), LOW),
@@ -1249,13 +1279,9 @@
             shaped((tokens, channels), LOW),
             shaped((16, width), F32),
         ],
-        [dx3, attended, output_weight, qkv, lse, a4, project_weight, x2, vec, valid, fixed],
-        [
-            pltpu.VMEM((tokens, width), LOW),
-            pltpu.VMEM((tokens, width), LOW),
-            pltpu.VMEM((tokens, 3 * width), LOW),
-        ],
-        int(6.7e9 * SCALE),
+        [dx3, attended, a4, d_out, d_proj, project_weight, x2, vec, fixed],
+        [],
+        int(3e9 * SCALE),
     )
     if tuned:
         pro = Stream(
@@ -1267,7 +1293,7 @@
                 (3 * width * width // 2048, width // 8, (width, width)),
             ],
         )
-        advance(chain, [fee])
+        advance(chain, [pro])
     left_keep, left_send, d_a2, d_right, wide_sums = chain.run(
         lambda *refs: inner_backward_kernel(pieces, per, refs),
         [

time: 169 us -> 163 us (0.964)
  starting transfers between devices: 56.5 us -> 48.2 us
  waiting for transfers between devices: 56.5 us -> 63.5 us
  Pallas kernels: 51.1 us -> 46.9 us
    ppermute x36, starting transfers between devices: 52 us -> 43.6 us  [flat_swap(): lax.ppermute(values, ('dp', 'mp'), [(at, partner(at)) for at in range(cou...]
    ppermute x36, waiting for transfers between devices: 48.9 us -> 54.5 us  [flat_swap(): lax.ppermute(values, ('dp', 'mp'), [(at, partner(at)) for at in range(cou...]
    pallas_call x42, Pallas kernels: 46.4 us -> 42.2 us  [run(): pl.pallas_call(call, out_shape=outs, in_specs=specs, out_specs=[pl.BlockS...]
  transfers between devices with their start and end apart: 42 -> 42, of which waited for: 21 -> 29; matrix products, arithmetic and copies ran while one was open for 0% -> 0% of each run, Pallas kernels for 25% -> 22%
where the time goes in v6:
time: 163 us; the launch traced here: 162 us
  waiting for transfers between devices  63.5 us (39%)
  starting transfers between devices  48.2 us (30%)
  Pallas kernels  46.9 us (29%)
  between operations  2.05 us (1%)
  local copies, waits for them, and re-layouts  1.72 us (1%)
    ppermute x36, waiting for transfers between devices, flat_swap(): lax.ppermute(values, ('dp', 'mp'), [(at, partner(at)) for at in range(cou...  54.5 us
    ppermute x36, starting transfers between devices, flat_swap(): lax.ppermute(values, ('dp', 'mp'), [(at, partner(at)) for at in range(cou...  43.6 us
    pallas_call x42, Pallas kernels, run(): pl.pallas_call(call, out_shape=outs, in_specs=specs, out_specs=[pl.BlockS...  42.2 us
    ppermute x6, waiting for transfers between devices, swap(): return lax.ppermute(values, axis, [(at, at ^ bit) for at in range(count)])  8.98 us
    pallas_call x2, Pallas kernels, cut(): pl.pallas_call(kernel, out_shape=outs, in_specs=[pl.BlockSpec(memory_spac...  4.77 us
    ppermute x6, starting transfers between devices, swap(): return lax.ppermute(values, axis, [(at, at ^ bit) for at in range(count)])  4.57 us
  transfers between devices with their start and end apart: 42, of which 29 were waited for; matrix products, arithmetic and copies ran while one was open for 0% of the time, Pallas kernels for 22%

profile of v6, /device:TPU:0, one launch (start us, length us, event | category | flops | bytes accessed | tf_op | source)
XLA Modules:
  0.0 162.3 jit_solution(10707381845265339372)
XLA Ops:
  0.8 2.8 %shard_map.373 = (bf16[832,256]{1,0:T(8,128)(2,1)}, bf16[64,256]{1,0:T(8,128)(2,1)}) custom-call(bf16[512,1024]{1,0:T(8,128)(2,1)} %refs_9_.3, bf16[1024,256]{1,0:T(8,128)(2,1)} %refs_7_.3, bf16[1024]{0:T(1024)(128)(2,1)} %refs_2_.5, bf16[1024]{0:T(1024)(128)(2,1)} %refs_3_.4, bf16[2,1024]{1,0:T(2,128)(2,1)} %refs_4_.3, bf16[9,1024]{1,0:T(8,128)(2,1)} %refs_5_.4), custom_call_target="tpu_custom_call" | custom-call | tf_op jit(solution)/shard_map/pallas_call | solution.py:767
  3.6 3.0 %collective-permute-start = (bf16[832,256]{1,0:T(8,128)(2,1)}, bf16[832,256]{1,0:T(8,128)(2,1)S(1)}, u32[]{:S(2)}, u32[]{:S(2)}) collective-permute-start(bf16[832,256]{1,0:T(8,128)(2,1)} %get-tuple-element.138), channel_id=1, source_target_pairs={{0,1},{1,0},{2,3},{3,2},{4,5},{5,4},{6,7},{7,6},{8,9},{9,8},{10,11... | collective-permute-start | bytes 1277960 | tf_op jit(solution)/shard_map/ppermute | solution.py:39
  12.3 4.4 %collective-permute-done.refs_8_.refs_7_.refs_9_.refs_13_ = bf16[832,256]{1,0:T(8,128)(2,1)S(1)} collective-permute-done((bf16[832,256]{1,0:T(8,128)(2,1)}, bf16[832,256]{1,0:T(8,128)(2,1)S(1)}, u32[]{:S(2)}, u32[]{:S(2)}) %collective-permute-start) | collective-permute-done | bytes 426016 | tf_op jit(solution)/shard_map/ppermute | solution.py:39
  19.9 4.9 %collective-permute-done.1.refs_9_.refs_8_.refs_10_.refs_14_ = bf16[832,256]{1,0:T(8,128)(2,1)S(1)} collective-permute-done((bf16[832,256]{1,0:T(8,128)(2,1)S(1)}, bf16[832,256]{1,0:T(8,128)(2,1)S(1)}, u32[]{:S(2)}, u32[]{:S(2)}) %collective-permute-start.1) | collective-permute-done | bytes 426016 | tf_op jit(solution)/shard_map/ppermute | solution.py:783
  26.5 3.7 %shard_map.376 = (bf16[256,2048]{1,0:T(8,128)(2,1)S(1)}, bf16[256,2048]{1,0:T(8,128)(2,1)S(1)}, bf16[256,2048]{1,0:T(8,128)(2,1)S(1)}, f32[256,128]{1,0:T(8,128)S(1)}, bf16[1,512,1024]{2,1,0:T(8,128)(2,1)S(1)}) custom-call(bf16[256,512]{1,0:T(8,128)(2,1)S(1)} %get-tuple-element.131.refs_0_.refs_5_.refs_4_, bf16[256,256]{1,0:T(8,128)(2,1)S(1)} %get-tuple-element.132.refs_1_, ...), custom_call_target="tpu_custom_call" | custom-call | flops 6500000 | bytes 8551376 | tf_op jit(solution)/shard_map/pallas_call | solution.py:175
  32.7 3.2 %shard_map.377 = (f32[256,512]{1,0:T(8,128)S(1)}, bf16[256,512]{1,0:T(8,128)(2,1)S(1)}, bf16[256,1536]{1,0:T(8,128)(2,1)S(1)}, f32[256,128]{1,0:T(8,128)S(1)}, b...) custom-call(f32[256,512]{1,0:T(8,128)S(1)} %get-tuple-element.130.re, ...), custom_call_target="tpu_custom_call" | custom-call | flops 4400000 | bytes 9304000 | tf_op jit(solution)/shard_map/pallas_call | solution.py:175
  36.0 2.1 %shard_map.378 = (bf16[2,1024,256]{2,1,0:T(8,128)(2,1)S(1)}, bf16[2,1024,256]{2,1,0:T(8,128)(2,1)S(1)}, f32[256,512]{1,0:T(8,128)S(1)}, f32[256,512]{1,0:T(8,128)S(1)}, f32[8,1024]{1,0:T(8,128)S(1)}) custom-call(bf16[256,512]{1,0:T(8,128)(2,1)S(1)} %get-tuple-element.146.refs_0_, bf16[256,512]{1,0:T(8,128)(2,1)S(1)} %copy-done.13, ...), custom_call_target="tpu_custom_call" | custom-call | flops 3000000 | bytes 5892704 | tf_op jit(solution)/shard_map/pallas_call | solution.py:175
  38.1 2.2 %collective-permute-done.5.refs_14_ = bf16[1024,256]{1,0:T(8,128)(2,1)S(1)} collective-permute-done((bf16[1024,256]{1,0:T(8,128)(2,1)S(1)}, bf16[1024,256]{1,0:T(8,128)(2,1)S(1)}, u32[]{:S(2)}, u32[]{:S(2)}) %collective-permute-start.5) | collective-permute-done | bytes 524320 | tf_op jit(solution)/shard_map/ppermute | solution.py:783
  42.3 3.2 %shard_map.379 = (bf16[256,512]{1,0:T(8,128)(2,1)}, bf16[4,1024,256]{2,1,0:T(8,128)(2,1)S(1)}, bf16[4,1024,256]{2,1,0:T(8,128)(2,1)S(1)}, f32[256,512]{1,0:T(8,1...) custom-call(bf16[256,512]{1,0:T(8,128)(2,1)S(1)} %get-tuple-element.146.refs_0_, ...), custom_call_target="tpu_custom_call" | custom-call | flops 32000000000 | bytes 653139968 | tf_op jit(solution)/shard_map/pallas_call | solution.py:175
  45.6 3.7 %shard_map.380 = (bf16[256,512]{1,0:T(8,128)(2,1)S(1)}, bf16[256,1536]{1,0:T(8,128)(2,1)S(1)}) custom-call(f32[256,512]{1,0:T(8,128)S(1)} %get-tuple-element.158.refs_0_, bf16[256,512]{1,0:T(8,128)(2,1)S(1)} %get-tuple-element.159.refs_1_, bf16[512,512]{1,0:T(8,128)(2,1)S(1)} %copy-done.8, bf16[256,1536]{1,0:T(8,128)(2,1)S(1)} %get-tuple-element.161.refs_3_, ...), custom_call_target="tpu_custom_call" | custom-call | flops 20000000000 | bytes 403284992 | tf_op jit(solution)/shard_map/pallas_call | solution.py:175
  56.4 7.3 %shard_map.384 = (bf16[4,768,256]{2,1,0:T(8,128)(2,1)S(1)}, bf16[4,768,256]{2,1,0:T(8,128)(2,1)S(1)}, f32[256,512]{1,0:T(8,128)S(1)}, f32[256,256]{1,0:T(8,128)S(1)}, f32[16,2048]{1,0:T(8,128)S(1)}) custom-call(bf16[256,256]{1,0:T(8,128)(2,1)S(1)} %get-tuple-element.169.refs_0_, bf16[256,2048]{1,0:T(8,128)(2,1)S(1)} %get-tuple-element.143.refs_1_, ...), custom_call_target="tpu_custom_call" | custom-call | flops 46000001024 | bytes 932812288 | tf_op jit(solution)/shard_map/pallas_call | solution.py:175
  63.7 3.2 %collective-permute-done.10.refs_1_ = bf16[2,1024,256]{2,1,0:T(8,128)(2,1)S(1)} collective-permute-done((bf16[2,1024,256]{2,1,0:T(8,128)(2,1)S(1)}, bf16[2,1024,256]{2,1,0:T(8,128)(2,1)S(1)}, u32[]{:S(2)}, u32[]{:S(2)}) %collective-permute-start.10) | collective-permute-done | bytes 1048608 | tf_op jit(solution)/shard_map/ppermute | solution.py:783
  68.7 2.8 %shard_map.386 = (bf16[4,480,256]{2,1,0:T(8,128)(2,1)S(1)}, bf16[4,480,256]{2,1,0:T(8,128)(2,1)S(1)}, f32[256,512]{1,0:T(8,128)}, f32[16,512]{1,0:T(8,128)S(1)}) custom-call(f32[256,512]{1,0:T(8,128)S(1)} %get-tuple-element.179.refs_0_, f32[256,256]{1,0:T(8,128)S(1)} %get-tuple-element.180.refs_1_, f32[256,256]{1,0:T(8,128)S(1)} %get-tuple-element.181.refs_2_, ...), custom_call_target="tpu_custom_call" | custom-call | flops 16000000000 | bytes 328617984 | tf_op jit(solution)/shard_map/pallas_call | solution.py:175
  72.0 3.6 %collective-permute-done.13.refs_1_ = bf16[2,512,256]{2,1,0:T(8,128)(2,1)S(1)} collective-permute-done((bf16[2,512,256]{2,1,0:T(8,128)(2,1)S(1)}, bf16[2,512,256]{2,1,0:T(8,128)(2,1)S(1)}, u32[]{:S(2)}, u32[]{:S(2)}) %collective-permute-start.13) | collective-permute-done | bytes 524320 | tf_op jit(solution)/shard_map/ppermute | solution.py:783
  78.8 3.3 %collective-permute-done.16.refs_1_ = bf16[1,512,256]{2,1,0:T(8,128)(2,1)S(1)} collective-permute-done((bf16[1,512,256]{2,1,0:T(8,128)(2,1)S(1)}, bf16[1,512,256]{2,1,0:T(8,128)(2,1)S(1)}, u32[]{:S(2)}, u32[]{:S(2)}) %collective-permute-start.16) | collective-permute-done | bytes 262176 | tf_op jit(solution)/shard_map/ppermute | solution.py:783
  84.7 2.0 %collective-permute-done.15.refs_1_ = bf16[1,512,256]{2,1,0:T(8,128)(2,1)S(1)} collective-permute-done((bf16[1,512,256]{2,1,0:T(8,128)(2,1)S(1)}, bf16[1,512,256]{2,1,0:T(8,128)(2,1)S(1)}, u32[]{:S(2)}, u32[]{:S(2)}) %collective-permute-start.15) | collective-permute-done | bytes 262176 | tf_op jit(solution)/shard_map/ppermute | solution.py:783
  86.8 2.7 %collective-permute-start.21 = (bf16[1,512,256]{2,1,0:T(8,128)(2,1)S(1)}, bf16[1,512,256]{2,1,0:T(8,128)(2,1)S(1)}, u32[]{:S(2)}, u32[]{:S(2)}) collective-permute-start(bf16[1,512,256]{2,1,0:T(8,128)(2,1)S(1)} %shard_map.391.refs_2_.refs_0_), channel_id=1, source_target_pairs={{0,16},{1,17},{2,18},{3,19},{4,20},{5,21},{6,22},{7,23},{8,24},{9,... | collective-permute-start | bytes 786440 | tf_op jit(solution)/shard_map/ppermute | solution.py:783
  89.5 2.6 %collective-permute-done.14.refs_1_ = bf16[2,480,256]{2,1,0:T(8,128)(2,1)S(1)} collective-permute-done((bf16[2,480,256]{2,1,0:T(8,128)(2,1)S(1)}, bf16[2,480,256]{2,1,0:T(8,128)(2,1)S(1)}, u32[]{:S(2)}, u32[]{:S(2)}) %collective-permute-start.14) | collective-permute-done | bytes 491552 | tf_op jit(solution)/shard_map/ppermute | solution.py:783
  95.7 5.5 %collective-permute-done.17.refs_1_ = bf16[1,480,256]{2,1,0:T(8,128)(2,1)S(1)} collective-permute-done((bf16[1,480,256]{2,1,0:T(8,128)(2,1)S(1)}, bf16[1,480,256]{2,1,0:T(8,128)(2,1)S(1)}, u32[]{:S(2)}, u32[]{:S(2)}) %collective-permute-start.17) | collective-permute-done | bytes 245792 | tf_op jit(solution)/shard_map/ppermute | solution.py:783
  102.4 2.7 %collective-permute-start.28 = (bf16[1,256,256]{2,1,0:T(8,128)(2,1)S(1)}, bf16[1,256,256]{2,1,0:T(8,128)(2,1)S(1)}, u32[]{:S(2)}, u32[]{:S(2)}) collective-permute-start(bf16[1,256,256]{2,1,0:T(8,128)(2,1)S(1)} %shard_map.395.refs_2_.refs_0_), channel_id=1, source_target_pairs={{0,16},{1,17},{2,18},{3,19},{4,20},{5,21},{6,22},{7,23},{8,24},{9,... | collective-permute-start | bytes 393224 | tf_op jit(solution)/shard_map/ppermute | solution.py:783
  110.2 2.1 %collective-permute-done.24.refs_1_ = bf16[1,512,256]{2,1,0:T(8,128)(2,1)S(1)} collective-permute-done((bf16[1,512,256]{2,1,0:T(8,128)(2,1)S(1)}, bf16[1,512,256]{2,1,0:T(8,128)(2,1)S(1)}, u32[]{:S(2)}, u32[]{:S(2)}) %collective-permute-start.24) | collective-permute-done | bytes 262176 | tf_op jit(solution)/shard_map/ppermute | solution.py:783
  114.9 2.5 %collective-permute-start.26 = (bf16[1,240,256]{2,1,0:T(8,128)(2,1)S(1)}, bf16[1,240,256]{2,1,0:T(8,128)(2,1)S(1)}, u32[]{:S(2)}, u32[]{:S(2)}) collective-permute-start(bf16[1,240,256]{2,1,0:T(8,128)(2,1)S(1)} %shard_map.400.refs_2_.refs_0_), channel_id=1, source_target_pairs={{0,8},{1,9},{2,10},{3,11},{4,12},{5,13},{6,14},{7,15},{8,0},{9,1},... | collective-permute-start | bytes 368648 | tf_op jit(solution)/shard_map/ppermute | solution.py:783
  117.5 2.0 %collective-permute-start.30 = (bf16[1,256,256]{2,1,0:T(8,128)(2,1)S(1)}, bf16[1,256,256]{2,1,0:T(8,128)(2,1)S(1)}, u32[]{:S(2)}, u32[]{:S(2)}) collective-permute-start(bf16[1,256,256]{2,1,0:T(8,128)(2,1)S(1)} %shard_map.401.refs_2_.refs_0_), channel_id=1, source_target_pairs={{0,8},{1,9},{2,10},{3,11},{4,12},{5,13},{6,14},{7,15},{8,0},{9,1},... | collective-permute-start | bytes 393224 | tf_op jit(solution)/shard_map/ppermute | solution.py:783
  121.0 4.6 %collective-permute-done.27.refs_1_ = bf16[1,384,256]{2,1,0:T(8,128)(2,1)S(1)} collective-permute-done((bf16[1,384,256]{2,1,0:T(8,128)(2,1)S(1)}, bf16[1,384,256]{2,1,0:T(8,128)(2,1)S(1)}, u32[]{:S(2)}, u32[]{:S(2)}) %collective-permute-start.27) | collective-permute-done | bytes 196640 | tf_op jit(solution)/shard_map/ppermute | solution.py:783
  125.7 2.0 %collective-permute-start.34 = (bf16[1,384,256]{2,1,0:T(8,128)(2,1)S(1)}, bf16[1,384,256]{2,1,0:T(8,128)(2,1)S(1)}, u32[]{:S(2)}, u32[]{:S(2)}) collective-permute-start(bf16[1,384,256]{2,1,0:T(8,128)(2,1)S(1)} %shard_map.402.refs_2_.refs_0_), channel_id=1, source_target_pairs={{0,16},{1,17},{2,18},{3,19},{4,20},{5,21},{6,22},{7,23},{8,24},{9,... | collective-permute-start | bytes 589832 | tf_op jit(solution)/shard_map/ppermute | solution.py:783
  129.9 6.7 %collective-permute-done.29.refs_1_ = bf16[1,480,256]{2,1,0:T(8,128)(2,1)S(1)} collective-permute-done((bf16[1,480,256]{2,1,0:T(8,128)(2,1)S(1)}, bf16[1,480,256]{2,1,0:T(8,128)(2,1)S(1)}, u32[]{:S(2)}, u32[]{:S(2)}) %collective-permute-start.29) | collective-permute-done | bytes 245792 | tf_op jit(solution)/shard_map/ppermute | solution.py:783
  139.4 2.8 %collective-permute-done.33.refs_1_ = bf16[1,512,256]{2,1,0:T(8,128)(2,1)S(1)} collective-permute-done((bf16[1,512,256]{2,1,0:T(8,128)(2,1)S(1)}, bf16[1,512,256]{2,1,0:T(8,128)(2,1)S(1)}, u32[]{:S(2)}, u32[]{:S(2)}) %collective-permute-start.33) | collective-permute-done | bytes 262176 | tf_op jit(solution)/shard_map/ppermute | solution.py:783
  148.3 2.6 %shard_map.411 = (f32[512,1024]{1,0:T(8,128)}, f32[3,512,256]{2,1,0:T(8,128)}, f32[4,2,512]{2,1,0:T(2,128)}, f32[1,1024]{1,0:T(1,128)}, f32[1,1024]{1,0:T(1,128)...) custom-call(bf16[4,480,256]{2,1,0:T(8,128)(2,1)S(1)} %shard_map.409., ...), custom_call_target="tpu_custom_call" | custom-call | flops 20000000000 | bytes 405724160 | tf_op jit(solution)/shard_map/pallas_call | solution.py:175
  152.4 2.1 %shard_map.413 = (f32[1024,512]{1,0:T(8,128)}, f32[512,1024]{1,0:T(8,128)}, f32[8,128]{1,0:T(8,128)S(1)}) custom-call(bf16[2,1024,256]{2,1,0:T(8,128)(2,1)S(1)} %shard_map.408.refs_2_.refs_0_, bf16[2,1024,256]{2,1,0:T(8,128)(2,1)S(1)} %collective-permute-done.40.refs_1_, bf16[4,512,256]{2,1,0:T(8,128)(2,1)S(1)} %shard_map.412.refs_2_.refs_0_), custom_call_target="tpu_custom_call" | custom-call | flops 20000000000 | bytes 406295552 | tf_op jit(solution)/shard_map/pallas_call | solution.py:175
  155.0 2.1 %shard_map.414 = (f32[512,1536]{1,0:T(8,128)}, f32[512,512]{1,0:T(8,128)}, f32[8,128]{1,0:T(8,128)S(1)}) custom-call(bf16[4,512,256]{2,1,0:T(8,128)(2,1)S(1)} %shard_map.412.refs_2_.refs_0_, bf16[4,512,256]{2,1,0:T(8,128)(2,1)S(1)} %collective-permute-done.39.refs_1_, f32[8,128]{1,0:T(8,128)S(1)} %get-tuple-element.220.refs_2_), custom_call_target="tpu_custom_call" | custom-call | flops 20000000000 | bytes 406295552 | tf_op jit(solution)/shard_map/pallas_call | solution.py:175
  157.5 2.3 %collective-permute-done.41.refs_1_ = bf16[2,768,256]{2,1,0:T(8,128)(2,1)S(1)} collective-permute-done((bf16[2,768,256]{2,1,0:T(8,128)(2,1)S(1)}, bf16[2,768,256]{2,1,0:T(8,128)(2,1)S(1)}, u32[]{:S(2)}, u32[]{:S(2)}) %collective-permute-start.41) | collective-permute-done | bytes 786464 | tf_op jit(solution)/shard_map/ppermute | solution.py:783
  159.8 2.4 %shard_map.416 = (f32[512,1024]{1,0:T(8,128)}, f32[1024,256]{1,0:T(8,128)}, f32[8,128]{1,0:T(8,128)}) custom-call(bf16[2,768,256]{2,1,0:T(8,128)(2,1)S(1)} %shard_map.415.refs_0_.refs_2_, bf16[2,768,256]{2,1,0:T(8,128)(2,1)S(1)} %collective-permute-done.41.refs_1_, bf16[2,768,256]{2,1,0:T(8,128)(2,1)S(1)} %shard_map.415.refs_0_.refs_2_), custom_call_target="tpu_custom_call" | custom-call | flops 20000000000 | bytes 404722688 | tf_op jit(solution)/shard_map/pallas_call | solution.py:175
  (140 shorter events, 57.6 us)
Async XLA Ops:
  3.6 13.0 %collective-permute-start = (bf16[832,256]{1,0:T(8,128)(2,1)}, bf16[832,256]{1,0:T(8,128)(2,1)S(1)}, u32[]{:S(2)}, u32[]{:S(2)}) collective-permute-start(bf16[832,256]{1,0:T(8,128)(2,1)} %get-tuple-element.138), channel_id=1, source_target_pairs={{0,1},{1,0},{2,3},{3,2},{4,5},{5,4},{6,7},{7,6},{8,9},{9,8},{10,11... | collective-permute-start | bytes 1277960 | tf_op jit(solution)/shard_map/ppermute | solution.py:39
  16.6 8.1 %collective-permute-start.1 = (bf16[832,256]{1,0:T(8,128)(2,1)S(1)}, bf16[832,256]{1,0:T(8,128)(2,1)S(1)}, u32[]{:S(2)}, u32[]{:S(2)}) collective-permute-start(bf16[832,256]{1,0:T(8,128)(2,1)S(1)} %collective-permute-done.refs_8_.refs_7_.refs_9_.refs_13_), channel_id=1, source_target_pairs={{0,4},{1,5},{2,10},{3,11},{4,0},{5,1},{6,14},{7,15},{8,12},{9,13},... | collective-permute-start | bytes 1277960 | tf_op jit(solution)/shard_map/ppermute | solution.py:783
  18.4 12.8 %collective-permute-start.4 = (bf16[1024,256]{1,0:T(8,128)(2,1)}, bf16[1024,256]{1,0:T(8,128)(2,1)S(1)}, u32[]{:S(2)}, u32[]{:S(2)}) collective-permute-start(bf16[1024,256]{1,0:T(8,128)(2,1)} %shard_map.374.refs_13_), channel_id=1, source_target_pairs={{0,1},{1,0},{2,3},{3,2},{4,5},{5,4},{6,7},{7,6},{8,9},{9,8},{10,11... | collective-permute-start | bytes 1572872 | tf_op jit(solution)/shard_map/ppermute | solution.py:39
  31.2 9.2 %collective-permute-start.5 = (bf16[1024,256]{1,0:T(8,128)(2,1)S(1)}, bf16[1024,256]{1,0:T(8,128)(2,1)S(1)}, u32[]{:S(2)}, u32[]{:S(2)}) collective-permute-start(bf16[1024,256]{1,0:T(8,128)(2,1)S(1)} %collective-permute-done.4.refs_13_), channel_id=1, source_target_pairs={{0,4},{1,5},{2,10},{3,11},{4,0},{5,1},{6,14},{7,15},{8,12},{9,13},... | collective-permute-start | bytes 1572872 | tf_op jit(solution)/shard_map/ppermute | solution.py:783
  52.0 14.8 %collective-permute-start.10 = (bf16[2,1024,256]{2,1,0:T(8,128)(2,1)S(1)}, bf16[2,1024,256]{2,1,0:T(8,128)(2,1)S(1)}, u32[]{:S(2)}, u32[]{:S(2)}) collective-permute-start(bf16[2,1024,256]{2,1,0:T(8,128)(2,1)S(1)} %get-tuple-element.187), channel_id=1, source_target_pairs={{0,1},{1,0},{2,6},{3,7},{4,5},{5,4},{6,2},{7,3},{8,9},{9,8},{10,14... | collective-permute-start | bytes 3145736 | tf_op jit(solution)/shard_map/ppermute | solution.py:783
  54.8 20.8 %collective-permute-start.13 = (bf16[2,512,256]{2,1,0:T(8,128)(2,1)S(1)}, bf16[2,512,256]{2,1,0:T(8,128)(2,1)S(1)}, u32[]{:S(2)}, u32[]{:S(2)}) collective-permute-start(bf16[2,512,256]{2,1,0:T(8,128)(2,1)S(1)} %get-tuple-element.193), channel_id=1, source_target_pairs={{0,1},{1,0},{2,6},{3,7},{4,5},{5,4},{6,2},{7,3},{8,9},{9,8},{10,14... | collective-permute-start | bytes 1572872 | tf_op jit(solution)/shard_map/ppermute | solution.py:783
  67.1 10.4 %collective-permute-start.12 = (bf16[1,1024,256]{2,1,0:T(8,128)(2,1)S(1)}, bf16[1,1024,256]{2,1,0:T(8,128)(2,1)S(1)}, u32[]{:S(2)}, u32[]{:S(2)}) collective-permute-start(bf16[1,1024,256]{2,1,0:T(8,128)(2,1)S(1)} %get-tuple-element.192), channel_id=1, source_target_pairs={{0,4},{1,5},{2,3},{3,2},{4,0},{5,1},{6,7},{7,6},{8,12},{9,13},{10,... | collective-permute-start | bytes 1572872 | tf_op jit(solution)/shard_map/ppermute | solution.py:783
  71.5 7.1 %collective-permute-start.11 = (bf16[4,480,256]{2,1,0:T(8,128)(2,1)S(1)}, bf16[4,480,256]{2,1,0:T(8,128)(2,1)S(1)}, u32[]{:S(2)}, u32[]{:S(2)}) collective-permute-start(bf16[4,480,256]{2,1,0:T(8,128)(2,1)S(1)} %get-tuple-element.191), channel_id=1, source_target_pairs={{0,2},{1,3},{2,0},{3,1},{4,6},{5,7},{6,4},{7,5},{8,10},{9,11},{10,... | collective-permute-start | bytes 2949128 | tf_op jit(solution)/shard_map/ppermute | solution.py:783
  71.5 22.3 %collective-permute-start.18 = (bf16[4,768,256]{2,1,0:T(8,128)(2,1)S(1)}, bf16[4,768,256]{2,1,0:T(8,128)(2,1)S(1)}, u32[]{:S(2)}, u32[]{:S(2)}) collective-permute-start(bf16[4,768,256]{2,1,0:T(8,128)(2,1)S(1)} %get-tuple-element.205), channel_id=1, source_target_pairs={{0,2},{1,3},{2,0},{3,1},{4,6},{5,7},{6,4},{7,5},{8,10},{9,11},{10,... | collective-permute-start | bytes 4718600 | tf_op jit(solution)/shard_map/ppermute | solution.py:783
  75.7 6.4 %collective-permute-start.16 = (bf16[1,512,256]{2,1,0:T(8,128)(2,1)S(1)}, bf16[1,512,256]{2,1,0:T(8,128)(2,1)S(1)}, u32[]{:S(2)}, u32[]{:S(2)}) collective-permute-start(bf16[1,512,256]{2,1,0:T(8,128)(2,1)S(1)} %get-tuple-element.200), channel_id=1, source_target_pairs={{0,4},{1,5},{2,3},{3,2},{4,0},{5,1},{6,7},{7,6},{8,12},{9,13},{10,... | collective-permute-start | bytes 786440 | tf_op jit(solution)/shard_map/ppermute | solution.py:783
  77.6 9.2 %collective-permute-start.15 = (bf16[1,512,256]{2,1,0:T(8,128)(2,1)S(1)}, bf16[1,512,256]{2,1,0:T(8,128)(2,1)S(1)}, u32[]{:S(2)}, u32[]{:S(2)}) collective-permute-start(bf16[1,512,256]{2,1,0:T(8,128)(2,1)S(1)} %get-tuple-element.199), channel_id=1, source_target_pairs={{0,8},{1,9},{2,10},{3,11},{4,12},{5,13},{6,14},{7,15},{8,0},{9,1},... | collective-permute-start | bytes 786440 | tf_op jit(solution)/shard_map/ppermute | solution.py:783
  82.2 20.1 %collective-permute-start.22 = (bf16[1,256,256]{2,1,0:T(8,128)(2,1)S(1)}, bf16[1,256,256]{2,1,0:T(8,128)(2,1)S(1)}, u32[]{:S(2)}, u32[]{:S(2)}) collective-permute-start(bf16[1,256,256]{2,1,0:T(8,128)(2,1)S(1)} %get-tuple-element.210), channel_id=1, source_target_pairs={{0,8},{1,9},{2,10},{3,11},{4,12},{5,13},{6,14},{7,15},{8,0},{9,1},... | collective-permute-start | bytes 393224 | tf_op jit(solution)/shard_map/ppermute | solution.py:783
  83.2 8.8 %collective-permute-start.14 = (bf16[2,480,256]{2,1,0:T(8,128)(2,1)S(1)}, bf16[2,480,256]{2,1,0:T(8,128)(2,1)S(1)}, u32[]{:S(2)}, u32[]{:S(2)}) collective-permute-start(bf16[2,480,256]{2,1,0:T(8,128)(2,1)S(1)} %get-tuple-element.198), channel_id=1, source_target_pairs={{0,1},{1,0},{2,6},{3,7},{4,5},{5,4},{6,2},{7,3},{8,9},{9,8},{10,14... | collective-permute-start | bytes 1474568 | tf_op jit(solution)/shard_map/ppermute | solution.py:783
  86.8 18.2 %collective-permute-start.21 = (bf16[1,512,256]{2,1,0:T(8,128)(2,1)S(1)}, bf16[1,512,256]{2,1,0:T(8,128)(2,1)S(1)}, u32[]{:S(2)}, u32[]{:S(2)}) collective-permute-start(bf16[1,512,256]{2,1,0:T(8,128)(2,1)S(1)} %shard_map.391.refs_2_.refs_0_), channel_id=1, source_target_pairs={{0,16},{1,17},{2,18},{3,19},{4,20},{5,21},{6,22},{7,23},{8,24},{9,... | collective-permute-start | bytes 786440 | tf_op jit(solution)/shard_map/ppermute | solution.py:783
  92.2 9.0 %collective-permute-start.17 = (bf16[1,480,256]{2,1,0:T(8,128)(2,1)S(1)}, bf16[1,480,256]{2,1,0:T(8,128)(2,1)S(1)}, u32[]{:S(2)}, u32[]{:S(2)}) collective-permute-start(bf16[1,480,256]{2,1,0:T(8,128)(2,1)S(1)} %get-tuple-element.203), channel_id=1, source_target_pairs={{0,4},{1,5},{2,3},{3,2},{4,0},{5,1},{6,7},{7,6},{8,12},{9,13},{10,... | collective-permute-start | bytes 737288 | tf_op jit(solution)/shard_map/ppermute | solution.py:783
  94.1 12.1 %collective-permute-start.20 = (bf16[2,768,256]{2,1,0:T(8,128)(2,1)S(1)}, bf16[2,768,256]{2,1,0:T(8,128)(2,1)S(1)}, u32[]{:S(2)}, u32[]{:S(2)}) collective-permute-start(bf16[2,768,256]{2,1,0:T(8,128)(2,1)S(1)} %get-tuple-element.209), channel_id=1, source_target_pairs={{0,1},{1,0},{2,6},{3,7},{4,5},{5,4},{6,2},{7,3},{8,9},{9,8},{10,14... | collective-permute-start | bytes 2359304 | tf_op jit(solution)/shard_map/ppermute | solution.py:783
  101.2 7.7 %collective-permute-start.19 = (bf16[1,240,256]{2,1,0:T(8,128)(2,1)S(1)}, bf16[1,240,256]{2,1,0:T(8,128)(2,1)S(1)}, u32[]{:S(2)}, u32[]{:S(2)}) collective-permute-start(bf16[1,240,256]{2,1,0:T(8,128)(2,1)S(1)} %get-tuple-element.208), channel_id=1, source_target_pairs={{0,8},{1,9},{2,10},{3,11},{4,12},{5,13},{6,14},{7,15},{8,0},{9,1},... | collective-permute-start | bytes 368648 | tf_op jit(solution)/shard_map/ppermute | solution.py:783
  102.4 15.0 %collective-permute-start.28 = (bf16[1,256,256]{2,1,0:T(8,128)(2,1)S(1)}, bf16[1,256,256]{2,1,0:T(8,128)(2,1)S(1)}, u32[]{:S(2)}, u32[]{:S(2)}) collective-permute-start(bf16[1,256,256]{2,1,0:T(8,128)(2,1)S(1)} %shard_map.395.refs_2_.refs_0_), channel_id=1, source_target_pairs={{0,16},{1,17},{2,18},{3,19},{4,20},{5,21},{6,22},{7,23},{8,24},{9,... | collective-permute-start | bytes 393224 | tf_op jit(solution)/shard_map/ppermute | solution.py:783
  105.1 7.1 %collective-permute-start.24 = (bf16[1,512,256]{2,1,0:T(8,128)(2,1)S(1)}, bf16[1,512,256]{2,1,0:T(8,128)(2,1)S(1)}, u32[]{:S(2)}, u32[]{:S(2)}) collective-permute-start(bf16[1,512,256]{2,1,0:T(8,128)(2,1)S(1)} %shard_map.396.refs_2_.refs_0_), channel_id=1, source_target_pairs={{0,8},{1,9},{2,10},{3,11},{4,12},{5,13},{6,14},{7,15},{8,0},{9,1},... | collective-permute-start | bytes 786440 | tf_op jit(solution)/shard_map/ppermute | solution.py:783
  106.4 7.8 %collective-permute-start.25 = (bf16[1,768,256]{2,1,0:T(8,128)(2,1)S(1)}, bf16[1,768,256]{2,1,0:T(8,128)(2,1)S(1)}, u32[]{:S(2)}, u32[]{:S(2)}) collective-permute-start(bf16[1,768,256]{2,1,0:T(8,128)(2,1)S(1)} %get-tuple-element.212), channel_id=1, source_target_pairs={{0,4},{1,5},{2,3},{3,2},{4,0},{5,1},{6,7},{7,6},{8,12},{9,13},{10,... | collective-permute-start | bytes 1179656 | tf_op jit(solution)/shard_map/ppermute | solution.py:783
  114.9 12.8 %collective-permute-start.26 = (bf16[1,240,256]{2,1,0:T(8,128)(2,1)S(1)}, bf16[1,240,256]{2,1,0:T(8,128)(2,1)S(1)}, u32[]{:S(2)}, u32[]{:S(2)}) collective-permute-start(bf16[1,240,256]{2,1,0:T(8,128)(2,1)S(1)} %shard_map.400.refs_2_.refs_0_), channel_id=1, source_target_pairs={{0,8},{1,9},{2,10},{3,11},{4,12},{5,13},{6,14},{7,15},{8,0},{9,1},... | collective-permute-start | bytes 368648 | tf_op jit(solution)/shard_map/ppermute | solution.py:783
  117.3 8.3 %collective-permute-start.27 = (bf16[1,384,256]{2,1,0:T(8,128)(2,1)S(1)}, bf16[1,384,256]{2,1,0:T(8,128)(2,1)S(1)}, u32[]{:S(2)}, u32[]{:S(2)}) collective-permute-start(bf16[1,384,256]{2,1,0:T(8,128)(2,1)S(1)} %get-tuple-element.214), channel_id=1, source_target_pairs={{0,8},{1,9},{2,10},{3,11},{4,12},{5,13},{6,14},{7,15},{8,0},{9,1},... | collective-permute-start | bytes 589832 | tf_op jit(solution)/shard_map/ppermute | solution.py:783
  117.5 11.8 %collective-permute-start.30 = (bf16[1,256,256]{2,1,0:T(8,128)(2,1)S(1)}, bf16[1,256,256]{2,1,0:T(8,128)(2,1)S(1)}, u32[]{:S(2)}, u32[]{:S(2)}) collective-permute-start(bf16[1,256,256]{2,1,0:T(8,128)(2,1)S(1)} %shard_map.401.refs_2_.refs_0_), channel_id=1, source_target_pairs={{0,8},{1,9},{2,10},{3,11},{4,12},{5,13},{6,14},{7,15},{8,0},{9,1},... | collective-permute-start | bytes 393224 | tf_op jit(solution)/shard_map/ppermute | solution.py:783
  119.5 24.4 %collective-permute-start.32 = (bf16[1,1024,256]{2,1,0:T(8,128)(2,1)S(1)}, bf16[1,1024,256]{2,1,0:T(8,128)(2,1)S(1)}, u32[]{:S(2)}, u32[]{:S(2)}) collective-permute-start(bf16[1,1024,256]{2,1,0:T(8,128)(2,1)S(1)} %get-tuple-element.215.refs_0_), channel_id=1, source_target_pairs={{0,4},{1,5},{2,6},{3,7},{4,0},{5,1},{6,2},{7,3},{8,12},{9,13},{10,... | collective-permute-start | bytes 1572872 | tf_op jit(solution)/shard_map/ppermute | solution.py:783
  125.7 12.6 %collective-permute-start.34 = (bf16[1,384,256]{2,1,0:T(8,128)(2,1)S(1)}, bf16[1,384,256]{2,1,0:T(8,128)(2,1)S(1)}, u32[]{:S(2)}, u32[]{:S(2)}) collective-permute-start(bf16[1,384,256]{2,1,0:T(8,128)(2,1)S(1)} %shard_map.402.refs_2_.refs_0_), channel_id=1, source_target_pairs={{0,16},{1,17},{2,18},{3,19},{4,20},{5,21},{6,22},{7,23},{8,24},{9,... | collective-permute-start | bytes 589832 | tf_op jit(solution)/shard_map/ppermute | solution.py:783
  127.7 8.9 %collective-permute-start.29 = (bf16[1,480,256]{2,1,0:T(8,128)(2,1)S(1)}, bf16[1,480,256]{2,1,0:T(8,128)(2,1)S(1)}, u32[]{:S(2)}, u32[]{:S(2)}) collective-permute-start(bf16[1,480,256]{2,1,0:T(8,128)(2,1)S(1)} %shard_map.403.refs_2_.refs_0_), channel_id=1, source_target_pairs={{0,4},{1,5},{2,3},{3,2},{4,0},{5,1},{6,7},{7,6},{8,12},{9,13},{10,... | collective-permute-start | bytes 737288 | tf_op jit(solution)/shard_map/ppermute | solution.py:783
  129.3 12.9 %collective-permute-start.33 = (bf16[1,512,256]{2,1,0:T(8,128)(2,1)S(1)}, bf16[1,512,256]{2,1,0:T(8,128)(2,1)S(1)}, u32[]{:S(2)}, u32[]{:S(2)}) collective-permute-start(bf16[1,512,256]{2,1,0:T(8,128)(2,1)S(1)} %shard_map.404.refs_2_.refs_0_), channel_id=1, source_target_pairs={{0,4},{1,5},{2,3},{3,2},{4,0},{5,1},{6,7},{7,6},{8,12},{9,13},{10,... | collective-permute-start | bytes 786440 | tf_op jit(solution)/shard_map/ppermute | solution.py:783
  136.6 8.9 %collective-permute-start.31 = (bf16[2,480,256]{2,1,0:T(8,128)(2,1)S(1)}, bf16[2,480,256]{2,1,0:T(8,128)(2,1)S(1)}, u32[]{:S(2)}, u32[]{:S(2)}) collective-permute-start(bf16[2,480,256]{2,1,0:T(8,128)(2,1)S(1)} %shard_map.405.refs_2_.refs_0_), channel_id=1, source_target_pairs={{0,1},{1,0},{2,6},{3,7},{4,5},{5,4},{6,2},{7,3},{8,9},{9,8},{10,14... | collective-permute-start | bytes 1474568 | tf_op jit(solution)/shard_map/ppermute | solution.py:783
  138.3 7.4 %collective-permute-start.36 = (bf16[1,384,256]{2,1,0:T(8,128)(2,1)S(1)}, bf16[1,384,256]{2,1,0:T(8,128)(2,1)S(1)}, u32[]{:S(2)}, u32[]{:S(2)}) collective-permute-start(bf16[1,384,256]{2,1,0:T(8,128)(2,1)S(1)} %shard_map.406.refs_2_.refs_0_), channel_id=1, source_target_pairs={{0,8},{1,9},{2,10},{3,11},{4,12},{5,13},{6,14},{7,15},{8,0},{9,1},... | collective-permute-start | bytes 589832 | tf_op jit(solution)/shard_map/ppermute | solution.py:783
  142.3 9.2 %collective-permute-start.38 = (bf16[2,512,256]{2,1,0:T(8,128)(2,1)S(1)}, bf16[2,512,256]{2,1,0:T(8,128)(2,1)S(1)}, u32[]{:S(2)}, u32[]{:S(2)}) collective-permute-start(bf16[2,512,256]{2,1,0:T(8,128)(2,1)S(1)} %shard_map.407.refs_2_.refs_0_), channel_id=1, source_target_pairs={{0,1},{1,0},{2,6},{3,7},{4,5},{5,4},{6,2},{7,3},{8,9},{9,8},{10,14... | collective-permute-start | bytes 1572872 | tf_op jit(solution)/shard_map/ppermute | solution.py:783
  144.0 8.4 %collective-permute-start.40 = (bf16[2,1024,256]{2,1,0:T(8,128)(2,1)S(1)}, bf16[2,1024,256]{2,1,0:T(8,128)(2,1)S(1)}, u32[]{:S(2)}, u32[]{:S(2)}) collective-permute-start(bf16[2,1024,256]{2,1,0:T(8,128)(2,1)S(1)} %shard_map.408.refs_2_.refs_0_), channel_id=1, source_target_pairs={{0,2},{1,3},{2,0},{3,1},{4,6},{5,7},{6,4},{7,5},{8,10},{9,11},{10,... | collective-permute-start | bytes 3145736 | tf_op jit(solution)/shard_map/ppermute | solution.py:783
  145.8 11.6 %collective-permute-start.37 = (bf16[1,768,256]{2,1,0:T(8,128)(2,1)S(1)}, bf16[1,768,256]{2,1,0:T(8,128)(2,1)S(1)}, u32[]{:S(2)}, u32[]{:S(2)}) collective-permute-start(bf16[1,768,256]{2,1,0:T(8,128)(2,1)S(1)} %shard_map.410.refs_2_.refs_0_), channel_id=1, source_target_pairs={{0,4},{1,5},{2,6},{3,7},{4,0},{5,1},{6,2},{7,3},{8,12},{9,13},{10,... | collective-permute-start | bytes 1179656 | tf_op jit(solution)/shard_map/ppermute | solution.py:783
  (32 other events, 222.8 us)

commit v7 on v6

--- a/solution.py
+++ b/solution.py
@@ -793,6 +793,17 @@
     "far": lambda at: at ^ 16,
     "hop": lambda at: at ^ (8 if at & 2 else 4),
 }
+LENGTH_FIRST_STEPS = [
+    ("half_near", "near"),
+    ("quarter", "first"),
+    ("half_mix", "second"),
+    ("sum", "far"),
+    ("sum", "second"),
+    ("join_mix", "first"),
+    ("spread", "near"),
+    ("join_near", "core"),
+    ("final", None),
+]
 INNER_STEPS = [
     ("quarter", "first"),
     ("half_mix", "second"),
@@ -818,20 +829,20 @@
 
 PLAN = (
     "p",
+    "d",
+    "a",
+    "p",
+    "c",
     "a",
     "d",
-    "p",
-    "a",
-    "d",
-    "c",
     "d",
     "p",
     "a",
     "c",
     "d",
-    "ac",
-    "d",
-    "p",
+    "a",
+    "c",
+    "dp",
     "c",
     "d",
     "p",
@@ -851,11 +862,11 @@
 
 
 class Stream:
-    def __init__(self, inner, mine, other, parts):
+    def __init__(self, inner, mine, other, parts, steps=None):
         self.inner = inner
         self.mine = mine
         self.flight = flat_swap(other, PARTNERS["core"])
-        self.steps = list(INNER_STEPS if inner else SHARED_STEPS)
+        self.steps = list(steps or (INNER_STEPS if inner else SHARED_STEPS))
         self.parts = parts
 
 
@@ -885,14 +896,16 @@
             rows = keep.shape[1]
             for out, side in ((send, 1 - near), (keep, near)):
                 here = pl.ds(pl.multiple_of(side * rows, 16), rows)
-                out[0] = as_low(mine[0, here].astype(F32) + flight[0, here].astype(F32))
+                for at in range(keep.shape[0]):
+                    out[at] = as_low(mine[at, here].astype(F32) + flight[at, here].astype(F32))
         elif step == "sum":
             outs.pop(0)[0] = added(0)
         elif step == "join_near":
             out = outs.pop(0)
             rows = mine.shape[1]
-            out[0, pl.ds(pl.multiple_of(near * rows, 16), rows)] = mine[0]
-            out[0, pl.ds(pl.multiple_of((1 - near) * rows, 16), rows)] = flight[0]
+            for source, side in ((mine, near), (flight, 1 - near)):
+                for at in range(mine.shape[0]):
+                    out[at, pl.ds(pl.multiple_of(side * rows, 16), rows)] = source[at]
         elif step in ("join_y", "join_mix"):
             out = outs.pop(0)
             side = y if step == "join_y" else mix
@@ -1292,6 +1305,7 @@
                 (0, width // 8, (width, 3 * width)),
                 (3 * width * width // 2048, width // 8, (width, width)),
             ],
+            LENGTH_FIRST_STEPS,
         )
         advance(chain, [pro])
     left_keep, left_send, d_a2, d_right, wide_sums = chain.run(

time: 163 us -> 162 us (level)
  waiting for transfers between devices: 63.5 us -> 59 us
  starting transfers between devices: 48.2 us -> 50.4 us
  Pallas kernels: 46.9 us -> 48.9 us
    ppermute x36, waiting for transfers between devices: 54.5 us -> 50 us  [flat_swap(): lax.ppermute(values, ('dp', 'mp'), [(at, partner(at)) for at in range(cou...]
    ppermute x36, starting transfers between devices: 43.6 us -> 45.8 us  [flat_swap(): lax.ppermute(values, ('dp', 'mp'), [(at, partner(at)) for at in range(cou...]
    pallas_call x42, Pallas kernels: 42.2 us -> 44.2 us  [run(): pl.pallas_call(call, out_shape=outs, in_specs=specs, out_specs=[pl.BlockS...]
  transfers between devices with their start and end apart: 42 -> 42, of which waited for: 29 -> 26; matrix products, arithmetic and copies ran while one was open for 0% -> 0% of each run, Pallas kernels for 22% -> 24%
where the time goes in v7:
time: 162 us
  waiting for transfers between devices  59 us (36%)
  starting transfers between devices  50.4 us (31%)
  Pallas kernels  48.9 us (30%)
  between operations  2.07 us (1%)
  local copies, waits for them, and re-layouts  1.72 us (1%)
    ppermute x36, waiting for transfers between devices, flat_swap(): lax.ppermute(values, ('dp', 'mp'), [(at, partner(at)) for at in range(cou...  50 us
    ppermute x36, starting transfers between devices, flat_swap(): lax.ppermute(values, ('dp', 'mp'), [(at, partner(at)) for at in range(cou...  45.8 us
    pallas_call x42, Pallas kernels, run(): pl.pallas_call(call, out_shape=outs, in_specs=specs, out_specs=[pl.BlockS...  44.2 us
    ppermute x6, waiting for transfers between devices, swap(): return lax.ppermute(values, axis, [(at, at ^ bit) for at in range(count)])  8.98 us
    pallas_call x2, Pallas kernels, cut(): pl.pallas_call(kernel, out_shape=outs, in_specs=[pl.BlockSpec(memory_spac...  4.77 us
    ppermute x6, starting transfers between devices, swap(): return lax.ppermute(values, axis, [(at, at ^ bit) for at in range(count)])  4.57 us
  transfers between devices with their start and end apart: 42, of which 26 were waited for; matrix products, arithmetic and copies ran while one was open for 0% of the time, Pallas kernels for 24%

profile of v7, /device:TPU:0, one launch (start us, length us, event | category | flops | bytes accessed | tf_op | source)
XLA Modules:
  0.0 162.2 jit_solution(11523783270187060430)
XLA Ops:
  0.8 2.8 %shard_map.373 = (bf16[832,256]{1,0:T(8,128)(2,1)}, bf16[64,256]{1,0:T(8,128)(2,1)}) custom-call(bf16[512,1024]{1,0:T(8,128)(2,1)} %refs_9_.3, bf16[1024,256]{1,0:T(8,128)(2,1)} %refs_7_.3, bf16[1024]{0:T(1024)(128)(2,1)} %refs_2_.5, bf16[1024]{0:T(1024)(128)(2,1)} %refs_3_.4, bf16[2,1024]{1,0:T(2,128)(2,1)} %refs_4_.3, bf16[9,1024]{1,0:T(8,128)(2,1)} %refs_5_.4), custom_call_target="tpu_custom_call" | custom-call | tf_op jit(solution)/shard_map/pallas_call | solution.py:767
  3.6 3.0 %collective-permute-start = (bf16[832,256]{1,0:T(8,128)(2,1)}, bf16[832,256]{1,0:T(8,128)(2,1)S(1)}, u32[]{:S(2)}, u32[]{:S(2)}) collective-permute-start(bf16[832,256]{1,0:T(8,128)(2,1)} %get-tuple-element.139), channel_id=1, source_target_pairs={{0,1},{1,0},{2,3},{3,2},{4,5},{5,4},{6,7},{7,6},{8,9},{9,8},{10,11... | collective-permute-start | bytes 1277960 | tf_op jit(solution)/shard_map/ppermute | solution.py:39
  12.3 4.4 %collective-permute-done.refs_8_.refs_7_.refs_9_.refs_13_ = bf16[832,256]{1,0:T(8,128)(2,1)S(1)} collective-permute-done((bf16[832,256]{1,0:T(8,128)(2,1)}, bf16[832,256]{1,0:T(8,128)(2,1)S(1)}, u32[]{:S(2)}, u32[]{:S(2)}) %collective-permute-start) | collective-permute-done | bytes 426016 | tf_op jit(solution)/shard_map/ppermute | solution.py:39
  19.9 4.9 %collective-permute-done.1.refs_9_.refs_8_.refs_10_.refs_14_ = bf16[832,256]{1,0:T(8,128)(2,1)S(1)} collective-permute-done((bf16[832,256]{1,0:T(8,128)(2,1)S(1)}, bf16[832,256]{1,0:T(8,128)(2,1)S(1)}, u32[]{:S(2)}, u32[]{:S(2)}) %collective-permute-start.1) | collective-permute-done | bytes 426016 | tf_op jit(solution)/shard_map/ppermute | solution.py:783
  26.5 3.7 %shard_map.376 = (bf16[256,2048]{1,0:T(8,128)(2,1)S(1)}, bf16[256,2048]{1,0:T(8,128)(2,1)S(1)}, bf16[256,2048]{1,0:T(8,128)(2,1)S(1)}, f32[256,128]{1,0:T(8,128)S(1)}, bf16[1,512,1024]{2,1,0:T(8,128)(2,1)S(1)}) custom-call(bf16[256,512]{1,0:T(8,128)(2,1)S(1)} %get-tuple-element.132.refs_0_.refs_5_.refs_4_, bf16[256,256]{1,0:T(8,128)(2,1)S(1)} %get-tuple-element.133.refs_1_, ...), custom_call_target="tpu_custom_call" | custom-call | flops 6500000 | bytes 8551376 | tf_op jit(solution)/shard_map/pallas_call | solution.py:175
  32.7 3.2 %shard_map.377 = (f32[256,512]{1,0:T(8,128)S(1)}, bf16[256,512]{1,0:T(8,128)(2,1)S(1)}, bf16[256,1536]{1,0:T(8,128)(2,1)S(1)}, f32[256,128]{1,0:T(8,128)S(1)}, b...) custom-call(f32[256,512]{1,0:T(8,128)S(1)} %get-tuple-element.131.re, ...), custom_call_target="tpu_custom_call" | custom-call | flops 4400000 | bytes 9304000 | tf_op jit(solution)/shard_map/pallas_call | solution.py:175
  36.0 2.1 %shard_map.378 = (bf16[2,1024,256]{2,1,0:T(8,128)(2,1)S(1)}, bf16[2,1024,256]{2,1,0:T(8,128)(2,1)S(1)}, f32[256,512]{1,0:T(8,128)S(1)}, f32[256,512]{1,0:T(8,128)S(1)}, f32[8,1024]{1,0:T(8,128)S(1)}) custom-call(bf16[256,512]{1,0:T(8,128)(2,1)S(1)} %get-tuple-element.147.refs_0_, bf16[256,512]{1,0:T(8,128)(2,1)S(1)} %copy-done.13, ...), custom_call_target="tpu_custom_call" | custom-call | flops 3000000 | bytes 5892704 | tf_op jit(solution)/shard_map/pallas_call | solution.py:175
  38.1 2.2 %collective-permute-done.5.refs_14_ = bf16[1024,256]{1,0:T(8,128)(2,1)S(1)} collective-permute-done((bf16[1024,256]{1,0:T(8,128)(2,1)S(1)}, bf16[1024,256]{1,0:T(8,128)(2,1)S(1)}, u32[]{:S(2)}, u32[]{:S(2)}) %collective-permute-start.5) | collective-permute-done | bytes 524320 | tf_op jit(solution)/shard_map/ppermute | solution.py:783
  42.3 3.2 %shard_map.379 = (bf16[256,512]{1,0:T(8,128)(2,1)}, bf16[4,1024,256]{2,1,0:T(8,128)(2,1)S(1)}, bf16[4,1024,256]{2,1,0:T(8,128)(2,1)S(1)}, f32[256,512]{1,0:T(8,1...) custom-call(bf16[256,512]{1,0:T(8,128)(2,1)S(1)} %get-tuple-element.147.refs_0_, ...), custom_call_target="tpu_custom_call" | custom-call | flops 32000000000 | bytes 653139968 | tf_op jit(solution)/shard_map/pallas_call | solution.py:175
  45.6 3.7 %shard_map.380 = (bf16[256,512]{1,0:T(8,128)(2,1)S(1)}, bf16[256,1536]{1,0:T(8,128)(2,1)S(1)}) custom-call(f32[256,512]{1,0:T(8,128)S(1)} %get-tuple-element.159.refs_0_, bf16[256,512]{1,0:T(8,128)(2,1)S(1)} %get-tuple-element.160.refs_1_, bf16[512,512]{1,0:T(8,128)(2,1)S(1)} %copy-done.8, bf16[256,1536]{1,0:T(8,128)(2,1)S(1)} %get-tuple-element.162.refs_3_, ...), custom_call_target="tpu_custom_call" | custom-call | flops 20000000000 | bytes 403284992 | tf_op jit(solution)/shard_map/pallas_call | solution.py:175
  55.8 7.3 %shard_map.384 = (bf16[4,768,256]{2,1,0:T(8,128)(2,1)S(1)}, bf16[4,768,256]{2,1,0:T(8,128)(2,1)S(1)}, f32[256,512]{1,0:T(8,128)S(1)}, f32[256,256]{1,0:T(8,128)S(1)}, f32[16,2048]{1,0:T(8,128)S(1)}) custom-call(bf16[256,256]{1,0:T(8,128)(2,1)S(1)} %get-tuple-element.170.refs_0_, bf16[256,2048]{1,0:T(8,128)(2,1)S(1)} %get-tuple-element.144.refs_1_, ...), custom_call_target="tpu_custom_call" | custom-call | flops 46000001024 | bytes 932812288 | tf_op jit(solution)/shard_map/pallas_call | solution.py:175
  63.1 3.7 %collective-permute-done.10.refs_1_ = bf16[2,1024,256]{2,1,0:T(8,128)(2,1)S(1)} collective-permute-done((bf16[2,1024,256]{2,1,0:T(8,128)(2,1)S(1)}, bf16[2,1024,256]{2,1,0:T(8,128)(2,1)S(1)}, u32[]{:S(2)}, u32[]{:S(2)}) %collective-permute-start.10) | collective-permute-done | bytes 1048608 | tf_op jit(solution)/shard_map/ppermute | solution.py:783
  68.7 2.8 %shard_map.386 = (bf16[4,480,256]{2,1,0:T(8,128)(2,1)S(1)}, bf16[4,480,256]{2,1,0:T(8,128)(2,1)S(1)}, f32[256,512]{1,0:T(8,128)}, f32[16,512]{1,0:T(8,128)S(1)}) custom-call(f32[256,512]{1,0:T(8,128)S(1)} %get-tuple-element.180.refs_0_, f32[256,256]{1,0:T(8,128)S(1)} %get-tuple-element.181.refs_1_, f32[256,256]{1,0:T(8,128)S(1)} %get-tuple-element.182.refs_2_, ...), custom_call_target="tpu_custom_call" | custom-call | flops 16000000000 | bytes 328617984 | tf_op jit(solution)/shard_map/pallas_call | solution.py:175
  74.3 3.5 %collective-permute-done.14.refs_1_ = bf16[1,1024,256]{2,1,0:T(8,128)(2,1)S(1)} collective-permute-done((bf16[1,1024,256]{2,1,0:T(8,128)(2,1)S(1)}, bf16[1,1024,256]{2,1,0:T(8,128)(2,1)S(1)}, u32[]{:S(2)}, u32[]{:S(2)}) %collective-permute-start.14) | collective-permute-done | bytes 524320 | tf_op jit(solution)/shard_map/ppermute | solution.py:783
  80.9 3.4 %collective-permute-done.15.refs_1_ = bf16[1,512,256]{2,1,0:T(8,128)(2,1)S(1)} collective-permute-done((bf16[1,512,256]{2,1,0:T(8,128)(2,1)S(1)}, bf16[1,512,256]{2,1,0:T(8,128)(2,1)S(1)}, u32[]{:S(2)}, u32[]{:S(2)}) %collective-permute-start.15) | collective-permute-done | bytes 262176 | tf_op jit(solution)/shard_map/ppermute | solution.py:783
  84.4 3.8 %collective-permute-done.13.refs_1_ = bf16[2,480,256]{2,1,0:T(8,128)(2,1)S(1)} collective-permute-done((bf16[2,480,256]{2,1,0:T(8,128)(2,1)S(1)}, bf16[2,480,256]{2,1,0:T(8,128)(2,1)S(1)}, u32[]{:S(2)}, u32[]{:S(2)}) %collective-permute-start.13) | collective-permute-done | bytes 491552 | tf_op jit(solution)/shard_map/ppermute | solution.py:783
  88.3 3.1 %collective-permute-start.18 = (bf16[1,480,256]{2,1,0:T(8,128)(2,1)S(1)}, bf16[1,480,256]{2,1,0:T(8,128)(2,1)S(1)}, u32[]{:S(2)}, u32[]{:S(2)}) collective-permute-start(bf16[1,480,256]{2,1,0:T(8,128)(2,1)S(1)} %get-tuple-element.207), channel_id=1, source_target_pairs={{0,4},{1,5},{2,3},{3,2},{4,0},{5,1},{6,7},{7,6},{8,12},{9,13},{10,... | collective-permute-start | bytes 737288 | tf_op jit(solution)/shard_map/ppermute | solution.py:783
  91.4 2.6 %collective-permute-start.21 = (bf16[1,512,256]{2,1,0:T(8,128)(2,1)S(1)}, bf16[1,512,256]{2,1,0:T(8,128)(2,1)S(1)}, u32[]{:S(2)}, u32[]{:S(2)}) collective-permute-start(bf16[1,512,256]{2,1,0:T(8,128)(2,1)S(1)} %shard_map.392.refs_2_.refs_0_), channel_id=1, source_target_pairs={{0,16},{1,17},{2,18},{3,19},{4,20},{5,21},{6,22},{7,23},{8,24},{9,... | collective-permute-start | bytes 786440 | tf_op jit(solution)/shard_map/ppermute | solution.py:783
  95.5 2.7 %collective-permute-done.18.refs_1_ = bf16[1,480,256]{2,1,0:T(8,128)(2,1)S(1)} collective-permute-done((bf16[1,480,256]{2,1,0:T(8,128)(2,1)S(1)}, bf16[1,480,256]{2,1,0:T(8,128)(2,1)S(1)}, u32[]{:S(2)}, u32[]{:S(2)}) %collective-permute-start.18) | collective-permute-done | bytes 245792 | tf_op jit(solution)/shard_map/ppermute | solution.py:783
  101.1 2.6 %collective-permute-start.24 = (bf16[1,256,256]{2,1,0:T(8,128)(2,1)S(1)}, bf16[1,256,256]{2,1,0:T(8,128)(2,1)S(1)}, u32[]{:S(2)}, u32[]{:S(2)}) collective-permute-start(bf16[1,256,256]{2,1,0:T(8,128)(2,1)S(1)} %shard_map.395.refs_2_), channel_id=1, source_target_pairs={{0,16},{1,17},{2,18},{3,19},{4,20},{5,21},{6,22},{7,23},{8,24},{9,... | collective-permute-start | bytes 393224 | tf_op jit(solution)/shard_map/ppermute | solution.py:783
  107.9 2.2 %collective-permute-start.25 = (bf16[1,768,256]{2,1,0:T(8,128)(2,1)S(1)}, bf16[1,768,256]{2,1,0:T(8,128)(2,1)S(1)}, u32[]{:S(2)}, u32[]{:S(2)}) collective-permute-start(bf16[1,768,256]{2,1,0:T(8,128)(2,1)S(1)} %get-tuple-element.213), channel_id=1, source_target_pairs={{0,4},{1,5},{2,3},{3,2},{4,0},{5,1},{6,7},{7,6},{8,12},{9,13},{10,... | collective-permute-start | bytes 1179656 | tf_op jit(solution)/shard_map/ppermute | solution.py:783
  110.1 3.3 %collective-permute-done.26.refs_1_ = bf16[1,512,256]{2,1,0:T(8,128)(2,1)S(1)} collective-permute-done((bf16[1,512,256]{2,1,0:T(8,128)(2,1)S(1)}, bf16[1,512,256]{2,1,0:T(8,128)(2,1)S(1)}, u32[]{:S(2)}, u32[]{:S(2)}) %collective-permute-start.26) | collective-permute-done | bytes 262176 | tf_op jit(solution)/shard_map/ppermute | solution.py:783
  114.2 2.6 %collective-permute-start.32 = (bf16[1,1024,256]{2,1,0:T(8,128)(2,1)}, bf16[1,1024,256]{2,1,0:T(8,128)(2,1)}, u32[]{:S(2)}, u32[]{:S(2)}) collective-permute-start(bf16[1,1024,256]{2,1,0:T(8,128)(2,1)} %shard_map.399.refs_2_.refs_0_), channel_id=1, source_target_pairs={{0,4},{1,5},{2,6},{3,7},{4,0},{5,1},{6,2},{7,3},{8,12},{9,13},{10,... | collective-permute-start | bytes 1572872 | tf_op jit(solution)/shard_map/ppermute | solution.py:783
  122.6 3.3 %collective-permute-done.28.refs_1_ = bf16[1,384,256]{2,1,0:T(8,128)(2,1)S(1)} collective-permute-done((bf16[1,384,256]{2,1,0:T(8,128)(2,1)S(1)}, bf16[1,384,256]{2,1,0:T(8,128)(2,1)S(1)}, u32[]{:S(2)}, u32[]{:S(2)}) %collective-permute-start.28) | collective-permute-done | bytes 196640 | tf_op jit(solution)/shard_map/ppermute | solution.py:783
  131.3 4.9 %collective-permute-done.29.refs_1_ = bf16[1,480,256]{2,1,0:T(8,128)(2,1)S(1)} collective-permute-done((bf16[1,480,256]{2,1,0:T(8,128)(2,1)S(1)}, bf16[1,480,256]{2,1,0:T(8,128)(2,1)S(1)}, u32[]{:S(2)}, u32[]{:S(2)}) %collective-permute-start.29) | collective-permute-done | bytes 245792 | tf_op jit(solution)/shard_map/ppermute | solution.py:783
  141.3 3.9 %collective-permute-done.31.refs_1_ = bf16[2,480,256]{2,1,0:T(8,128)(2,1)S(1)} collective-permute-done((bf16[2,480,256]{2,1,0:T(8,128)(2,1)S(1)}, bf16[2,480,256]{2,1,0:T(8,128)(2,1)S(1)}, u32[]{:S(2)}, u32[]{:S(2)}) %collective-permute-start.31) | collective-permute-done | bytes 491552 | tf_op jit(solution)/shard_map/ppermute | solution.py:783
  145.4 2.0 %collective-permute-start.37 = (bf16[1,768,256]{2,1,0:T(8,128)(2,1)S(1)}, bf16[1,768,256]{2,1,0:T(8,128)(2,1)S(1)}, u32[]{:S(2)}, u32[]{:S(2)}) collective-permute-start(bf16[1,768,256]{2,1,0:T(8,128)(2,1)S(1)} %shard_map.410.refs_2_.refs_0_), channel_id=1, source_target_pairs={{0,4},{1,5},{2,6},{3,7},{4,0},{5,1},{6,2},{7,3},{8,12},{9,13},{10,... | collective-permute-start | bytes 1179656 | tf_op jit(solution)/shard_map/ppermute | solution.py:783
  147.9 2.6 %shard_map.411 = (f32[512,1024]{1,0:T(8,128)}, f32[3,512,256]{2,1,0:T(8,128)}, f32[4,2,512]{2,1,0:T(2,128)}, f32[1,1024]{1,0:T(1,128)}, f32[1,1024]{1,0:T(1,128)...) custom-call(bf16[4,480,256]{2,1,0:T(8,128)(2,1)S(1)} %shard_map.409., ...), custom_call_target="tpu_custom_call" | custom-call | flops 20000000000 | bytes 405724160 | tf_op jit(solution)/shard_map/pallas_call | solution.py:175
  151.5 2.1 %shard_map.413 = (f32[1024,512]{1,0:T(8,128)}, f32[512,1024]{1,0:T(8,128)}, f32[8,128]{1,0:T(8,128)S(1)}) custom-call(bf16[2,1024,256]{2,1,0:T(8,128)(2,1)S(1)} %shard_map.408.refs_2_.refs_0_, bf16[2,1024,256]{2,1,0:T(8,128)(2,1)S(1)} %collective-permute-done.40.refs_1_, bf16[4,512,256]{2,1,0:T(8,128)(2,1)S(1)} %shard_map.412.refs_2_.refs_0_), custom_call_target="tpu_custom_call" | custom-call | flops 20000000000 | bytes 406295552 | tf_op jit(solution)/shard_map/pallas_call | solution.py:175
  154.0 2.1 %shard_map.414 = (f32[512,1536]{1,0:T(8,128)}, f32[512,512]{1,0:T(8,128)}, f32[8,128]{1,0:T(8,128)S(1)}) custom-call(bf16[4,512,256]{2,1,0:T(8,128)(2,1)S(1)} %shard_map.412.refs_2_.refs_0_, bf16[4,512,256]{2,1,0:T(8,128)(2,1)S(1)} %collective-permute-done.39.refs_1_, f32[8,128]{1,0:T(8,128)S(1)} %get-tuple-element.222.refs_2_), custom_call_target="tpu_custom_call" | custom-call | flops 20000000000 | bytes 406295552 | tf_op jit(solution)/shard_map/pallas_call | solution.py:175
  157.4 2.3 %collective-permute-done.41.refs_1_ = bf16[2,768,256]{2,1,0:T(8,128)(2,1)S(1)} collective-permute-done((bf16[2,768,256]{2,1,0:T(8,128)(2,1)S(1)}, bf16[2,768,256]{2,1,0:T(8,128)(2,1)S(1)}, u32[]{:S(2)}, u32[]{:S(2)}) %collective-permute-start.41) | collective-permute-done | bytes 786464 | tf_op jit(solution)/shard_map/ppermute | solution.py:783
  159.6 2.3 %shard_map.416 = (f32[512,1024]{1,0:T(8,128)}, f32[1024,256]{1,0:T(8,128)}, f32[8,128]{1,0:T(8,128)}) custom-call(bf16[2,768,256]{2,1,0:T(8,128)(2,1)S(1)} %shard_map.415.refs_0_.refs_2_, bf16[2,768,256]{2,1,0:T(8,128)(2,1)S(1)} %collective-permute-done.41.refs_1_, bf16[2,768,256]{2,1,0:T(8,128)(2,1)S(1)} %shard_map.415.refs_0_.refs_2_), custom_call_target="tpu_custom_call" | custom-call | flops 20000000000 | bytes 404722688 | tf_op jit(solution)/shard_map/pallas_call | solution.py:175
  (140 shorter events, 57.9 us)
Async XLA Ops:
  3.6 13.0 %collective-permute-start = (bf16[832,256]{1,0:T(8,128)(2,1)}, bf16[832,256]{1,0:T(8,128)(2,1)S(1)}, u32[]{:S(2)}, u32[]{:S(2)}) collective-permute-start(bf16[832,256]{1,0:T(8,128)(2,1)} %get-tuple-element.139), channel_id=1, source_target_pairs={{0,1},{1,0},{2,3},{3,2},{4,5},{5,4},{6,7},{7,6},{8,9},{9,8},{10,11... | collective-permute-start | bytes 1277960 | tf_op jit(solution)/shard_map/ppermute | solution.py:39
  16.6 8.1 %collective-permute-start.1 = (bf16[832,256]{1,0:T(8,128)(2,1)S(1)}, bf16[832,256]{1,0:T(8,128)(2,1)S(1)}, u32[]{:S(2)}, u32[]{:S(2)}) collective-permute-start(bf16[832,256]{1,0:T(8,128)(2,1)S(1)} %collective-permute-done.refs_8_.refs_7_.refs_9_.refs_13_), channel_id=1, source_target_pairs={{0,4},{1,5},{2,10},{3,11},{4,0},{5,1},{6,14},{7,15},{8,12},{9,13},... | collective-permute-start | bytes 1277960 | tf_op jit(solution)/shard_map/ppermute | solution.py:783
  18.4 12.8 %collective-permute-start.4 = (bf16[1024,256]{1,0:T(8,128)(2,1)}, bf16[1024,256]{1,0:T(8,128)(2,1)S(1)}, u32[]{:S(2)}, u32[]{:S(2)}) collective-permute-start(bf16[1024,256]{1,0:T(8,128)(2,1)} %shard_map.374.refs_13_), channel_id=1, source_target_pairs={{0,1},{1,0},{2,3},{3,2},{4,5},{5,4},{6,7},{7,6},{8,9},{9,8},{10,11... | collective-permute-start | bytes 1572872 | tf_op jit(solution)/shard_map/ppermute | solution.py:39
  31.2 9.2 %collective-permute-start.5 = (bf16[1024,256]{1,0:T(8,128)(2,1)S(1)}, bf16[1024,256]{1,0:T(8,128)(2,1)S(1)}, u32[]{:S(2)}, u32[]{:S(2)}) collective-permute-start(bf16[1024,256]{1,0:T(8,128)(2,1)S(1)} %collective-permute-done.4.refs_13_), channel_id=1, source_target_pairs={{0,4},{1,5},{2,10},{3,11},{4,0},{5,1},{6,14},{7,15},{8,12},{9,13},... | collective-permute-start | bytes 1572872 | tf_op jit(solution)/shard_map/ppermute | solution.py:783
  52.0 14.8 %collective-permute-start.10 = (bf16[2,1024,256]{2,1,0:T(8,128)(2,1)S(1)}, bf16[2,1024,256]{2,1,0:T(8,128)(2,1)S(1)}, u32[]{:S(2)}, u32[]{:S(2)}) collective-permute-start(bf16[2,1024,256]{2,1,0:T(8,128)(2,1)S(1)} %get-tuple-element.188), channel_id=1, source_target_pairs={{0,1},{1,0},{2,6},{3,7},{4,5},{5,4},{6,2},{7,3},{8,9},{9,8},{10,14... | collective-permute-start | bytes 3145736 | tf_op jit(solution)/shard_map/ppermute | solution.py:783
  54.8 17.2 %collective-permute-start.12 = (bf16[4,256,256]{2,1,0:T(8,128)(2,1)S(1)}, bf16[4,256,256]{2,1,0:T(8,128)(2,1)S(1)}, u32[]{:S(2)}, u32[]{:S(2)}) collective-permute-start(bf16[4,256,256]{2,1,0:T(8,128)(2,1)S(1)} %get-tuple-element.193), channel_id=1, source_target_pairs={{0,8},{1,9},{2,10},{3,11},{4,12},{5,13},{6,14},{7,15},{8,0},{9,1},... | collective-permute-start | bytes 1572872 | tf_op jit(solution)/shard_map/ppermute | solution.py:783
  67.1 10.7 %collective-permute-start.14 = (bf16[1,1024,256]{2,1,0:T(8,128)(2,1)S(1)}, bf16[1,1024,256]{2,1,0:T(8,128)(2,1)S(1)}, u32[]{:S(2)}, u32[]{:S(2)}) collective-permute-start(bf16[1,1024,256]{2,1,0:T(8,128)(2,1)S(1)} %get-tuple-element.198), channel_id=1, source_target_pairs={{0,4},{1,5},{2,3},{3,2},{4,0},{5,1},{6,7},{7,6},{8,12},{9,13},{10,... | collective-permute-start | bytes 1572872 | tf_op jit(solution)/shard_map/ppermute | solution.py:783
  71.5 9.1 %collective-permute-start.16 = (bf16[4,768,256]{2,1,0:T(8,128)(2,1)S(1)}, bf16[4,768,256]{2,1,0:T(8,128)(2,1)S(1)}, u32[]{:S(2)}, u32[]{:S(2)}) collective-permute-start(bf16[4,768,256]{2,1,0:T(8,128)(2,1)S(1)} %get-tuple-element.202), channel_id=1, source_target_pairs={{0,2},{1,3},{2,0},{3,1},{4,6},{5,7},{6,4},{7,5},{8,10},{9,11},{10,... | collective-permute-start | bytes 4718600 | tf_op jit(solution)/shard_map/ppermute | solution.py:783
  72.1 8.3 %collective-permute-start.17 = (bf16[2,256,256]{2,1,0:T(8,128)(2,1)S(1)}, bf16[2,256,256]{2,1,0:T(8,128)(2,1)S(1)}, u32[]{:S(2)}, u32[]{:S(2)}) collective-permute-start(bf16[2,256,256]{2,1,0:T(8,128)(2,1)S(1)} %get-tuple-element.203), channel_id=1, source_target_pairs={{0,1},{1,0},{2,6},{3,7},{4,5},{5,4},{6,2},{7,3},{8,9},{9,8},{10,14... | collective-permute-start | bytes 786440 | tf_op jit(solution)/shard_map/ppermute | solution.py:783
  77.9 6.4 %collective-permute-start.15 = (bf16[1,512,256]{2,1,0:T(8,128)(2,1)S(1)}, bf16[1,512,256]{2,1,0:T(8,128)(2,1)S(1)}, u32[]{:S(2)}, u32[]{:S(2)}) collective-permute-start(bf16[1,512,256]{2,1,0:T(8,128)(2,1)S(1)} %get-tuple-element.200), channel_id=1, source_target_pairs={{0,8},{1,9},{2,10},{3,11},{4,12},{5,13},{6,14},{7,15},{8,0},{9,1},... | collective-permute-start | bytes 786440 | tf_op jit(solution)/shard_map/ppermute | solution.py:783
  79.0 9.2 %collective-permute-start.13 = (bf16[2,480,256]{2,1,0:T(8,128)(2,1)S(1)}, bf16[2,480,256]{2,1,0:T(8,128)(2,1)S(1)}, u32[]{:S(2)}, u32[]{:S(2)}) collective-permute-start(bf16[2,480,256]{2,1,0:T(8,128)(2,1)S(1)} %get-tuple-element.197), channel_id=1, source_target_pairs={{0,1},{1,0},{2,6},{3,7},{4,5},{5,4},{6,2},{7,3},{8,9},{9,8},{10,14... | collective-permute-start | bytes 1474568 | tf_op jit(solution)/shard_map/ppermute | solution.py:783
  88.3 9.9 %collective-permute-start.18 = (bf16[1,480,256]{2,1,0:T(8,128)(2,1)S(1)}, bf16[1,480,256]{2,1,0:T(8,128)(2,1)S(1)}, u32[]{:S(2)}, u32[]{:S(2)}) collective-permute-start(bf16[1,480,256]{2,1,0:T(8,128)(2,1)S(1)} %get-tuple-element.207), channel_id=1, source_target_pairs={{0,4},{1,5},{2,3},{3,2},{4,0},{5,1},{6,7},{7,6},{8,12},{9,13},{10,... | collective-permute-start | bytes 737288 | tf_op jit(solution)/shard_map/ppermute | solution.py:783
  91.4 9.7 %collective-permute-start.22 = (bf16[1,256,256]{2,1,0:T(8,128)(2,1)S(1)}, bf16[1,256,256]{2,1,0:T(8,128)(2,1)S(1)}, u32[]{:S(2)}, u32[]{:S(2)}) collective-permute-start(bf16[1,256,256]{2,1,0:T(8,128)(2,1)S(1)} %get-tuple-element.211), channel_id=1, source_target_pairs={{0,4},{1,5},{2,3},{3,2},{4,0},{5,1},{6,7},{7,6},{8,12},{9,13},{10,... | collective-permute-start | bytes 393224 | tf_op jit(solution)/shard_map/ppermute | solution.py:783
  91.4 12.4 %collective-permute-start.21 = (bf16[1,512,256]{2,1,0:T(8,128)(2,1)S(1)}, bf16[1,512,256]{2,1,0:T(8,128)(2,1)S(1)}, u32[]{:S(2)}, u32[]{:S(2)}) collective-permute-start(bf16[1,512,256]{2,1,0:T(8,128)(2,1)S(1)} %shard_map.392.refs_2_.refs_0_), channel_id=1, source_target_pairs={{0,16},{1,17},{2,18},{3,19},{4,20},{5,21},{6,22},{7,23},{8,24},{9,... | collective-permute-start | bytes 786440 | tf_op jit(solution)/shard_map/ppermute | solution.py:783
  94.0 12.0 %collective-permute-start.20 = (bf16[2,768,256]{2,1,0:T(8,128)(2,1)S(1)}, bf16[2,768,256]{2,1,0:T(8,128)(2,1)S(1)}, u32[]{:S(2)}, u32[]{:S(2)}) collective-permute-start(bf16[2,768,256]{2,1,0:T(8,128)(2,1)S(1)} %get-tuple-element.210), channel_id=1, source_target_pairs={{0,1},{1,0},{2,6},{3,7},{4,5},{5,4},{6,2},{7,3},{8,9},{9,8},{10,14... | collective-permute-start | bytes 2359304 | tf_op jit(solution)/shard_map/ppermute | solution.py:783
  98.3 7.9 %collective-permute-start.19 = (bf16[1,240,256]{2,1,0:T(8,128)(2,1)S(1)}, bf16[1,240,256]{2,1,0:T(8,128)(2,1)S(1)}, u32[]{:S(2)}, u32[]{:S(2)}) collective-permute-start(bf16[1,240,256]{2,1,0:T(8,128)(2,1)S(1)} %get-tuple-element.209), channel_id=1, source_target_pairs={{0,8},{1,9},{2,10},{3,11},{4,12},{5,13},{6,14},{7,15},{8,0},{9,1},... | collective-permute-start | bytes 368648 | tf_op jit(solution)/shard_map/ppermute | solution.py:783
  101.1 18.8 %collective-permute-start.24 = (bf16[1,256,256]{2,1,0:T(8,128)(2,1)S(1)}, bf16[1,256,256]{2,1,0:T(8,128)(2,1)S(1)}, u32[]{:S(2)}, u32[]{:S(2)}) collective-permute-start(bf16[1,256,256]{2,1,0:T(8,128)(2,1)S(1)} %shard_map.395.refs_2_), channel_id=1, source_target_pairs={{0,16},{1,17},{2,18},{3,19},{4,20},{5,21},{6,22},{7,23},{8,24},{9,... | collective-permute-start | bytes 393224 | tf_op jit(solution)/shard_map/ppermute | solution.py:783
  103.9 9.4 %collective-permute-start.26 = (bf16[1,512,256]{2,1,0:T(8,128)(2,1)S(1)}, bf16[1,512,256]{2,1,0:T(8,128)(2,1)S(1)}, u32[]{:S(2)}, u32[]{:S(2)}) collective-permute-start(bf16[1,512,256]{2,1,0:T(8,128)(2,1)S(1)} %shard_map.396.refs_2_.refs_0_), channel_id=1, source_target_pairs={{0,8},{1,9},{2,10},{3,11},{4,12},{5,13},{6,14},{7,15},{8,0},{9,1},... | collective-permute-start | bytes 786440 | tf_op jit(solution)/shard_map/ppermute | solution.py:783
  106.2 13.6 %collective-permute-start.23 = (bf16[1,240,256]{2,1,0:T(8,128)(2,1)S(1)}, bf16[1,240,256]{2,1,0:T(8,128)(2,1)S(1)}, u32[]{:S(2)}, u32[]{:S(2)}) collective-permute-start(bf16[1,240,256]{2,1,0:T(8,128)(2,1)S(1)} %shard_map.398.refs_2_.refs_0_), channel_id=1, source_target_pairs={{0,16},{1,17},{2,18},{3,19},{4,20},{5,21},{6,22},{7,23},{8,24},{9,... | collective-permute-start | bytes 368648 | tf_op jit(solution)/shard_map/ppermute | solution.py:783
  107.9 10.8 %collective-permute-start.25 = (bf16[1,768,256]{2,1,0:T(8,128)(2,1)S(1)}, bf16[1,768,256]{2,1,0:T(8,128)(2,1)S(1)}, u32[]{:S(2)}, u32[]{:S(2)}) collective-permute-start(bf16[1,768,256]{2,1,0:T(8,128)(2,1)S(1)} %get-tuple-element.213), channel_id=1, source_target_pairs={{0,4},{1,5},{2,3},{3,2},{4,0},{5,1},{6,7},{7,6},{8,12},{9,13},{10,... | collective-permute-start | bytes 1179656 | tf_op jit(solution)/shard_map/ppermute | solution.py:783
  114.2 25.7 %collective-permute-start.32 = (bf16[1,1024,256]{2,1,0:T(8,128)(2,1)}, bf16[1,1024,256]{2,1,0:T(8,128)(2,1)}, u32[]{:S(2)}, u32[]{:S(2)}) collective-permute-start(bf16[1,1024,256]{2,1,0:T(8,128)(2,1)} %shard_map.399.refs_2_.refs_0_), channel_id=1, source_target_pairs={{0,4},{1,5},{2,6},{3,7},{4,0},{5,1},{6,2},{7,3},{8,12},{9,13},{10,... | collective-permute-start | bytes 1572872 | tf_op jit(solution)/shard_map/ppermute | solution.py:783
  118.8 7.0 %collective-permute-start.28 = (bf16[1,384,256]{2,1,0:T(8,128)(2,1)S(1)}, bf16[1,384,256]{2,1,0:T(8,128)(2,1)S(1)}, u32[]{:S(2)}, u32[]{:S(2)}) collective-permute-start(bf16[1,384,256]{2,1,0:T(8,128)(2,1)S(1)} %get-tuple-element.216), channel_id=1, source_target_pairs={{0,8},{1,9},{2,10},{3,11},{4,12},{5,13},{6,14},{7,15},{8,0},{9,1},... | collective-permute-start | bytes 589832 | tf_op jit(solution)/shard_map/ppermute | solution.py:783
  119.9 7.3 %collective-permute-start.27 = (bf16[1,240,256]{2,1,0:T(8,128)(2,1)S(1)}, bf16[1,240,256]{2,1,0:T(8,128)(2,1)S(1)}, u32[]{:S(2)}, u32[]{:S(2)}) collective-permute-start(bf16[1,240,256]{2,1,0:T(8,128)(2,1)S(1)} %get-tuple-element.215.refs_2_.refs_0_), channel_id=1, source_target_pairs={{0,8},{1,9},{2,10},{3,11},{4,12},{5,13},{6,14},{7,15},{8,0},{9,1},... | collective-permute-start | bytes 368648 | tf_op jit(solution)/shard_map/ppermute | solution.py:783
  121.1 8.2 %collective-permute-start.30 = (bf16[1,256,256]{2,1,0:T(8,128)(2,1)S(1)}, bf16[1,256,256]{2,1,0:T(8,128)(2,1)S(1)}, u32[]{:S(2)}, u32[]{:S(2)}) collective-permute-start(bf16[1,256,256]{2,1,0:T(8,128)(2,1)S(1)} %get-tuple-element.217.refs_0_), channel_id=1, source_target_pairs={{0,4},{1,5},{2,3},{3,2},{4,0},{5,1},{6,7},{7,6},{8,12},{9,13},{10,... | collective-permute-start | bytes 393224 | tf_op jit(solution)/shard_map/ppermute | solution.py:783
  125.9 11.7 %collective-permute-start.34 = (bf16[1,384,256]{2,1,0:T(8,128)(2,1)S(1)}, bf16[1,384,256]{2,1,0:T(8,128)(2,1)S(1)}, u32[]{:S(2)}, u32[]{:S(2)}) collective-permute-start(bf16[1,384,256]{2,1,0:T(8,128)(2,1)S(1)} %shard_map.402.refs_2_.refs_0_), channel_id=1, source_target_pairs={{0,16},{1,17},{2,18},{3,19},{4,20},{5,21},{6,22},{7,23},{8,24},{9,... | collective-permute-start | bytes 589832 | tf_op jit(solution)/shard_map/ppermute | solution.py:783
  127.3 9.0 %collective-permute-start.29 = (bf16[1,480,256]{2,1,0:T(8,128)(2,1)S(1)}, bf16[1,480,256]{2,1,0:T(8,128)(2,1)S(1)}, u32[]{:S(2)}, u32[]{:S(2)}) collective-permute-start(bf16[1,480,256]{2,1,0:T(8,128)(2,1)S(1)} %shard_map.403.refs_2_.refs_0_), channel_id=1, source_target_pairs={{0,4},{1,5},{2,3},{3,2},{4,0},{5,1},{6,7},{7,6},{8,12},{9,13},{10,... | collective-permute-start | bytes 737288 | tf_op jit(solution)/shard_map/ppermute | solution.py:783
  129.3 9.3 %collective-permute-start.33 = (bf16[2,256,256]{2,1,0:T(8,128)(2,1)S(1)}, bf16[2,256,256]{2,1,0:T(8,128)(2,1)S(1)}, u32[]{:S(2)}, u32[]{:S(2)}) collective-permute-start(bf16[2,256,256]{2,1,0:T(8,128)(2,1)S(1)} %shard_map.404.refs_2_.refs_0_), channel_id=1, source_target_pairs={{0,1},{1,0},{2,6},{3,7},{4,5},{5,4},{6,2},{7,3},{8,9},{9,8},{10,14... | collective-permute-start | bytes 786440 | tf_op jit(solution)/shard_map/ppermute | solution.py:783
  136.3 8.9 %collective-permute-start.31 = (bf16[2,480,256]{2,1,0:T(8,128)(2,1)S(1)}, bf16[2,480,256]{2,1,0:T(8,128)(2,1)S(1)}, u32[]{:S(2)}, u32[]{:S(2)}) collective-permute-start(bf16[2,480,256]{2,1,0:T(8,128)(2,1)S(1)} %shard_map.405.refs_2_.refs_0_), channel_id=1, source_target_pairs={{0,1},{1,0},{2,6},{3,7},{4,5},{5,4},{6,2},{7,3},{8,9},{9,8},{10,14... | collective-permute-start | bytes 1474568 | tf_op jit(solution)/shard_map/ppermute | solution.py:783
  137.7 7.7 %collective-permute-start.36 = (bf16[1,384,256]{2,1,0:T(8,128)(2,1)S(1)}, bf16[1,384,256]{2,1,0:T(8,128)(2,1)S(1)}, u32[]{:S(2)}, u32[]{:S(2)}) collective-permute-start(bf16[1,384,256]{2,1,0:T(8,128)(2,1)S(1)} %shard_map.406.refs_2_.refs_0_), channel_id=1, source_target_pairs={{0,8},{1,9},{2,10},{3,11},{4,12},{5,13},{6,14},{7,15},{8,0},{9,1},... | collective-permute-start | bytes 589832 | tf_op jit(solution)/shard_map/ppermute | solution.py:783
  138.6 11.9 %collective-permute-start.38 = (bf16[4,256,256]{2,1,0:T(8,128)(2,1)S(1)}, bf16[4,256,256]{2,1,0:T(8,128)(2,1)S(1)}, u32[]{:S(2)}, u32[]{:S(2)}) collective-permute-start(bf16[4,256,256]{2,1,0:T(8,128)(2,1)S(1)} %shard_map.407.refs_2_.refs_0_), channel_id=1, source_target_pairs={{0,8},{1,9},{2,10},{3,11},{4,12},{5,13},{6,14},{7,15},{8,0},{9,1},... | collective-permute-start | bytes 1572872 | tf_op jit(solution)/shard_map/ppermute | solution.py:783
  141.2 10.3 %collective-permute-start.40 = (bf16[2,1024,256]{2,1,0:T(8,128)(2,1)S(1)}, bf16[2,1024,256]{2,1,0:T(8,128)(2,1)S(1)}, u32[]{:S(2)}, u32[]{:S(2)}) collective-permute-start(bf16[2,1024,256]{2,1,0:T(8,128)(2,1)S(1)} %shard_map.408.refs_2_.refs_0_), channel_id=1, source_target_pairs={{0,2},{1,3},{2,0},{3,1},{4,6},{5,7},{6,4},{7,5},{8,10},{9,11},{10,... | collective-permute-start | bytes 3145736 | tf_op jit(solution)/shard_map/ppermute | solution.py:783
  145.4 11.8 %collective-permute-start.37 = (bf16[1,768,256]{2,1,0:T(8,128)(2,1)S(1)}, bf16[1,768,256]{2,1,0:T(8,128)(2,1)S(1)}, u32[]{:S(2)}, u32[]{:S(2)}) collective-permute-start(bf16[1,768,256]{2,1,0:T(8,128)(2,1)S(1)} %shard_map.410.refs_2_.refs_0_), channel_id=1, source_target_pairs={{0,4},{1,5},{2,6},{3,7},{4,0},{5,1},{6,2},{7,3},{8,12},{9,13},{10,... | collective-permute-start | bytes 1179656 | tf_op jit(solution)/shard_map/ppermute | solution.py:783
  (32 other events, 219.5 us)

commit v8 on v7

--- a/solution.py
+++ b/solution.py
@@ -922,10 +922,11 @@
     info, mine, flight, refs = refs[0], refs[1], refs[2], list(refs[3:])
     core = info[0]
     outs = [refs.pop(0) for _ in parts]
-    smalls = [refs.pop(0) for _ in range(11)] if small else []
+    small_outs = [refs.pop(0) for _ in range(11)] if small else []
     link = refs.pop(0)
     link[...] = jnp.zeros_like(link)
     held = [refs.pop(0) for _ in parts]
+    smalls = [refs.pop(0) for _ in small_outs]
     sems = refs.pop(0)
     copies = []
     quarters = mine.shape[0]
@@ -978,6 +979,9 @@
             output[:, lanes] = block[12:13]
             shrink[:, lanes] = block[13:14]
             (conv if part == 0 else point)[...] = block[14:15]
+        for source, target in zip(smalls, small_outs):
+            copies.append(pltpu.make_async_copy(source, target, sems.at[len(copies)]))
+            copies[-1].start()
     for copy in copies:
         copy.wait()
 
@@ -988,18 +992,20 @@
     scratch = [
         pltpu.VMEM((2,) + shape[:-2] + (shape[-2] // 2, shape[-1]), F32) for _, _, shape in parts
     ]
-    scratch.append(pltpu.SemaphoreType.DMA((2 * len(parts),)))
     names = []
     if small:
+        names = [shaped(shape, F32) for shape in small[1]]
+    scratch += [pltpu.VMEM(item.shape, F32) for item in names]
+    scratch.append(pltpu.SemaphoreType.DMA((2 * len(parts) + len(names),)))
+    if small:
         scratch.append(pltpu.VMEM((256, 256), F32))
-        names = [shaped(shape, F32) for shape in small[1]]
     stream.mine = chain.run(
         lambda *refs: finish_kernel(parts, small[0] if small else None, refs),
         shapes + names + [shaped((8, 128), F32)],
         [stream.mine, stream.flight],
         scratch,
         ADV,
-        len(parts),
+        len(parts) + len(names),
     )
 
 

time: 162 us -> 162 us (level)
  no operation moved by 1% of the time
where the time goes in v8:
time: 162 us
  waiting for transfers between devices  59 us (36%)
  starting transfers between devices  50.4 us (31%)
  Pallas kernels  49 us (30%)
  between operations  2.07 us (1%)
  local copies, waits for them, and re-layouts  1.72 us (1%)
    ppermute x36, waiting for transfers between devices, flat_swap(): lax.ppermute(values, ('dp', 'mp'), [(at, partner(at)) for at in range(cou...  50 us
    ppermute x36, starting transfers between devices, flat_swap(): lax.ppermute(values, ('dp', 'mp'), [(at, partner(at)) for at in range(cou...  45.8 us
    pallas_call x42, Pallas kernels, run(): pl.pallas_call(call, out_shape=outs, in_specs=specs, out_specs=[pl.BlockS...  44.2 us
    ppermute x6, waiting for transfers between devices, swap(): return lax.ppermute(values, axis, [(at, at ^ bit) for at in range(count)])  8.98 us
    pallas_call x2, Pallas kernels, cut(): pl.pallas_call(kernel, out_shape=outs, in_specs=[pl.BlockSpec(memory_spac...  4.77 us
    ppermute x6, starting transfers between devices, swap(): return lax.ppermute(values, axis, [(at, at ^ bit) for at in range(count)])  4.57 us
  transfers between devices with their start and end apart: 42, of which 26 were waited for; matrix products, arithmetic and copies ran while one was open for 0% of the time, Pallas kernels for 24%

profile of v8, /device:TPU:0, one launch (start us, length us, event | category | flops | bytes accessed | tf_op | source)
XLA Modules:
  0.0 162.2 jit_solution(1129455802956936489)
XLA Ops:
  0.8 2.8 %shard_map.373 = (bf16[832,256]{1,0:T(8,128)(2,1)}, bf16[64,256]{1,0:T(8,128)(2,1)}) custom-call(bf16[512,1024]{1,0:T(8,128)(2,1)} %refs_9_.3, bf16[1024,256]{1,0:T(8,128)(2,1)} %refs_7_.3, bf16[1024]{0:T(1024)(128)(2,1)} %refs_2_.5, bf16[1024]{0:T(1024)(128)(2,1)} %refs_3_.4, bf16[2,1024]{1,0:T(2,128)(2,1)} %refs_4_.3, bf16[9,1024]{1,0:T(8,128)(2,1)} %refs_5_.4), custom_call_target="tpu_custom_call" | custom-call | tf_op jit(solution)/shard_map/pallas_call | solution.py:767
  3.6 3.0 %collective-permute-start = (bf16[832,256]{1,0:T(8,128)(2,1)}, bf16[832,256]{1,0:T(8,128)(2,1)S(1)}, u32[]{:S(2)}, u32[]{:S(2)}) collective-permute-start(bf16[832,256]{1,0:T(8,128)(2,1)} %get-tuple-element.139), channel_id=1, source_target_pairs={{0,1},{1,0},{2,3},{3,2},{4,5},{5,4},{6,7},{7,6},{8,9},{9,8},{10,11... | collective-permute-start | bytes 1277960 | tf_op jit(solution)/shard_map/ppermute | solution.py:39
  12.3 4.4 %collective-permute-done.refs_8_.refs_7_.refs_9_.refs_13_ = bf16[832,256]{1,0:T(8,128)(2,1)S(1)} collective-permute-done((bf16[832,256]{1,0:T(8,128)(2,1)}, bf16[832,256]{1,0:T(8,128)(2,1)S(1)}, u32[]{:S(2)}, u32[]{:S(2)}) %collective-permute-start) | collective-permute-done | bytes 426016 | tf_op jit(solution)/shard_map/ppermute | solution.py:39
  19.9 4.9 %collective-permute-done.1.refs_9_.refs_8_.refs_10_.refs_14_ = bf16[832,256]{1,0:T(8,128)(2,1)S(1)} collective-permute-done((bf16[832,256]{1,0:T(8,128)(2,1)S(1)}, bf16[832,256]{1,0:T(8,128)(2,1)S(1)}, u32[]{:S(2)}, u32[]{:S(2)}) %collective-permute-start.1) | collective-permute-done | bytes 426016 | tf_op jit(solution)/shard_map/ppermute | solution.py:783
  26.5 3.7 %shard_map.376 = (bf16[256,2048]{1,0:T(8,128)(2,1)S(1)}, bf16[256,2048]{1,0:T(8,128)(2,1)S(1)}, bf16[256,2048]{1,0:T(8,128)(2,1)S(1)}, f32[256,128]{1,0:T(8,128)S(1)}, bf16[1,512,1024]{2,1,0:T(8,128)(2,1)S(1)}) custom-call(bf16[256,512]{1,0:T(8,128)(2,1)S(1)} %get-tuple-element.132.refs_0_.refs_5_.refs_4_, bf16[256,256]{1,0:T(8,128)(2,1)S(1)} %get-tuple-element.133.refs_1_, ...), custom_call_target="tpu_custom_call" | custom-call | flops 6500000 | bytes 8551376 | tf_op jit(solution)/shard_map/pallas_call | solution.py:175
  32.7 3.2 %shard_map.377 = (f32[256,512]{1,0:T(8,128)S(1)}, bf16[256,512]{1,0:T(8,128)(2,1)S(1)}, bf16[256,1536]{1,0:T(8,128)(2,1)S(1)}, f32[256,128]{1,0:T(8,128)S(1)}, b...) custom-call(f32[256,512]{1,0:T(8,128)S(1)} %get-tuple-element.131.re, ...), custom_call_target="tpu_custom_call" | custom-call | flops 4400000 | bytes 9304000 | tf_op jit(solution)/shard_map/pallas_call | solution.py:175
  36.0 2.1 %shard_map.378 = (bf16[2,1024,256]{2,1,0:T(8,128)(2,1)S(1)}, bf16[2,1024,256]{2,1,0:T(8,128)(2,1)S(1)}, f32[256,512]{1,0:T(8,128)S(1)}, f32[256,512]{1,0:T(8,128)S(1)}, f32[8,1024]{1,0:T(8,128)S(1)}) custom-call(bf16[256,512]{1,0:T(8,128)(2,1)S(1)} %get-tuple-element.147.refs_0_, bf16[256,512]{1,0:T(8,128)(2,1)S(1)} %copy-done.13, ...), custom_call_target="tpu_custom_call" | custom-call | flops 3000000 | bytes 5892704 | tf_op jit(solution)/shard_map/pallas_call | solution.py:175
  38.1 2.2 %collective-permute-done.5.refs_14_ = bf16[1024,256]{1,0:T(8,128)(2,1)S(1)} collective-permute-done((bf16[1024,256]{1,0:T(8,128)(2,1)S(1)}, bf16[1024,256]{1,0:T(8,128)(2,1)S(1)}, u32[]{:S(2)}, u32[]{:S(2)}) %collective-permute-start.5) | collective-permute-done | bytes 524320 | tf_op jit(solution)/shard_map/ppermute | solution.py:783
  42.3 3.2 %shard_map.379 = (bf16[256,512]{1,0:T(8,128)(2,1)}, bf16[4,1024,256]{2,1,0:T(8,128)(2,1)S(1)}, bf16[4,1024,256]{2,1,0:T(8,128)(2,1)S(1)}, f32[256,512]{1,0:T(8,1...) custom-call(bf16[256,512]{1,0:T(8,128)(2,1)S(1)} %get-tuple-element.147.refs_0_, ...), custom_call_target="tpu_custom_call" | custom-call | flops 32000000000 | bytes 653139968 | tf_op jit(solution)/shard_map/pallas_call | solution.py:175
  45.6 3.7 %shard_map.380 = (bf16[256,512]{1,0:T(8,128)(2,1)S(1)}, bf16[256,1536]{1,0:T(8,128)(2,1)S(1)}) custom-call(f32[256,512]{1,0:T(8,128)S(1)} %get-tuple-element.159.refs_0_, bf16[256,512]{1,0:T(8,128)(2,1)S(1)} %get-tuple-element.160.refs_1_, bf16[512,512]{1,0:T(8,128)(2,1)S(1)} %copy-done.8, bf16[256,1536]{1,0:T(8,128)(2,1)S(1)} %get-tuple-element.162.refs_3_, ...), custom_call_target="tpu_custom_call" | custom-call | flops 20000000000 | bytes 403284992 | tf_op jit(solution)/shard_map/pallas_call | solution.py:175
  55.8 7.3 %shard_map.384 = (bf16[4,768,256]{2,1,0:T(8,128)(2,1)S(1)}, bf16[4,768,256]{2,1,0:T(8,128)(2,1)S(1)}, f32[256,512]{1,0:T(8,128)S(1)}, f32[256,256]{1,0:T(8,128)S(1)}, f32[16,2048]{1,0:T(8,128)S(1)}) custom-call(bf16[256,256]{1,0:T(8,128)(2,1)S(1)} %get-tuple-element.170.refs_0_, bf16[256,2048]{1,0:T(8,128)(2,1)S(1)} %get-tuple-element.144.refs_1_, ...), custom_call_target="tpu_custom_call" | custom-call | flops 46000001024 | bytes 932812288 | tf_op jit(solution)/shard_map/pallas_call | solution.py:175
  63.1 3.7 %collective-permute-done.10.refs_1_ = bf16[2,1024,256]{2,1,0:T(8,128)(2,1)S(1)} collective-permute-done((bf16[2,1024,256]{2,1,0:T(8,128)(2,1)S(1)}, bf16[2,1024,256]{2,1,0:T(8,128)(2,1)S(1)}, u32[]{:S(2)}, u32[]{:S(2)}) %collective-permute-start.10) | collective-permute-done | bytes 1048608 | tf_op jit(solution)/shard_map/ppermute | solution.py:783
  68.7 2.8 %shard_map.386 = (bf16[4,480,256]{2,1,0:T(8,128)(2,1)S(1)}, bf16[4,480,256]{2,1,0:T(8,128)(2,1)S(1)}, f32[256,512]{1,0:T(8,128)}, f32[16,512]{1,0:T(8,128)S(1)}) custom-call(f32[256,512]{1,0:T(8,128)S(1)} %get-tuple-element.180.refs_0_, f32[256,256]{1,0:T(8,128)S(1)} %get-tuple-element.181.refs_1_, f32[256,256]{1,0:T(8,128)S(1)} %get-tuple-element.182.refs_2_, ...), custom_call_target="tpu_custom_call" | custom-call | flops 16000000000 | bytes 328617984 | tf_op jit(solution)/shard_map/pallas_call | solution.py:175
  74.3 3.5 %collective-permute-done.14.refs_1_ = bf16[1,1024,256]{2,1,0:T(8,128)(2,1)S(1)} collective-permute-done((bf16[1,1024,256]{2,1,0:T(8,128)(2,1)S(1)}, bf16[1,1024,256]{2,1,0:T(8,128)(2,1)S(1)}, u32[]{:S(2)}, u32[]{:S(2)}) %collective-permute-start.14) | collective-permute-done | bytes 524320 | tf_op jit(solution)/shard_map/ppermute | solution.py:783
  80.9 3.4 %collective-permute-done.15.refs_1_ = bf16[1,512,256]{2,1,0:T(8,128)(2,1)S(1)} collective-permute-done((bf16[1,512,256]{2,1,0:T(8,128)(2,1)S(1)}, bf16[1,512,256]{2,1,0:T(8,128)(2,1)S(1)}, u32[]{:S(2)}, u32[]{:S(2)}) %collective-permute-start.15) | collective-permute-done | bytes 262176 | tf_op jit(solution)/shard_map/ppermute | solution.py:783
  84.4 3.8 %collective-permute-done.13.refs_1_ = bf16[2,480,256]{2,1,0:T(8,128)(2,1)S(1)} collective-permute-done((bf16[2,480,256]{2,1,0:T(8,128)(2,1)S(1)}, bf16[2,480,256]{2,1,0:T(8,128)(2,1)S(1)}, u32[]{:S(2)}, u32[]{:S(2)}) %collective-permute-start.13) | collective-permute-done | bytes 491552 | tf_op jit(solution)/shard_map/ppermute | solution.py:783
  88.3 3.1 %collective-permute-start.18 = (bf16[1,480,256]{2,1,0:T(8,128)(2,1)S(1)}, bf16[1,480,256]{2,1,0:T(8,128)(2,1)S(1)}, u32[]{:S(2)}, u32[]{:S(2)}) collective-permute-start(bf16[1,480,256]{2,1,0:T(8,128)(2,1)S(1)} %get-tuple-element.207), channel_id=1, source_target_pairs={{0,4},{1,5},{2,3},{3,2},{4,0},{5,1},{6,7},{7,6},{8,12},{9,13},{10,... | collective-permute-start | bytes 737288 | tf_op jit(solution)/shard_map/ppermute | solution.py:783
  91.4 2.6 %collective-permute-start.21 = (bf16[1,512,256]{2,1,0:T(8,128)(2,1)S(1)}, bf16[1,512,256]{2,1,0:T(8,128)(2,1)S(1)}, u32[]{:S(2)}, u32[]{:S(2)}) collective-permute-start(bf16[1,512,256]{2,1,0:T(8,128)(2,1)S(1)} %shard_map.392.refs_2_.refs_0_), channel_id=1, source_target_pairs={{0,16},{1,17},{2,18},{3,19},{4,20},{5,21},{6,22},{7,23},{8,24},{9,... | collective-permute-start | bytes 786440 | tf_op jit(solution)/shard_map/ppermute | solution.py:783
  95.5 2.7 %collective-permute-done.18.refs_1_ = bf16[1,480,256]{2,1,0:T(8,128)(2,1)S(1)} collective-permute-done((bf16[1,480,256]{2,1,0:T(8,128)(2,1)S(1)}, bf16[1,480,256]{2,1,0:T(8,128)(2,1)S(1)}, u32[]{:S(2)}, u32[]{:S(2)}) %collective-permute-start.18) | collective-permute-done | bytes 245792 | tf_op jit(solution)/shard_map/ppermute | solution.py:783
  101.1 2.6 %collective-permute-start.24 = (bf16[1,256,256]{2,1,0:T(8,128)(2,1)S(1)}, bf16[1,256,256]{2,1,0:T(8,128)(2,1)S(1)}, u32[]{:S(2)}, u32[]{:S(2)}) collective-permute-start(bf16[1,256,256]{2,1,0:T(8,128)(2,1)S(1)} %shard_map.395.refs_2_), channel_id=1, source_target_pairs={{0,16},{1,17},{2,18},{3,19},{4,20},{5,21},{6,22},{7,23},{8,24},{9,... | collective-permute-start | bytes 393224 | tf_op jit(solution)/shard_map/ppermute | solution.py:783
  107.9 2.2 %collective-permute-start.25 = (bf16[1,768,256]{2,1,0:T(8,128)(2,1)S(1)}, bf16[1,768,256]{2,1,0:T(8,128)(2,1)S(1)}, u32[]{:S(2)}, u32[]{:S(2)}) collective-permute-start(bf16[1,768,256]{2,1,0:T(8,128)(2,1)S(1)} %get-tuple-element.213), channel_id=1, source_target_pairs={{0,4},{1,5},{2,3},{3,2},{4,0},{5,1},{6,7},{7,6},{8,12},{9,13},{10,... | collective-permute-start | bytes 1179656 | tf_op jit(solution)/shard_map/ppermute | solution.py:783
  110.1 3.3 %collective-permute-done.26.refs_1_ = bf16[1,512,256]{2,1,0:T(8,128)(2,1)S(1)} collective-permute-done((bf16[1,512,256]{2,1,0:T(8,128)(2,1)S(1)}, bf16[1,512,256]{2,1,0:T(8,128)(2,1)S(1)}, u32[]{:S(2)}, u32[]{:S(2)}) %collective-permute-start.26) | collective-permute-done | bytes 262176 | tf_op jit(solution)/shard_map/ppermute | solution.py:783
  114.2 2.6 %collective-permute-start.32 = (bf16[1,1024,256]{2,1,0:T(8,128)(2,1)}, bf16[1,1024,256]{2,1,0:T(8,128)(2,1)}, u32[]{:S(2)}, u32[]{:S(2)}) collective-permute-start(bf16[1,1024,256]{2,1,0:T(8,128)(2,1)} %shard_map.399.refs_2_.refs_0_), channel_id=1, source_target_pairs={{0,4},{1,5},{2,6},{3,7},{4,0},{5,1},{6,2},{7,3},{8,12},{9,13},{10,... | collective-permute-start | bytes 1572872 | tf_op jit(solution)/shard_map/ppermute | solution.py:783
  122.6 3.3 %collective-permute-done.28.refs_1_ = bf16[1,384,256]{2,1,0:T(8,128)(2,1)S(1)} collective-permute-done((bf16[1,384,256]{2,1,0:T(8,128)(2,1)S(1)}, bf16[1,384,256]{2,1,0:T(8,128)(2,1)S(1)}, u32[]{:S(2)}, u32[]{:S(2)}) %collective-permute-start.28) | collective-permute-done | bytes 196640 | tf_op jit(solution)/shard_map/ppermute | solution.py:783
  131.3 4.9 %collective-permute-done.29.refs_1_ = bf16[1,480,256]{2,1,0:T(8,128)(2,1)S(1)} collective-permute-done((bf16[1,480,256]{2,1,0:T(8,128)(2,1)S(1)}, bf16[1,480,256]{2,1,0:T(8,128)(2,1)S(1)}, u32[]{:S(2)}, u32[]{:S(2)}) %collective-permute-start.29) | collective-permute-done | bytes 245792 | tf_op jit(solution)/shard_map/ppermute | solution.py:783
  141.3 3.9 %collective-permute-done.31.refs_1_ = bf16[2,480,256]{2,1,0:T(8,128)(2,1)S(1)} collective-permute-done((bf16[2,480,256]{2,1,0:T(8,128)(2,1)S(1)}, bf16[2,480,256]{2,1,0:T(8,128)(2,1)S(1)}, u32[]{:S(2)}, u32[]{:S(2)}) %collective-permute-start.31) | collective-permute-done | bytes 491552 | tf_op jit(solution)/shard_map/ppermute | solution.py:783
  145.4 2.0 %collective-permute-start.37 = (bf16[1,768,256]{2,1,0:T(8,128)(2,1)S(1)}, bf16[1,768,256]{2,1,0:T(8,128)(2,1)S(1)}, u32[]{:S(2)}, u32[]{:S(2)}) collective-permute-start(bf16[1,768,256]{2,1,0:T(8,128)(2,1)S(1)} %shard_map.410.refs_2_.refs_0_), channel_id=1, source_target_pairs={{0,4},{1,5},{2,6},{3,7},{4,0},{5,1},{6,2},{7,3},{8,12},{9,13},{10,... | collective-permute-start | bytes 1179656 | tf_op jit(solution)/shard_map/ppermute | solution.py:783
  147.9 2.7 %shard_map.411 = (f32[512,1024]{1,0:T(8,128)}, f32[3,512,256]{2,1,0:T(8,128)}, f32[4,2,512]{2,1,0:T(2,128)}, f32[1,1024]{1,0:T(1,128)}, f32[1,1024]{1,0:T(1,128)...) custom-call(bf16[4,480,256]{2,1,0:T(8,128)(2,1)S(1)} %shard_map.409., ...), custom_call_target="tpu_custom_call" | custom-call | flops 20000000000 | bytes 405724160 | tf_op jit(solution)/shard_map/pallas_call | solution.py:175
  151.6 2.1 %shard_map.413 = (f32[1024,512]{1,0:T(8,128)}, f32[512,1024]{1,0:T(8,128)}, f32[8,128]{1,0:T(8,128)S(1)}) custom-call(bf16[2,1024,256]{2,1,0:T(8,128)(2,1)S(1)} %shard_map.408.refs_2_.refs_0_, bf16[2,1024,256]{2,1,0:T(8,128)(2,1)S(1)} %collective-permute-done.40.refs_1_, bf16[4,512,256]{2,1,0:T(8,128)(2,1)S(1)} %shard_map.412.refs_2_.refs_0_), custom_call_target="tpu_custom_call" | custom-call | flops 20000000000 | bytes 406295552 | tf_op jit(solution)/shard_map/pallas_call | solution.py:175
  154.1 2.1 %shard_map.414 = (f32[512,1536]{1,0:T(8,128)}, f32[512,512]{1,0:T(8,128)}, f32[8,128]{1,0:T(8,128)S(1)}) custom-call(bf16[4,512,256]{2,1,0:T(8,128)(2,1)S(1)} %shard_map.412.refs_2_.refs_0_, bf16[4,512,256]{2,1,0:T(8,128)(2,1)S(1)} %collective-permute-done.39.refs_1_, f32[8,128]{1,0:T(8,128)S(1)} %get-tuple-element.222.refs_2_), custom_call_target="tpu_custom_call" | custom-call | flops 20000000000 | bytes 406295552 | tf_op jit(solution)/shard_map/pallas_call | solution.py:175
  157.4 2.3 %collective-permute-done.41.refs_1_ = bf16[2,768,256]{2,1,0:T(8,128)(2,1)S(1)} collective-permute-done((bf16[2,768,256]{2,1,0:T(8,128)(2,1)S(1)}, bf16[2,768,256]{2,1,0:T(8,128)(2,1)S(1)}, u32[]{:S(2)}, u32[]{:S(2)}) %collective-permute-start.41) | collective-permute-done | bytes 786464 | tf_op jit(solution)/shard_map/ppermute | solution.py:783
  159.6 2.3 %shard_map.416 = (f32[512,1024]{1,0:T(8,128)}, f32[1024,256]{1,0:T(8,128)}, f32[8,128]{1,0:T(8,128)}) custom-call(bf16[2,768,256]{2,1,0:T(8,128)(2,1)S(1)} %shard_map.415.refs_0_.refs_2_, bf16[2,768,256]{2,1,0:T(8,128)(2,1)S(1)} %collective-permute-done.41.refs_1_, bf16[2,768,256]{2,1,0:T(8,128)(2,1)S(1)} %shard_map.415.refs_0_.refs_2_), custom_call_target="tpu_custom_call" | custom-call | flops 20000000000 | bytes 404722688 | tf_op jit(solution)/shard_map/pallas_call | solution.py:175
  (140 shorter events, 57.8 us)
Async XLA Ops:
  3.6 13.0 %collective-permute-start = (bf16[832,256]{1,0:T(8,128)(2,1)}, bf16[832,256]{1,0:T(8,128)(2,1)S(1)}, u32[]{:S(2)}, u32[]{:S(2)}) collective-permute-start(bf16[832,256]{1,0:T(8,128)(2,1)} %get-tuple-element.139), channel_id=1, source_target_pairs={{0,1},{1,0},{2,3},{3,2},{4,5},{5,4},{6,7},{7,6},{8,9},{9,8},{10,11... | collective-permute-start | bytes 1277960 | tf_op jit(solution)/shard_map/ppermute | solution.py:39
  16.6 8.1 %collective-permute-start.1 = (bf16[832,256]{1,0:T(8,128)(2,1)S(1)}, bf16[832,256]{1,0:T(8,128)(2,1)S(1)}, u32[]{:S(2)}, u32[]{:S(2)}) collective-permute-start(bf16[832,256]{1,0:T(8,128)(2,1)S(1)} %collective-permute-done.refs_8_.refs_7_.refs_9_.refs_13_), channel_id=1, source_target_pairs={{0,4},{1,5},{2,10},{3,11},{4,0},{5,1},{6,14},{7,15},{8,12},{9,13},... | collective-permute-start | bytes 1277960 | tf_op jit(solution)/shard_map/ppermute | solution.py:783
  18.4 12.8 %collective-permute-start.4 = (bf16[1024,256]{1,0:T(8,128)(2,1)}, bf16[1024,256]{1,0:T(8,128)(2,1)S(1)}, u32[]{:S(2)}, u32[]{:S(2)}) collective-permute-start(bf16[1024,256]{1,0:T(8,128)(2,1)} %shard_map.374.refs_13_), channel_id=1, source_target_pairs={{0,1},{1,0},{2,3},{3,2},{4,5},{5,4},{6,7},{7,6},{8,9},{9,8},{10,11... | collective-permute-start | bytes 1572872 | tf_op jit(solution)/shard_map/ppermute | solution.py:39
  31.2 9.2 %collective-permute-start.5 = (bf16[1024,256]{1,0:T(8,128)(2,1)S(1)}, bf16[1024,256]{1,0:T(8,128)(2,1)S(1)}, u32[]{:S(2)}, u32[]{:S(2)}) collective-permute-start(bf16[1024,256]{1,0:T(8,128)(2,1)S(1)} %collective-permute-done.4.refs_13_), channel_id=1, source_target_pairs={{0,4},{1,5},{2,10},{3,11},{4,0},{5,1},{6,14},{7,15},{8,12},{9,13},... | collective-permute-start | bytes 1572872 | tf_op jit(solution)/shard_map/ppermute | solution.py:783
  52.0 14.8 %collective-permute-start.10 = (bf16[2,1024,256]{2,1,0:T(8,128)(2,1)S(1)}, bf16[2,1024,256]{2,1,0:T(8,128)(2,1)S(1)}, u32[]{:S(2)}, u32[]{:S(2)}) collective-permute-start(bf16[2,1024,256]{2,1,0:T(8,128)(2,1)S(1)} %get-tuple-element.188), channel_id=1, source_target_pairs={{0,1},{1,0},{2,6},{3,7},{4,5},{5,4},{6,2},{7,3},{8,9},{9,8},{10,14... | collective-permute-start | bytes 3145736 | tf_op jit(solution)/shard_map/ppermute | solution.py:783
  54.8 17.2 %collective-permute-start.12 = (bf16[4,256,256]{2,1,0:T(8,128)(2,1)S(1)}, bf16[4,256,256]{2,1,0:T(8,128)(2,1)S(1)}, u32[]{:S(2)}, u32[]{:S(2)}) collective-permute-start(bf16[4,256,256]{2,1,0:T(8,128)(2,1)S(1)} %get-tuple-element.193), channel_id=1, source_target_pairs={{0,8},{1,9},{2,10},{3,11},{4,12},{5,13},{6,14},{7,15},{8,0},{9,1},... | collective-permute-start | bytes 1572872 | tf_op jit(solution)/shard_map/ppermute | solution.py:783
  67.1 10.7 %collective-permute-start.14 = (bf16[1,1024,256]{2,1,0:T(8,128)(2,1)S(1)}, bf16[1,1024,256]{2,1,0:T(8,128)(2,1)S(1)}, u32[]{:S(2)}, u32[]{:S(2)}) collective-permute-start(bf16[1,1024,256]{2,1,0:T(8,128)(2,1)S(1)} %get-tuple-element.198), channel_id=1, source_target_pairs={{0,4},{1,5},{2,3},{3,2},{4,0},{5,1},{6,7},{7,6},{8,12},{9,13},{10,... | collective-permute-start | bytes 1572872 | tf_op jit(solution)/shard_map/ppermute | solution.py:783
  71.5 9.1 %collective-permute-start.16 = (bf16[4,768,256]{2,1,0:T(8,128)(2,1)S(1)}, bf16[4,768,256]{2,1,0:T(8,128)(2,1)S(1)}, u32[]{:S(2)}, u32[]{:S(2)}) collective-permute-start(bf16[4,768,256]{2,1,0:T(8,128)(2,1)S(1)} %get-tuple-element.202), channel_id=1, source_target_pairs={{0,2},{1,3},{2,0},{3,1},{4,6},{5,7},{6,4},{7,5},{8,10},{9,11},{10,... | collective-permute-start | bytes 4718600 | tf_op jit(solution)/shard_map/ppermute | solution.py:783
  72.1 8.3 %collective-permute-start.17 = (bf16[2,256,256]{2,1,0:T(8,128)(2,1)S(1)}, bf16[2,256,256]{2,1,0:T(8,128)(2,1)S(1)}, u32[]{:S(2)}, u32[]{:S(2)}) collective-permute-start(bf16[2,256,256]{2,1,0:T(8,128)(2,1)S(1)} %get-tuple-element.203), channel_id=1, source_target_pairs={{0,1},{1,0},{2,6},{3,7},{4,5},{5,4},{6,2},{7,3},{8,9},{9,8},{10,14... | collective-permute-start | bytes 786440 | tf_op jit(solution)/shard_map/ppermute | solution.py:783
  77.9 6.4 %collective-permute-start.15 = (bf16[1,512,256]{2,1,0:T(8,128)(2,1)S(1)}, bf16[1,512,256]{2,1,0:T(8,128)(2,1)S(1)}, u32[]{:S(2)}, u32[]{:S(2)}) collective-permute-start(bf16[1,512,256]{2,1,0:T(8,128)(2,1)S(1)} %get-tuple-element.200), channel_id=1, source_target_pairs={{0,8},{1,9},{2,10},{3,11},{4,12},{5,13},{6,14},{7,15},{8,0},{9,1},... | collective-permute-start | bytes 786440 | tf_op jit(solution)/shard_map/ppermute | solution.py:783
  79.0 9.2 %collective-permute-start.13 = (bf16[2,480,256]{2,1,0:T(8,128)(2,1)S(1)}, bf16[2,480,256]{2,1,0:T(8,128)(2,1)S(1)}, u32[]{:S(2)}, u32[]{:S(2)}) collective-permute-start(bf16[2,480,256]{2,1,0:T(8,128)(2,1)S(1)} %get-tuple-element.197), channel_id=1, source_target_pairs={{0,1},{1,0},{2,6},{3,7},{4,5},{5,4},{6,2},{7,3},{8,9},{9,8},{10,14... | collective-permute-start | bytes 1474568 | tf_op jit(solution)/shard_map/ppermute | solution.py:783
  88.3 9.9 %collective-permute-start.18 = (bf16[1,480,256]{2,1,0:T(8,128)(2,1)S(1)}, bf16[1,480,256]{2,1,0:T(8,128)(2,1)S(1)}, u32[]{:S(2)}, u32[]{:S(2)}) collective-permute-start(bf16[1,480,256]{2,1,0:T(8,128)(2,1)S(1)} %get-tuple-element.207), channel_id=1, source_target_pairs={{0,4},{1,5},{2,3},{3,2},{4,0},{5,1},{6,7},{7,6},{8,12},{9,13},{10,... | collective-permute-start | bytes 737288 | tf_op jit(solution)/shard_map/ppermute | solution.py:783
  91.4 9.7 %collective-permute-start.22 = (bf16[1,256,256]{2,1,0:T(8,128)(2,1)S(1)}, bf16[1,256,256]{2,1,0:T(8,128)(2,1)S(1)}, u32[]{:S(2)}, u32[]{:S(2)}) collective-permute-start(bf16[1,256,256]{2,1,0:T(8,128)(2,1)S(1)} %get-tuple-element.211), channel_id=1, source_target_pairs={{0,4},{1,5},{2,3},{3,2},{4,0},{5,1},{6,7},{7,6},{8,12},{9,13},{10,... | collective-permute-start | bytes 393224 | tf_op jit(solution)/shard_map/ppermute | solution.py:783
  91.4 12.4 %collective-permute-start.21 = (bf16[1,512,256]{2,1,0:T(8,128)(2,1)S(1)}, bf16[1,512,256]{2,1,0:T(8,128)(2,1)S(1)}, u32[]{:S(2)}, u32[]{:S(2)}) collective-permute-start(bf16[1,512,256]{2,1,0:T(8,128)(2,1)S(1)} %shard_map.392.refs_2_.refs_0_), channel_id=1, source_target_pairs={{0,16},{1,17},{2,18},{3,19},{4,20},{5,21},{6,22},{7,23},{8,24},{9,... | collective-permute-start | bytes 786440 | tf_op jit(solution)/shard_map/ppermute | solution.py:783
  94.0 12.0 %collective-permute-start.20 = (bf16[2,768,256]{2,1,0:T(8,128)(2,1)S(1)}, bf16[2,768,256]{2,1,0:T(8,128)(2,1)S(1)}, u32[]{:S(2)}, u32[]{:S(2)}) collective-permute-start(bf16[2,768,256]{2,1,0:T(8,128)(2,1)S(1)} %get-tuple-element.210), channel_id=1, source_target_pairs={{0,1},{1,0},{2,6},{3,7},{4,5},{5,4},{6,2},{7,3},{8,9},{9,8},{10,14... | collective-permute-start | bytes 2359304 | tf_op jit(solution)/shard_map/ppermute | solution.py:783
  98.3 7.9 %collective-permute-start.19 = (bf16[1,240,256]{2,1,0:T(8,128)(2,1)S(1)}, bf16[1,240,256]{2,1,0:T(8,128)(2,1)S(1)}, u32[]{:S(2)}, u32[]{:S(2)}) collective-permute-start(bf16[1,240,256]{2,1,0:T(8,128)(2,1)S(1)} %get-tuple-element.209), channel_id=1, source_target_pairs={{0,8},{1,9},{2,10},{3,11},{4,12},{5,13},{6,14},{7,15},{8,0},{9,1},... | collective-permute-start | bytes 368648 | tf_op jit(solution)/shard_map/ppermute | solution.py:783
  101.1 18.8 %collective-permute-start.24 = (bf16[1,256,256]{2,1,0:T(8,128)(2,1)S(1)}, bf16[1,256,256]{2,1,0:T(8,128)(2,1)S(1)}, u32[]{:S(2)}, u32[]{:S(2)}) collective-permute-start(bf16[1,256,256]{2,1,0:T(8,128)(2,1)S(1)} %shard_map.395.refs_2_), channel_id=1, source_target_pairs={{0,16},{1,17},{2,18},{3,19},{4,20},{5,21},{6,22},{7,23},{8,24},{9,... | collective-permute-start | bytes 393224 | tf_op jit(solution)/shard_map/ppermute | solution.py:783
  103.9 9.4 %collective-permute-start.26 = (bf16[1,512,256]{2,1,0:T(8,128)(2,1)S(1)}, bf16[1,512,256]{2,1,0:T(8,128)(2,1)S(1)}, u32[]{:S(2)}, u32[]{:S(2)}) collective-permute-start(bf16[1,512,256]{2,1,0:T(8,128)(2,1)S(1)} %shard_map.396.refs_2_.refs_0_), channel_id=1, source_target_pairs={{0,8},{1,9},{2,10},{3,11},{4,12},{5,13},{6,14},{7,15},{8,0},{9,1},... | collective-permute-start | bytes 786440 | tf_op jit(solution)/shard_map/ppermute | solution.py:783
  106.2 13.6 %collective-permute-start.23 = (bf16[1,240,256]{2,1,0:T(8,128)(2,1)S(1)}, bf16[1,240,256]{2,1,0:T(8,128)(2,1)S(1)}, u32[]{:S(2)}, u32[]{:S(2)}) collective-permute-start(bf16[1,240,256]{2,1,0:T(8,128)(2,1)S(1)} %shard_map.398.refs_2_.refs_0_), channel_id=1, source_target_pairs={{0,16},{1,17},{2,18},{3,19},{4,20},{5,21},{6,22},{7,23},{8,24},{9,... | collective-permute-start | bytes 368648 | tf_op jit(solution)/shard_map/ppermute | solution.py:783
  107.9 10.8 %collective-permute-start.25 = (bf16[1,768,256]{2,1,0:T(8,128)(2,1)S(1)}, bf16[1,768,256]{2,1,0:T(8,128)(2,1)S(1)}, u32[]{:S(2)}, u32[]{:S(2)}) collective-permute-start(bf16[1,768,256]{2,1,0:T(8,128)(2,1)S(1)} %get-tuple-element.213), channel_id=1, source_target_pairs={{0,4},{1,5},{2,3},{3,2},{4,0},{5,1},{6,7},{7,6},{8,12},{9,13},{10,... | collective-permute-start | bytes 1179656 | tf_op jit(solution)/shard_map/ppermute | solution.py:783
  114.2 25.7 %collective-permute-start.32 = (bf16[1,1024,256]{2,1,0:T(8,128)(2,1)}, bf16[1,1024,256]{2,1,0:T(8,128)(2,1)}, u32[]{:S(2)}, u32[]{:S(2)}) collective-permute-start(bf16[1,1024,256]{2,1,0:T(8,128)(2,1)} %shard_map.399.refs_2_.refs_0_), channel_id=1, source_target_pairs={{0,4},{1,5},{2,6},{3,7},{4,0},{5,1},{6,2},{7,3},{8,12},{9,13},{10,... | collective-permute-start | bytes 1572872 | tf_op jit(solution)/shard_map/ppermute | solution.py:783
  118.8 7.0 %collective-permute-start.28 = (bf16[1,384,256]{2,1,0:T(8,128)(2,1)S(1)}, bf16[1,384,256]{2,1,0:T(8,128)(2,1)S(1)}, u32[]{:S(2)}, u32[]{:S(2)}) collective-permute-start(bf16[1,384,256]{2,1,0:T(8,128)(2,1)S(1)} %get-tuple-element.216), channel_id=1, source_target_pairs={{0,8},{1,9},{2,10},{3,11},{4,12},{5,13},{6,14},{7,15},{8,0},{9,1},... | collective-permute-start | bytes 589832 | tf_op jit(solution)/shard_map/ppermute | solution.py:783
  119.9 7.3 %collective-permute-start.27 = (bf16[1,240,256]{2,1,0:T(8,128)(2,1)S(1)}, bf16[1,240,256]{2,1,0:T(8,128)(2,1)S(1)}, u32[]{:S(2)}, u32[]{:S(2)}) collective-permute-start(bf16[1,240,256]{2,1,0:T(8,128)(2,1)S(1)} %get-tuple-element.215.refs_2_.refs_0_), channel_id=1, source_target_pairs={{0,8},{1,9},{2,10},{3,11},{4,12},{5,13},{6,14},{7,15},{8,0},{9,1},... | collective-permute-start | bytes 368648 | tf_op jit(solution)/shard_map/ppermute | solution.py:783
  121.1 8.2 %collective-permute-start.30 = (bf16[1,256,256]{2,1,0:T(8,128)(2,1)S(1)}, bf16[1,256,256]{2,1,0:T(8,128)(2,1)S(1)}, u32[]{:S(2)}, u32[]{:S(2)}) collective-permute-start(bf16[1,256,256]{2,1,0:T(8,128)(2,1)S(1)} %get-tuple-element.217.refs_0_), channel_id=1, source_target_pairs={{0,4},{1,5},{2,3},{3,2},{4,0},{5,1},{6,7},{7,6},{8,12},{9,13},{10,... | collective-permute-start | bytes 393224 | tf_op jit(solution)/shard_map/ppermute | solution.py:783
  125.9 11.7 %collective-permute-start.34 = (bf16[1,384,256]{2,1,0:T(8,128)(2,1)S(1)}, bf16[1,384,256]{2,1,0:T(8,128)(2,1)S(1)}, u32[]{:S(2)}, u32[]{:S(2)}) collective-permute-start(bf16[1,384,256]{2,1,0:T(8,128)(2,1)S(1)} %shard_map.402.refs_2_.refs_0_), channel_id=1, source_target_pairs={{0,16},{1,17},{2,18},{3,19},{4,20},{5,21},{6,22},{7,23},{8,24},{9,... | collective-permute-start | bytes 589832 | tf_op jit(solution)/shard_map/ppermute | solution.py:783
  127.3 9.0 %collective-permute-start.29 = (bf16[1,480,256]{2,1,0:T(8,128)(2,1)S(1)}, bf16[1,480,256]{2,1,0:T(8,128)(2,1)S(1)}, u32[]{:S(2)}, u32[]{:S(2)}) collective-permute-start(bf16[1,480,256]{2,1,0:T(8,128)(2,1)S(1)} %shard_map.403.refs_2_.refs_0_), channel_id=1, source_target_pairs={{0,4},{1,5},{2,3},{3,2},{4,0},{5,1},{6,7},{7,6},{8,12},{9,13},{10,... | collective-permute-start | bytes 737288 | tf_op jit(solution)/shard_map/ppermute | solution.py:783
  129.3 9.3 %collective-permute-start.33 = (bf16[2,256,256]{2,1,0:T(8,128)(2,1)S(1)}, bf16[2,256,256]{2,1,0:T(8,128)(2,1)S(1)}, u32[]{:S(2)}, u32[]{:S(2)}) collective-permute-start(bf16[2,256,256]{2,1,0:T(8,128)(2,1)S(1)} %shard_map.404.refs_2_.refs_0_), channel_id=1, source_target_pairs={{0,1},{1,0},{2,6},{3,7},{4,5},{5,4},{6,2},{7,3},{8,9},{9,8},{10,14... | collective-permute-start | bytes 786440 | tf_op jit(solution)/shard_map/ppermute | solution.py:783
  136.3 8.9 %collective-permute-start.31 = (bf16[2,480,256]{2,1,0:T(8,128)(2,1)S(1)}, bf16[2,480,256]{2,1,0:T(8,128)(2,1)S(1)}, u32[]{:S(2)}, u32[]{:S(2)}) collective-permute-start(bf16[2,480,256]{2,1,0:T(8,128)(2,1)S(1)} %shard_map.405.refs_2_.refs_0_), channel_id=1, source_target_pairs={{0,1},{1,0},{2,6},{3,7},{4,5},{5,4},{6,2},{7,3},{8,9},{9,8},{10,14... | collective-permute-start | bytes 1474568 | tf_op jit(solution)/shard_map/ppermute | solution.py:783
  137.7 7.7 %collective-permute-start.36 = (bf16[1,384,256]{2,1,0:T(8,128)(2,1)S(1)}, bf16[1,384,256]{2,1,0:T(8,128)(2,1)S(1)}, u32[]{:S(2)}, u32[]{:S(2)}) collective-permute-start(bf16[1,384,256]{2,1,0:T(8,128)(2,1)S(1)} %shard_map.406.refs_2_.refs_0_), channel_id=1, source_target_pairs={{0,8},{1,9},{2,10},{3,11},{4,12},{5,13},{6,14},{7,15},{8,0},{9,1},... | collective-permute-start | bytes 589832 | tf_op jit(solution)/shard_map/ppermute | solution.py:783
  138.6 11.9 %collective-permute-start.38 = (bf16[4,256,256]{2,1,0:T(8,128)(2,1)S(1)}, bf16[4,256,256]{2,1,0:T(8,128)(2,1)S(1)}, u32[]{:S(2)}, u32[]{:S(2)}) collective-permute-start(bf16[4,256,256]{2,1,0:T(8,128)(2,1)S(1)} %shard_map.407.refs_2_.refs_0_), channel_id=1, source_target_pairs={{0,8},{1,9},{2,10},{3,11},{4,12},{5,13},{6,14},{7,15},{8,0},{9,1},... | collective-permute-start | bytes 1572872 | tf_op jit(solution)/shard_map/ppermute | solution.py:783
  141.2 10.4 %collective-permute-start.40 = (bf16[2,1024,256]{2,1,0:T(8,128)(2,1)S(1)}, bf16[2,1024,256]{2,1,0:T(8,128)(2,1)S(1)}, u32[]{:S(2)}, u32[]{:S(2)}) collective-permute-start(bf16[2,1024,256]{2,1,0:T(8,128)(2,1)S(1)} %shard_map.408.refs_2_.refs_0_), channel_id=1, source_target_pairs={{0,2},{1,3},{2,0},{3,1},{4,6},{5,7},{6,4},{7,5},{8,10},{9,11},{10,... | collective-permute-start | bytes 3145736 | tf_op jit(solution)/shard_map/ppermute | solution.py:783
  145.4 11.8 %collective-permute-start.37 = (bf16[1,768,256]{2,1,0:T(8,128)(2,1)S(1)}, bf16[1,768,256]{2,1,0:T(8,128)(2,1)S(1)}, u32[]{:S(2)}, u32[]{:S(2)}) collective-permute-start(bf16[1,768,256]{2,1,0:T(8,128)(2,1)S(1)} %shard_map.410.refs_2_.refs_0_), channel_id=1, source_target_pairs={{0,4},{1,5},{2,6},{3,7},{4,0},{5,1},{6,2},{7,3},{8,12},{9,13},{10,... | collective-permute-start | bytes 1179656 | tf_op jit(solution)/shard_map/ppermute | solution.py:783
  (32 other events, 219.5 us)
